TPU v7x, 32 devices: a whole 2x2x4 slice. The times are simulated.
32 devices in a mesh: row: 4 (over z), col: 8 (over y, x, core).
Axes of the slice: x: 2, y: 2, z: 4, core: 2. Of those that a mesh axis runs over, the one named last changes fastest.
Arguments:
- block_in: bfloat16 [4, 1024, 2048], P(None, 'row', 'col'), may hold values from -6 to 6
- grad_out: bfloat16 [4, 1024, 2048], P(None, 'row', 'col'), may hold values from -6 to 6
- gain_attn: float32 [2048], replicated, may hold values from 0.25 to 1.75
- gain_ffn: float32 [2048], replicated, may hold values from 0.25 to 1.75
- router_attn: bfloat16 [2048, 8], replicated, may hold values from -0.125 to 0.125
- router_ffn: bfloat16 [2048, 8], replicated, may hold values from -0.125 to 0.125
- w_query: bfloat16 [8, 2048, 2048], P(None, 'row', 'col'), may hold values from -0.125 to 0.125
- key_weight: bfloat16 [2048, 2048], P('row', 'col'), may hold values from -0.125 to 0.125
- value_weight: bfloat16 [2048, 2048], P('row', 'col'), may hold values from -0.125 to 0.125
- w_out: bfloat16 [8, 2048, 2048], P(None, 'col', 'row'), may hold values from -0.75 to 0.75
- w_gate: bfloat16 [8, 2048, 5632], P(None, 'row', 'col'), may hold values from -0.125 to 0.125
- w_up: bfloat16 [8, 2048, 5632], P(None, 'row', 'col'), may hold values from -0.125 to 0.125
- w_down: bfloat16 [8, 5632, 2048], P(None, 'col', 'row'), may hold values from -0.078125 to 0.078125
- routes_attn: int32 [4, 1024, 2], P(None, 'row'), may hold values from 0 to 7, all different within a row
- routes_ffn: int32 [4, 1024, 2], P(None, 'row'), may hold values from 0 to 7, all different within a row
- order_attn: int32 [4, 4, 512], P(None, 'row'), may hold values from 0 to 511, each once within a row
- order_ffn: int32 [4, 4, 512], P(None, 'row'), may hold values from 0 to 511, each once within a row
- block_ids: int32 [4, 1024], replicated, may hold values from 0 to 9, never falling along the last dimension, each value on 1 to 256 neighbouring positions
Outputs:
- block_out: bfloat16 [4, 1024, 2048], P(None, 'row', 'col')
- grad_in: float32 [4, 1024, 2048], P(None, 'row', 'col')
- grad_gain_attn: float32 [2048], replicated
- grad_gain_ffn: float32 [2048], replicated
- grad_router_attn: float32 [2048, 8], replicated
- grad_router_ffn: float32 [2048, 8], replicated
- grad_w_query: float32 [8, 2048, 2048], P(None, 'row', 'col')
- grad_w_key: float32 [2048, 2048], P('row', 'col')
- grad_w_value: float32 [2048, 2048], P('row', 'col')
- grad_w_out: float32 [8, 2048, 2048], P(None, 'col', 'row')
- grad_w_gate: float32 [8, 2048, 5632], P(None, 'row', 'col')
- grad_w_up: float32 [8, 2048, 5632], P(None, 'row', 'col')
- grad_w_down: float32 [8, 5632, 2048], P(None, 'col', 'row')
Inputs may be any that keep to these rules, and one draw needn't show every extreme that they name: `routes_attn`: each token names two different experts. `routes_ffn`: each token names two different experts. `order_attn`: each row along the last dimension is a permutation of the pair numbers of one routing block. `order_ffn`: each row along the last dimension is a permutation of the pair numbers of one routing block. `block_ids`: along a sequence the attention block ids never fall and start at 0; each id covers consecutive positions, at most 256 and at most half of a sequence.
All inputs are finite; a program needn't handle non-finite values.
Results may differ from a plain program's by a relative error of at most 0.02.
Values may be sent and summed in bfloat16 or wider, within the bound.
No kernel may reach another device: no remote copies, remote signals or barrier semaphores. Data moves between devices by JAX's collectives and lax.ppermute only.
A program may use at most 640 MiB of HBM per device.

v0:
```python
from functools import partial
import math

import jax
import jax.numpy as jnp
from jax import lax
from jax.sharding import PartitionSpec as P

HEAD_DIM = 128


EPSILON = 1e-05
ROPE_BASE = 10000.0
MASKED_SCORE = -1e30


def rope_tables(positions, width):
    half_width = width // 2
    frequency = jnp.exp(
        -math.log(ROPE_BASE) * jnp.arange(half_width, dtype=jnp.float32) * (2.0 / width)
    )
    angles = positions.astype(jnp.float32)[..., None] * frequency
    angles = jnp.concatenate([angles, angles], axis=-1)
    return (jnp.cos(angles), jnp.sin(angles))


def rotate(values, cosine, sine, sign):
    half_width = values.shape[-1] // 2
    turned = jnp.concatenate([-values[..., half_width:], values[..., :half_width]], axis=-1)
    return values * cosine[..., None, :] + sign * turned * sine[..., None, :]


def slot_table(pair_experts, pair_order, capacity, experts):
    pair_count = pair_experts.shape[0]
    same_expert = pair_experts[:, None] == pair_experts[None, :]
    earlier = pair_order[None, :] < pair_order[:, None]
    rank_count = jnp.sum(jnp.logical_and(same_expert, earlier).astype(jnp.int32), axis=1)
    keep_mask = rank_count < capacity
    target = jnp.where(keep_mask, pair_experts * capacity + rank_count, -1)
    matches = target[:, None] == jnp.arange(experts * capacity, dtype=jnp.int32)[None, :]
    pair_ids = jnp.arange(pair_count, dtype=jnp.int32)
    source = jnp.sum(jnp.where(matches, pair_ids[:, None], 0), axis=0)
    filled = jnp.any(matches, axis=0)
    return (target, keep_mask, source, filled)


def local_tables(routes, order, capacity, experts):
    seq_count = routes.shape[0]
    pairs = routes.reshape(seq_count, -1)
    ranking = order.reshape(seq_count, -1)
    target, keep_mask, source, filled = jax.vmap(
        partial(slot_table, capacity=capacity, experts=experts)
    )(pairs, ranking)
    return (jnp.where(keep_mask, target, 0), keep_mask, source, filled)


def normalize_rows(wide):
    inverse = lax.rsqrt(jnp.mean(wide * wide, axis=-1, keepdims=True) + EPSILON)
    return (wide * inverse, inverse)


def route_gates(hidden_state, router_matrix, routes):
    router_logits = jnp.einsum(
        "std,de->ste", hidden_state, router_matrix, preferred_element_type=jnp.float32
    )
    return jax.nn.softmax(jnp.take_along_axis(router_logits, routes, axis=-1), axis=-1)


def dispatch_rows(hidden_state, source, filled):
    slot_rows = jnp.take_along_axis(hidden_state, (source // 2)[..., None], axis=1)
    return jnp.where(filled[..., None], slot_rows, jnp.zeros((), hidden_state.dtype))


def pair_weights(gate_probs, keep_mask):
    return jnp.where(keep_mask, gate_probs.reshape(keep_mask.shape), 0.0)


def combine_rows(slot_values, target, weights):
    picked = jnp.take_along_axis(slot_values, target[..., None], axis=1)
    summed = picked * weights[..., None]
    return jnp.sum(summed.reshape(summed.shape[0], -1, 2, summed.shape[-1]), axis=2)


def combine_back(slot_values, target, keep_mask, weights, grad_rows, source, filled):
    seq_count = target.shape[0]
    width = grad_rows.shape[-1]
    slot_weight = jnp.where(filled, jnp.take_along_axis(weights, source, axis=1), 0.0)
    token_rows = jnp.take_along_axis(grad_rows, (source // 2)[..., None], axis=1)
    slot_grad = (token_rows * slot_weight[..., None]).astype(jnp.bfloat16)
    picked = jnp.take_along_axis(slot_values, target[..., None], axis=1)
    dots = jnp.sum(picked.reshape(seq_count, -1, 2, width) * grad_rows[:, :, None, :], axis=-1)
    return (slot_grad, jnp.where(keep_mask.reshape(dots.shape), dots, 0.0))


def gather_back(slot_grads, target, keep_mask):
    picked = jnp.take_along_axis(slot_grads, target[..., None], axis=1)
    picked = jnp.where(keep_mask[..., None], picked, 0.0)
    return jnp.sum(picked.reshape(picked.shape[0], -1, 2, picked.shape[-1]), axis=2)


def gate_back(gate_probs, dots):
    return gate_probs * (dots - jnp.sum(gate_probs * dots, axis=-1, keepdims=True))


def router_back(hidden_state, router_matrix, routes, dchosen):
    experts = router_matrix.shape[1]
    onehot = routes[..., None] == jnp.arange(experts, dtype=jnp.int32)
    dlogits = jnp.sum(jnp.where(onehot, dchosen[..., None], 0.0), axis=-2).astype(jnp.bfloat16)
    grad_router = jnp.einsum(
        "std,ste->de", hidden_state, dlogits, preferred_element_type=jnp.float32
    )
    grad_hidden = jnp.einsum(
        "ste,de->std", dlogits, router_matrix, preferred_element_type=jnp.float32
    )
    return (grad_router, grad_hidden)


def norm_back(normed, inverse, gain, grad_hidden):
    grad_normed = grad_hidden * gain
    grad_wide = inverse * (
        grad_normed - normed * jnp.mean(grad_normed * normed, axis=-1, keepdims=True)
    )
    return (grad_wide, jnp.sum(grad_hidden * normed, axis=(0, 1)))


def masked_scores(queries, key_rows, query_blocks, key_blocks):
    raw = jnp.einsum("qhd,khd->hqk", queries, key_rows, preferred_element_type=jnp.float32)
    allowed = key_blocks[None, None, :] <= query_blocks[None, :, None]
    return jnp.where(allowed, raw * HEAD_DIM ** (-0.5), MASKED_SCORE)


def full_rows(part):
    return lax.all_gather(part, "col", axis=2, tiled=True)


def branch_sum(part):
    return lax.psum_scatter(part, "col", scatter_dimension=2, tiled=True)


def hidden_sum(part, dots):
    return lax.psum((part, dots), "col")


def col_share(whole, width):
    return lax.dynamic_slice_in_dim(whole, lax.axis_index("col") * width, width, 2)


def per_device(
    block_in,
    grad_out,
    gain_attn,
    gain_ffn,
    router_attn,
    router_ffn,
    w_query,
    key_weight,
    value_weight,
    w_out,
    w_gate,
    w_up,
    w_down,
    routes_attn,
    routes_ffn,
    order_attn,
    order_ffn,
    block_ids,
):
    seq_count, seq_dev, share_width = block_in.shape
    experts = w_query.shape[0]
    capacity = 18 * seq_dev // (8 * experts)
    slot_count = experts * capacity
    head_cols = key_weight.shape[1]
    heads_local = head_cols // HEAD_DIM
    seq_len = block_ids.shape[1]
    row_start = lax.axis_index("row") * seq_dev
    positions = row_start + jnp.arange(seq_dev, dtype=jnp.int32)
    tok_cos, tok_sin = rope_tables(positions, HEAD_DIM)
    target_a, keep_a, source_a, filled_a = local_tables(routes_attn, order_attn, capacity, experts)
    target_f, keep_f, source_f, filled_f = local_tables(routes_ffn, order_ffn, capacity, experts)
    in_wide = full_rows(block_in).astype(jnp.float32)
    normed_attn, inverse_attn = normalize_rows(in_wide)
    attention_hidden = (normed_attn * gain_attn).astype(jnp.bfloat16)
    gates_attn = route_gates(attention_hidden, router_attn, routes_attn)
    query_all, key_all, value_all, out_all = (
        lax.all_gather(w_query, "row", axis=1, tiled=True),
        lax.all_gather(key_weight, "row", axis=0, tiled=True),
        lax.all_gather(value_weight, "row", axis=0, tiled=True),
        lax.all_gather(w_out, "row", axis=2, tiled=True),
    )
    key_before_rotation = jnp.einsum(
        "std,df->stf", attention_hidden, key_all, preferred_element_type=jnp.float32
    )
    key_rot = rotate(
        key_before_rotation.reshape(seq_count, seq_dev, heads_local, HEAD_DIM),
        tok_cos,
        tok_sin,
        1.0,
    )
    key_rot = key_rot.reshape(seq_count, seq_dev, head_cols).astype(jnp.bfloat16)
    value_token_rows = jnp.einsum(
        "std,df->stf", attention_hidden, value_all, preferred_element_type=jnp.float32
    ).astype(jnp.bfloat16)
    keys_seq, values_seq = (
        lax.all_gather(key_rot, "row", axis=1, tiled=True),
        lax.all_gather(value_token_rows, "row", axis=1, tiled=True),
    )
    slot_in_attn = dispatch_rows(attention_hidden, source_a, filled_a).reshape(
        seq_count, experts, capacity, -1
    )
    slot_pos = row_start + source_a // 2
    slot_cos, slot_sin = rope_tables(slot_pos, HEAD_DIM)
    query_pre = jnp.einsum(
        "secd,edf->secf", slot_in_attn, query_all, preferred_element_type=jnp.float32
    )
    queries = rotate(
        query_pre.reshape(seq_count, slot_count, heads_local, HEAD_DIM), slot_cos, slot_sin, 1.0
    )
    queries = queries.astype(jnp.bfloat16)
    query_blocks = jnp.take_along_axis(block_ids, slot_pos, axis=1)
    key_heads = keys_seq.reshape(seq_count, seq_len, heads_local, HEAD_DIM)
    value_heads = values_seq.reshape(seq_count, seq_len, heads_local, HEAD_DIM)
    attended_list = []
    log_totals = []
    for seq_index in range(seq_count):
        scores = masked_scores(
            queries[seq_index], key_heads[seq_index], query_blocks[seq_index], block_ids[seq_index]
        )
        row_max = jnp.max(scores, axis=-1, keepdims=True)
        exp_terms = jnp.exp(scores - row_max)
        totals = jnp.sum(exp_terms, axis=-1, keepdims=True)
        soft_weights = (exp_terms / totals).astype(jnp.bfloat16)
        log_totals.append(row_max + jnp.log(totals))
        attended_list.append(
            jnp.einsum(
                "hqk,khd->qhd",
                soft_weights,
                value_heads[seq_index],
                preferred_element_type=jnp.float32,
            )
        )
    attended = (
        jnp.stack(attended_list)
        .reshape(seq_count, experts, capacity, head_cols)
        .astype(jnp.bfloat16)
    )
    out_slots = jnp.einsum("secf,efd->secd", attended, out_all, preferred_element_type=jnp.float32)
    out_slots = out_slots.reshape(seq_count, slot_count, -1)
    weights_attn = pair_weights(gates_attn, keep_a)
    mid = block_in.astype(jnp.float32) + branch_sum(combine_rows(out_slots, target_a, weights_attn))
    mid_wide = full_rows(mid.astype(jnp.bfloat16)).astype(jnp.float32)
    normed_ffn, inverse_ffn = normalize_rows(mid_wide)
    hidden_ffn = (normed_ffn * gain_ffn).astype(jnp.bfloat16)
    gates_ffn = route_gates(hidden_ffn, router_ffn, routes_ffn)
    gate_all, up_all, down_all = (
        lax.all_gather(w_gate, "row", axis=1, tiled=True),
        lax.all_gather(w_up, "row", axis=1, tiled=True),
        lax.all_gather(w_down, "row", axis=2, tiled=True),
    )
    slot_in_ffn = dispatch_rows(hidden_ffn, source_f, filled_f).reshape(
        seq_count, experts, capacity, -1
    )
    gate_pre = jnp.einsum(
        "secd,edf->secf", slot_in_ffn, gate_all, preferred_element_type=jnp.float32
    )
    up_pre = jnp.einsum("secd,edf->secf", slot_in_ffn, up_all, preferred_element_type=jnp.float32)
    gate_sig = jax.nn.sigmoid(gate_pre)
    gate_silu = gate_pre * gate_sig
    activated = (gate_silu * up_pre).astype(jnp.bfloat16)
    down_slots = jnp.einsum(
        "secf,efd->secd", activated, down_all, preferred_element_type=jnp.float32
    )
    down_slots = down_slots.reshape(seq_count, slot_count, -1)
    weights_ffn = pair_weights(gates_ffn, keep_f)
    block_out = (mid + branch_sum(combine_rows(down_slots, target_f, weights_ffn))).astype(
        jnp.bfloat16
    )
    out_wide = full_rows(grad_out).astype(jnp.float32)
    gate_use, up_use, down_use = (
        lax.all_gather(w_gate, "row", axis=1, tiled=True),
        lax.all_gather(w_up, "row", axis=1, tiled=True),
        lax.all_gather(w_down, "row", axis=2, tiled=True),
    )
    grad_down, dots_ffn = combine_back(
        down_slots, target_f, keep_f, weights_ffn, out_wide, source_f, filled_f
    )
    grad_down = grad_down.reshape(seq_count, experts, capacity, -1)
    grad_act = jnp.einsum("secd,efd->secf", grad_down, down_use, preferred_element_type=jnp.float32)
    grad_gate = (grad_act * up_pre * (gate_sig * (1.0 + gate_pre * (1.0 - gate_sig)))).astype(
        jnp.bfloat16
    )
    grad_up = (grad_act * gate_silu).astype(jnp.bfloat16)
    grad_w_down = jnp.einsum(
        "secf,secd->efd", activated, grad_down, preferred_element_type=jnp.float32
    )
    grad_w_gate = jnp.einsum(
        "secd,secf->edf", slot_in_ffn, grad_gate, preferred_element_type=jnp.float32
    )
    grad_w_up = jnp.einsum(
        "secd,secf->edf", slot_in_ffn, grad_up, preferred_element_type=jnp.float32
    )
    grad_gate_own, grad_up_own, grad_down_own = (
        lax.psum_scatter(
            grad_w_gate.astype(jnp.bfloat16), "row", scatter_dimension=1, tiled=True
        ).astype(jnp.float32),
        lax.psum_scatter(
            grad_w_up.astype(jnp.bfloat16), "row", scatter_dimension=1, tiled=True
        ).astype(jnp.float32),
        lax.psum_scatter(
            grad_w_down.astype(jnp.bfloat16), "row", scatter_dimension=2, tiled=True
        ).astype(jnp.float32),
    )
    slot_grad_ffn = jnp.einsum(
        "secf,edf->secd", grad_gate, gate_use, preferred_element_type=jnp.float32
    ) + jnp.einsum("secf,edf->secd", grad_up, up_use, preferred_element_type=jnp.float32)
    slot_grad_ffn = slot_grad_ffn.reshape(seq_count, slot_count, -1)
    part_ffn, dots_ffn = hidden_sum(gather_back(slot_grad_ffn, target_f, keep_f), dots_ffn)
    grad_router_ffn, router_part_ffn = router_back(
        hidden_ffn, router_ffn, routes_ffn, gate_back(gates_ffn, dots_ffn)
    )
    grad_mid_wide, grad_gain_ffn = norm_back(
        normed_ffn, inverse_ffn, gain_ffn, part_ffn + router_part_ffn
    )
    grad_mid = grad_out.astype(jnp.float32) + col_share(grad_mid_wide, share_width)
    mid_grad_wide = lax.all_gather(grad_mid, "col", axis=2, tiled=True)
    query_use, key_use, value_use, out_use, keys_use, values_use = (
        lax.all_gather(w_query, "row", axis=1, tiled=True),
        lax.all_gather(key_weight, "row", axis=0, tiled=True),
        lax.all_gather(value_weight, "row", axis=0, tiled=True),
        lax.all_gather(w_out, "row", axis=2, tiled=True),
        lax.all_gather(key_rot, "row", axis=1, tiled=True),
        lax.all_gather(value_token_rows, "row", axis=1, tiled=True),
    )
    grad_outslots, dots_attn = combine_back(
        out_slots, target_a, keep_a, weights_attn, mid_grad_wide, source_a, filled_a
    )
    grad_outslots = grad_outslots.reshape(seq_count, experts, capacity, -1)
    grad_attended = jnp.einsum(
        "secd,efd->secf", grad_outslots, out_use, preferred_element_type=jnp.float32
    ).astype(jnp.bfloat16)
    grad_w_out = jnp.einsum(
        "secf,secd->efd", attended, grad_outslots, preferred_element_type=jnp.float32
    )
    grad_att_heads = grad_attended.reshape(seq_count, slot_count, heads_local, HEAD_DIM)
    key_use_heads = keys_use.reshape(seq_count, seq_len, heads_local, HEAD_DIM)
    value_use_heads = values_use.reshape(seq_count, seq_len, heads_local, HEAD_DIM)
    grad_query_list = []
    grad_key_list = []
    grad_value_list = []
    for seq_index in range(seq_count):
        scores = masked_scores(
            queries[seq_index],
            key_use_heads[seq_index],
            query_blocks[seq_index],
            block_ids[seq_index],
        )
        soft_full = jnp.exp(scores - log_totals[seq_index])
        grad_soft = jnp.einsum(
            "qhd,khd->hqk",
            grad_att_heads[seq_index],
            value_use_heads[seq_index],
            preferred_element_type=jnp.float32,
        )
        row_inner = jnp.sum(soft_full * grad_soft, axis=-1, keepdims=True)
        grad_scores = (soft_full * (grad_soft - row_inner) * HEAD_DIM ** (-0.5)).astype(
            jnp.bfloat16
        )
        grad_query_list.append(
            jnp.einsum(
                "hqk,khd->qhd",
                grad_scores,
                key_use_heads[seq_index],
                preferred_element_type=jnp.float32,
            )
        )
        grad_key_list.append(
            jnp.einsum(
                "hqk,qhd->khd", grad_scores, queries[seq_index], preferred_element_type=jnp.float32
            )
        )
        grad_value_list.append(
            jnp.einsum(
                "hqk,qhd->khd",
                soft_full.astype(jnp.bfloat16),
                grad_att_heads[seq_index],
                preferred_element_type=jnp.float32,
            )
        )
    grad_keys_seq = jnp.stack(grad_key_list).reshape(seq_count, seq_len, head_cols)
    grad_values_seq = jnp.stack(grad_value_list).reshape(seq_count, seq_len, head_cols)
    grad_keys, grad_values = (
        lax.psum_scatter(
            grad_keys_seq.astype(jnp.bfloat16), "row", scatter_dimension=1, tiled=True
        ).astype(jnp.float32),
        lax.psum_scatter(
            grad_values_seq.astype(jnp.bfloat16), "row", scatter_dimension=1, tiled=True
        ).astype(jnp.float32),
    )
    grad_key_pre = rotate(
        grad_keys.reshape(seq_count, seq_dev, heads_local, HEAD_DIM), tok_cos, tok_sin, -1.0
    )
    grad_key_pre = grad_key_pre.reshape(seq_count, seq_dev, head_cols).astype(jnp.bfloat16)
    grad_value_pre = grad_values.astype(jnp.bfloat16)
    grad_query_pre = rotate(jnp.stack(grad_query_list), slot_cos, slot_sin, -1.0)
    grad_query_pre = grad_query_pre.reshape(seq_count, experts, capacity, head_cols).astype(
        jnp.bfloat16
    )
    grad_w_query = jnp.einsum(
        "secd,secf->edf", slot_in_attn, grad_query_pre, preferred_element_type=jnp.float32
    )
    grad_w_key = jnp.einsum(
        "std,stf->df", attention_hidden, grad_key_pre, preferred_element_type=jnp.float32
    )
    grad_w_value = jnp.einsum(
        "std,stf->df", attention_hidden, grad_value_pre, preferred_element_type=jnp.float32
    )
    grad_query_own, grad_key_own, grad_value_own, grad_out_own = (
        lax.psum_scatter(
            grad_w_query.astype(jnp.bfloat16), "row", scatter_dimension=1, tiled=True
        ).astype(jnp.float32),
        lax.psum_scatter(
            grad_w_key.astype(jnp.bfloat16), "row", scatter_dimension=0, tiled=True
        ).astype(jnp.float32),
        lax.psum_scatter(
            grad_w_value.astype(jnp.bfloat16), "row", scatter_dimension=0, tiled=True
        ).astype(jnp.float32),
        lax.psum_scatter(
            grad_w_out.astype(jnp.bfloat16), "row", scatter_dimension=2, tiled=True
        ).astype(jnp.float32),
    )
    slot_grad_attn = jnp.einsum(
        "secf,edf->secd", grad_query_pre, query_use, preferred_element_type=jnp.float32
    )
    slot_grad_attn = slot_grad_attn.reshape(seq_count, slot_count, -1)
    token_part = (
        gather_back(slot_grad_attn, target_a, keep_a)
        + jnp.einsum("stf,df->std", grad_key_pre, key_use, preferred_element_type=jnp.float32)
        + jnp.einsum("stf,df->std", grad_value_pre, value_use, preferred_element_type=jnp.float32)
    )
    part_attn, dots_attn = hidden_sum(token_part, dots_attn)
    grad_router_attn, router_part_attn = router_back(
        attention_hidden, router_attn, routes_attn, gate_back(gates_attn, dots_attn)
    )
    grad_in_wide, grad_gain_attn = norm_back(
        normed_attn, inverse_attn, gain_attn, part_attn + router_part_attn
    )
    grad_in = grad_mid + col_share(grad_in_wide, share_width)
    gain_attn_sum, gain_ffn_sum, router_attn_sum, router_ffn_sum = (
        lax.psum(grad_gain_attn.astype(jnp.bfloat16), "row").astype(jnp.float32),
        lax.psum(grad_gain_ffn.astype(jnp.bfloat16), "row").astype(jnp.float32),
        lax.psum(grad_router_attn.astype(jnp.bfloat16), "row").astype(jnp.float32),
        lax.psum(grad_router_ffn.astype(jnp.bfloat16), "row").astype(jnp.float32),
    )
    return (
        block_out,
        grad_in,
        gain_attn_sum,
        gain_ffn_sum,
        router_attn_sum,
        router_ffn_sum,
        grad_query_own,
        grad_key_own,
        grad_value_own,
        grad_out_own,
        grad_gate_own,
        grad_up_own,
        grad_down_own,
    )


def solution(mesh):
    in_specs = (
        P(None, "row", "col"),
        P(None, "row", "col"),
        P(),
        P(),
        P(),
        P(),
        P(None, "row", "col"),
        P("row", "col"),
        P("row", "col"),
        P(None, "col", "row"),
        P(None, "row", "col"),
        P(None, "row", "col"),
        P(None, "col", "row"),
        P(None, "row", None),
        P(None, "row", None),
        P(None, "row", None),
        P(None, "row", None),
        P(),
    )
    out_specs = (
        P(None, "row", "col"),
        P(None, "row", "col"),
        P(),
        P(),
        P(),
        P(),
        P(None, "row", "col"),
        P("row", "col"),
        P("row", "col"),
        P(None, "col", "row"),
        P(None, "row", "col"),
        P(None, "row", "col"),
        P(None, "col", "row"),
    )
    return jax.shard_map(
        per_device, mesh=mesh, in_specs=in_specs, out_specs=out_specs, check_vma=False
    )
```

profile of v0, /device:TPU:0, one launch (start us, length us, event | category | flops | bytes accessed | tf_op | source)
XLA Modules:
  0.0 4655.1 jit_solution(17053334046986615791)
XLA Ops:
  10.6 39.5 all-gather.14.cloned.1.call-done
  59.7 19.9 all-gather.16.cloned.1.call-done
  85.5 23.8 all-gather.22.cloned.1.call-done
  120.3 18.9 gather_fusion
  153.1 48.8 %gather_fusion.1 = bf16[2304,2048]{1,0:T(8,128)(2,1)} fusion(bf16[4,256,2048]{2,1,0:T(8,128)(2,1)} %get-tuple-element.45, s32[2304]{0:T(1024)S(1)} %reshape.855), kind=kCustom, calls=%fused_computation.clone | custom fusion | bytes 18892800 | tf_op jit(solution)/shard_map/jit(take_along_axis)/gather | solution.py:70
  239.6 113.8 %all-gather.20.cloned.1.call-done = bf16[8,2048,256]{2,1,0:T(8,128)(2,1)} async-done(((bf16[8,512,256]{2,1,0:T(8,128)(2,1)}), bf16[8,2048,256]{2,1,0:T(8,128)(2,1)}) %all-gather.20.cloned.1.call-update) | async-done | bytes 8388624 | tf_op jit(solution)/shard_map/all_gather | solution.py:185
  389.8 113.0 %all-gather.26.cloned.1.call-done = bf16[8,256,2048]{2,1,0:T(8,128)(2,1)} async-done(((bf16[8,256,512]{2,1,0:T(8,128)(2,1)}), bf16[8,256,2048]{2,1,0:T(8,128)(2,1)}) %all-gather.26.cloned.1.call-update) | async-done | bytes 8388624 | tf_op jit(solution)/shard_map/all_gather | solution.py:188
  514.9 51.3 %gather_fusion.2 = f32[2048,2048]{1,0:T(8,128)} fusion(f32[4,576,2048]{2,1,0:T(8,128)} %bitcast.463, s32[2048]{0:T(1024)S(1)} %bitcast.465), kind=kCustom, calls=%fused_computation.1.clone | custom fusion | bytes 33570816 | tf_op jit(solution)/shard_map/jit(take_along_axis)/gather | solution.py:79
  577.8 20.0 reshape.743
  597.9 24.9 reduce_sum.288
  623.6 68.8 %reduce-scatter.12.cloned.1.call-done = f32[4,256,256]{2,1,0:T(8,128)} async-done(((f32[4,256,2048]{2,1,0:T(8,128)}), f32[4,256,256]{2,1,0:T(8,128)}) %reduce-scatter.12.cloned.1.call-update) | async-done | bytes 1048592 | tf_op jit(solution)/shard_map/reduce_scatter | solution.py:137
  704.1 27.8 all-gather.36.cloned.1.call-done
  742.4 20.8 mul.476
  769.9 51.0 %gather_fusion.7 = f32[2304,2048]{1,0:T(8,128)} fusion(f32[4,256,2048]{2,1,0:T(8,128)} %convert_element_type.219, s32[2304]{0:T(1024)S(1)} %reshape.868), kind=kCustom, calls=%fused_computation.3.clone | custom fusion | bytes 37767168 | tf_op jit(solution)/shard_map/jit(take_along_axis)/gather | solution.py:88
  830.3 49.2 %gather_fusion.4 = bf16[2304,2048]{1,0:T(8,128)(2,1)} fusion(bf16[4,256,2048]{2,1,0:T(8,128)(2,1)} %get-tuple-element.47, s32[2304]{0:T(1024)S(1)} %reshape.868), kind=kCustom, calls=%fused_computation.5.clone | custom fusion | bytes 18892800 | tf_op jit(solution)/shard_map/jit(take_along_axis)/gather | solution.py:70
  909.4 255.3 %all-gather.30.cloned.1.call-done = bf16[8,2048,704]{1,2,0:T(8,128)(2,1)} async-done(((bf16[8,512,704]{1,2,0:T(8,128)(2,1)}), bf16[8,2048,704]{1,2,0:T(8,128)(2,1)}) %all-gather.30.cloned.1.call-update) | async-done | bytes 23068688 | tf_op jit(solution)/shard_map/all_gather | solution.py:255
  1164.6 19.9 fusion.10
  1184.5 371.1 %all-gather.32.cloned.1.call-done = bf16[8,2048,704]{1,2,0:T(8,128)(2,1)} async-done(((bf16[8,512,704]{1,2,0:T(8,128)(2,1)}), bf16[8,2048,704]{1,2,0:T(8,128)(2,1)}) %all-gather.32.cloned.1.call-update) | async-done | bytes 23068688 | tf_op jit(solution)/shard_map/all_gather | solution.py:256
  1555.6 27.6 fusion.39
  1583.2 363.5 %all-gather.34.cloned.1.call-done = bf16[8,704,2048]{2,1,0:T(8,128)(2,1)} async-done(((bf16[8,704,512]{2,1,0:T(8,128)(2,1)}), bf16[8,704,2048]{2,1,0:T(8,128)(2,1)}) %all-gather.34.cloned.1.call-update) | async-done | bytes 23068688 | tf_op jit(solution)/shard_map/all_gather | solution.py:257
  1976.2 51.2 %gather_fusion.5 = f32[2048,2048]{1,0:T(8,128)} fusion(f32[4,576,2048]{2,1,0:T(8,128)} %bitcast.464, s32[2048]{0:T(1024)S(1)} %bitcast.467), kind=kCustom, calls=%fused_computation.6.clone | custom fusion | bytes 33570816 | tf_op jit(solution)/shard_map/jit(take_along_axis)/gather | solution.py:79
  2054.2 19.0 gather_fusion.8
  2085.0 21.6 fusion.37
  2123.3 26.8 add_bitcast_fusion
  2163.0 51.5 %gather_fusion.9 = f32[2048,2048]{1,0:T(8,128)} fusion(f32[4,576,2048]{2,1,0:T(8,128)} %bitcast.461, s32[2048]{0:T(1024)S(1)} %bitcast.468), kind=kCustom, calls=%fused_computation.7.clone | custom fusion | bytes 33570816 | tf_op jit(solution)/shard_map/jit(take_along_axis)/gather | solution.py:96
  2214.5 21.7 select_select_fusion.1
  2236.2 20.0 reshape.750
  2256.3 24.8 reduce_sum.296
  2281.9 122.5 %all-reduce.5.cloned.1.call-done = f32[4,256,2048]{2,1,0:T(8,128)} async-done(((f32[4,256,2048]{2,1,0:T(8,128)}), f32[4,256,2048]{2,1,0:T(8,128)}) %all-reduce.5.cloned.1.call-update) | async-done | bytes 8388624 | tf_op jit(solution)/shard_map/psum | solution.py:141
  2413.9 19.0 gather_fusion.11
  2433.1 36.8 all-gather.38.cloned.1.call-done
  2469.9 52.4 %gather_fusion.10 = f32[2304,2048]{1,0:T(8,128)} fusion(f32[4,256,2048]{2,1,0:T(8,128)} %all-gather.38.cloned.1.call-done, s32[2304]{0:T(1024)S(1)} %copy-done.8), kind=kCustom, calls=%fused_computation.10.clone | custom fusion | bytes 37767168 | tf_op jit(solution)/shard_map/jit(take_along_axis)/gather | solution.py:88
  2727.4 51.1 %gather_fusion.12 = f32[2048,2048]{1,0:T(8,128)} fusion(f32[4,576,2048]{2,1,0:T(8,128)} %bitcast.462, s32[2048]{0:T(1024)S(1)} %bitcast.466), kind=kCustom, calls=%fused_computation.8.clone | custom fusion | bytes 33570816 | tf_op jit(solution)/shard_map/jit(take_along_axis)/gather | solution.py:96
  2790.4 20.5 mul.515
  2810.9 23.0 multiply_reduce_fusion
  2833.8 20.0 reshape.753
  2853.9 24.8 reduce_sum.305
  2896.5 20.7 reshape.747
  2917.2 24.8 reduce_sum.295
  2972.8 49.7 %all-reduce.7.cloned.1.call-done = f32[4,256,2048]{2,1,0:T(8,128)} async-done(((f32[4,256,2048]{2,1,0:T(8,128)}), f32[4,256,2048]{2,1,0:T(8,128)}) %all-reduce.7.cloned.1.call-update) | async-done | bytes 8388624 | tf_op jit(solution)/shard_map/psum | solution.py:141
  3073.1 18.7 bitcast_convert_fusion.2
  3129.0 26.5 reduce-scatter.22.cloned.1.call-done
  3160.1 31.4 all-reduce.9.cloned.1.call-done
  3196.8 141.6 %reduce-scatter.26.cloned.1.call-done = bf16[8,256,512]{2,1,0:T(8,128)(2,1)} async-done(((bf16[8,256,2048]{2,1,0:T(8,128)(2,1)}), bf16[8,256,512]{2,1,0:T(8,128)(2,1)}) %reduce-scatter.26.cloned.1.call-update) | async-done | bytes 2097168 | tf_op jit(solution)/shard_map/reduce_scatter | solution.py:426
  3342.7 143.4 %reduce-scatter.20.cloned.1.call-done = bf16[8,512,256]{2,1,0:T(8,128)(2,1)} async-done(((bf16[8,2048,256]{2,1,0:T(8,128)(2,1)}), bf16[8,512,256]{2,1,0:T(8,128)(2,1)}) %reduce-scatter.20.cloned.1.call-update) | async-done | bytes 2097168 | tf_op jit(solution)/shard_map/reduce_scatter | solution.py:417
  3490.0 379.9 %reduce-scatter.32.cloned.1.call-done = bf16[8,704,512]{2,1,0:T(8,128)(2,1)} async-done(((bf16[8,704,2048]{2,1,0:T(8,128)(2,1)}), bf16[8,704,512]{2,1,0:T(8,128)(2,1)}) %reduce-scatter.32.cloned.1.call-update) | async-done | bytes 5767184 | tf_op jit(solution)/shard_map/reduce_scatter | solution.py:308
  3878.6 376.0 %reduce-scatter.28.cloned.1.call-done = bf16[8,512,704]{1,2,0:T(8,128)(2,1)} async-done(((bf16[8,2048,704]{1,2,0:T(8,128)(2,1)}), bf16[8,512,704]{1,2,0:T(8,128)(2,1)}) %reduce-scatter.28.cloned.1.call-update) | async-done | bytes 5767184 | tf_op jit(solution)/shard_map/reduce_scatter | solution.py:302
  4263.2 376.1 %reduce-scatter.30.cloned.1.call-done = bf16[8,512,704]{1,2,0:T(8,128)(2,1)} async-done(((bf16[8,2048,704]{1,2,0:T(8,128)(2,1)}), bf16[8,512,704]{1,2,0:T(8,128)(2,1)}) %reduce-scatter.30.cloned.1.call-update) | async-done | bytes 5767184 | tf_op jit(solution)/shard_map/reduce_scatter | solution.py:305
  (579 shorter events, 713.9 us)
Async XLA Ops:
  7.2 872.3 %copy-start = (bf16[2048,8]{0,1:T(8,128)(2,1)S(1)}, bf16[2048,8]{0,1:T(8,128)(2,1)}, u32[]{:S(2)}) copy-start(bf16[2048,8]{0,1:T(8,128)(2,1)} %param.33) | copy-start | bytes 98308
  7.2 42.9 all-gather.14.cloned.1.call-start
  7.9 71.7 %all-gather.16.cloned.1.call-start = ((), (), s32[]{:S(2)}) async-start(), calls=%async_computation.12 | async-start | bytes 1310720 | tf_op jit(solution)/shard_map/all_gather | solution.py:187
  8.7 100.5 %all-gather.22.cloned.1.call-start = ((), (), s32[]{:S(2)}) async-start(), calls=%async_computation.15 | async-start | bytes 1310720 | tf_op jit(solution)/shard_map/all_gather | solution.py:186
  10.6 222.2 %all-gather.18.cloned.1.call-start = ((), (), s32[]{:S(2)}) async-start(), calls=%async_computation.13 | async-start | bytes 2621440 | tf_op jit(solution)/shard_map/all_gather | solution.py:205
  84.2 152.3 %all-gather.24.cloned.1.call-start = ((), (), s32[]{:S(2)}) async-start(), calls=%async_computation.16 | async-start | bytes 2621440 | tf_op jit(solution)/shard_map/all_gather | solution.py:204
  114.9 238.4 %all-gather.20.cloned.1.call-start = ((), (), s32[]{:S(2)}) async-start(), calls=%async_computation.14 | async-start | bytes 10485760 | tf_op jit(solution)/shard_map/all_gather | solution.py:185
  115.5 387.3 %all-gather.26.cloned.1.call-start = ((), (), s32[]{:S(2)}) async-start(), calls=%async_computation.17 | async-start | bytes 10485760 | tf_op jit(solution)/shard_map/all_gather | solution.py:188
  116.3 576.1 %reduce-scatter.12.cloned.1.call-start = ((), (), s32[]{:S(2)}) async-start(), calls=%async_computation.18 | async-start | bytes 9437184 | tf_op jit(solution)/shard_map/reduce_scatter | solution.py:137
  223.2 343.0 %copy-start.1 = (f32[4,512]{1,0:T(4,128)}, f32[4,512]{1,0:T(4,128)S(1)}, u32[]{:S(2)}) copy-start(f32[4,512]{1,0:T(4,128)S(1)} %broadcast_select_fusion.3) | copy-start | bytes 24580
  236.3 146.2 %copy-start.42 = (bf16[1024,2,128]{2,1,0:T(2,128)(2,1)}, bf16[1024,2,128]{2,1,0:T(2,128)(2,1)S(1)}, u32[]{:S(2)}) copy-start(bf16[1024,2,128]{2,1,0:T(2,128)(2,1)S(1)} %squeeze.38) | copy-start | bytes 1572868
  236.5 151.5 %copy-start.40 = (bf16[1024,2,128]{2,1,0:T(2,128)(2,1)}, bf16[1024,2,128]{2,1,0:T(2,128)(2,1)S(1)}, u32[]{:S(2)}) copy-start(bf16[1024,2,128]{2,1,0:T(2,128)(2,1)S(1)} %squeeze.81) | copy-start | bytes 1572868
  373.3 129.5 %copy-start.49 = (bf16[1,8,72,256]{3,2,1,0:T(8,128)(2,1)}, bf16[1,8,72,256]{3,2,1,0:T(8,128)(2,1)S(1)}, u32[]{:S(2)}) copy-start(bf16[1,8,72,256]{3,2,1,0:T(8,128)(2,1)S(1)} %stack.70) | copy-start | bytes 884740
  379.0 123.8 %copy-start.51 = (bf16[1,8,72,256]{3,2,1,0:T(8,128)(2,1)}, bf16[1,8,72,256]{3,2,1,0:T(8,128)(2,1)S(1)}, u32[]{:S(2)}) copy-start(bf16[1,8,72,256]{3,2,1,0:T(8,128)(2,1)S(1)} %stack.71) | copy-start | bytes 884740
  384.3 118.5 %copy-start.53 = (bf16[1,8,72,256]{3,2,1,0:T(8,128)(2,1)}, bf16[1,8,72,256]{3,2,1,0:T(8,128)(2,1)S(1)}, u32[]{:S(2)}) copy-start(bf16[1,8,72,256]{3,2,1,0:T(8,128)(2,1)S(1)} %stack.72) | copy-start | bytes 884740
  389.8 118.1 %copy-start.55 = (bf16[1,8,72,256]{3,2,1,0:T(8,128)(2,1)}, bf16[1,8,72,256]{3,2,1,0:T(8,128)(2,1)S(1)}, u32[]{:S(2)}) copy-start(bf16[1,8,72,256]{3,2,1,0:T(8,128)(2,1)S(1)} %stack.73) | copy-start | bytes 884740
  622.8 69.6 %copy-start.25 = (bf16[4,256,256]{2,1,0:T(8,128)(2,1)S(1)}, bf16[4,256,256]{2,1,0:T(8,128)(2,1)}, u32[]{:S(2)}) copy-start(bf16[4,256,256]{2,1,0:T(8,128)(2,1)} %param.28) | copy-start | bytes 1572868
  622.8 109.1 %all-gather.36.cloned.1.call-start = ((), (), s32[]{:S(2)}) async-start(), calls=%async_computation.24 | async-start | bytes 4718592 | tf_op jit(solution)/shard_map/all_gather | solution.py:133
  623.5 197.4 %all-gather.28.cloned.1.call-start = ((), (), s32[]{:S(2)}) async-start(), calls=%async_computation.19 | async-start | bytes 4718592 | tf_op jit(solution)/shard_map/all_gather | solution.py:133
  694.6 470.1 %all-gather.30.cloned.1.call-start = ((), (), s32[]{:S(2)}) async-start(), calls=%async_computation.20 | async-start | bytes 28835840 | tf_op jit(solution)/shard_map/all_gather | solution.py:255
  695.3 860.3 %all-gather.32.cloned.1.call-start = ((), (), s32[]{:S(2)}) async-start(), calls=%async_computation.21 | async-start | bytes 28835840 | tf_op jit(solution)/shard_map/all_gather | solution.py:256
  695.9 1250.8 %all-gather.34.cloned.1.call-start = ((), (), s32[]{:S(2)}) async-start(), calls=%async_computation.22 | async-start | bytes 28835840 | tf_op jit(solution)/shard_map/all_gather | solution.py:257
  696.6 1707.7 %all-reduce.5.cloned.1.call-start = ((), (), s32[]{:S(2)}) async-start(), calls=%async_computation.25 | async-start | bytes 16777216 | tf_op jit(solution)/shard_map/psum | solution.py:141
  2281.1 123.2 %copy-start.100 = (f32[4,256]{1,0:T(4,128)S(1)}, f32[4,256]{1,0:T(4,128)}, u32[]{:S(2)}) copy-start(f32[4,256]{1,0:T(4,128)} %copy-done.99) | copy-start | bytes 12292
  2281.1 123.2 %copy-start.106 = (f32[2048]{0:T(1024)S(1)}, f32[2048]{0:T(1024)}, u32[]{:S(2)}) copy-start(f32[2048]{0:T(1024)} %param.31) | copy-start | bytes 24580
  2281.1 188.8 %all-gather.38.cloned.1.call-start = ((), (), s32[]{:S(2)}) async-start(), calls=%async_computation.26 | async-start | bytes 9437184 | tf_op jit(solution)/shard_map/all_gather | solution.py:324
  2281.8 129.2 %copy-start.85 = (bf16[4,256,8]{1,2,0:T(8,128)(2,1)}, bf16[4,256,8]{1,2,0:T(8,128)(2,1)S(1)}, u32[]{:S(2)}) copy-start(bf16[4,256,8]{1,2,0:T(8,128)(2,1)S(1)} %select_reduce_fusion.3) | copy-start | bytes 49156
  2281.8 129.2 %copy-start.39 = (bf16[4,256,256]{2,1,0:T(8,128)(2,1)S(1)}, bf16[4,256,256]{2,1,0:T(8,128)(2,1)}, u32[]{:S(2)}) copy-start(bf16[4,256,256]{2,1,0:T(8,128)(2,1)} %param.29) | copy-start | bytes 1572868
  2413.6 465.0 %reduce-scatter.16.cloned.1.call-start = ((), (), s32[]{:S(2)}) async-start(), calls=%async_computation.27 | async-start | bytes 2621440 | tf_op jit(solution)/shard_map/reduce_scatter | solution.py:391
  2433.1 89.2 %copy-start.110 = (pred[4,576]{1,0:T(4,128)(4,1)S(1)}, pred[4,576]{1,0:T(4,128)(4,1)}, u32[]{:S(2)}) copy-start(pred[4,576]{1,0:T(4,128)(4,1)} %and_bitcast_fusion.1) | copy-start | bytes 6916
  2607.1 278.8 %reduce-scatter.18.cloned.1.call-start = ((), (), s32[]{:S(2)}) async-start(), calls=%async_computation.28 | async-start | bytes 2621440 | tf_op jit(solution)/shard_map/reduce_scatter | solution.py:394
  2698.2 324.3 %all-reduce.7.cloned.1.call-start = ((), (), s32[]{:S(2)}) async-start(), calls=%async_computation.29 | async-start | bytes 16777216 | tf_op jit(solution)/shard_map/psum | solution.py:141
  2896.4 214.2 %reduce-scatter.14.cloned.1.call-start = ((), (), s32[]{:S(2)}) async-start(), calls=%async_computation.23 | async-start | bytes 9437184 | tf_op jit(solution)/shard_map/reduce_scatter | solution.py:137
  2942.0 185.2 %reduce-scatter.24.cloned.1.call-start = ((), (), s32[]{:S(2)}) async-start(), calls=%async_computation.32 | async-start | bytes 1310720 | tf_op jit(solution)/shard_map/reduce_scatter | solution.py:423
  2948.2 207.3 %reduce-scatter.22.cloned.1.call-start = ((), (), s32[]{:S(2)}) async-start(), calls=%async_computation.31 | async-start | bytes 1310720 | tf_op jit(solution)/shard_map/reduce_scatter | solution.py:420
  2952.8 69.7 %copy-start.88 = (bf16[2048,8]{0,1:T(8,128)(2,1)S(1)}, bf16[2048,8]{0,1:T(8,128)(2,1)}, u32[]{:S(2)}) copy-start(bf16[2048,8]{0,1:T(8,128)(2,1)} %param.32) | copy-start | bytes 98308
  2952.8 69.7 %copy-start.98 = (f32[4,256]{1,0:T(4,128)S(1)}, f32[4,256]{1,0:T(4,128)}, u32[]{:S(2)}) copy-start(f32[4,256]{1,0:T(4,128)} %copy-done.97) | copy-start | bytes 12292
  2952.8 69.7 %copy-start.108 = (f32[2048]{0:T(1024)S(1)}, f32[2048]{0:T(1024)}, u32[]{:S(2)}) copy-start(f32[2048]{0:T(1024)} %param.30) | copy-start | bytes 24580
  2952.8 238.7 %all-reduce.9.cloned.1.call-start = ((), (), s32[]{:S(2)}) async-start(), calls=%async_computation.37 | async-start | bytes 147456 | tf_op jit(solution)/shard_map/psum | solution.py:448
  2972.8 58.4 %copy-start.50 = (bf16[1,8,72,256]{3,2,1,0:T(8,128)(2,1)S(1)}, bf16[1,8,72,256]{3,2,1,0:T(8,128)(2,1)}, u32[]{:S(2)}) copy-start(bf16[1,8,72,256]{3,2,1,0:T(8,128)(2,1)} %copy-done.49) | copy-start | bytes 884740
  2972.8 58.4 %copy-start.52 = (bf16[1,8,72,256]{3,2,1,0:T(8,128)(2,1)S(1)}, bf16[1,8,72,256]{3,2,1,0:T(8,128)(2,1)}, u32[]{:S(2)}) copy-start(bf16[1,8,72,256]{3,2,1,0:T(8,128)(2,1)} %copy-done.51) | copy-start | bytes 884740
  2972.8 58.4 %copy-start.54 = (bf16[1,8,72,256]{3,2,1,0:T(8,128)(2,1)S(1)}, bf16[1,8,72,256]{3,2,1,0:T(8,128)(2,1)}, u32[]{:S(2)}) copy-start(bf16[1,8,72,256]{3,2,1,0:T(8,128)(2,1)} %copy-done.53) | copy-start | bytes 884740
  2972.8 58.4 %copy-start.56 = (bf16[1,8,72,256]{3,2,1,0:T(8,128)(2,1)S(1)}, bf16[1,8,72,256]{3,2,1,0:T(8,128)(2,1)}, u32[]{:S(2)}) copy-start(bf16[1,8,72,256]{3,2,1,0:T(8,128)(2,1)} %copy-done.55) | copy-start | bytes 884740
  3031.1 307.3 %reduce-scatter.26.cloned.1.call-start = ((), (), s32[]{:S(2)}) async-start(), calls=%async_computation.33 | async-start | bytes 10485760 | tf_op jit(solution)/shard_map/reduce_scatter | solution.py:426
  3043.0 443.0 %reduce-scatter.20.cloned.1.call-start = ((), (), s32[]{:S(2)}) async-start(), calls=%async_computation.30 | async-start | bytes 10485760 | tf_op jit(solution)/shard_map/reduce_scatter | solution.py:417
  3054.4 815.5 %reduce-scatter.32.cloned.1.call-start = ((), (), s32[]{:S(2)}) async-start(), calls=%async_computation.36 | async-start | bytes 28835840 | tf_op jit(solution)/shard_map/reduce_scatter | solution.py:308
  3073.1 1181.5 %reduce-scatter.28.cloned.1.call-start = ((), (), s32[]{:S(2)}) async-start(), calls=%async_computation.34 | async-start | bytes 28835840 | tf_op jit(solution)/shard_map/reduce_scatter | solution.py:302
  3091.8 1547.5 %reduce-scatter.30.cloned.1.call-start = ((), (), s32[]{:S(2)}) async-start(), calls=%async_computation.35 | async-start | bytes 28835840 | tf_op jit(solution)/shard_map/reduce_scatter | solution.py:305
  (116 other events, 1302.6 us)
Sparse Core Ops, SparseCore 0:
  9.9 40.1 all-gather.13
  51.7 27.9 all-gather.15
  81.8 27.4 all-gather.21
  111.2 45.4 all-gather.17
  158.7 45.3 all-gather.23
  205.5 147.8 all-gather.19
  354.9 147.8 all-gather.25
  622.9 69.4 reduce-scatter.11
  694.4 37.4 all-gather.35
  734.4 37.4 all-gather.27
  773.5 391.0 all-gather.29
  1166.2 389.3 all-gather.31
  1557.2 389.3 all-gather.33
  2281.2 123.0 all-reduce.4
  2413.7 56.1 all-gather.37
  2607.2 43.4 reduce-scatter.15
  2698.4 43.3 reduce-scatter.17
  2896.5 125.9 all-reduce.6
  3026.4 71.4 reduce-scatter.13
  3100.0 27.1 reduce-scatter.23
  3129.6 25.7 reduce-scatter.21
  3158.6 32.8 all-reduce.8
  3194.0 144.4 reduce-scatter.25
  3340.8 145.1 reduce-scatter.19
  3488.5 381.3 reduce-scatter.31
  3872.1 382.3 reduce-scatter.27
  4256.9 382.3 reduce-scatter.29
where the time goes:
time: 4670 us; the launch traced here: 4660 us
  waiting for transfers between devices  3100 us (66%)
  local copies, waits for them, and re-layouts  745 us (16%)
  matrix products  437 us (9%)
  other arithmetic  329 us (7%)
    reduce_scatter x1, waiting for transfers between devices, per_device(): lax.psum_scatter(grad_w_down.astype(jnp.bfloat16), 'row', scatter_dimensi...  380 us
    reduce_scatter x1, waiting for transfers between devices, per_device(): lax.psum_scatter(grad_w_up.astype(jnp.bfloat16), 'row', scatter_dimension...  376 us
    reduce_scatter x1, waiting for transfers between devices, per_device(): lax.psum_scatter(grad_w_gate.astype(jnp.bfloat16), 'row', scatter_dimensi...  376 us
    all_gather x1, waiting for transfers between devices, per_device(): lax.all_gather(w_up, 'row', axis=1, tiled=True)  371 us
    all_gather x1, waiting for transfers between devices, per_device(): lax.all_gather(w_down, 'row', axis=2, tiled=True)  363 us
    all_gather x1, waiting for transfers between devices, per_device(): lax.all_gather(w_gate, 'row', axis=1, tiled=True)  255 us
    psum x2, waiting for transfers between devices, hidden_sum(): return lax.psum((part, dots), 'col')  172 us
    reduce_scatter x1, waiting for transfers between devices, per_device(): lax.psum_scatter(grad_w_query.astype(jnp.bfloat16), 'row', scatter_dimens...  143 us
  transfers between devices with their start and end apart: 27, of which 21 were waited for; matrix products, arithmetic and copies ran while one was open for 19% of the time, Pallas kernels for 0%

commit v1 on v0

v1 whole, which is shorter than its diff:
```python
from functools import partial
import math

import jax
import jax.numpy as jnp
from jax import lax
from jax.experimental import pallas as pl
from jax.experimental.pallas import tpu as pltpu
from jax.sharding import PartitionSpec as P

HEAD_DIM = 128
EPSILON = 1e-05
ROPE_BASE = 10000.0
MASKED_SCORE = -1e30
BF16 = jnp.bfloat16
F32 = jnp.float32


def dot_f32(spec, left, right):
    return jnp.einsum(spec, left, right, preferred_element_type=F32)


def rope_tables(positions):
    half_width = HEAD_DIM // 2
    frequency = jnp.exp(
        -math.log(ROPE_BASE) * jnp.arange(half_width, dtype=F32) * (2.0 / HEAD_DIM)
    )
    angles = positions.astype(F32)[..., None] * frequency
    angles = jnp.concatenate([angles, angles], axis=-1)
    return (jnp.cos(angles), jnp.sin(angles))


def rotate(values, cosine, sine, sign):
    heads = values.reshape(*values.shape[:-1], -1, HEAD_DIM)
    half_width = HEAD_DIM // 2
    turned = jnp.concatenate([-heads[..., half_width:], heads[..., :half_width]], axis=-1)
    out = heads * cosine[..., None, :] + sign * turned * sine[..., None, :]
    return out.reshape(values.shape)


def pair_ranks(routes, order):
    pairs = routes.reshape(order.shape)
    earlier = (order[..., None, :] < order[..., :, None]).astype(BF16)
    same = (pairs[..., None, :] == pairs[..., :, None]).astype(BF16)
    ranks = jnp.sum((earlier * same).astype(F32), axis=-1).astype(jnp.int32)
    return ranks.reshape(routes.shape)


def slot_match(routes, ranks, expert, capacity):
    chosen = jnp.where(routes == expert, ranks, -1)
    rank_here = jnp.max(chosen, axis=-1)
    slots = jnp.arange(capacity, dtype=jnp.int32)[:, None]
    return rank_here[..., None, :] == slots


def gate_table(hidden, router, routes):
    experts = router.shape[1]
    logits = jnp.dot(hidden, router, preferred_element_type=F32)
    ids = jnp.arange(experts, dtype=jnp.int32)
    chosen = jnp.any(routes[..., None] == ids, axis=-2)
    masked = jnp.where(chosen, logits, MASKED_SCORE)
    top = jnp.max(masked, axis=-1, keepdims=True)
    exps = jnp.where(chosen, jnp.exp(masked - top), 0.0)
    return exps / jnp.sum(exps, axis=-1, keepdims=True)


def normalize_rows(wide):
    inverse = lax.rsqrt(jnp.mean(wide * wide, axis=-1, keepdims=True) + EPSILON)
    return (wide * inverse, inverse)


def pick(match, per_token):
    return jnp.sum(jnp.where(match, per_token[..., None, :], 0), axis=-1)


def scores_of(q, k, qblk, kblk):
    raw = lax.dot_general(q, k, (((1,), (1,)), ((), ())), preferred_element_type=F32)
    return jnp.where(kblk <= qblk, raw * HEAD_DIM ** (-0.5), MASKED_SCORE)


def attend_kernel(q_ref, k_ref, v_ref, qblk_ref, kblk_ref, out_ref, lse_ref):
    scores = scores_of(q_ref[0], k_ref[0], qblk_ref[0], kblk_ref[0])
    top = jnp.max(scores, axis=-1, keepdims=True)
    exps = jnp.exp(scores - top)
    total = jnp.sum(exps, axis=-1, keepdims=True)
    probs = (exps * (1.0 / total)).astype(BF16)
    out = jnp.dot(probs, v_ref[0], preferred_element_type=F32)
    out_ref[0] = out.astype(BF16)
    lse_ref[0, 0] = top + jnp.log(total)


def attend(q, k, v, qblk, kblk):
    seqs, rows, cols = q.shape
    keys = k.shape[1]
    heads = cols // HEAD_DIM
    q_spec = pl.BlockSpec((1, rows, HEAD_DIM), lambda s, h: (s, 0, h))
    k_spec = pl.BlockSpec((1, keys, HEAD_DIM), lambda s, h: (s, 0, h))
    return pl.pallas_call(
        attend_kernel,
        grid=(seqs, heads),
        in_specs=[
            q_spec,
            k_spec,
            k_spec,
            pl.BlockSpec((1, rows, 1), lambda s, h: (s, 0, 0)),
            pl.BlockSpec((1, 1, keys), lambda s, h: (s, 0, 0)),
        ],
        out_specs=[q_spec, pl.BlockSpec((1, 1, rows, 1), lambda s, h: (s, h, 0, 0))],
        out_shape=[
            jax.ShapeDtypeStruct(q.shape, BF16),
            jax.ShapeDtypeStruct((seqs, heads, rows, 1), F32),
        ],
        compiler_params=pltpu.CompilerParams(vmem_limit_bytes=48 * 1024 * 1024),
        cost_estimate=pl.CostEstimate(
            flops=4 * seqs * rows * keys * cols,
            bytes_accessed=4 * q.size + 4 * k.size,
            transcendentals=seqs * heads * rows * keys,
        ),
        name="attend",
    )(q, k, v, qblk, kblk)


def attend_back_kernel(
    q_ref, k_ref, v_ref, g_ref, lse_ref, qblk_ref, kblk_ref, dq_ref, dk_ref, dv_ref
):
    q, k, g = q_ref[0], k_ref[0], g_ref[0]
    probs = jnp.exp(scores_of(q, k, qblk_ref[0], kblk_ref[0]) - lse_ref[0, 0])
    grad = lax.dot_general(g, v_ref[0], (((1,), (1,)), ((), ())), preferred_element_type=F32)
    inner = jnp.sum(probs * grad, axis=-1, keepdims=True)
    grad_scores = (probs * (grad - inner) * HEAD_DIM ** (-0.5)).astype(BF16)
    first = (((0,), (0,)), ((), ()))
    dq_ref[0] = jnp.dot(grad_scores, k, preferred_element_type=F32)
    dk_ref[0] = lax.dot_general(grad_scores, q, first, preferred_element_type=F32)
    dv = lax.dot_general(probs.astype(BF16), g, first, preferred_element_type=F32)
    dv_ref[0] = dv.astype(BF16)


def attend_back(q, k, v, grad, lse, qblk, kblk):
    seqs, rows, cols = q.shape
    keys = k.shape[1]
    heads = cols // HEAD_DIM
    q_spec = pl.BlockSpec((1, rows, HEAD_DIM), lambda s, h: (s, 0, h))
    k_spec = pl.BlockSpec((1, keys, HEAD_DIM), lambda s, h: (s, 0, h))
    return pl.pallas_call(
        attend_back_kernel,
        grid=(seqs, heads),
        in_specs=[
            q_spec,
            k_spec,
            k_spec,
            q_spec,
            pl.BlockSpec((1, 1, rows, 1), lambda s, h: (s, h, 0, 0)),
            pl.BlockSpec((1, rows, 1), lambda s, h: (s, 0, 0)),
            pl.BlockSpec((1, 1, keys), lambda s, h: (s, 0, 0)),
        ],
        out_specs=[q_spec, k_spec, k_spec],
        out_shape=[
            jax.ShapeDtypeStruct(q.shape, F32),
            jax.ShapeDtypeStruct(k.shape, F32),
            jax.ShapeDtypeStruct(k.shape, BF16),
        ],
        compiler_params=pltpu.CompilerParams(vmem_limit_bytes=56 * 1024 * 1024),
        cost_estimate=pl.CostEstimate(
            flops=10 * seqs * rows * keys * cols,
            bytes_accessed=8 * q.size + 10 * k.size,
            transcendentals=seqs * heads * rows * keys,
        ),
        name="attend_back",
    )(q, k, v, grad, lse, qblk, kblk)


def all_tokens(own):
    rows = lax.all_gather(own, "row", axis=1, tiled=True)
    return lax.all_gather(rows, "col", axis=2, tiled=True)


def to_experts(weight, split):
    ranks = lax.axis_size("row")
    experts, height, width = weight.shape
    local = experts // ranks
    grouped = weight.reshape(ranks, local, height, width)
    whole = []
    for j in range(local):
        got = lax.all_to_all(grouped[:, j], "row", 0, 0)
        if split == 1:
            whole.append(got.reshape(ranks * height, width))
        else:
            whole.append(got.transpose(1, 0, 2).reshape(height, ranks * width))
    return whole


def to_owners(grads, split):
    ranks = lax.axis_size("row")
    got = []
    for grad in grads:
        height, width = grad.shape
        if split == 1:
            parts = grad.reshape(ranks, height // ranks, width)
        else:
            parts = grad.reshape(height, ranks, width // ranks).transpose(1, 0, 2)
        got.append(lax.all_to_all(parts, "row", 0, 0))
    stacked = jnp.stack(got, axis=1)
    return stacked.reshape(-1, *stacked.shape[2:]).astype(F32)


def slots_home(slot_rows, seqs, capacity):
    ranks = lax.axis_size("row")
    got = []
    for rows in slot_rows:
        own = lax.psum_scatter(rows, "col", scatter_dimension=1, tiled=True)
        own = own.reshape(seqs, ranks, capacity, -1)
        got.append(lax.all_to_all(own, "row", 1, 1))
    stacked = jnp.stack(got, axis=2)
    return stacked.reshape(seqs, -1, stacked.shape[-1])


def per_device(
    block_in,
    grad_out,
    gain_attn,
    gain_ffn,
    router_attn,
    router_ffn,
    w_query,
    key_weight,
    value_weight,
    w_out,
    w_gate,
    w_up,
    w_down,
    routes_attn,
    routes_ffn,
    order_attn,
    order_ffn,
    block_ids,
):
    seqs, seq_dev, share = block_in.shape
    experts = w_query.shape[0]
    capacity = 18 * seq_dev // (8 * experts)
    head_cols = key_weight.shape[1]
    width = gain_attn.shape[0]
    seq_len = block_ids.shape[1]
    ranks = lax.axis_size("row")
    local = experts // ranks
    row_at, col_at = lax.axis_index("row"), lax.axis_index("col")
    slot_rows = seqs * ranks * capacity

    def own_features(whole):
        return lax.dynamic_slice_in_dim(whole, col_at * share, share, whole.ndim - 1)

    def own_tokens(whole):
        return lax.dynamic_slice_in_dim(whole, row_at * seq_dev, seq_dev, 1)

    small = jnp.stack(
        [
            routes_attn.reshape(seqs, -1),
            order_attn.reshape(seqs, -1),
            routes_ffn.reshape(seqs, -1),
            order_ffn.reshape(seqs, -1),
        ]
    )
    small = lax.all_gather(small, "row", axis=2, tiled=False)
    routes_a = small[0].reshape(seqs, ranks, seq_dev, 2)
    routes_f = small[2].reshape(seqs, ranks, seq_dev, 2)
    ranks_a = pair_ranks(routes_a, small[1])
    ranks_f = pair_ranks(routes_f, small[3])
    mine = [row_at * local + j for j in range(local)]
    match_a = [slot_match(routes_a, ranks_a, e, capacity) for e in mine]
    match_f = [slot_match(routes_f, ranks_f, e, capacity) for e in mine]

    def home_match(routes, rank):
        at = lambda whole: lax.dynamic_index_in_dim(whole, row_at, 1, keepdims=False)
        routes_here, ranks_here = at(routes), at(rank)
        every = [slot_match(routes_here, ranks_here, e, capacity) for e in range(experts)]
        return jnp.concatenate(every, axis=1).astype(BF16)

    home_a = home_match(routes_a, ranks_a)
    home_f = home_match(routes_f, ranks_f)

    def dispatch(match, tokens):
        blocks = tokens.reshape(seqs, ranks, seq_dev, -1)
        return [
            jnp.einsum("snct,sntd->sncd", m.astype(BF16), blocks).reshape(slot_rows, -1)
            for m in match
        ]

    def come_home(match, rows):
        return dot_f32("sct,scf->stf", match, rows)

    def slot_gates(match, gates):
        blocks = gates.reshape(seqs, ranks, seq_dev, experts)
        out = []
        for m, e in zip(match, mine):
            one = lax.dynamic_index_in_dim(blocks, e, 3, keepdims=False)
            out.append(pick(m, one).reshape(slot_rows, 1))
        return out

    def gate_dots(match, dots):
        per_token = []
        for m, d in zip(match, dots):
            spread = jnp.where(m, d.reshape(seqs, ranks, capacity, 1), 0.0)
            per_token.append(jnp.sum(spread, axis=2))
        both = jnp.stack(per_token, axis=-1)
        both = lax.psum(both, "col")
        got = lax.all_to_all(both, "row", 1, 1)
        return got.transpose(0, 2, 1, 3).reshape(seqs, seq_dev, experts)

    in_all = all_tokens(block_in)
    normed_a, inverse_a = normalize_rows(in_all.astype(F32))
    hidden_a = (normed_a * gain_attn).astype(BF16)
    key_all = lax.all_gather(key_weight, "row", axis=0, tiled=True)
    value_all = lax.all_gather(value_weight, "row", axis=0, tiled=True)
    query_w = to_experts(w_query, 1)
    out_w = to_experts(w_out, 2)
    tok_cos, tok_sin = rope_tables(jnp.arange(seq_len, dtype=jnp.int32))
    keys = rotate(dot_f32("std,df->stf", hidden_a, key_all), tok_cos, tok_sin, 1.0).astype(BF16)
    values = dot_f32("std,df->stf", hidden_a, value_all).astype(BF16)
    gates_a = gate_table(hidden_a, router_attn, routes_a.reshape(seqs, seq_len, 2))
    weights_a = slot_gates(match_a, gates_a)
    slot_in_a = dispatch(match_a, hidden_a)
    token_at = jnp.arange(seq_len, dtype=jnp.int32).reshape(1, ranks, seq_dev)
    block_at = block_ids.reshape(seqs, ranks, seq_dev)
    tables = [rope_tables(pick(m, token_at).reshape(slot_rows)) for m in match_a]
    queries = [
        rotate(jnp.dot(x, w, preferred_element_type=F32), c, s, 1.0).astype(BF16)
        for x, w, (c, s) in zip(slot_in_a, query_w, tables)
    ]

    def by_seq(parts):
        return jnp.concatenate([p.reshape(seqs, -1, p.shape[-1]) for p in parts], axis=1)

    def by_expert(whole):
        split = whole.reshape(seqs, local, ranks * capacity, whole.shape[-1])
        return [split[:, j].reshape(slot_rows, -1) for j in range(local)]

    q_seq = by_seq(queries)
    qblk = by_seq([pick(m, block_at).reshape(slot_rows, 1) for m in match_a])
    kblk = block_ids.reshape(seqs, 1, seq_len)
    attended_seq, log_totals = attend(q_seq, keys, values, qblk, kblk)
    attended = by_expert(attended_seq)
    out_slots = [
        (jnp.dot(a, w, preferred_element_type=F32) * g).astype(BF16)
        for a, w, g in zip(attended, out_w, weights_a)
    ]
    mid = block_in.astype(F32) + come_home(home_a, slots_home(out_slots, seqs, capacity))

    mid_low = mid.astype(BF16)
    mid_all = all_tokens(mid_low)
    normed_f, inverse_f = normalize_rows(mid_all.astype(F32))
    hidden_f = (normed_f * gain_ffn).astype(BF16)
    gate_w = to_experts(w_gate, 1)
    up_w = to_experts(w_up, 1)
    down_w = to_experts(w_down, 2)
    gates_f = gate_table(hidden_f, router_ffn, routes_f.reshape(seqs, seq_len, 2))
    weights_f = slot_gates(match_f, gates_f)
    slot_in_f = dispatch(match_f, hidden_f)
    out_grad_all = all_tokens(grad_out)
    slot_grad_out = dispatch(match_f, out_grad_all)
    down_slots, slot_grads_f, dots_f = [], [], []
    grads_gate, grads_up, grads_down = [], [], []
    for j in range(local):
        gate_pre = jnp.dot(slot_in_f[j], gate_w[j], preferred_element_type=F32)
        up_pre = jnp.dot(slot_in_f[j], up_w[j], preferred_element_type=F32)
        gate_sig = jax.nn.sigmoid(gate_pre)
        gate_silu = gate_pre * gate_sig
        activated = gate_silu * up_pre
        scaled = (activated * weights_f[j]).astype(BF16)
        down = jnp.dot(scaled, down_w[j], preferred_element_type=F32)
        down_slots.append(down.astype(BF16))
        grad_raw = dot_f32("rd,fd->rf", slot_grad_out[j], down_w[j])
        dots_f.append(jnp.sum(grad_raw * activated, axis=-1))
        grad_act = grad_raw * weights_f[j]
        grad_gate = grad_act * up_pre * (gate_sig * (1.0 + gate_pre * (1.0 - gate_sig)))
        grad_gate = grad_gate.astype(BF16)
        grad_up = (grad_act * gate_silu).astype(BF16)
        grads_down.append(dot_f32("rf,rd->fd", scaled, slot_grad_out[j]).astype(BF16))
        grads_gate.append(dot_f32("rd,rf->df", slot_in_f[j], grad_gate).astype(BF16))
        grads_up.append(dot_f32("rd,rf->df", slot_in_f[j], grad_up).astype(BF16))
        slot_grad = dot_f32("rf,df->rd", grad_gate, gate_w[j])
        slot_grad = slot_grad + dot_f32("rf,df->rd", grad_up, up_w[j])
        slot_grads_f.append(slot_grad.astype(BF16))
    block_out = (mid + come_home(home_f, slots_home(down_slots, seqs, capacity))).astype(BF16)
    grad_down_own = to_owners(grads_down, 2)
    grad_gate_own = to_owners(grads_gate, 1)
    grad_up_own = to_owners(grads_up, 1)

    def sublayer_back(own_in, inverse_all, gain, router, gates_all, dots, dhidden):
        gates = own_tokens(gates_all)
        inverse = own_tokens(inverse_all)
        dlogits = gates * (dots - jnp.sum(gates * dots, axis=-1, keepdims=True))
        dlogits = dlogits.astype(BF16)
        gain_own = own_features(gain)
        router_own = lax.dynamic_slice_in_dim(router, col_at * share, share, 0)
        normed = own_in.astype(F32) * inverse
        hidden = (normed * gain_own).astype(BF16)
        dhidden = dhidden + dot_f32("ste,fe->stf", dlogits, router_own)
        grad_router = dot_f32("stf,ste->fe", hidden, dlogits)
        grad_gain = jnp.sum(dhidden * normed, axis=(0, 1))
        dn = dhidden * gain_own
        inner = lax.psum(jnp.sum(dn * normed, axis=-1, keepdims=True), "col") / width
        grad = inverse * (dn - normed * inner)
        grads = jnp.concatenate([grad_router, grad_gain[:, None]], axis=1)
        return grad, grads

    dhidden_f = come_home(home_f, slots_home(slot_grads_f, seqs, capacity))
    dots_home_f = gate_dots(match_f, dots_f)
    grad_mid, small_f = sublayer_back(
        mid_low, inverse_f, gain_ffn, router_ffn, gates_f, dots_home_f, dhidden_f
    )
    grad_mid = grad_out.astype(F32) + grad_mid

    mid_grad_all = all_tokens(grad_mid.astype(BF16))
    slot_grad_mid = dispatch(match_a, mid_grad_all)
    grad_att, dots_a, grads_out = [], [], []
    for j in range(local):
        grad_raw = dot_f32("rd,fd->rf", slot_grad_mid[j], out_w[j])
        dots_a.append(jnp.sum(grad_raw * attended[j].astype(F32), axis=-1))
        grad_att.append((grad_raw * weights_a[j]).astype(BF16))
        scaled = (attended[j].astype(F32) * weights_a[j]).astype(BF16)
        grads_out.append(dot_f32("rf,rd->fd", scaled, slot_grad_mid[j]).astype(BF16))
    dq, dk, dv = attend_back(q_seq, keys, values, by_seq(grad_att), log_totals, qblk, kblk)
    grad_key_pre = rotate(dk, tok_cos, tok_sin, -1.0).astype(BF16)
    grad_value_pre = dv
    grads_query, token_part = [], 0.0
    for j, dq_j in enumerate(by_expert(dq)):
        pre = rotate(dq_j, *tables[j], -1.0).astype(BF16)
        grads_query.append(dot_f32("rd,rf->df", slot_in_a[j], pre).astype(BF16))
        slot_grad = dot_f32("rf,df->rd", pre, query_w[j]).astype(BF16)
        slot_grad = slot_grad.reshape(seqs, ranks, capacity, width)
        token_part = token_part + dot_f32(
            "snct,sncd->sntd", match_a[j].astype(BF16), slot_grad
        )
    token_part = token_part.reshape(seqs, seq_len, width)
    token_part = token_part + dot_f32("stf,df->std", grad_key_pre, key_all)
    token_part = token_part + dot_f32("stf,df->std", grad_value_pre, value_all)
    part = lax.psum_scatter(token_part.astype(BF16), "col", scatter_dimension=2, tiled=True)
    dhidden_a = lax.psum_scatter(part, "row", scatter_dimension=1, tiled=True).astype(F32)
    grad_key = dot_f32("std,stf->df", hidden_a, grad_key_pre).astype(BF16)
    grad_value = dot_f32("std,stf->df", hidden_a, grad_value_pre).astype(BF16)
    grad_key_own = lax.psum_scatter(grad_key, "row", scatter_dimension=0, tiled=True).astype(F32)
    grad_value_own = lax.psum_scatter(
        grad_value, "row", scatter_dimension=0, tiled=True
    ).astype(F32)
    grad_query_own = to_owners(grads_query, 1)
    grad_out_own = to_owners(grads_out, 2)
    dots_home_a = gate_dots(match_a, dots_a)
    grad_in, small_a = sublayer_back(
        block_in, inverse_a, gain_attn, router_attn, gates_a, dots_home_a, dhidden_a
    )
    grad_in = grad_mid + grad_in

    def whole_small(grads):
        return lax.all_gather(lax.psum(grads, "row"), "col", axis=0, tiled=True)

    small_f, small_a = whole_small(small_f), whole_small(small_a)
    return (
        block_out,
        grad_in,
        small_a[:, experts],
        small_f[:, experts],
        small_a[:, :experts],
        small_f[:, :experts],
        grad_query_own,
        grad_key_own,
        grad_value_own,
        grad_out_own,
        grad_gate_own,
        grad_up_own,
        grad_down_own,
    )


def solution(mesh):
    in_specs = (
        P(None, "row", "col"),
        P(None, "row", "col"),
        P(),
        P(),
        P(),
        P(),
        P(None, "row", "col"),
        P("row", "col"),
        P("row", "col"),
        P(None, "col", "row"),
        P(None, "row", "col"),
        P(None, "row", "col"),
        P(None, "col", "row"),
        P(None, "row", None),
        P(None, "row", None),
        P(None, "row", None),
        P(None, "row", None),
        P(),
    )
    out_specs = (
        P(None, "row", "col"),
        P(None, "row", "col"),
        P(),
        P(),
        P(),
        P(),
        P(None, "row", "col"),
        P("row", "col"),
        P("row", "col"),
        P(None, "col", "row"),
        P(None, "row", "col"),
        P(None, "row", "col"),
        P(None, "col", "row"),
    )
    return jax.shard_map(
        per_device, mesh=mesh, in_specs=in_specs, out_specs=out_specs, check_vma=False
    )
```

time: 4670 us -> 2180 us (0.47)
  waiting for transfers between devices: 3100 us -> 880 us
  local copies, waits for them, and re-layouts: 745 us -> 187 us
  blocking collectives: 26.6 us -> 375 us
  other arithmetic: 329 us -> 202 us
  starting transfers between devices: 1.62 us -> 107 us
  matrix products: 437 us -> 362 us
    reduce_scatter x11 -> x10, waiting for transfers between devices: 1530 us -> 92.8 us  [the longest x6 92.8 us: slots_home(): own = lax.psum_scatter(rows, 'col', scatter_dimension=1, tiled=True)]
    all_gather x13 -> x10, waiting for transfers between devices: 1360 us -> 212 us  [the longest x4 158 us: all_tokens(): rows = lax.all_gather(own, 'row', axis=1, tiled=True)]
    all_to_all x0 -> x24, waiting for transfers between devices: none -> 573 us  [the longest x10 348 us: to_owners(): got.append(lax.all_to_all(parts, 'row', 0, 0))]
    gather x29 -> x0, local copies, waits for them, and re-layouts: 499 us -> none  [the longest x2 103 us: combine_back(): jnp.take_along_axis(grad_rows, (source // 2)[..., None], axis=1)]
    all_to_all x0 -> x4, blocking collectives: none -> 235 us  [to_experts(): got = lax.all_to_all(grouped[:, j], 'row', 0, 0)]
    psum x3 -> x0, waiting for transfers between devices: 204 us -> none  [the longest x2 172 us: hidden_sum(): return lax.psum((part, dots), 'col')]
    reduce_sum x20 -> x11, other arithmetic: 143 us -> 12.9 us  [the longest x2 8.78 us: pair_ranks(): ranks = jnp.sum((earlier * same).astype(F32), axis=-1).astype(jnp.int32)]
    all_to_all x0 -> x24, starting transfers between devices: none -> 106 us  [the longest x10 46 us: to_owners(): got.append(lax.all_to_all(parts, 'row', 0, 0))]
  transfers between devices with their start and end apart: 27 -> 44, of which waited for: 21 -> 26; matrix products, arithmetic and copies ran while one was open for 19% -> 30% of each run, Pallas kernels for 0% -> 1%
where the time goes in v1:
time: 2180 us; the launch traced here: 2170 us
  waiting for transfers between devices  880 us (40%)
  blocking collectives  375 us (17%)
  matrix products  362 us (17%)
  other arithmetic  202 us (9%)
  local copies, waits for them, and re-layouts  187 us (9%)
  starting transfers between devices  107 us (5%)
  Pallas kernels  37.4 us (2%)
    all_to_all x10, waiting for transfers between devices, to_owners(): got.append(lax.all_to_all(parts, 'row', 0, 0))  348 us
    all_to_all x4, blocking collectives, to_experts(): got = lax.all_to_all(grouped[:, j], 'row', 0, 0)  235 us
    dot_general x35, matrix products, dot_f32(): return jnp.einsum(spec, left, right, preferred_element_type=F32)  232 us
    all_to_all x6, waiting for transfers between devices, to_experts(): got = lax.all_to_all(grouped[:, j], 'row', 0, 0)  164 us
    all_gather x4, waiting for transfers between devices, all_tokens(): rows = lax.all_gather(own, 'row', axis=1, tiled=True)  158 us
    reduce_scatter x6, waiting for transfers between devices, slots_home(): own = lax.psum_scatter(rows, 'col', scatter_dimension=1, tiled=True)  92.8 us
    dot_general x8, matrix products, dispatch(): jnp.einsum('snct,sntd->sncd', m.astype(BF16), blocks).reshape(slot_rows, -1)  62.3 us
    all_to_all x6, waiting for transfers between devices, slots_home(): got.append(lax.all_to_all(own, 'row', 1, 1))  57.9 us
  transfers between devices with their start and end apart: 44, of which 26 were waited for; matrix products, arithmetic and copies ran while one was open for 30% of the time, Pallas kernels for 1%

profile of v1, /device:TPU:0, one launch (start us, length us, event | category | flops | bytes accessed | tf_op | source)
XLA Modules:
  0.0 2167.3 jit_solution(9364291650872173186)
XLA Ops:
  8.0 50.3 %all-gather.12.cloned.1.call-done = bf16[4,1024,256]{2,1,0:T(8,128)(2,1)} async-done(((bf16[4,256,256]{2,1,0:T(8,128)(2,1)}), bf16[4,1024,256]{2,1,0:T(8,128)(2,1)}) %all-gather.12.cloned.1.call-update) | async-done | bytes 2097168 | tf_op jit(solution)/shard_map/all_gather | solution.py:173
  66.6 31.1 %all-gather = s32[4,4,2048]{2,1,0:T(4,128)S(1)} all-gather(s32[4,4,512]{2,1,0:T(4,128)S(1)} %pad_add_fusion), channel_id=2, replica_groups=mesh['row'=4,'col'=8] {'row'}, dimensions={2}, use_global_device_ids=true | all-gather | bytes 163840 | tf_op jit(solution)/shard_map/all_gather | solution.py:262
  234.3 10.2 fusion.123
  244.6 10.0 pad_maximum_fusion.3
  286.0 12.7 convolution_convert_fusion.14.v_ref
  298.7 17.4 attend.1
  322.9 27.8 %all_to_all.140 = bf16[4,256,512]{2,1,0:T(8,128)(2,1)S(1)} all-to-all(bf16[4,256,512]{2,1,0:T(8,128)(2,1)S(1)} %copy-done.44), channel_id=1, replica_groups=mesh['row'=4,'col'=8] {'row'}, dimensions={0} | all-to-all | bytes 2097152 | tf_op jit(solution)/shard_map/all_to_all | solution.py:184
  362.2 12.6 reduce-scatter.13.cloned.1.call-done
  381.5 50.9 %reduce-scatter.11.cloned.1.call-done = bf16[1152,256]{1,0:T(8,128)(2,1)} async-done(((bf16[1152,2048]{1,0:T(8,128)(2,1)}), bf16[1152,256]{1,0:T(8,128)(2,1)}) %reduce-scatter.11.cloned.1.call-update) | async-done | bytes 589840 | tf_op jit(solution)/shard_map/reduce_scatter | solution.py:210
  439.3 30.4 %all-to-all-done.3 = bf16[4,4,72,256]{3,2,0,1:T(8,128)(2,1)S(1)} async-done(((bf16[4,4,72,256]{3,2,0,1:T(8,128)(2,1)}), bf16[4,4,72,256]{3,2,0,1:T(8,128)(2,1)S(1)}, u32[]{:S(2)}, u32[]{:S(2)}) %all-to-all-start.3) | async-done | bytes 589856 | tf_op jit(solution)/shard_map/all_to_all | solution.py:212
  472.1 17.3 all-gather.24.cloned.1.call-done
  489.4 46.1 %all-gather.20.cloned.1.call-done = bf16[4,1024,256]{2,1,0:T(8,128)(2,1)} async-done(((bf16[4,256,256]{2,1,0:T(8,128)(2,1)}), bf16[4,1024,256]{2,1,0:T(8,128)(2,1)}) %all-gather.20.cloned.1.call-update) | async-done | bytes 2097168 | tf_op jit(solution)/shard_map/all_gather | solution.py:173
  540.1 67.8 %all_to_all.141 = bf16[4,512,704]{1,2,0:T(8,128)(2,1)S(1)} all-to-all(bf16[4,512,704]{1,2,0:T(8,128)(2,1)S(1)} %get-tuple-element.63), channel_id=1, replica_groups=mesh['row'=4,'col'=8] {'row'}, dimensions={0} | all-to-all | bytes 5767168 | tf_op jit(solution)/shard_map/all_to_all | solution.py:184
  618.1 59.0 %all-to-all-done.10 = bf16[4,512,704]{1,2,0:T(8,128)(2,1)} async-done(((bf16[4,512,704]{1,2,0:T(8,128)(2,1)}), bf16[4,512,704]{1,2,0:T(8,128)(2,1)}, u32[]{:S(2)}, u32[]{:S(2)}) %all-to-all-start.10) | async-done | bytes 2883616 | tf_op jit(solution)/shard_map/all_to_all | solution.py:184
  677.2 69.6 %all_to_all.142 = bf16[4,512,704]{1,2,0:T(8,128)(2,1)} all-to-all(bf16[4,512,704]{1,2,0:T(8,128)(2,1)} %get-tuple-element.65), channel_id=1, replica_groups=mesh['row'=4,'col'=8] {'row'}, dimensions={0} | all-to-all | bytes 5767168 | tf_op jit(solution)/shard_map/all_to_all | solution.py:184
  757.0 58.6 %all-to-all-done.11 = bf16[4,512,704]{1,2,0:T(8,128)(2,1)} async-done(((bf16[4,512,704]{1,2,0:T(8,128)(2,1)}), bf16[4,512,704]{1,2,0:T(8,128)(2,1)}, u32[]{:S(2)}, u32[]{:S(2)}) %all-to-all-start.11) | async-done | bytes 2883616 | tf_op jit(solution)/shard_map/all_to_all | solution.py:184
  815.6 69.6 %all_to_all.143 = bf16[4,704,512]{2,1,0:T(8,128)(2,1)} all-to-all(bf16[4,704,512]{2,1,0:T(8,128)(2,1)} %get-tuple-element.67), channel_id=1, replica_groups=mesh['row'=4,'col'=8] {'row'}, dimensions={0} | all-to-all | bytes 5767168 | tf_op jit(solution)/shard_map/all_to_all | solution.py:184
  925.8 28.2 %all-to-all-done.12 = bf16[4,704,512]{2,1,0:T(8,128)(2,1)} async-done(((bf16[4,704,512]{2,1,0:T(8,128)(2,1)}), bf16[4,704,512]{2,1,0:T(8,128)(2,1)}, u32[]{:S(2)}, u32[]{:S(2)}) %all-to-all-start.12) | async-done | bytes 2883616 | tf_op jit(solution)/shard_map/all_to_all | solution.py:184
  957.8 11.2 fusion.25
  994.0 10.2 fusion.125
  1043.3 9.4 fusion.26
  1087.8 23.1 %psum.42 = f32[4,4,256,2]{2,1,0,3:T(4,128)S(1)} all-reduce(f32[4,4,256,2]{2,1,0,3:T(4,128)S(1)} %pad_maximum_fusion.13), channel_id=1, replica_groups=mesh['row'=4,'col'=8] {'col'}, use_global_device_ids=true, to_apply=%region_48.49 | all-reduce | flops 8192 | bytes 65536 | tf_op jit(solution)/shard_map/psum | solution.py:304
  1124.4 29.4 %reduce-scatter.21.cloned.1.call-done = bf16[1152,256]{1,0:T(8,128)(2,1)} async-done(((bf16[1152,2048]{1,0:T(8,128)(2,1)}), bf16[1152,256]{1,0:T(8,128)(2,1)}) %reduce-scatter.21.cloned.1.call-update) | async-done | bytes 589840 | tf_op jit(solution)/shard_map/reduce_scatter | solution.py:210
  1160.5 15.6 all-to-all-done.15
  1178.6 11.9 psum.43
  1191.8 44.0 %all-gather.28.cloned.1.call-done = bf16[4,1024,256]{2,1,0:T(8,128)(2,1)} async-done(((bf16[4,256,256]{2,1,0:T(8,128)(2,1)}), bf16[4,1024,256]{2,1,0:T(8,128)(2,1)}) %all-gather.28.cloned.1.call-update) | async-done | bytes 2097168 | tf_op jit(solution)/shard_map/all_gather | solution.py:173
  1275.3 54.1 %all-gather.30.cloned.1.call-done = bf16[4,1024,2048]{2,1,0:T(8,128)(2,1)} async-done(((bf16[4,1024,256]{2,1,0:T(8,128)(2,1)}), bf16[4,1024,2048]{2,1,0:T(8,128)(2,1)}) %all-gather.30.cloned.1.call-update) | async-done | bytes 16777232 | tf_op jit(solution)/shard_map/all_gather | solution.py:174
  1329.4 11.5 fusion.29
  1355.3 20.0 attend_back.1
  1408.6 10.2 slice_negate_fusion
  1433.9 16.7 fusion.31
  1451.8 13.1 fusion.52
  1465.0 21.4 convolution_add_fusion
  1486.4 29.0 %fusion.9 = bf16[4,1024,2048]{2,1,0:T(8,128)(2,1)} fusion(f32[4,1024,2048]{2,1,0:T(8,128)} %fusion.52, f32[4,4,256,2048]{3,2,1,0:T(8,128)} %convolution_add_fusion, bf16[4,1024,256]{2,1,0:T(8,128)(2,1)} %get-tuple-element.22, bf16[2048,256]{1,0:T(8,128)(2,1)S(1)} %copy-done.81), kind=kOutput, calls=%fused_computation.14 | convolution fusion | flops 4320133120 | bytes 87031808 | tf_op jit(solution)/shard_map/stf,df->std/dot_general | solution.py:20
  1538.6 56.0 %all-to-all-done.25 = bf16[4,512,704]{1,2,0:T(8,128)(2,1)} async-done(((bf16[4,512,704]{1,2,0:T(8,128)(2,1)}), bf16[4,512,704]{1,2,0:T(8,128)(2,1)}, u32[]{:S(2)}, u32[]{:S(2)}) %all-to-all-start.25) | async-done | bytes 2883616 | tf_op jit(solution)/shard_map/all_to_all | solution.py:201
  1607.9 56.3 %all-to-all-done.23 = bf16[4,512,704]{1,2,0:T(8,128)(2,1)} async-done(((bf16[4,512,704]{1,2,0:T(8,128)(2,1)}), bf16[4,512,704]{1,2,0:T(8,128)(2,1)}, u32[]{:S(2)}, u32[]{:S(2)}) %all-to-all-start.23) | async-done | bytes 2883616 | tf_op jit(solution)/shard_map/all_to_all | solution.py:201
  1677.4 56.0 %all-to-all-done.26 = bf16[4,704,512]{2,1,0:T(8,128)(2,1)} async-done(((bf16[4,704,512]{2,1,0:T(8,128)(2,1)}), bf16[4,704,512]{2,1,0:T(8,128)(2,1)}, u32[]{:S(2)}, u32[]{:S(2)}) %all-to-all-start.26) | async-done | bytes 2883616 | tf_op jit(solution)/shard_map/all_to_all | solution.py:201
  1746.6 56.0 %all-to-all-done.24 = bf16[4,512,704]{1,2,0:T(8,128)(2,1)} async-done(((bf16[4,512,704]{1,2,0:T(8,128)(2,1)}), bf16[4,512,704]{1,2,0:T(8,128)(2,1)}, u32[]{:S(2)}, u32[]{:S(2)}) %all-to-all-start.24) | async-done | bytes 2883616 | tf_op jit(solution)/shard_map/all_to_all | solution.py:201
  1809.3 62.7 %all-to-all-done.22 = bf16[4,512,704]{1,2,0:T(8,128)(2,1)} async-done(((bf16[4,512,704]{1,2,0:T(8,128)(2,1)}), bf16[4,512,704]{1,2,0:T(8,128)(2,1)}, u32[]{:S(2)}, u32[]{:S(2)}) %all-to-all-start.22) | async-done | bytes 2883616 | tf_op jit(solution)/shard_map/all_to_all | solution.py:201
  1879.9 11.9 all-to-all-done.13
  1895.4 12.4 fusion.15
  1908.5 22.7 %psum.44 = f32[4,4,256,2]{2,1,0,3:T(4,128)S(1)} all-reduce(f32[4,4,256,2]{2,1,0,3:T(4,128)S(1)} %pad_maximum_fusion.14), channel_id=1, replica_groups=mesh['row'=4,'col'=8] {'col'}, use_global_device_ids=true, to_apply=%region_58.59 | all-reduce | flops 8192 | bytes 65536 | tf_op jit(solution)/shard_map/psum | solution.py:304
  1947.4 9.8 fusion.14
  1962.4 23.3 %all-to-all-done.20 = bf16[4,256,512]{2,1,0:T(8,128)(2,1)S(1)} async-done(((bf16[4,256,512]{2,1,0:T(8,128)(2,1)}), bf16[4,256,512]{2,1,0:T(8,128)(2,1)S(1)}, u32[]{:S(2)}, u32[]{:S(2)}) %all-to-all-start.20) | async-done | bytes 1048608 | tf_op jit(solution)/shard_map/all_to_all | solution.py:201
  2034.8 35.0 %all-to-all-done.18 = bf16[4,512,256]{2,1,0:T(8,128)(2,1)} async-done(((bf16[4,512,256]{2,1,0:T(8,128)(2,1)}), bf16[4,512,256]{2,1,0:T(8,128)(2,1)}, u32[]{:S(2)}, u32[]{:S(2)}) %all-to-all-start.18) | async-done | bytes 1048608 | tf_op jit(solution)/shard_map/all_to_all | solution.py:201
  2104.1 17.1 all-reduce
  2121.2 12.7 all_gather.54
  2144.5 13.2 psum.45
  (660 shorter events, 705.2 us)
Async XLA Ops:
  7.2 986.8 %copy-start = (bf16[2048,8]{0,1:T(8,128)(2,1)S(1)}, bf16[2048,8]{0,1:T(8,128)(2,1)}, u32[]{:S(2)}) copy-start(bf16[2048,8]{0,1:T(8,128)(2,1)} %param.23) | copy-start | bytes 98308
  7.2 51.1 %all-gather.12.cloned.1.call-start = ((), (), s32[]{:S(2)}) async-start(), calls=%async_computation.38 | async-start | bytes 2621440 | tf_op jit(solution)/shard_map/all_gather | solution.py:173
  7.9 159.1 %all-gather.14.cloned.1.call-start = ((), (), s32[]{:S(2)}) async-start(), calls=%async_computation.39 | async-start | bytes 18874368 | tf_op jit(solution)/shard_map/all_gather | solution.py:174
  58.3 136.6 %all-gather.16.cloned.1.call-start = ((), (), s32[]{:S(2)}) async-start(), calls=%async_computation.40 | async-start | bytes 1310720 | tf_op jit(solution)/shard_map/all_gather | solution.py:311
  61.7 46.2 %all-to-all-start.1 = ((bf16[4,512,256]{2,1,0:T(8,128)(2,1)}), bf16[4,512,256]{2,1,0:T(8,128)(2,1)S(1)}, u32[]{:S(2)}, u32[]{:S(2)}) async-start(bf16[4,512,256]{2,1,0:T(8,128)(2,1)} %get-tuple-element.79), calls=%async_computation.1 | async-start | bytes 2097152 | tf_op jit(solution)/shard_map/all_to_all | solution.py:184
  65.3 220.6 %all-gather.18.cloned.1.call-start = ((), (), s32[]{:S(2)}) async-start(), calls=%async_computation.41 | async-start | bytes 1310720 | tf_op jit(solution)/shard_map/all_gather | solution.py:312
  107.9 27.3 %all-to-all-start = ((bf16[4,512,256]{2,1,0:T(8,128)(2,1)}), bf16[4,512,256]{2,1,0:T(8,128)(2,1)S(1)}, u32[]{:S(2)}, u32[]{:S(2)}) async-start(bf16[4,512,256]{2,1,0:T(8,128)(2,1)} %get-tuple-element.80), calls=%async_computation | async-start | bytes 2097152 | tf_op jit(solution)/shard_map/all_to_all | solution.py:184
  120.4 231.0 %copy-start.91 = (s32[4,4,256]{2,1,0:T(4,128)}, s32[4,4,256]{2,1,0:T(4,128)S(1)}, u32[]{:S(2)}) copy-start(s32[4,4,256]{2,1,0:T(4,128)S(1)} %copy.431) | copy-start | bytes 49156
  135.2 29.5 %all-to-all-start.4 = ((bf16[4,256,512]{2,1,0:T(8,128)(2,1)}), bf16[4,256,512]{2,1,0:T(8,128)(2,1)}, u32[]{:S(2)}, u32[]{:S(2)}) async-start(bf16[4,256,512]{2,1,0:T(8,128)(2,1)} %get-tuple-element.78), calls=%async_computation.5 | async-start | bytes 2097152 | tf_op jit(solution)/shard_map/all_to_all | solution.py:184
  139.4 235.3 %reduce-scatter.13.cloned.1.call-start = ((), (), s32[]{:S(2)}) async-start(), calls=%async_computation.43 | async-start | bytes 5308416 | tf_op jit(solution)/shard_map/reduce_scatter | solution.py:210
  139.6 159.1 %copy-start.8 = (s32[4,1,1024]{2,1,0:T(1,128)}, s32[4,1,1024]{2,1,0:T(1,128)S(1)}, u32[]{:S(2)}) copy-start(s32[4,1,1024]{2,1,0:T(1,128)S(1)} %reshape.707.kblk_ref) | copy-start | bytes 49156
  140.2 158.5 %copy-start.5 = (s32[4,576,1]{2,1,0:T(8,128)}, s32[4,576,1]{2,1,0:T(8,128)S(1)}, u32[]{:S(2)}) copy-start(s32[4,576,1]{2,1,0:T(8,128)S(1)} %copy.442.qblk_ref) | copy-start | bytes 27652
  321.7 110.6 %reduce-scatter.11.cloned.1.call-start = ((), (), s32[]{:S(2)}) async-start(), calls=%async_computation.42 | async-start | bytes 5308416 | tf_op jit(solution)/shard_map/reduce_scatter | solution.py:210
  355.5 133.8 %all-gather.24.cloned.1.call-start = ((), (), s32[]{:S(2)}) async-start(), calls=%async_computation.48 | async-start | bytes 2621440 | tf_op jit(solution)/shard_map/all_gather | solution.py:173
  376.7 57.6 %all-to-all-start.5 = ((bf16[4,4,72,256]{3,2,0,1:T(8,128)(2,1)}), bf16[4,4,72,256]{3,2,0,1:T(8,128)(2,1)S(1)}, u32[]{:S(2)}, u32[]{:S(2)}) async-start(bf16[4,4,72,256]{3,2,0,1:T(8,128)(2,1)} %copy.448), calls=%async_computation.7 | async-start | bytes 1179648 | tf_op jit(solution)/shard_map/all_to_all | solution.py:212
  434.3 35.4 %all-to-all-start.3 = ((bf16[4,4,72,256]{3,2,0,1:T(8,128)(2,1)}), bf16[4,4,72,256]{3,2,0,1:T(8,128)(2,1)S(1)}, u32[]{:S(2)}, u32[]{:S(2)}) async-start(bf16[4,4,72,256]{3,2,0,1:T(8,128)(2,1)} %copy.446), calls=%async_computation.4 | async-start | bytes 1179648 | tf_op jit(solution)/shard_map/all_to_all | solution.py:212
  439.1 96.4 %all-gather.20.cloned.1.call-start = ((), (), s32[]{:S(2)}) async-start(), calls=%async_computation.44 | async-start | bytes 2621440 | tf_op jit(solution)/shard_map/all_gather | solution.py:173
  472.0 485.8 %all-gather.26.cloned.1.call-start = ((), (), s32[]{:S(2)}) async-start(), calls=%async_computation.49 | async-start | bytes 18874368 | tf_op jit(solution)/shard_map/all_gather | solution.py:174
  489.3 485.7 %all-gather.22.cloned.1.call-start = ((), (), s32[]{:S(2)}) async-start(), calls=%async_computation.45 | async-start | bytes 18874368 | tf_op jit(solution)/shard_map/all_gather | solution.py:174
  607.9 69.3 %all-to-all-start.10 = ((bf16[4,512,704]{1,2,0:T(8,128)(2,1)}), bf16[4,512,704]{1,2,0:T(8,128)(2,1)}, u32[]{:S(2)}, u32[]{:S(2)}) async-start(bf16[4,512,704]{1,2,0:T(8,128)(2,1)} %get-tuple-element.64), calls=%async_computation.13 | async-start | bytes 5767168 | tf_op jit(solution)/shard_map/all_to_all | solution.py:184
  746.8 68.8 %all-to-all-start.11 = ((bf16[4,512,704]{1,2,0:T(8,128)(2,1)}), bf16[4,512,704]{1,2,0:T(8,128)(2,1)}, u32[]{:S(2)}, u32[]{:S(2)}) async-start(bf16[4,512,704]{1,2,0:T(8,128)(2,1)} %get-tuple-element.66), calls=%async_computation.14 | async-start | bytes 5767168 | tf_op jit(solution)/shard_map/all_to_all | solution.py:184
  885.2 68.8 %all-to-all-start.12 = ((bf16[4,704,512]{2,1,0:T(8,128)(2,1)}), bf16[4,704,512]{2,1,0:T(8,128)(2,1)}, u32[]{:S(2)}, u32[]{:S(2)}) async-start(bf16[4,704,512]{2,1,0:T(8,128)(2,1)} %get-tuple-element.68), calls=%async_computation.15 | async-start | bytes 5767168 | tf_op jit(solution)/shard_map/all_to_all | solution.py:184
  889.8 225.7 %reduce-scatter.19.cloned.1.call-start = ((), (), s32[]{:S(2)}) async-start(), calls=%async_computation.50 | async-start | bytes 5308416 | tf_op jit(solution)/shard_map/reduce_scatter | solution.py:210
  1042.8 110.9 %reduce-scatter.21.cloned.1.call-start = ((), (), s32[]{:S(2)}) async-start(), calls=%async_computation.51 | async-start | bytes 5308416 | tf_op jit(solution)/shard_map/reduce_scatter | solution.py:210
  1111.5 8.9 all-to-all-start.16
  1120.4 35.2 %all-to-all-start.14 = ((bf16[4,4,72,256]{3,2,0,1:T(8,128)(2,1)}), bf16[4,4,72,256]{3,2,0,1:T(8,128)(2,1)S(1)}, u32[]{:S(2)}, u32[]{:S(2)}) async-start(bf16[4,4,72,256]{3,2,0,1:T(8,128)(2,1)} %copy.476), calls=%async_computation.19 | async-start | bytes 1179648 | tf_op jit(solution)/shard_map/all_to_all | solution.py:212
  1155.7 20.5 all-to-all-start.15
  1160.2 75.5 %all-gather.28.cloned.1.call-start = ((), (), s32[]{:S(2)}) async-start(), calls=%async_computation.52 | async-start | bytes 2621440 | tf_op jit(solution)/shard_map/all_gather | solution.py:173
  1191.7 137.6 %all-gather.30.cloned.1.call-start = ((), (), s32[]{:S(2)}) async-start(), calls=%async_computation.53 | async-start | bytes 18874368 | tf_op jit(solution)/shard_map/all_gather | solution.py:174
  1235.8 571.6 %reduce-scatter.17.cloned.1.call-start = ((), (), s32[]{:S(2)}) async-start(), calls=%async_computation.47 | async-start | bytes 5308416 | tf_op jit(solution)/shard_map/reduce_scatter | solution.py:210
  1263.0 261.0 %all-to-all-start.27 = ((bf16[4,704,512]{2,1,0:T(8,128)(2,1)}), bf16[4,704,512]{2,1,0:T(8,128)(2,1)}, u32[]{:S(2)}, u32[]{:S(2)}) async-start(bf16[4,704,512]{2,1,0:T(8,128)(2,1)} %bitcast.361), calls=%async_computation.37 | async-start | bytes 5767168 | tf_op jit(solution)/shard_map/all_to_all | solution.py:201
  1267.8 610.1 %reduce-scatter.15.cloned.1.call-start = ((), (), s32[]{:S(2)}) async-start(), calls=%async_computation.46 | async-start | bytes 5308416 | tf_op jit(solution)/shard_map/reduce_scatter | solution.py:210
  1275.3 736.0 %reduce-scatter.23.cloned.1.call-start = ((), (), s32[]{:S(2)}) async-start(), calls=%async_computation.54 | async-start | bytes 18874368 | tf_op jit(solution)/shard_map/reduce_scatter | solution.py:436
  1523.9 70.7 %all-to-all-start.25 = ((bf16[4,512,704]{1,2,0:T(8,128)(2,1)}), bf16[4,512,704]{1,2,0:T(8,128)(2,1)}, u32[]{:S(2)}, u32[]{:S(2)}) async-start(bf16[4,512,704]{1,2,0:T(8,128)(2,1)} %bitcast.398), calls=%async_computation.35 | async-start | bytes 5767168 | tf_op jit(solution)/shard_map/all_to_all | solution.py:201
  1594.7 69.5 %all-to-all-start.23 = ((bf16[4,512,704]{1,2,0:T(8,128)(2,1)}), bf16[4,512,704]{1,2,0:T(8,128)(2,1)}, u32[]{:S(2)}, u32[]{:S(2)}) async-start(bf16[4,512,704]{1,2,0:T(8,128)(2,1)} %bitcast.399), calls=%async_computation.33 | async-start | bytes 5767168 | tf_op jit(solution)/shard_map/all_to_all | solution.py:201
  1664.2 69.2 %all-to-all-start.26 = ((bf16[4,704,512]{2,1,0:T(8,128)(2,1)}), bf16[4,704,512]{2,1,0:T(8,128)(2,1)}, u32[]{:S(2)}, u32[]{:S(2)}) async-start(bf16[4,704,512]{2,1,0:T(8,128)(2,1)} %bitcast.401), calls=%async_computation.36 | async-start | bytes 5767168 | tf_op jit(solution)/shard_map/all_to_all | solution.py:201
  1733.4 69.2 %all-to-all-start.24 = ((bf16[4,512,704]{1,2,0:T(8,128)(2,1)}), bf16[4,512,704]{1,2,0:T(8,128)(2,1)}, u32[]{:S(2)}, u32[]{:S(2)}) async-start(bf16[4,512,704]{1,2,0:T(8,128)(2,1)} %bitcast.400), calls=%async_computation.34 | async-start | bytes 5767168 | tf_op jit(solution)/shard_map/all_to_all | solution.py:201
  1802.6 69.3 %all-to-all-start.22 = ((bf16[4,512,704]{1,2,0:T(8,128)(2,1)}), bf16[4,512,704]{1,2,0:T(8,128)(2,1)}, u32[]{:S(2)}, u32[]{:S(2)}) async-start(bf16[4,512,704]{1,2,0:T(8,128)(2,1)} %bitcast.397), calls=%async_computation.32 | async-start | bytes 5767168 | tf_op jit(solution)/shard_map/all_to_all | solution.py:201
  1872.0 19.8 all-to-all-start.13
  1891.8 40.0 %all-to-all-start.9 = ((bf16[4,4,72,256]{3,2,0,1:T(8,128)(2,1)}), bf16[4,4,72,256]{3,2,0,1:T(8,128)(2,1)S(1)}, u32[]{:S(2)}, u32[]{:S(2)}) async-start(bf16[4,4,72,256]{3,2,0,1:T(8,128)(2,1)} %copy.468), calls=%async_computation.12 | async-start | bytes 1179648 | tf_op jit(solution)/shard_map/all_to_all | solution.py:212
  1895.3 202.5 %reduce-scatter.29.cloned.1.call-start = ((), (), s32[]{:S(2)}) async-start(), calls=%async_computation.57 | async-start | bytes 1310720 | tf_op jit(solution)/shard_map/reduce_scatter | solution.py:441
  1931.8 11.2 all-to-all-start.17
  1943.0 42.7 %all-to-all-start.20 = ((bf16[4,256,512]{2,1,0:T(8,128)(2,1)}), bf16[4,256,512]{2,1,0:T(8,128)(2,1)S(1)}, u32[]{:S(2)}, u32[]{:S(2)}) async-start(bf16[4,256,512]{2,1,0:T(8,128)(2,1)} %bitcast.372), calls=%async_computation.30 | async-start | bytes 2097152 | tf_op jit(solution)/shard_map/all_to_all | solution.py:201
  1947.4 152.3 %reduce-scatter.27.cloned.1.call-start = ((), (), s32[]{:S(2)}) async-start(), calls=%async_computation.56 | async-start | bytes 1310720 | tf_op jit(solution)/shard_map/reduce_scatter | solution.py:440
  1985.8 25.5 %all-to-all-start.19 = ((bf16[4,512,256]{2,1,0:T(8,128)(2,1)}), bf16[4,512,256]{2,1,0:T(8,128)(2,1)S(1)}, u32[]{:S(2)}, u32[]{:S(2)}) async-start(bf16[4,512,256]{2,1,0:T(8,128)(2,1)} %bitcast.491), calls=%async_computation.27 | async-start | bytes 2097152 | tf_op jit(solution)/shard_map/all_to_all | solution.py:201
  1989.3 112.2 %reduce-scatter.25.cloned.1.call-start = ((), (), s32[]{:S(2)}) async-start(), calls=%async_computation.55 | async-start | bytes 2621440 | tf_op jit(solution)/shard_map/reduce_scatter | solution.py:437
  2011.3 58.5 %all-to-all-start.18 = ((bf16[4,512,256]{2,1,0:T(8,128)(2,1)}), bf16[4,512,256]{2,1,0:T(8,128)(2,1)}, u32[]{:S(2)}, u32[]{:S(2)}) async-start(bf16[4,512,256]{2,1,0:T(8,128)(2,1)} %bitcast.494), calls=%async_computation.26 | async-start | bytes 2097152 | tf_op jit(solution)/shard_map/all_to_all | solution.py:201
  2069.8 23.8 %all-to-all-start.21 = ((bf16[4,256,512]{2,1,0:T(8,128)(2,1)}), bf16[4,256,512]{2,1,0:T(8,128)(2,1)}, u32[]{:S(2)}, u32[]{:S(2)}) async-start(bf16[4,256,512]{2,1,0:T(8,128)(2,1)} %bitcast.370), calls=%async_computation.31 | async-start | bytes 2097152 | tf_op jit(solution)/shard_map/all_to_all | solution.py:201
  (139 other events, 2132.5 us)
Sparse Core Ops, SparseCore 0:
  9.6 48.6 all-gather.11
  60.2 91.8 all-gather.13
  154.2 27.9 all-gather.15
  183.6 27.4 all-gather.17
  321.9 52.8 reduce-scatter.12
  378.5 53.8 reduce-scatter.10
  434.0 55.3 all-gather.23
  491.5 43.9 all-gather.19
  537.3 91.8 all-gather.25
  630.9 93.1 all-gather.21
  1043.0 52.9 reduce-scatter.18
  1099.7 54.0 reduce-scatter.20
  1191.9 43.8 all-gather.27
  1237.5 91.8 all-gather.29
  1332.7 53.8 reduce-scatter.16
  1390.8 53.8 reduce-scatter.14
  1515.5 116.1 reduce-scatter.22
  1908.1 27.5 reduce-scatter.28
  1957.4 35.4 reduce-scatter.26
  2011.4 62.7 reduce-scatter.24

commit v2 on v1

v2 whole, which is shorter than its diff:
```python
from functools import partial
import math

import jax
import jax.numpy as jnp
from jax import lax
from jax.experimental import pallas as pl
from jax.experimental.pallas import tpu as pltpu
from jax.sharding import PartitionSpec as P

HEAD_DIM = 128
EPSILON = 1e-05
ROPE_BASE = 10000.0
MASKED_SCORE = -1e30
BF16 = jnp.bfloat16
F32 = jnp.float32


def dot_f32(spec, left, right):
    return jnp.einsum(spec, left, right, preferred_element_type=F32)


def tie(value, *others):
    return lax.optimization_barrier((value, others))[0]


def rope_tables(length):
    half_width = HEAD_DIM // 2
    frequency = jnp.exp(
        -math.log(ROPE_BASE) * jnp.arange(half_width, dtype=F32) * (2.0 / HEAD_DIM)
    )
    angles = jnp.arange(length, dtype=jnp.int32).astype(F32)[:, None] * frequency
    cosine, sine = jnp.cos(angles), jnp.sin(angles)
    return (
        jnp.concatenate([cosine, cosine], axis=-1),
        jnp.concatenate([-sine, sine], axis=-1),
    )


def expert_ranks(pairs, order, expert):
    names, places = (jnp.concatenate([a[0], a[1]], axis=-1) for a in (pairs, order))
    ahead = jnp.logical_and(
        places[..., None, :] < places[..., :, None], names[..., None, :] == expert
    )
    rank = jnp.sum(ahead.astype(F32), axis=-1).astype(jnp.int32)
    chosen = jnp.where(names == expert, rank, -1)
    half = chosen.shape[-1] // 2
    return jnp.maximum(chosen[..., :half], chosen[..., half:])


def all_ranks(pairs, order):
    names, places = (jnp.concatenate([a[0], a[1]], axis=-1) for a in (pairs, order))
    ahead = jnp.logical_and(
        places[..., None, :] < places[..., :, None], names[..., None, :] == names[..., :, None]
    )
    rank = jnp.sum(ahead.astype(F32), axis=-1).astype(jnp.int32)
    half = rank.shape[-1] // 2
    return jnp.stack([rank[..., :half], rank[..., half:]])


def slot_match(pairs, ranks, expert, capacity):
    rank_here = jnp.max(jnp.where(pairs == expert, ranks, -1), axis=0)
    slots = jnp.arange(capacity, dtype=jnp.int32)[:, None]
    return rank_here[..., None, :] == slots


def gate_table(logits, routes):
    ids = jnp.arange(logits.shape[-1], dtype=jnp.int32)
    chosen = jnp.any(routes[..., None] == ids, axis=0)
    masked = jnp.where(chosen, logits, MASKED_SCORE)
    top = jnp.max(masked, axis=-1, keepdims=True)
    exps = jnp.where(chosen, jnp.exp(masked - top), 0.0)
    return exps / jnp.sum(exps, axis=-1, keepdims=True)


def normalize_rows(wide):
    inverse = lax.rsqrt(jnp.mean(wide * wide, axis=-1, keepdims=True) + EPSILON)
    return (wide * inverse, inverse)


def roll_half(values):
    return pltpu.roll(values, HEAD_DIM // 2, 1)


def project_kernel(
    rotated, x_ref, gain_ref, router_ref, weight_ref, cos_ref, sin_ref,
    hidden_ref, inverse_ref, logits_ref, out_ref,
):
    normed, inverse = normalize_rows(x_ref[...].astype(F32))
    hidden = (normed * gain_ref[...]).astype(BF16)
    hidden_ref[...] = hidden
    inverse_ref[...] = inverse
    logits_ref[...] = jnp.dot(hidden, router_ref[...], preferred_element_type=F32)
    made = jnp.dot(hidden, weight_ref[...], preferred_element_type=F32)
    cosine, sine = cos_ref[...], sin_ref[...]
    for at, turn in enumerate(rotated):
        columns = slice(at * HEAD_DIM, (at + 1) * HEAD_DIM)
        one = made[:, columns]
        if turn:
            one = one * cosine + roll_half(one) * sine
        out_ref[:, columns] = one.astype(BF16)


def project(x, gain, router, weight, cosine, sine, rotated):
    count, width = x.shape
    experts, cols = router.shape[1], weight.shape[1]
    length = cosine.shape[0]
    tile = 512
    row = lambda n: pl.BlockSpec((tile, n), lambda i: (i, 0))
    whole = lambda a: pl.BlockSpec(a.shape, lambda i: (0, 0))
    table = pl.BlockSpec((tile, HEAD_DIM), lambda i: (lax.rem(i, length // tile), 0))
    return pl.pallas_call(
        partial(project_kernel, rotated),
        grid=(count // tile,),
        in_specs=[row(width), pl.BlockSpec((1, width), lambda i: (0, 0)), whole(router),
                  whole(weight), table, table],
        out_specs=[row(width), row(1), row(experts), row(cols)],
        out_shape=[
            jax.ShapeDtypeStruct((count, width), BF16),
            jax.ShapeDtypeStruct((count, 1), F32),
            jax.ShapeDtypeStruct((count, experts), F32),
            jax.ShapeDtypeStruct((count, cols), BF16),
        ],
        compiler_params=pltpu.CompilerParams(vmem_limit_bytes=48 * 1024 * 1024),
        cost_estimate=pl.CostEstimate(
            flops=2 * count * width * cols,
            bytes_accessed=4 * count * width + 2 * count * cols,
            transcendentals=count,
        ),
        name="project",
    )(x, gain.reshape(1, width), router, weight, cosine, sine)


def scores_of(q, k, qblk, kblk):
    raw = lax.dot_general(q, k, (((1,), (1,)), ((), ())), preferred_element_type=F32)
    return jnp.where(kblk <= qblk, raw * HEAD_DIM ** (-0.5), MASKED_SCORE)


def head_part(ref, at):
    return ref[0, :, at * HEAD_DIM : (at + 1) * HEAD_DIM]


def pick_rows(match, tokens):
    return jnp.dot(match, tokens, preferred_element_type=F32).astype(BF16)


def put_rows(match, rows):
    first = (((0,), (0,)), ((), ()))
    return lax.dot_general(match, rows, first, preferred_element_type=F32)


def slot_rows_of(target_ref, kblk, rows):
    local, length = target_ref.shape[1:]
    at = lax.broadcasted_iota(jnp.int32, (rows, length), 0)
    found = [target_ref[0, j : j + 1] == at for j in range(local)]
    blocks = [
        jnp.sum(jnp.where(m, kblk.astype(F32), 0.0), axis=-1, keepdims=True) for m in found
    ]
    return found, [jnp.where(m, 1.0, 0.0).astype(BF16) for m in found], blocks


def attend_kernel(
    rows, qkv_ref, target_ref, gate_ref, kblk_ref, slot_ref, plain_ref, scaled_ref, lse_ref
):
    local = target_ref.shape[1]
    kblk = kblk_ref[0]
    found, match, blocks = slot_rows_of(target_ref, kblk, rows)
    q = jnp.concatenate([pick_rows(match[j], head_part(qkv_ref, j)) for j in range(local)], axis=0)
    k, v = head_part(qkv_ref, local), head_part(qkv_ref, local + 1)
    scores = scores_of(q, k, jnp.concatenate(blocks, axis=0), kblk.astype(F32))
    top = jnp.max(scores, axis=-1, keepdims=True)
    exps = jnp.exp(scores - top)
    total = jnp.sum(exps, axis=-1, keepdims=True)
    probs = (exps * (1.0 / total)).astype(BF16)
    out = jnp.dot(probs, v, preferred_element_type=F32).astype(BF16)
    lse_ref[0, 0] = top + jnp.log(total)
    for j in range(local):
        here = out[j * rows : (j + 1) * rows]
        gate = jnp.sum(jnp.where(found[j], gate_ref[0, j : j + 1], 0.0), axis=-1, keepdims=True)
        scaled = (here.astype(F32) * gate).astype(BF16)
        columns = slice(j * HEAD_DIM, (j + 1) * HEAD_DIM)
        slot_ref[j, 0] = scaled
        plain_ref[0, :, columns] = put_rows(match[j], here).astype(BF16)
        scaled_ref[0, :, columns] = put_rows(match[j], scaled).astype(BF16)


def attend(qkv, target, gates, kblk, rows, heads):
    seqs, length, cols = qkv.shape
    local = target.shape[1]
    token = lambda n: pl.BlockSpec((1, length, n * HEAD_DIM), lambda s, h: (s, 0, h))
    lane = lambda n: pl.BlockSpec((1, n, length), lambda s, h: (s, 0, 0))
    of_tokens = jax.ShapeDtypeStruct((seqs, length, heads * local * HEAD_DIM), BF16)
    total = local * rows
    return pl.pallas_call(
        partial(attend_kernel, rows),
        grid=(seqs, heads),
        in_specs=[token(local + 2), lane(local), lane(local), lane(1)],
        out_specs=[
            pl.BlockSpec((local, 1, rows, HEAD_DIM), lambda s, h: (0, s, 0, h)),
            token(local),
            token(local),
            pl.BlockSpec((1, 1, total, 1), lambda s, h: (s, h, 0, 0)),
        ],
        out_shape=[
            jax.ShapeDtypeStruct((local, seqs, rows, heads * HEAD_DIM), BF16),
            of_tokens,
            of_tokens,
            jax.ShapeDtypeStruct((seqs, heads, total, 1), F32),
        ],
        compiler_params=pltpu.CompilerParams(vmem_limit_bytes=56 * 1024 * 1024),
        cost_estimate=pl.CostEstimate(
            flops=12 * seqs * heads * total * length * HEAD_DIM,
            bytes_accessed=4 * qkv.size,
            transcendentals=seqs * heads * total * length,
        ),
        name="attend",
    )(qkv, target, gates, kblk)


def attend_back_kernel(
    rows, qkv_ref, target_ref, kblk_ref, lse_ref, plain_ref, raw_ref, gate_ref, cos_ref, sin_ref,
    out_ref, dots_ref,
):
    local = target_ref.shape[1]
    kblk = kblk_ref[0]
    _, match, blocks = slot_rows_of(target_ref, kblk, rows)
    q = jnp.concatenate([pick_rows(match[j], head_part(qkv_ref, j)) for j in range(local)], axis=0)
    k, v = head_part(qkv_ref, local), head_part(qkv_ref, local + 1)
    grads, dots = [], []
    for j in range(local):
        raw = head_part(raw_ref, j)
        gated = (raw * gate_ref[0, :, j : j + 1]).astype(BF16)
        grads.append(pick_rows(match[j], gated))
        dots.append(jnp.sum(raw * head_part(plain_ref, j).astype(F32), axis=-1, keepdims=True))
    g = jnp.concatenate(grads, axis=0)
    scores = scores_of(q, k, jnp.concatenate(blocks, axis=0), kblk.astype(F32))
    probs = jnp.exp(scores - lse_ref[0, 0])
    grad = lax.dot_general(g, v, (((1,), (1,)), ((), ())), preferred_element_type=F32)
    inner = jnp.sum(probs * grad, axis=-1, keepdims=True)
    grad_scores = (probs * (grad - inner) * HEAD_DIM ** (-0.5)).astype(BF16)
    dq = jnp.dot(grad_scores, k, preferred_element_type=F32)
    cosine, sine = cos_ref[...], sin_ref[...]
    inner_sum = 0.0
    turn = lambda value: (value * cosine - roll_half(value) * sine).astype(BF16)
    for j in range(local):
        here = dq[j * rows : (j + 1) * rows]
        high = here.astype(BF16)
        low = (here - high.astype(F32)).astype(BF16)
        placed = put_rows(match[j], high) + put_rows(match[j], low)
        out_ref[0, :, j * HEAD_DIM : (j + 1) * HEAD_DIM] = turn(placed)
        inner_sum = inner_sum + placed * head_part(qkv_ref, j).astype(F32)
    dk = put_rows(grad_scores, q)
    out_ref[0, :, local * HEAD_DIM : (local + 1) * HEAD_DIM] = turn(dk)
    dv = put_rows(probs.astype(BF16), g)
    out_ref[0, :, (local + 1) * HEAD_DIM : (local + 2) * HEAD_DIM] = dv.astype(BF16)
    inner_sum = inner_sum + dk * k.astype(F32) + dv * v.astype(F32)
    dots.append(jnp.sum(inner_sum, axis=-1, keepdims=True))
    for at in range(local + 1):

        @pl.when(pl.program_id(1) == 0)
        def _():
            dots_ref[0, :, at : at + 1] = dots[at]

        @pl.when(pl.program_id(1) > 0)
        def _():
            dots_ref[0, :, at : at + 1] = dots_ref[0, :, at : at + 1] + dots[at]


def attend_back(qkv, target, kblk, lse, plain, raw, gate_cols, cosine, sine, rows, heads):
    seqs, length, cols = qkv.shape
    local = target.shape[1]
    token = lambda n: pl.BlockSpec((1, length, n * HEAD_DIM), lambda s, h: (s, 0, h))
    lane = lambda n: pl.BlockSpec((1, n, length), lambda s, h: (s, 0, 0))
    total = local * rows
    column = pl.BlockSpec((1, length, local), lambda s, h: (s, 0, 0))
    table = pl.BlockSpec((length, HEAD_DIM), lambda s, h: (0, 0))
    return pl.pallas_call(
        partial(attend_back_kernel, rows),
        grid=(seqs, heads),
        in_specs=[
            token(local + 2),
            lane(local),
            lane(1),
            pl.BlockSpec((1, 1, total, 1), lambda s, h: (s, h, 0, 0)),
            token(local),
            token(local),
            column,
            table,
            table,
        ],
        out_specs=[
            token(local + 2),
            pl.BlockSpec((1, length, local + 1), lambda s, h: (s, 0, 0)),
        ],
        out_shape=[
            jax.ShapeDtypeStruct(qkv.shape, BF16),
            jax.ShapeDtypeStruct((seqs, length, local + 1), F32),
        ],
        compiler_params=pltpu.CompilerParams(vmem_limit_bytes=60 * 1024 * 1024),
        cost_estimate=pl.CostEstimate(
            flops=24 * seqs * heads * total * length * HEAD_DIM,
            bytes_accessed=8 * qkv.size,
            transcendentals=seqs * heads * total * length,
        ),
        name="attend_back",
    )(qkv, target, kblk, lse, plain, raw, gate_cols, cosine, sine)


def gather_rows(own):
    return lax.all_gather(own, "row", axis=1, tiled=True)


def gather_cols(rows):
    return lax.all_gather(rows, "col", axis=2, tiled=True)


def exchange(parts):
    return lax.all_to_all(parts, "row", 0, 0)


def exchange_pieces(piece_for):
    ranks, row = lax.axis_size("row"), lax.axis_index("row")
    got = [piece_for(row)]
    for m in range(1, ranks):
        steps = [(i, (i + m) % ranks) for i in range(ranks)]
        got.append(lax.ppermute(piece_for(lax.rem(row + m, ranks)), "row", steps))
    return got


def assemble(pieces, body, outs, name):
    ranks, each = len(pieces), len(pieces[0])

    def kernel(row_ref, *refs):
        for m in range(ranks):

            @pl.when(pl.program_id(0) == m)
            def _():
                body(m, refs[m * each : (m + 1) * each], refs[ranks * each :])

    def at(index):
        return lambda m, row: index(lax.rem(row[0] - m + ranks, ranks))

    flat = [a for piece in pieces for a in piece]
    whole = lambda a: pl.BlockSpec(a.shape, lambda m, row: (0,) * a.ndim)
    return pl.pallas_call(
        kernel,
        grid_spec=pltpu.PrefetchScalarGridSpec(
            num_scalar_prefetch=1,
            grid=(ranks,),
            in_specs=[whole(a) for a in flat],
            out_specs=[pl.BlockSpec(block, at(index)) for _, _, block, index in outs],
        ),
        out_shape=[jax.ShapeDtypeStruct(shape, dtype) for shape, dtype, _, _ in outs],
        compiler_params=pltpu.CompilerParams(vmem_limit_bytes=48 * 1024 * 1024),
        cost_estimate=pl.CostEstimate(
            flops=0, bytes_accessed=4 * sum(a.size for a in flat), transcendentals=0
        ),
        name=name,
    )(lax.axis_index("row").astype(jnp.int32).reshape(1), *flat)


def place_rows(outs, at, pieces, dtype):
    first = 0
    for piece in pieces:
        rows = slice(first, first + piece.shape[0])
        if at is None:
            outs[rows] = piece[...].astype(dtype)
        else:
            outs[at, rows] = piece[...].astype(dtype)
        first += piece.shape[0]


def spread_kernel(into_ref, weight_ref, extra_ref, out_ref):
    last = (((1,), (1,)), ((), ()))
    tokens, copies = into_ref.shape[1], out_ref.shape[2] // extra_ref.shape[2]
    rows = lax.dot_general(into_ref[0], weight_ref[...], last, preferred_element_type=F32)
    out_ref[0, :tokens] = rows.astype(BF16)
    share = extra_ref.shape[2]
    for at in range(copies):
        out_ref[0, tokens:, at * share : (at + 1) * share] = extra_ref[0]


def spread(into, weight, extra):
    blocks, tokens, depth = into.shape
    width = weight.shape[0]
    rows = tokens + extra.shape[1]
    block = lambda a: pl.BlockSpec((1, *a.shape[1:]), lambda i: (i, 0, 0))
    return pl.pallas_call(
        spread_kernel,
        grid=(blocks,),
        in_specs=[block(into), pl.BlockSpec(weight.shape, lambda i: (0, 0)), block(extra)],
        out_specs=pl.BlockSpec((1, rows, width), lambda i: (i, 0, 0)),
        out_shape=jax.ShapeDtypeStruct((blocks, rows, width), BF16),
        compiler_params=pltpu.CompilerParams(vmem_limit_bytes=48 * 1024 * 1024),
        cost_estimate=pl.CostEstimate(
            flops=2 * blocks * tokens * depth * width,
            bytes_accessed=2 * blocks * (tokens * depth + rows * width),
            transcendentals=0,
        ),
        name="spread",
    )(into, weight, extra)


def sum_cols(rows):
    return lax.psum_scatter(rows, "col", scatter_dimension=1, tiled=True)


def round_up(count, unit):
    return -(-count // unit) * unit


def rows_home(own, seqs, capacity, extra=None):
    ranks, share = lax.axis_size("row"), own.shape[-1]
    rows = own.reshape(-1, seqs, ranks, capacity, share).transpose(2, 1, 0, 3, 4)
    rows = rows.reshape(ranks, -1, share)
    count = rows.shape[1]
    if extra is not None:
        rows = jnp.concatenate([rows, extra], axis=1)
    got = exchange(rows)
    home = got[:, :count].reshape(ranks, seqs, -1, share).swapaxes(0, 1)
    return home.reshape(seqs, -1, share), got[:, count:]


def per_device(
    block_in,
    grad_out,
    gain_attn,
    gain_ffn,
    router_attn,
    router_ffn,
    w_query,
    key_weight,
    value_weight,
    w_out,
    w_gate,
    w_up,
    w_down,
    routes_attn,
    routes_ffn,
    order_attn,
    order_ffn,
    block_ids,
):
    seqs, seq_dev, share = block_in.shape
    experts, depth, head_cols = w_query.shape
    capacity = 18 * seq_dev // (8 * experts)
    heads = head_cols // HEAD_DIM
    hidden_units = w_gate.shape[2]
    width = gain_attn.shape[0]
    seq_len = block_ids.shape[1]
    ranks = lax.axis_size("row")
    local = experts // ranks
    row_at, col_at = lax.axis_index("row"), lax.axis_index("col")
    slot_rows = seqs * ranks * capacity
    count = seqs * seq_len

    def own_features(whole):
        return lax.dynamic_slice_in_dim(whole, col_at * share, share, whole.ndim - 1)

    def own_tokens(whole):
        return lax.dynamic_slice_in_dim(whole, row_at * seq_dev, seq_dev, 1)

    def by_pair(table):
        return table.reshape(seqs, seq_dev, 2).transpose(2, 0, 1)

    small = jnp.stack([by_pair(t) for t in (routes_attn, order_attn, routes_ffn, order_ffn)])
    split = jnp.concatenate([small % 256, small[1::2] // 256]).astype(BF16)
    split = split.transpose(2, 0, 1, 3).reshape(seqs, -1)
    held = split.shape[1]
    table_rows = round_up(held, 16 * share) // share
    split = jnp.pad(split, ((0, 0), (0, table_rows * share - held)))
    in_rows = gather_rows(
        jnp.concatenate([block_in, split.reshape(seqs, table_rows, share)], axis=1)
    ).reshape(seqs, ranks, -1, share)
    split = in_rows[:, :, seq_dev:].reshape(seqs, ranks, -1)[..., :held].astype(jnp.int32)
    split = split.reshape(seqs, ranks, 6, 2, seq_dev).transpose(2, 3, 0, 1, 4)
    small_all = [split[0], split[1] + 256 * split[4], split[2], split[3] + 256 * split[5]]
    in_rows = in_rows[:, :, :seq_dev].reshape(seqs, seq_len, share)

    def expert_in(weight, j, *after, half=None):
        weight = tie(weight, *after)
        _, height, columns = weight.shape
        first, rows = (0, height) if half is None else (half * (height // 2), height // 2)

        def piece_for(n):
            block = (1, rows, columns)
            return lax.dynamic_slice(weight, (n * local + j, first, 0), block)[0]

        return exchange_pieces(piece_for)

    def in_body(m, ins, outs):
        place_rows(outs[0], None, ins, BF16)

    def rows_in(*got):
        block = (hidden_units, depth)
        out = ((hidden_units, width), BF16, block, lambda b: (0, b))
        return assemble(list(zip(*got)), in_body, [out], "rows_in")[0]

    w_gate, w_up = w_gate.swapaxes(1, 2), w_up.swapaxes(1, 2)

    def group_in(weight, *after):
        grouped = tie(weight, *after).reshape(ranks, local, *weight.shape[1:])
        return lambda n: lax.dynamic_index_in_dim(grouped, n, 0, keepdims=False)

    parts = local + 2
    query_for = group_in(w_query)
    key_value = jnp.stack([key_weight, value_weight])
    query_got = exchange_pieces(lambda n: jnp.concatenate([query_for(n), key_value]))

    def query_body(m, ins, outs):
        for h in range(heads):
            for p in range(parts):
                at = (h * parts + p) * HEAD_DIM
                piece = ins[0][p, :, h * HEAD_DIM : (h + 1) * HEAD_DIM]
                outs[0][:, at : at + HEAD_DIM] = piece

    made = heads * parts * HEAD_DIM
    query_w = assemble(
        [(p,) for p in query_got],
        query_body,
        [((width, made), BF16, (depth, made), lambda b: (b, 0))],
        "query_in",
    )[0]

    mine = [row_at * local + j for j in range(local)]

    def tokens_to_slots(pairs, order):
        first = jnp.arange(ranks, dtype=jnp.int32)[:, None] * capacity
        out = []
        for e in mine:
            rank = expert_ranks(pairs, order, e)
            kept = jnp.logical_and(rank >= 0, rank < capacity)
            out.append(jnp.where(kept, first + rank, -1).reshape(seqs, seq_len))
        return jnp.stack(out, axis=1)

    target_a = tokens_to_slots(small_all[0], small_all[1])
    target_f = tokens_to_slots(small_all[2], small_all[3])
    routes_a = small_all[0].reshape(2, seqs, seq_len)
    routes_f = small_all[2].reshape(2, seqs, seq_len)
    out_for = group_in(w_out, *small_all)
    out_got = exchange_pieces(out_for)
    gate_first = expert_in(w_gate, 0, *query_got, half=0)

    def home_match(pairs, order):
        ranks_here = all_ranks(pairs, order)
        every = [slot_match(pairs, ranks_here, e, capacity) for e in range(experts)]
        return jnp.concatenate(every, axis=1).astype(BF16)

    home_a = home_match(small[0], small[1])
    home_f = home_match(small[2], small[3])

    def come_home(match, rows):
        return dot_f32("sct,scf->stf", match, rows)

    def my_gates(gates):
        return jnp.stack(
            [lax.dynamic_index_in_dim(gates, e, 2, keepdims=False) for e in mine], axis=1
        )

    in_all = gather_cols(in_rows).reshape(count, width)
    cosine, sine = rope_tables(seq_len)
    rotated = ([True] * (local + 1) + [False]) * heads
    hidden_a, inverse_a, logits_a, qkv = project(
        in_all, gain_attn, router_attn, query_w, cosine, sine, rotated
    )
    qkv = qkv.reshape(seqs, seq_len, -1)
    grad_rows = gather_rows(tie(grad_out, in_all))
    gates_a = gate_table(
        logits_a.reshape(seqs, seq_len, experts), routes_a
    )
    my_gates_a = my_gates(gates_a)
    kblk = block_ids.reshape(seqs, 1, seq_len)
    rows_each = ranks * capacity
    att_slot, att_plain, att_scaled, log_totals = attend(
        qkv, target_a, my_gates_a, kblk, rows_each, heads
    )
    def out_body(m, ins, outs):
        for j in range(local):
            outs[1][j] = ins[0][j]
            for h in range(heads):
                at = (h * local + j) * HEAD_DIM
                outs[0][at : at + HEAD_DIM] = ins[0][j, h * HEAD_DIM : (h + 1) * HEAD_DIM]

    rows_cat = heads * local * HEAD_DIM
    out_cat, out_w = assemble(
        [(p,) for p in tie(out_got, att_slot)],
        out_body,
        [
            ((rows_cat, width), BF16, (rows_cat, depth), lambda b: (0, b)),
            ((local, head_cols, width), BF16, (local, head_cols, depth), lambda b: (0, 0, b)),
        ],
        "out_in",
    )

    out_slots = dot_f32(
        "jrf,jfd->jrd", att_slot.reshape(local, slot_rows, head_cols), out_w
    ).astype(BF16)
    out_slots = tie(out_slots.reshape(-1, width), grad_rows, *gate_first)
    gate_got_in = [(gate_first, expert_in(w_gate, 0, *out_got, *gate_first, half=1))]
    up_first = expert_in(w_up, 0, *out_got, *gate_first, half=0)
    out_own = tie(sum_cols(out_slots), *gate_got_in[0][1], *up_first)
    out_home, _ = rows_home(out_own, seqs, capacity)
    mid = block_in.astype(F32) + come_home(home_a, out_home)

    mid_low = mid.astype(BF16)
    mid_rows = gather_rows(mid_low)
    mid_all = gather_cols(mid_rows).reshape(count, width)
    up_got_in = [(up_first, expert_in(w_up, 0, mid_rows, half=1))]
    down_got_in = [(expert_in(w_down, 0, mid_rows),)]
    mid_all = tie(mid_all, *up_got_in[0][1], *down_got_in[0][0])
    out_grad_all = gather_cols(tie(grad_rows, mid_all))
    normed_f, inverse_f = normalize_rows(mid_all.astype(F32))
    hidden_f = (normed_f * gain_ffn).astype(BF16)
    logits_f = jnp.dot(hidden_f, router_ffn, preferred_element_type=F32)
    gates_f = gate_table(
        logits_f.reshape(seqs, seq_len, experts), routes_f
    )
    my_gates_f = my_gates(gates_f)
    blocked = lambda a: a.reshape(seqs, ranks, seq_dev)
    slots_at = jnp.arange(capacity, dtype=jnp.int32)[:, None]
    first_at = jnp.arange(ranks, dtype=jnp.int32)[:, None, None] * capacity
    match_f = [blocked(target_f[:, j])[:, :, None, :] == first_at + slots_at for j in range(local)]
    weights_f = [
        jnp.sum(
            jnp.where(match_f[j], blocked(my_gates_f[:, j])[:, :, None, :], 0.0), axis=-1
        ).reshape(slot_rows, 1)
        for j in range(local)
    ]

    def dispatch(tokens, j):
        blocks = tokens.reshape(seqs, ranks, seq_dev, width)
        picked = jnp.einsum("snct,sntd->sncd", match_f[j].astype(BF16), blocks)
        return picked.reshape(slot_rows, width)

    down_slots, slot_grads_f, dots_f = [], [], []
    grads_gate, grads_up, grads_down = [], [], []
    for j in range(local):
        slot_in = dispatch(hidden_f, j)
        if j == 0 and local > 1:
            gate_got_in.append((expert_in(w_gate, 1, mid_all),))
            slot_in = tie(slot_in, *gate_got_in[1][0])
        if j + 1 < local:
            up_got_in.append((expert_in(w_up, j + 1, slot_in),))
        gate_w, up_w = rows_in(*gate_got_in[j]), rows_in(*up_got_in[j])
        gate_pre = dot_f32("rd,fd->rf", slot_in, gate_w)
        up_pre = dot_f32("rd,fd->rf", slot_in, up_w)
        down_w = rows_in(*down_got_in[j])
        gate_sig = jax.nn.sigmoid(gate_pre)
        gate_silu = gate_pre * gate_sig
        activated = gate_silu * up_pre
        scaled = (activated * weights_f[j]).astype(BF16)
        slot_grad_out = dispatch(out_grad_all, j)
        grads_down.append(dot_f32("rf,rd->fd", scaled, slot_grad_out).astype(BF16))
        down = jnp.dot(scaled, down_w, preferred_element_type=F32)
        down_slots.append(down.astype(BF16))
        grad_raw = dot_f32("rd,fd->rf", slot_grad_out, down_w)
        grad_act = grad_raw * weights_f[j]
        grad_gate = grad_act * up_pre * (gate_sig * (1.0 + gate_pre * (1.0 - gate_sig)))
        grad_gate = grad_gate.astype(BF16)
        grad_up = (grad_act * gate_silu).astype(BF16)
        grads_gate.append(dot_f32("rf,rd->fd", grad_gate, slot_in).astype(BF16))
        grads_up.append(dot_f32("rf,rd->fd", grad_up, slot_in).astype(BF16))
        slot_grad = dot_f32("rf,fd->rd", grad_gate, gate_w)
        slot_grad = slot_grad + dot_f32("rf,fd->rd", grad_up, up_w)
        slot_grad = slot_grad.astype(BF16)
        if j + 1 < local:
            slot_grad = tie(slot_grad, *up_got_in[-1][0])
            down_got_in.append((expert_in(w_down, j + 1, slot_grad),))
            if j + 2 < local:
                gate_got_in.append((expert_in(w_gate, j + 2, slot_grad),))
        slot_grads_f.append(slot_grad)
        inner = grad_gate.astype(F32) * gate_pre + grad_up.astype(F32) * up_pre
        dots = jnp.stack([jnp.sum(grad_raw * activated, axis=-1), jnp.sum(inner, axis=-1)])
        dots = dots.reshape(2, seqs, ranks, capacity).transpose(2, 0, 1, 3).reshape(ranks, -1)
        dots_f.append(dots.astype(BF16))

    def columns_out(grad, *after, half=None):
        grad = tie(grad, *after)
        size = grad.shape[0] // ranks
        first, rows = (0, size) if half is None else (half * (size // 2), size // 2)
        return exchange_pieces(lambda n: lax.dynamic_slice_in_dim(grad, n * size + first, rows, 0))

    def rows_out(grad, *after, half=None):
        grad = tie(grad, *after)
        height = grad.shape[0]
        first, rows = (0, height) if half is None else (half * (height // 2), height // 2)
        return exchange_pieces(
            lambda n: lax.dynamic_slice(grad, (first, n * depth), (rows, depth))
        )

    def whole_grad(got):
        counts = [len(parts) for parts in got]
        rows = sum(part[0].shape[0] for part in got[0])
        columns = got[0][0][0].shape[1]
        pieces = [tuple(part[m] for parts in got for part in parts) for m in range(ranks)]

        def body(m, ins, outs):
            first = 0
            for j, held in enumerate(counts):
                place_rows(outs[0], j, ins[first : first + held], F32)
                first += held

        out = ((experts, rows, columns), F32, (local, rows, columns), lambda b: (b, 0, 0))
        return assemble(pieces, body, [out], "whole_grad")[0]

    def sublayer_back(own_in, inverse_all, gain, router, gates_all, logits_all, dots, inner, dhidden):
        gates = own_tokens(gates_all)
        inverse = own_tokens(inverse_all)
        dlogits = gates * (dots - jnp.sum(gates * dots, axis=-1, keepdims=True))
        dlogits = dlogits.astype(BF16)
        gain_own = own_features(gain)
        router_own = lax.dynamic_slice_in_dim(router, col_at * share, share, 0)
        normed = own_in.astype(F32) * inverse
        hidden = (normed * gain_own).astype(BF16)
        dhidden = dhidden + dot_f32("ste,fe->stf", dlogits, router_own)
        grad_router = dot_f32("ste,stf->ef", dlogits, hidden)
        grad_gain = jnp.sum(dhidden * normed, axis=(0, 1))
        dn = dhidden * gain_own
        inner = inner + jnp.sum(dlogits.astype(F32) * own_tokens(logits_all), axis=-1)
        grad = inverse * (dn - normed * (inner / width)[..., None])
        return grad, jnp.concatenate([grad_router, grad_gain[None]], axis=0)

    seq3 = lambda a: a.reshape(seqs, seq_len, -1)
    last = down_got_in[-1][-1]
    down_got = [[rows_out(grads_down[0], *last)]]
    gate_first = rows_out(grads_gate[0], *last, half=0)
    per_row = dots_f[0].shape[1]
    dot_rows = round_up(per_row, share) // share
    under = round_up(ranks * dot_rows, 16)
    own_rows, own_dots = [], []
    for rows, dots in zip(slot_grads_f, dots_f):
        dots = jnp.pad(dots, ((0, 0), (0, dot_rows * share - per_row)))
        dots = jnp.pad(dots.reshape(-1, share), ((0, under - ranks * dot_rows), (0, 0)))
        dots = jnp.tile(dots, (1, width // share))
        own = sum_cols(jnp.concatenate([rows, dots], axis=0))
        own_rows.append(own[:slot_rows])
        own_dots.append(own[slot_rows : slot_rows + ranks * dot_rows].reshape(ranks, -1, share))
    own_rows = tie(
        jnp.concatenate(own_rows, axis=0),
        *down_got[0][0],
        *gate_first,
        *grads_gate,
        *grads_up,
        *grads_down,
        *down_slots,
    )
    grad_home, dots_home = rows_home(
        own_rows, seqs, capacity, jnp.concatenate(own_dots, axis=1)
    )
    dhidden_f = come_home(home_f, grad_home)
    dots_home = dots_home.reshape(ranks, local, -1)[..., :per_row].astype(F32)
    dots_home = dots_home.reshape(experts, 2, seqs, capacity, 1).transpose(1, 2, 0, 3, 4)
    match_home = home_f.reshape(seqs, experts, capacity, seq_dev).astype(F32)
    dots_home = jnp.sum(dots_home * match_home, axis=3).swapaxes(2, 3)
    logits_f = logits_f.reshape(seqs, seq_len, experts)
    grad_mid, small_f = sublayer_back(
        mid_low, seq3(inverse_f), gain_ffn, router_ffn, gates_f, logits_f,
        dots_home[0], jnp.sum(dots_home[1], axis=-1), dhidden_f,
    )
    grad_mid = grad_out.astype(F32) + grad_mid

    mid_grad_rows = gather_rows(grad_mid.astype(BF16))
    mid_grad_all = gather_cols(mid_grad_rows).reshape(count, width)
    gate_got = [[gate_first, rows_out(grads_gate[0], mid_grad_rows, half=1)]]
    up_got = [[rows_out(grads_up[0], mid_grad_rows)]]
    mid_grad_all = tie(mid_grad_all, *gate_got[0][1], *up_got[0][0])
    down_slots = tie(jnp.concatenate(down_slots, axis=0), mid_grad_all)
    down_own = sum_cols(down_slots)
    grad_raw = dot_f32("rd,fd->rf", mid_grad_all, out_cat)
    early = []
    for j in range(1, local):
        down_got.append([rows_out(grads_down[j], mid_grad_all)])
        gate_got.append([rows_out(grads_gate[j], mid_grad_all, half=0)])
        early += [*down_got[-1][0], *gate_got[-1][0]]
    into, dots_a = attend_back(
        qkv, target_a, kblk, log_totals, att_plain, seq3(grad_raw), my_gates_a.swapaxes(1, 2),
        cosine, sine, rows_each, heads,
    )
    last = ()
    for j in range(1, local):
        gate_got[j].append(rows_out(grads_gate[j], into, *early, half=1))
        up_got.append([rows_out(grads_up[j], into, *early)])
        last += (*gate_got[j][1], *up_got[-1][0])
    grad_out_cat = dot_f32("rf,rd->fd", att_scaled.reshape(count, -1), mid_grad_all).astype(BF16)
    placed = jnp.zeros((seqs, ranks, experts, seq_dev), F32)
    dots_a = dots_a.reshape(seqs, ranks, seq_dev, local + 1).swapaxes(2, 3)
    placed = lax.dynamic_update_slice_in_dim(placed, dots_a[:, :, :local], row_at * local, 2)
    extra = jnp.concatenate([placed, dots_a[:, :, local:]], axis=2).astype(BF16)
    extra = extra.reshape(seqs * ranks, -1)
    held = extra.shape[1]
    under = round_up(held, 16 * share) // share
    extra = jnp.pad(extra, ((0, 0), (0, under * share - held)))
    token_part = spread(
        into.reshape(seqs * ranks, seq_dev, -1), query_w, extra.reshape(-1, under, share)
    ).reshape(seqs, -1, width)
    token_part = tie(token_part, down_own, *early)
    down_home, _ = rows_home(tie(down_own, token_part), seqs, capacity)
    part = lax.psum_scatter(token_part, "col", scatter_dimension=2, tiled=True)
    out_pieces = rows_out(grad_out_cat, token_part, *last)
    part = tie(part, *last, *out_pieces, down_home)
    own = lax.psum_scatter(part, "row", scatter_dimension=1, tiled=True)
    dhidden_a = own[:, :seq_dev].astype(F32)
    dots_a = own[:, seq_dev:].reshape(seqs, -1)[:, :held].astype(F32)
    dots_a = dots_a.reshape(seqs, experts + 1, seq_dev).swapaxes(1, 2)

    def out_grad_body(m, ins, outs):
        for j in range(local):
            for h in range(heads):
                at = (h * local + j) * HEAD_DIM
                piece = ins[0][at : at + HEAD_DIM].astype(F32)
                outs[0][j, h * HEAD_DIM : (h + 1) * HEAD_DIM] = piece

    grad_out_own = assemble(
        [(p,) for p in out_pieces],
        out_grad_body,
        [((experts, head_cols, depth), F32, (local, head_cols, depth), lambda b: (b, 0, 0))],
        "out_grad",
    )[0]

    def query_grad_body(m, ins, outs):
        for h in range(heads):
            columns = slice(h * HEAD_DIM, (h + 1) * HEAD_DIM)
            for p in range(parts):
                at = (h * parts + p) * HEAD_DIM
                piece = ins[0][:, at : at + HEAD_DIM].astype(F32)
                if p < local:
                    outs[0][p, :, columns] = piece
                elif m == 0:
                    outs[1 + p - local][:, columns] = piece
                else:
                    outs[1 + p - local][:, columns] = outs[1 + p - local][:, columns] + piece

    grad_query_cat = dot_f32("rd,rf->df", hidden_a, into.reshape(count, -1)).astype(BF16)
    shared = ((depth, head_cols), F32, (depth, head_cols), lambda b: (0, 0))
    grad_query_own, grad_key_own, grad_value_own = assemble(
        [(p,) for p in columns_out(grad_query_cat, part)],
        query_grad_body,
        [
            ((experts, depth, head_cols), F32, (local, depth, head_cols), lambda b: (b, 0, 0)),
            shared,
            shared,
        ],
        "query_grad",
    )
    logits_a = logits_a.reshape(seqs, seq_len, experts)
    grad_in, small_a = sublayer_back(
        block_in, seq3(inverse_a), gain_attn, router_attn, gates_a, logits_a,
        dots_a[..., :experts], dots_a[..., experts], dhidden_a,
    )
    grad_in = grad_mid + grad_in
    block_out = (mid + come_home(home_f, down_home)).astype(BF16)

    smalls = jnp.concatenate([small_a, small_f], axis=0)
    smalls = lax.all_gather(smalls, ("row", "col"), axis=0, tiled=False)
    smalls = smalls.reshape(ranks, -1, 2 * experts + 2, share)
    smalls = jnp.sum(smalls, axis=0).transpose(1, 0, 2).reshape(-1, width)
    return (
        block_out,
        grad_in,
        smalls[experts],
        smalls[2 * experts + 1],
        smalls[:experts].T,
        smalls[experts + 1 : 2 * experts + 1].T,
        grad_query_own,
        grad_key_own,
        grad_value_own,
        grad_out_own,
        whole_grad(gate_got).swapaxes(1, 2),
        whole_grad(up_got).swapaxes(1, 2),
        whole_grad(down_got),
    )


def solution(mesh):
    in_specs = (
        P(None, "row", "col"),
        P(None, "row", "col"),
        P(),
        P(),
        P(),
        P(),
        P(None, "row", "col"),
        P("row", "col"),
        P("row", "col"),
        P(None, "col", "row"),
        P(None, "row", "col"),
        P(None, "row", "col"),
        P(None, "col", "row"),
        P(None, "row", None),
        P(None, "row", None),
        P(None, "row", None),
        P(None, "row", None),
        P(),
    )
    out_specs = (
        P(None, "row", "col"),
        P(None, "row", "col"),
        P(),
        P(),
        P(),
        P(),
        P(None, "row", "col"),
        P("row", "col"),
        P("row", "col"),
        P(None, "col", "row"),
        P(None, "row", "col"),
        P(None, "row", "col"),
        P(None, "col", "row"),
    )
    return jax.shard_map(
        per_device, mesh=mesh, in_specs=in_specs, out_specs=out_specs, check_vma=False
    )
```

time: 2180 us -> 1680 us (0.77)
  blocking collectives: 375 us -> 40 us
  Pallas kernels: 37.4 us -> 169 us
  other arithmetic: 202 us -> 77.5 us
  matrix products: 362 us -> 247 us
  local copies, waits for them, and re-layouts: 187 us -> 114 us
  starting transfers between devices: 107 us -> 156 us
  waiting for transfers between devices: 880 us -> 846 us
    ppermute x0 -> x60, waiting for transfers between devices: none -> 647 us  [exchange_pieces(): got.append(lax.ppermute(piece_for(lax.rem(row + m, ranks)), 'row', steps))]
    all_to_all x24 -> x3, waiting for transfers between devices: 573 us -> 50.2 us  [exchange(): return lax.all_to_all(parts, 'row', 0, 0)]
    all_to_all x4 -> x0, blocking collectives: 235 us -> none  [to_experts(): got = lax.all_to_all(grouped[:, j], 'row', 0, 0)]
    ppermute x0 -> x60, starting transfers between devices: none -> 142 us  [exchange_pieces(): got.append(lax.ppermute(piece_for(lax.rem(row + m, ranks)), 'row', steps))]
    pallas_call x2 -> x17, Pallas kernels: 37.4 us -> 169 us  [the longest x1 43.7 us: attend_back(): pl.pallas_call(partial(attend_back_kernel, rows), grid=(seqs, heads), in_...]
    all_to_all x24 -> x3, starting transfers between devices: 106 us -> 13.2 us  [exchange(): return lax.all_to_all(parts, 'row', 0, 0)]
    psum x5 -> x0, blocking collectives: 88 us -> none  [the longest x2 45.8 us: gate_dots(): both = lax.psum(both, 'col')]
    reduce_scatter x10 -> x6, waiting for transfers between devices: 92.8 us -> 8.69 us  [the longest x4 8.68 us: sum_cols(): return lax.psum_scatter(rows, 'col', scatter_dimension=1, tiled=True)]
  transfers between devices with their start and end apart: 44 -> 77, of which waited for: 26 -> 28; matrix products, arithmetic and copies ran while one was open for 30% -> 22% of each run, Pallas kernels for 1% -> 10%
where the time goes in v2:
time: 1680 us; the launch traced here: 1670 us
  waiting for transfers between devices  846 us (50%)
  matrix products  247 us (15%)
  Pallas kernels  169 us (10%)
  starting transfers between devices  156 us (9%)
  local copies, waits for them, and re-layouts  114 us (7%)
  other arithmetic  77.5 us (5%)
  blocking collectives  40 us (2%)
    ppermute x60, waiting for transfers between devices, exchange_pieces(): got.append(lax.ppermute(piece_for(lax.rem(row + m, ranks)), 'row', steps))  647 us
    dot_general x27, matrix products, dot_f32(): return jnp.einsum(spec, left, right, preferred_element_type=F32)  183 us
    ppermute x60, starting transfers between devices, exchange_pieces(): got.append(lax.ppermute(piece_for(lax.rem(row + m, ranks)), 'row', steps))  142 us
    all_gather x4, waiting for transfers between devices, gather_rows(): return lax.all_gather(own, 'row', axis=1, tiled=True)  140 us
    all_to_all x3, waiting for transfers between devices, exchange(): return lax.all_to_all(parts, 'row', 0, 0)  50.2 us
    unnamed x329, local copies, waits for them, and re-layouts  45.8 us
    pallas_call x1, Pallas kernels, attend_back(): pl.pallas_call(partial(attend_back_kernel, rows), grid=(seqs, heads), in_...  43.7 us
    dot_general x4, matrix products, dispatch(): picked = jnp.einsum('snct,sntd->sncd', match_f[j].astype(BF16), blocks)  40.4 us
  transfers between devices with their start and end apart: 77, of which 28 were waited for; matrix products, arithmetic and copies ran while one was open for 22% of the time, Pallas kernels for 10%

profile of v2, /device:TPU:0, one launch (start us, length us, event | category | flops | bytes accessed | tf_op | source)
XLA Modules:
  0.0 1665.3 jit_solution(12331126801991759497)
XLA Ops:
  13.4 51.1 %all-gather.11.cloned.1.call-done = bf16[4,1088,256]{2,1,0:T(8,128)(2,1)} async-done(((bf16[4,272,256]{2,1,0:T(8,128)(2,1)}), bf16[4,1088,256]{2,1,0:T(8,128)(2,1)}) %all-gather.11.cloned.1.call-update) | async-done | bytes 2228240 | tf_op jit(solution)/shard_map/all_gather | solution.py:310
  83.7 36.8 %collective-permute-done.2.refs_3_ = bf16[4,512,256]{2,1,0:T(8,128)(2,1)S(1)} collective-permute-done((bf16[4,512,256]{2,1,0:T(8,128)(2,1)}, bf16[4,512,256]{2,1,0:T(8,128)(2,1)S(1)}, u32[]{:S(2)}, u32[]{:S(2)}) %collective-permute-start.2) | collective-permute-done | bytes 1048608 | tf_op jit(solution)/shard_map/ppermute | solution.py:326
  120.5 65.7 %collective-permute-done.1.refs_2_ = bf16[4,512,256]{2,1,0:T(8,128)(2,1)} collective-permute-done((bf16[4,512,256]{2,1,0:T(8,128)(2,1)}, bf16[4,512,256]{2,1,0:T(8,128)(2,1)}, u32[]{:S(2)}, u32[]{:S(2)}) %collective-permute-start.1) | collective-permute-done | bytes 1048608 | tf_op jit(solution)/shard_map/ppermute | solution.py:326
  216.2 31.9 %project.1 = (bf16[4096,2048]{1,0:T(8,128)(2,1)}, f32[4096,1]{1,0:T(8,128)S(1)}, f32[4096,8]{1,0:T(8,128)S(1)}, bf16[4096,1024]{1,0:T(8,128)(2,1)}) custom-call(bf16[4096,2048]{1,0:T(8,128)(2,1)} %bitcast.493, f32[1,2048]{1,0:T(1,128)S(1)} %bitcast.387, bf16[2048,8]{1,0:T(8,128)(2,1)S(1)} %copy-done.47, bf16[2048,1024]{1,0:T(8,128)(2,1)} %query_in.1.weight_ref, ...), custom_call_target="tpu_custom_call" | custom-call | flops 17179869184 | bytes 41943040 | tf_op jit(solution)/shard_map/project/pallas_call | solution.py:112
  254.1 29.8 %attend.1 = (bf16[2,4,288,256]{3,2,1,0:T(8,128)(2,1)}, bf16[4,1024,512]{2,1,0:T(8,128)(2,1)}, bf16[4,1024,512]{2,1,0:T(8,128)(2,1)}, f32[4,2,576,1]{3,2,1,0:T(8,128)}) custom-call(bf16[4,1024,1024]{2,1,0:T(8,128)(2,1)} %bitcast.496, s32[4,2,1024]{2,1,0:T(2,128)} %pad_add_fusion.3.target_ref, f32[4,2,1024]{2,1,0:T(2,128)} %copy.229.gate_ref, ...), custom_call_target="tpu_custom_call" | custom-call | flops 7247757312 | bytes 16777216 | tf_op jit(solution)/shard_map/attend/pallas_call | solution.py:194
  287.9 9.1 convolution_convert_fusion
  313.5 17.0 %collective-permute-start.12 = (bf16[352,512]{1,0:T(8,128)(2,1)S(1)}, bf16[352,512]{1,0:T(8,128)(2,1)S(1)}, u32[]{:S(2)}, u32[]{:S(2)}) collective-permute-start(bf16[352,512]{1,0:T(8,128)(2,1)S(1)} %get-tuple-element.175), channel_id=1, source_target_pairs={{0,8},{8,16},{16,24},{24,0},{1,9},{9,17},{17,25},{25,1},{2,10},{10... | collective-permute-start | bytes 1081352 | tf_op jit(solution)/shard_map/ppermute | solution.py:326
  331.6 21.5 %collective-permute-done.10.refs_5_ = bf16[352,512]{1,0:T(8,128)(2,1)S(1)} collective-permute-done((bf16[352,512]{1,0:T(8,128)(2,1)}, bf16[352,512]{1,0:T(8,128)(2,1)S(1)}, u32[]{:S(2)}, u32[]{:S(2)}) %collective-permute-start.10) | collective-permute-done | bytes 360480 | tf_op jit(solution)/shard_map/ppermute | solution.py:326
  353.1 12.3 collective-permute-done.13.refs_4_
  366.1 8.7 reduce-scatter.7.cloned.1.call-done
  387.1 23.2 %all-to-all-done = bf16[4,576,256]{2,1,0:T(8,128)(2,1)} async-done(((bf16[4,576,256]{2,1,0:T(8,128)(2,1)}), bf16[4,576,256]{2,1,0:T(8,128)(2,1)}, u32[]{:S(2)}, u32[]{:S(2)}) %all-to-all-start) | async-done | bytes 1179680 | tf_op jit(solution)/shard_map/all_to_all | solution.py:318
  415.2 44.2 %all-gather.17.cloned.1.call-done = bf16[4,1024,256]{2,1,0:T(8,128)(2,1)} async-done(((bf16[4,256,256]{2,1,0:T(8,128)(2,1)}), bf16[4,1024,256]{2,1,0:T(8,128)(2,1)}) %all-gather.17.cloned.1.call-update) | async-done | bytes 2097168 | tf_op jit(solution)/shard_map/all_gather | solution.py:310
  473.0 82.4 %collective-permute-done.16.refs_5_ = bf16[352,512]{1,0:T(8,128)(2,1)S(1)} collective-permute-done((bf16[352,512]{1,0:T(8,128)(2,1)S(1)}, bf16[352,512]{1,0:T(8,128)(2,1)S(1)}, u32[]{:S(2)}, u32[]{:S(2)}) %collective-permute-start.16) | collective-permute-done | bytes 360480 | tf_op jit(solution)/shard_map/ppermute | solution.py:326
  580.0 9.7 fusion
  591.7 9.4 fusion.2
  601.2 10.9 fusion.86
  623.0 11.4 fusion.9
  634.4 11.0 fusion.13
  645.5 37.9 %collective-permute-done.22.refs_2_ = bf16[704,512]{1,0:T(8,128)(2,1)S(1)} collective-permute-done((bf16[704,512]{1,0:T(8,128)(2,1)S(1)}, bf16[704,512]{1,0:T(8,128)(2,1)S(1)}, u32[]{:S(2)}, u32[]{:S(2)}) %collective-permute-start.22) | collective-permute-done | bytes 720928 | tf_op jit(solution)/shard_map/ppermute | solution.py:326
  687.4 9.0 fusion.85
  696.5 8.0 fusion.84
  704.4 8.9 fusion.11
  713.4 7.9 multiply_reduce_fusion.2
  732.6 14.6 collective-permute-done.25.refs_2_
  749.9 8.9 fusion.87
  760.8 8.3 fusion.88
  774.3 9.0 fusion.7
  787.1 47.8 %collective-permute-done.28.refs_2_ = bf16[704,512]{1,0:T(8,128)(2,1)S(1)} collective-permute-done((bf16[704,512]{1,0:T(8,128)(2,1)S(1)}, bf16[704,512]{1,0:T(8,128)(2,1)S(1)}, u32[]{:S(2)}, u32[]{:S(2)}) %collective-permute-start.28) | collective-permute-done | bytes 720928 | tf_op jit(solution)/shard_map/ppermute | solution.py:326
  835.7 10.4 multiply_reduce_fusion.1
  868.0 7.7 convolution_convert_fusion.9
  925.2 57.3 %collective-permute-done.34.refs_8_ = bf16[352,512]{1,0:T(8,128)(2,1)} collective-permute-done((bf16[352,512]{1,0:T(8,128)(2,1)}, bf16[352,512]{1,0:T(8,128)(2,1)}, u32[]{:S(2)}, u32[]{:S(2)}) %collective-permute-start.34) | collective-permute-done | bytes 360480 | tf_op jit(solution)/shard_map/ppermute | solution.py:326
  991.8 26.9 %all-to-all-done.1 = bf16[4,582,256]{2,1,0:T(8,128)(2,1)} async-done(((bf16[4,582,256]{2,1,0:T(8,128)(2,1)}), bf16[4,582,256]{2,1,0:T(8,128)(2,1)}, u32[]{:S(2)}, u32[]{:S(2)}) %all-to-all-start.1) | async-done | bytes 1191968 | tf_op jit(solution)/shard_map/all_to_all | solution.py:318
  1025.5 44.5 %all-gather.23.cloned.1.call-done = bf16[4,1024,256]{2,1,0:T(8,128)(2,1)} async-done(((bf16[4,256,256]{2,1,0:T(8,128)(2,1)}), bf16[4,1024,256]{2,1,0:T(8,128)(2,1)}) %all-gather.23.cloned.1.call-update) | async-done | bytes 2097168 | tf_op jit(solution)/shard_map/all_gather | solution.py:310
  1086.0 7.6 pad_maximum_fusion
  1093.6 12.8 collective-permute-done.37.refs_9_
  1113.7 53.4 %collective-permute-done.40.refs_4_ = bf16[704,512]{1,0:T(8,128)(2,1)S(1)} collective-permute-done((bf16[704,512]{1,0:T(8,128)(2,1)}, bf16[704,512]{1,0:T(8,128)(2,1)S(1)}, u32[]{:S(2)}, u32[]{:S(2)}) %collective-permute-start.40) | collective-permute-done | bytes 720928 | tf_op jit(solution)/shard_map/ppermute | solution.py:326
  1181.5 15.9 fusion.92
  1197.3 43.7 %attend_back.1 = (bf16[4,1024,1024]{2,1,0:T(8,128)(2,1)}, f32[4,1024,3]{2,1,0:T(8,128)}) custom-call(bf16[4,1024,1024]{2,1,0:T(8,128)(2,1)} %bitcast.497, s32[4,2,1024]{2,1,0:T(2,128)} %pad_add_fusion.3.target_ref, s32[4,1,1024]{2,1,0:T(1,128)} %reshape.520.kblk_ref, f32[4,2,576,1]{3,2,1,0:T(8,128)} %get-tuple-element.93.lse_ref, ...), custom_call_target="tpu_custom_call" | custom-call | flops 14495514624 | bytes 33554432 | tf_op jit(solution)/shard_map/attend_back/pallas_call | solution.py:277
  1243.5 20.0 %collective-permute-start.45 = (bf16[352,512]{1,0:T(8,128)(2,1)}, bf16[352,512]{1,0:T(8,128)(2,1)S(1)}, u32[]{:S(2)}, u32[]{:S(2)}) collective-permute-start(bf16[352,512]{1,0:T(8,128)(2,1)} %get-tuple-element.199), channel_id=1, source_target_pairs={{0,8},{8,16},{16,24},{24,0},{1,9},{9,17},{17,25},{25,1},{2,10},{10... | collective-permute-start | bytes 1081352 | tf_op jit(solution)/shard_map/ppermute | solution.py:326
  1265.7 23.7 %spread.1 = bf16[16,272,2048]{2,1,0:T(8,128)(2,1)} custom-call(bf16[16,256,1024]{2,1,0:T(8,128)(2,1)} %bitcast.498, bf16[2048,1024]{1,0:T(8,128)(2,1)S(1)} %copy-done.1, bf16[16,16,256]{2,1,0:T(8,128)(2,1)S(1)} %bitcast.386), custom_call_target="tpu_custom_call" | custom-call | flops 17179869184 | bytes 26214400 | tf_op jit(solution)/shard_map/spread/pallas_call | solution.py:388
  1306.7 14.3 collective-permute-start.51
  1321.0 13.8 convolution_convert_fusion.10
  1336.2 66.4 %collective-permute-done.52.refs_5_ = bf16[704,512]{1,0:T(8,128)(2,1)} collective-permute-done((bf16[704,512]{1,0:T(8,128)(2,1)}, bf16[704,512]{1,0:T(8,128)(2,1)}, u32[]{:S(2)}, u32[]{:S(2)}) %collective-permute-start.52) | collective-permute-done | bytes 720928 | tf_op jit(solution)/shard_map/ppermute | solution.py:326
  1404.9 23.0 %collective-permute-start.55 = (bf16[512,512]{1,0:T(8,128)(2,1)}, bf16[512,512]{1,0:T(8,128)(2,1)}, u32[]{:S(2)}, u32[]{:S(2)}) collective-permute-start(bf16[512,512]{1,0:T(8,128)(2,1)} %get-tuple-element.222), channel_id=1, source_target_pairs={{0,16},{8,24},{16,0},{24,8},{1,17},{9,25},{17,1},{25,9},{2,18},{10... | collective-permute-start | bytes 1572872 | tf_op jit(solution)/shard_map/ppermute | solution.py:326
  1438.4 35.6 %collective-permute-done.55.refs_2_ = bf16[512,512]{1,0:T(8,128)(2,1)} collective-permute-done((bf16[512,512]{1,0:T(8,128)(2,1)}, bf16[512,512]{1,0:T(8,128)(2,1)}, u32[]{:S(2)}, u32[]{:S(2)}) %collective-permute-start.55) | collective-permute-done | bytes 524320 | tf_op jit(solution)/shard_map/ppermute | solution.py:326
  1474.0 23.0 %convolution_convert_fusion.3 = bf16[2048,1024]{1,0:T(8,128)(2,1)S(1)} fusion(bf16[4096,2048]{1,0:T(8,128)(2,1)} %get-tuple-element.108, bf16[4096,1024]{1,0:T(8,128)(2,1)} %bitcast.499), kind=kOutput, calls=%fused_computation.24 | convolution fusion | flops 17181966336 | bytes 29360128 | tf_op jit(solution)/shard_map/rd,rf->df/dot_general | solution.py:20
  1538.7 68.3 %collective-permute-done.58.refs_2_ = bf16[512,1024]{1,0:T(8,128)(2,1)} collective-permute-done((bf16[512,1024]{1,0:T(8,128)(2,1)}, bf16[512,1024]{1,0:T(8,128)(2,1)}, u32[]{:S(2)}, u32[]{:S(2)}) %collective-permute-start.58) | collective-permute-done | bytes 1048608 | tf_op jit(solution)/shard_map/ppermute | solution.py:326
  1616.9 40.0 %all-gather.1 = f32[32,18,256]{2,1,0:T(8,128)S(1)} all-gather(f32[1,18,256]{2,1,0:T(8,128)S(1)} %maximum_bitcast_fusion), channel_id=2, replica_groups=mesh['row'=4,'col'=8] {'row','col'}, dimensions={0}, use_global_device_ids=true | all-gather | bytes 608256 | tf_op jit(solution)/shard_map/all_gather | solution.py:854
  (698 shorter events, 393.6 us)
Async XLA Ops:
  13.4 200.4 %all-gather.13.cloned.1.call-start = ((), (), s32[]{:S(2)}) async-start(), calls=%async_computation.10 | async-start | bytes 18874368 | tf_op jit(solution)/shard_map/all_gather | solution.py:314
  67.6 229.3 %all-gather.15.cloned.1.call-start = ((), (), s32[]{:S(2)}) async-start(), calls=%async_computation.11 | async-start | bytes 2621440 | tf_op jit(solution)/shard_map/all_gather | solution.py:310
  72.5 113.6 %collective-permute-start.1 = (bf16[4,512,256]{2,1,0:T(8,128)(2,1)}, bf16[4,512,256]{2,1,0:T(8,128)(2,1)}, u32[]{:S(2)}, u32[]{:S(2)}) collective-permute-start(bf16[4,512,256]{2,1,0:T(8,128)(2,1)} %get-tuple-element.238), channel_id=1, source_target_pairs={{0,16},{8,24},{16,0},{24,8},{1,17},{9,25},{17,1},{25,9},{2,18},{10... | collective-permute-start | bytes 3145736 | tf_op jit(solution)/shard_map/ppermute | solution.py:326
  75.0 208.8 %collective-permute-start.5 = (bf16[2,256,512]{2,1,0:T(8,128)(2,1)}, bf16[2,256,512]{2,1,0:T(8,128)(2,1)}, u32[]{:S(2)}, u32[]{:S(2)}) collective-permute-start(bf16[2,256,512]{2,1,0:T(8,128)(2,1)} %get-tuple-element.225), channel_id=1, source_target_pairs={{0,24},{8,0},{16,8},{24,16},{1,25},{9,1},{17,9},{25,17},{2,26},{10... | collective-permute-start | bytes 1572872 | tf_op jit(solution)/shard_map/ppermute | solution.py:326
  76.4 208.0 %collective-permute-start.4 = (bf16[2,256,512]{2,1,0:T(8,128)(2,1)}, bf16[2,256,512]{2,1,0:T(8,128)(2,1)}, u32[]{:S(2)}, u32[]{:S(2)}) collective-permute-start(bf16[2,256,512]{2,1,0:T(8,128)(2,1)} %get-tuple-element.226), channel_id=1, source_target_pairs={{0,16},{8,24},{16,0},{24,8},{1,17},{9,25},{17,1},{25,9},{2,18},{10... | collective-permute-start | bytes 1572872 | tf_op jit(solution)/shard_map/ppermute | solution.py:326
  120.5 164.0 %collective-permute-start.3 = (bf16[2,256,512]{2,1,0:T(8,128)(2,1)}, bf16[2,256,512]{2,1,0:T(8,128)(2,1)}, u32[]{:S(2)}, u32[]{:S(2)}) collective-permute-start(bf16[2,256,512]{2,1,0:T(8,128)(2,1)} %get-tuple-element.227), channel_id=1, source_target_pairs={{0,8},{8,16},{16,24},{24,0},{1,9},{9,17},{17,25},{25,1},{2,10},{10... | collective-permute-start | bytes 1572872 | tf_op jit(solution)/shard_map/ppermute | solution.py:326
  188.5 108.5 %collective-permute-start.8 = (bf16[352,512]{1,0:T(8,128)(2,1)}, bf16[352,512]{1,0:T(8,128)(2,1)}, u32[]{:S(2)}, u32[]{:S(2)}) collective-permute-start(bf16[352,512]{1,0:T(8,128)(2,1)} %get-tuple-element.181), channel_id=1, source_target_pairs={{0,24},{8,0},{16,8},{24,16},{1,25},{9,1},{17,9},{25,17},{2,26},{10... | collective-permute-start | bytes 1081352 | tf_op jit(solution)/shard_map/ppermute | solution.py:326
  191.0 106.0 %collective-permute-start.7 = (bf16[352,512]{1,0:T(8,128)(2,1)}, bf16[352,512]{1,0:T(8,128)(2,1)}, u32[]{:S(2)}, u32[]{:S(2)}) collective-permute-start(bf16[352,512]{1,0:T(8,128)(2,1)} %get-tuple-element.182), channel_id=1, source_target_pairs={{0,16},{8,24},{16,0},{24,8},{1,17},{9,25},{17,1},{25,9},{2,18},{10... | collective-permute-start | bytes 1081352 | tf_op jit(solution)/shard_map/ppermute | solution.py:326
  213.8 161.0 %reduce-scatter.7.cloned.1.call-start = ((), (), s32[]{:S(2)}) async-start(), calls=%async_computation.12 | async-start | bytes 10616832 | tf_op jit(solution)/shard_map/reduce_scatter | solution.py:405
  381.7 77.7 %all-gather.17.cloned.1.call-start = ((), (), s32[]{:S(2)}) async-start(), calls=%async_computation.13 | async-start | bytes 2621440 | tf_op jit(solution)/shard_map/all_gather | solution.py:310
  415.2 143.4 %all-gather.19.cloned.1.call-start = ((), (), s32[]{:S(2)}) async-start(), calls=%async_computation.14 | async-start | bytes 18874368 | tf_op jit(solution)/shard_map/all_gather | solution.py:314
  459.4 245.0 %all-gather.21.cloned.1.call-start = ((), (), s32[]{:S(2)}) async-start(), calls=%async_computation.15 | async-start | bytes 18874368 | tf_op jit(solution)/shard_map/all_gather | solution.py:314
  464.0 92.8 %collective-permute-start.20 = (bf16[704,512]{1,0:T(8,128)(2,1)S(1)}, bf16[704,512]{1,0:T(8,128)(2,1)S(1)}, u32[]{:S(2)}, u32[]{:S(2)}) collective-permute-start(bf16[704,512]{1,0:T(8,128)(2,1)S(1)} %get-tuple-element.165), channel_id=1, source_target_pairs={{0,24},{8,0},{16,8},{24,16},{1,25},{9,1},{17,9},{25,17},{2,26},{10... | collective-permute-start | bytes 2162696 | tf_op jit(solution)/shard_map/ppermute | solution.py:326
  465.4 91.4 %collective-permute-start.19 = (bf16[704,512]{1,0:T(8,128)(2,1)S(1)}, bf16[704,512]{1,0:T(8,128)(2,1)S(1)}, u32[]{:S(2)}, u32[]{:S(2)}) collective-permute-start(bf16[704,512]{1,0:T(8,128)(2,1)S(1)} %get-tuple-element.166), channel_id=1, source_target_pairs={{0,16},{8,24},{16,0},{24,8},{1,17},{9,25},{17,1},{25,9},{2,18},{10... | collective-permute-start | bytes 2162696 | tf_op jit(solution)/shard_map/ppermute | solution.py:326
  466.4 91.3 %collective-permute-start.18 = (bf16[704,512]{1,0:T(8,128)(2,1)S(1)}, bf16[704,512]{1,0:T(8,128)(2,1)S(1)}, u32[]{:S(2)}, u32[]{:S(2)}) collective-permute-start(bf16[704,512]{1,0:T(8,128)(2,1)S(1)} %get-tuple-element.167), channel_id=1, source_target_pairs={{0,8},{8,16},{16,24},{24,0},{1,9},{9,17},{17,25},{25,1},{2,10},{10... | collective-permute-start | bytes 2162696 | tf_op jit(solution)/shard_map/ppermute | solution.py:326
  466.4 88.9 %collective-permute-start.16 = (bf16[352,512]{1,0:T(8,128)(2,1)S(1)}, bf16[352,512]{1,0:T(8,128)(2,1)S(1)}, u32[]{:S(2)}, u32[]{:S(2)}) collective-permute-start(bf16[352,512]{1,0:T(8,128)(2,1)S(1)} %get-tuple-element.170), channel_id=1, source_target_pairs={{0,16},{8,24},{16,0},{24,8},{1,17},{9,25},{17,1},{25,9},{2,18},{10... | collective-permute-start | bytes 1081352 | tf_op jit(solution)/shard_map/ppermute | solution.py:326
  473.0 83.1 %collective-permute-start.15 = (bf16[352,512]{1,0:T(8,128)(2,1)S(1)}, bf16[352,512]{1,0:T(8,128)(2,1)S(1)}, u32[]{:S(2)}, u32[]{:S(2)}) collective-permute-start(bf16[352,512]{1,0:T(8,128)(2,1)S(1)} %get-tuple-element.171), channel_id=1, source_target_pairs={{0,8},{8,16},{16,24},{24,0},{1,9},{9,17},{17,25},{25,1},{2,10},{10... | collective-permute-start | bytes 1081352 | tf_op jit(solution)/shard_map/ppermute | solution.py:326
  558.6 358.1 %reduce-scatter.9.cloned.1.call-start = ((), (), s32[]{:S(2)}) async-start(), calls=%async_computation.16 | async-start | bytes 5382144 | tf_op jit(solution)/shard_map/reduce_scatter | solution.py:405
  618.2 65.2 %collective-permute-start.22 = (bf16[704,512]{1,0:T(8,128)(2,1)S(1)}, bf16[704,512]{1,0:T(8,128)(2,1)S(1)}, u32[]{:S(2)}, u32[]{:S(2)}) collective-permute-start(bf16[704,512]{1,0:T(8,128)(2,1)S(1)} %get-tuple-element.162), channel_id=1, source_target_pairs={{0,16},{8,24},{16,0},{24,8},{1,17},{9,25},{17,1},{25,9},{2,18},{10... | collective-permute-start | bytes 2162696 | tf_op jit(solution)/shard_map/ppermute | solution.py:326
  620.9 62.5 %collective-permute-start.21 = (bf16[704,512]{1,0:T(8,128)(2,1)S(1)}, bf16[704,512]{1,0:T(8,128)(2,1)S(1)}, u32[]{:S(2)}, u32[]{:S(2)}) collective-permute-start(bf16[704,512]{1,0:T(8,128)(2,1)S(1)} %get-tuple-element.163), channel_id=1, source_target_pairs={{0,8},{8,16},{16,24},{24,0},{1,9},{9,17},{17,25},{25,1},{2,10},{10... | collective-permute-start | bytes 2162696 | tf_op jit(solution)/shard_map/ppermute | solution.py:326
  684.8 62.4 %collective-permute-start.25 = (bf16[704,512]{1,0:T(8,128)(2,1)}, bf16[704,512]{1,0:T(8,128)(2,1)S(1)}, u32[]{:S(2)}, u32[]{:S(2)}) collective-permute-start(bf16[704,512]{1,0:T(8,128)(2,1)} %get-tuple-element.158), channel_id=1, source_target_pairs={{0,16},{8,24},{16,0},{24,8},{1,17},{9,25},{17,1},{25,9},{2,18},{10... | collective-permute-start | bytes 2162696 | tf_op jit(solution)/shard_map/ppermute | solution.py:326
  684.8 62.4 %collective-permute-start.24 = (bf16[704,512]{1,0:T(8,128)(2,1)}, bf16[704,512]{1,0:T(8,128)(2,1)S(1)}, u32[]{:S(2)}, u32[]{:S(2)}) collective-permute-start(bf16[704,512]{1,0:T(8,128)(2,1)} %get-tuple-element.159), channel_id=1, source_target_pairs={{0,8},{8,16},{16,24},{24,0},{1,9},{9,17},{17,25},{25,1},{2,10},{10... | collective-permute-start | bytes 2162696 | tf_op jit(solution)/shard_map/ppermute | solution.py:326
  749.8 169.5 %reduce-scatter.11.cloned.1.call-start = ((), (), s32[]{:S(2)}) async-start(), calls=%async_computation.17 | async-start | bytes 5382144 | tf_op jit(solution)/shard_map/reduce_scatter | solution.py:405
  769.4 65.6 %collective-permute-start.28 = (bf16[704,512]{1,0:T(8,128)(2,1)S(1)}, bf16[704,512]{1,0:T(8,128)(2,1)S(1)}, u32[]{:S(2)}, u32[]{:S(2)}) collective-permute-start(bf16[704,512]{1,0:T(8,128)(2,1)S(1)} %get-tuple-element.154), channel_id=1, source_target_pairs={{0,16},{8,24},{16,0},{24,8},{1,17},{9,25},{17,1},{25,9},{2,18},{10... | collective-permute-start | bytes 2162696 | tf_op jit(solution)/shard_map/ppermute | solution.py:326
  772.3 62.6 %collective-permute-start.27 = (bf16[704,512]{1,0:T(8,128)(2,1)S(1)}, bf16[704,512]{1,0:T(8,128)(2,1)S(1)}, u32[]{:S(2)}, u32[]{:S(2)}) collective-permute-start(bf16[704,512]{1,0:T(8,128)(2,1)S(1)} %get-tuple-element.155), channel_id=1, source_target_pairs={{0,8},{8,16},{16,24},{24,0},{1,9},{9,17},{17,25},{25,1},{2,10},{10... | collective-permute-start | bytes 2162696 | tf_op jit(solution)/shard_map/ppermute | solution.py:326
  890.3 93.1 %collective-permute-start.32 = (bf16[704,512]{1,0:T(8,128)(2,1)}, bf16[704,512]{1,0:T(8,128)(2,1)S(1)}, u32[]{:S(2)}, u32[]{:S(2)}) collective-permute-start(bf16[704,512]{1,0:T(8,128)(2,1)} %get-tuple-element.217), channel_id=1, source_target_pairs={{0,24},{8,0},{16,8},{24,16},{1,25},{9,1},{17,9},{25,17},{2,26},{10... | collective-permute-start | bytes 2162696 | tf_op jit(solution)/shard_map/ppermute | solution.py:326
  891.5 91.8 %collective-permute-start.31 = (bf16[704,512]{1,0:T(8,128)(2,1)}, bf16[704,512]{1,0:T(8,128)(2,1)S(1)}, u32[]{:S(2)}, u32[]{:S(2)}) collective-permute-start(bf16[704,512]{1,0:T(8,128)(2,1)} %get-tuple-element.218), channel_id=1, source_target_pairs={{0,16},{8,24},{16,0},{24,8},{1,17},{9,25},{17,1},{25,9},{2,18},{10... | collective-permute-start | bytes 2162696 | tf_op jit(solution)/shard_map/ppermute | solution.py:326
  893.8 89.6 %collective-permute-start.30 = (bf16[704,512]{1,0:T(8,128)(2,1)}, bf16[704,512]{1,0:T(8,128)(2,1)S(1)}, u32[]{:S(2)}, u32[]{:S(2)}) collective-permute-start(bf16[704,512]{1,0:T(8,128)(2,1)} %get-tuple-element.219), channel_id=1, source_target_pairs={{0,8},{8,16},{16,24},{24,0},{1,9},{9,17},{17,25},{25,1},{2,10},{10... | collective-permute-start | bytes 2162696 | tf_op jit(solution)/shard_map/ppermute | solution.py:326
  915.2 67.4 %collective-permute-start.34 = (bf16[352,512]{1,0:T(8,128)(2,1)}, bf16[352,512]{1,0:T(8,128)(2,1)}, u32[]{:S(2)}, u32[]{:S(2)}) collective-permute-start(bf16[352,512]{1,0:T(8,128)(2,1)} %get-tuple-element.214), channel_id=1, source_target_pairs={{0,16},{8,24},{16,0},{24,8},{1,17},{9,25},{17,1},{25,9},{2,18},{10... | collective-permute-start | bytes 1081352 | tf_op jit(solution)/shard_map/ppermute | solution.py:326
  921.1 61.5 %collective-permute-start.33 = (bf16[352,512]{1,0:T(8,128)(2,1)}, bf16[352,512]{1,0:T(8,128)(2,1)S(1)}, u32[]{:S(2)}, u32[]{:S(2)}) collective-permute-start(bf16[352,512]{1,0:T(8,128)(2,1)} %get-tuple-element.215), channel_id=1, source_target_pairs={{0,8},{8,16},{16,24},{24,0},{1,9},{9,17},{17,25},{25,1},{2,10},{10... | collective-permute-start | bytes 1081352 | tf_op jit(solution)/shard_map/ppermute | solution.py:326
  989.4 80.7 %all-gather.23.cloned.1.call-start = ((), (), s32[]{:S(2)}) async-start(), calls=%async_computation.18 | async-start | bytes 2621440 | tf_op jit(solution)/shard_map/all_gather | solution.py:310
  1025.5 141.6 %all-gather.25.cloned.1.call-start = ((), (), s32[]{:S(2)}) async-start(), calls=%async_computation.19 | async-start | bytes 18874368 | tf_op jit(solution)/shard_map/all_gather | solution.py:314
  1070.1 220.2 %reduce-scatter.13.cloned.1.call-start = ((), (), s32[]{:S(2)}) async-start(), calls=%async_computation.20 | async-start | bytes 10616832 | tf_op jit(solution)/shard_map/reduce_scatter | solution.py:405
  1079.2 87.9 %collective-permute-start.40 = (bf16[704,512]{1,0:T(8,128)(2,1)}, bf16[704,512]{1,0:T(8,128)(2,1)S(1)}, u32[]{:S(2)}, u32[]{:S(2)}) collective-permute-start(bf16[704,512]{1,0:T(8,128)(2,1)} %get-tuple-element.206), channel_id=1, source_target_pairs={{0,16},{8,24},{16,0},{24,8},{1,17},{9,25},{17,1},{25,9},{2,18},{10... | collective-permute-start | bytes 2162696 | tf_op jit(solution)/shard_map/ppermute | solution.py:326
  1086.0 81.1 %collective-permute-start.39 = (bf16[704,512]{1,0:T(8,128)(2,1)}, bf16[704,512]{1,0:T(8,128)(2,1)}, u32[]{:S(2)}, u32[]{:S(2)}) collective-permute-start(bf16[704,512]{1,0:T(8,128)(2,1)} %get-tuple-element.207), channel_id=1, source_target_pairs={{0,8},{8,16},{16,24},{24,0},{1,9},{9,17},{17,25},{25,1},{2,10},{10... | collective-permute-start | bytes 2162696 | tf_op jit(solution)/shard_map/ppermute | solution.py:326
  1168.0 306.0 %reduce-scatter.15.cloned.1.call-start = ((), (), s32[]{:S(2)}) async-start(), calls=%async_computation.21 | async-start | bytes 20054016 | tf_op jit(solution)/shard_map/reduce_scatter | solution.py:798
  1173.3 116.9 %collective-permute-start.44 = (bf16[704,512]{1,0:T(8,128)(2,1)}, bf16[704,512]{1,0:T(8,128)(2,1)S(1)}, u32[]{:S(2)}, u32[]{:S(2)}) collective-permute-start(bf16[704,512]{1,0:T(8,128)(2,1)} %get-tuple-element.201), channel_id=1, source_target_pairs={{0,24},{8,0},{16,8},{24,16},{1,25},{9,1},{17,9},{25,17},{2,26},{10... | collective-permute-start | bytes 2162696 | tf_op jit(solution)/shard_map/ppermute | solution.py:326
  1173.3 116.9 %collective-permute-start.43 = (bf16[704,512]{1,0:T(8,128)(2,1)}, bf16[704,512]{1,0:T(8,128)(2,1)}, u32[]{:S(2)}, u32[]{:S(2)}) collective-permute-start(bf16[704,512]{1,0:T(8,128)(2,1)} %get-tuple-element.202), channel_id=1, source_target_pairs={{0,16},{8,24},{16,0},{24,8},{1,17},{9,25},{17,1},{25,9},{2,18},{10... | collective-permute-start | bytes 2162696 | tf_op jit(solution)/shard_map/ppermute | solution.py:326
  1176.3 113.9 %collective-permute-start.42 = (bf16[704,512]{1,0:T(8,128)(2,1)}, bf16[704,512]{1,0:T(8,128)(2,1)}, u32[]{:S(2)}, u32[]{:S(2)}) collective-permute-start(bf16[704,512]{1,0:T(8,128)(2,1)} %get-tuple-element.203), channel_id=1, source_target_pairs={{0,8},{8,16},{16,24},{24,0},{1,9},{9,17},{17,25},{25,1},{2,10},{10... | collective-permute-start | bytes 2162696 | tf_op jit(solution)/shard_map/ppermute | solution.py:326
  1179.5 64.0 %collective-permute-start.47 = (bf16[352,512]{1,0:T(8,128)(2,1)}, bf16[352,512]{1,0:T(8,128)(2,1)S(1)}, u32[]{:S(2)}, u32[]{:S(2)}) collective-permute-start(bf16[352,512]{1,0:T(8,128)(2,1)} %get-tuple-element.197), channel_id=1, source_target_pairs={{0,24},{8,0},{16,8},{24,16},{1,25},{9,1},{17,9},{25,17},{2,26},{10... | collective-permute-start | bytes 1081352 | tf_op jit(solution)/shard_map/ppermute | solution.py:326
  1181.4 108.0 %collective-permute-start.46 = (bf16[352,512]{1,0:T(8,128)(2,1)}, bf16[352,512]{1,0:T(8,128)(2,1)}, u32[]{:S(2)}, u32[]{:S(2)}) collective-permute-start(bf16[352,512]{1,0:T(8,128)(2,1)} %get-tuple-element.198), channel_id=1, source_target_pairs={{0,16},{8,24},{16,0},{24,8},{1,17},{9,25},{17,1},{25,9},{2,18},{10... | collective-permute-start | bytes 1081352 | tf_op jit(solution)/shard_map/ppermute | solution.py:326
  1301.2 101.5 %collective-permute-start.52 = (bf16[704,512]{1,0:T(8,128)(2,1)}, bf16[704,512]{1,0:T(8,128)(2,1)}, u32[]{:S(2)}, u32[]{:S(2)}) collective-permute-start(bf16[704,512]{1,0:T(8,128)(2,1)} %get-tuple-element.190), channel_id=1, source_target_pairs={{0,16},{8,24},{16,0},{24,8},{1,17},{9,25},{17,1},{25,9},{2,18},{10... | collective-permute-start | bytes 2162696 | tf_op jit(solution)/shard_map/ppermute | solution.py:326
  1302.3 127.6 %all-to-all-start.2 = ((bf16[4,576,256]{2,1,0:T(8,128)(2,1)}), bf16[4,576,256]{2,1,0:T(8,128)(2,1)}, u32[]{:S(2)}, u32[]{:S(2)}) async-start(bf16[4,576,256]{2,1,0:T(8,128)(2,1)} %bitcast.408), calls=%async_computation.6 | async-start | bytes 2359296 | tf_op jit(solution)/shard_map/all_to_all | solution.py:318
  1306.6 305.3 %reduce-scatter.17.cloned.1.call-start = ((), (), s32[]{:S(2)}) async-start(), calls=%async_computation.22 | async-start | bytes 2785280 | tf_op jit(solution)/shard_map/reduce_scatter | solution.py:801
  1306.7 96.0 %collective-permute-start.51 = (bf16[704,512]{1,0:T(8,128)(2,1)}, bf16[704,512]{1,0:T(8,128)(2,1)S(1)}, u32[]{:S(2)}, u32[]{:S(2)}) collective-permute-start(bf16[704,512]{1,0:T(8,128)(2,1)} %get-tuple-element.191), channel_id=1, source_target_pairs={{0,8},{8,16},{16,24},{24,0},{1,9},{9,17},{17,25},{25,1},{2,10},{10... | collective-permute-start | bytes 2162696 | tf_op jit(solution)/shard_map/ppermute | solution.py:326
  1404.9 69.1 %collective-permute-start.55 = (bf16[512,512]{1,0:T(8,128)(2,1)}, bf16[512,512]{1,0:T(8,128)(2,1)}, u32[]{:S(2)}, u32[]{:S(2)}) collective-permute-start(bf16[512,512]{1,0:T(8,128)(2,1)} %get-tuple-element.222), channel_id=1, source_target_pairs={{0,16},{8,24},{16,0},{24,8},{1,17},{9,25},{17,1},{25,9},{2,18},{10... | collective-permute-start | bytes 1572872 | tf_op jit(solution)/shard_map/ppermute | solution.py:326
  1498.9 108.2 %collective-permute-start.58 = (bf16[512,1024]{1,0:T(8,128)(2,1)}, bf16[512,1024]{1,0:T(8,128)(2,1)}, u32[]{:S(2)}, u32[]{:S(2)}) collective-permute-start(bf16[512,1024]{1,0:T(8,128)(2,1)} %get-tuple-element.186), channel_id=1, source_target_pairs={{0,16},{8,24},{16,0},{24,8},{1,17},{9,25},{17,1},{25,9},{2,18},{10... | collective-permute-start | bytes 3145736 | tf_op jit(solution)/shard_map/ppermute | solution.py:326
  1498.9 108.2 %collective-permute-start.57 = (bf16[512,1024]{1,0:T(8,128)(2,1)}, bf16[512,1024]{1,0:T(8,128)(2,1)}, u32[]{:S(2)}, u32[]{:S(2)}) collective-permute-start(bf16[512,1024]{1,0:T(8,128)(2,1)} %get-tuple-element.187), channel_id=1, source_target_pairs={{0,8},{8,16},{16,24},{24,0},{1,9},{9,17},{17,25},{25,1},{2,10},{10... | collective-permute-start | bytes 3145736 | tf_op jit(solution)/shard_map/ppermute | solution.py:326
  (186 other events, 4061.2 us)
Sparse Core Ops, SparseCore 0:
  13.5 50.9 all-gather.10
  67.7 91.9 all-gather.12
  213.9 51.0 all-gather.14
  297.1 77.5 reduce-scatter.6
  415.3 44.0 all-gather.16
  461.1 91.8 all-gather.18
  558.7 92.9 all-gather.20
  749.9 56.8 reduce-scatter.8
  859.3 54.5 reduce-scatter.10
  1025.6 44.4 all-gather.22
  1071.9 91.8 all-gather.24
  1167.7 76.6 reduce-scatter.12
  1290.5 119.0 reduce-scatter.14
  1474.1 60.2 reduce-scatter.16

commit v3 on v2

--- a/solution.py
+++ b/solution.py
@@ -306,6 +306,119 @@
     )(qkv, target, kblk, lse, plain, raw, gate_cols, cosine, sine)
 
 
+def dispatch_body(target_ref, tokens, out_refs):
+    rows = out_refs[0].shape[1]
+    at = lax.broadcasted_iota(jnp.int32, (rows, tokens.shape[0]), 0)
+    for j, out_ref in enumerate(out_refs):
+        match = jnp.where(target_ref[0, j : j + 1] == at, 1.0, 0.0).astype(BF16)
+        out_ref[0] = pick_rows(match, tokens[...])
+
+
+def dispatch_kernel(x_ref, target_ref, *out_refs):
+    dispatch_body(target_ref, x_ref.at[0], out_refs)
+
+
+def norm_dispatch_kernel(step, x_ref, target_ref, gain_ref, router_ref, *refs):
+    *out_refs, inverse_ref, logits_ref, hidden_ref = refs
+    for first in range(0, x_ref.shape[1], step):
+        rows = slice(first, first + step)
+        normed, inverse = normalize_rows(x_ref[0, rows].astype(F32))
+        hidden = (normed * gain_ref[...]).astype(BF16)
+        hidden_ref[rows] = hidden
+        inverse_ref[0, rows] = inverse
+        logits_ref[0, rows] = jnp.dot(hidden, router_ref[...], preferred_element_type=F32)
+    dispatch_body(target_ref, hidden_ref, out_refs)
+
+
+def dispatch(x, target, rows, norm=None):
+    seqs, length, width = x.shape
+    local = target.shape[1]
+    token = lambda n: pl.BlockSpec((1, length, n), lambda s: (s, 0, 0))
+    in_specs = [token(width), pl.BlockSpec((1, local, length), lambda s: (s, 0, 0))]
+    out_specs = [pl.BlockSpec((1, rows, width), lambda s: (s, 0, 0)) for _ in range(local)]
+    out_shape = [jax.ShapeDtypeStruct((seqs, rows, width), BF16) for _ in range(local)]
+    args, kernel, scratch = [x, target], dispatch_kernel, []
+    if norm is not None:
+        gain, router = norm
+        experts = router.shape[1]
+        in_specs += [
+            pl.BlockSpec((1, width), lambda s: (0, 0)),
+            pl.BlockSpec(router.shape, lambda s: (0, 0)),
+        ]
+        out_specs += [token(1), token(experts)]
+        out_shape += [
+            jax.ShapeDtypeStruct((seqs, length, 1), F32),
+            jax.ShapeDtypeStruct((seqs, length, experts), F32),
+        ]
+        args += [gain.reshape(1, width), router]
+        kernel = partial(norm_dispatch_kernel, 256)
+        scratch = [pltpu.VMEM((length, width), BF16)]
+    return pl.pallas_call(
+        kernel,
+        grid=(seqs,),
+        in_specs=in_specs,
+        out_specs=out_specs,
+        out_shape=out_shape,
+        scratch_shapes=scratch,
+        compiler_params=pltpu.CompilerParams(vmem_limit_bytes=56 * 1024 * 1024),
+        cost_estimate=pl.CostEstimate(
+            flops=2 * local * seqs * rows * length * width,
+            bytes_accessed=2 * x.size + 2 * local * seqs * rows * width,
+            transcendentals=0,
+        ),
+        name="dispatch",
+    )(*args)
+
+
+def expert_kernel(
+    x_ref, grad_ref, weight_ref, gate_ref, up_ref, down_ref,
+    scaled_ref, grad_gate_ref, grad_up_ref, back_ref, dots_ref,
+):
+    last = (((1,), (1,)), ((), ()))
+    x, weight = x_ref[...], weight_ref[...]
+    gate_pre = lax.dot_general(x, gate_ref[...], last, preferred_element_type=F32)
+    up_pre = lax.dot_general(x, up_ref[...], last, preferred_element_type=F32)
+    raw = lax.dot_general(grad_ref[...], down_ref[...], last, preferred_element_type=F32)
+    gate_sig = jax.nn.sigmoid(gate_pre)
+    gate_silu = gate_pre * gate_sig
+    activated = gate_silu * up_pre
+    scaled_ref[...] = (activated * weight).astype(BF16)
+    grad_act = raw * weight
+    grad_gate = grad_act * up_pre * (gate_sig * (1.0 + gate_pre * (1.0 - gate_sig)))
+    grad_gate = grad_gate.astype(BF16)
+    grad_up = (grad_act * gate_silu).astype(BF16)
+    grad_gate_ref[...] = grad_gate
+    grad_up_ref[...] = grad_up
+    back = jnp.dot(grad_gate, gate_ref[...], preferred_element_type=F32)
+    back = back + jnp.dot(grad_up, up_ref[...], preferred_element_type=F32)
+    back_ref[...] = back.astype(BF16)
+    inner = grad_gate.astype(F32) * gate_pre + grad_up.astype(F32) * up_pre
+    dots_ref[:, 0:1] = jnp.sum(raw * activated, axis=-1, keepdims=True)
+    dots_ref[:, 1:2] = jnp.sum(inner, axis=-1, keepdims=True)
+
+
+def expert_step(x, grad, weight, gate_w, up_w, down_w, tile):
+    count, width = x.shape
+    units = gate_w.shape[0]
+    row = lambda n: pl.BlockSpec((tile, n), lambda i: (i, 0))
+    whole = pl.BlockSpec((units, width), lambda i: (0, 0))
+    shape = lambda n, dtype=BF16: jax.ShapeDtypeStruct((count, n), dtype)
+    return pl.pallas_call(
+        expert_kernel,
+        grid=(count // tile,),
+        in_specs=[row(width), row(width), row(1), whole, whole, whole],
+        out_specs=[row(units), row(units), row(units), row(width), row(2)],
+        out_shape=[shape(units), shape(units), shape(units), shape(width), shape(2, F32)],
+        compiler_params=pltpu.CompilerParams(vmem_limit_bytes=56 * 1024 * 1024),
+        cost_estimate=pl.CostEstimate(
+            flops=10 * count * width * units,
+            bytes_accessed=6 * count * (width + units) + 6 * width * units,
+            transcendentals=count * units,
+        ),
+        name="expert_step",
+    )(x, grad, weight, gate_w, up_w, down_w)
+
+
 def gather_rows(own):
     return lax.all_gather(own, "row", axis=1, tiled=True)
 
@@ -318,13 +431,33 @@
     return lax.all_to_all(parts, "row", 0, 0)
 
 
-def exchange_pieces(piece_for):
+def cut_pieces(piece_for):
     ranks, row = lax.axis_size("row"), lax.axis_index("row")
-    got = [piece_for(row)]
+    return [piece_for(lax.rem(row + m, ranks)) for m in range(ranks)]
+
+
+def exchange_pieces(pieces, *after):
+    ranks = lax.axis_size("row")
+    got = pieces[:1]
     for m in range(1, ranks):
         steps = [(i, (i + m) % ranks) for i in range(ranks)]
-        got.append(lax.ppermute(piece_for(lax.rem(row + m, ranks)), "row", steps))
+        got.append(lax.ppermute(tie(pieces[m], *after), "row", steps))
     return got
+
+
+def cut_group(*parts):
+    pieces = cut_pieces(lambda n: jnp.concatenate([piece_for(n) for piece_for, _ in parts], axis=0))
+    return pieces, [rows for _, rows in parts]
+
+
+def exchange_group(group, *after):
+    pieces, counts = group
+    got = exchange_pieces(pieces, *after)
+    placed, first = [], 0
+    for rows in counts:
+        placed.append((got, first, rows))
+        first += rows
+    return got, placed
 
 
 def assemble(pieces, body, outs, name):
@@ -359,15 +492,15 @@
     )(lax.axis_index("row").astype(jnp.int32).reshape(1), *flat)
 
 
-def place_rows(outs, at, pieces, dtype):
-    first = 0
-    for piece in pieces:
-        rows = slice(first, first + piece.shape[0])
+def place_rows(outs, at, refs, spans, dtype):
+    to = 0
+    for ref, (first, rows) in zip(refs, spans):
+        piece = ref[first : first + rows].astype(dtype)
         if at is None:
-            outs[rows] = piece[...].astype(dtype)
+            outs[to : to + rows] = piece
         else:
-            outs[at, rows] = piece[...].astype(dtype)
-        first += piece.shape[0]
+            outs[at, to : to + rows] = piece
+        to += rows
 
 
 def spread_kernel(into_ref, weight_ref, extra_ref, out_ref):
@@ -477,35 +610,42 @@
     small_all = [split[0], split[1] + 256 * split[4], split[2], split[3] + 256 * split[5]]
     in_rows = in_rows[:, :, :seq_dev].reshape(seqs, seq_len, share)
 
-    def expert_in(weight, j, *after, half=None):
-        weight = tie(weight, *after)
-        _, height, columns = weight.shape
-        first, rows = (0, height) if half is None else (half * (height // 2), height // 2)
+    def halves(height, half):
+        return (0, height) if half is None else (half * (height // 2), height // 2)
+
+    def expert_part(weight, j, half=None):
+        first, rows = halves(weight.shape[1], half)
 
         def piece_for(n):
-            block = (1, rows, columns)
-            return lax.dynamic_slice(weight, (n * local + j, first, 0), block)[0]
-
-        return exchange_pieces(piece_for)
-
-    def in_body(m, ins, outs):
-        place_rows(outs[0], None, ins, BF16)
-
-    def rows_in(*got):
-        block = (hidden_units, depth)
-        out = ((hidden_units, width), BF16, block, lambda b: (0, b))
-        return assemble(list(zip(*got)), in_body, [out], "rows_in")[0]
+            at = (n * local + j, first, 0)
+            return lax.dynamic_slice(weight, at, (1, rows, weight.shape[2]))[0]
+
+        return piece_for, rows
+
+    def rows_in(placed):
+        spans = [part[1:] for part in placed]
+        pieces = [tuple(part[0][m] for part in placed) for m in range(ranks)]
+
+        def body(m, ins, outs):
+            place_rows(outs[0], None, ins, spans, BF16)
+
+        out = ((hidden_units, width), BF16, (hidden_units, depth), lambda b: (0, b))
+        return assemble(pieces, body, [out], "rows_in")[0]
 
     w_gate, w_up = w_gate.swapaxes(1, 2), w_up.swapaxes(1, 2)
 
-    def group_in(weight, *after):
-        grouped = tie(weight, *after).reshape(ranks, local, *weight.shape[1:])
+    def group_in(weight):
+        grouped = weight.reshape(ranks, local, *weight.shape[1:])
         return lambda n: lax.dynamic_index_in_dim(grouped, n, 0, keepdims=False)
 
     parts = local + 2
+    key_value = jnp.stack([key_weight, value_weight])
+
     query_for = group_in(w_query)
-    key_value = jnp.stack([key_weight, value_weight])
-    query_got = exchange_pieces(lambda n: jnp.concatenate([query_for(n), key_value]))
+    cosine, sine = rope_tables(seq_len)
+    query_parts = cut_pieces(lambda n: jnp.concatenate([query_for(n), key_value]))
+    in_rows = tie(in_rows, cosine, sine, *query_parts)
+    query_got = exchange_pieces(query_parts, in_rows)
 
     def query_body(m, ins, outs):
         for h in range(heads):
@@ -514,11 +654,11 @@
                 piece = ins[0][p, :, h * HEAD_DIM : (h + 1) * HEAD_DIM]
                 outs[0][:, at : at + HEAD_DIM] = piece
 
-    made = heads * parts * HEAD_DIM
+    made_cols = heads * parts * HEAD_DIM
     query_w = assemble(
         [(p,) for p in query_got],
         query_body,
-        [((width, made), BF16, (depth, made), lambda b: (b, 0))],
+        [((width, made_cols), BF16, (depth, made_cols), lambda b: (b, 0))],
         "query_in",
     )[0]
 
@@ -537,9 +677,15 @@
     target_f = tokens_to_slots(small_all[2], small_all[3])
     routes_a = small_all[0].reshape(2, seqs, seq_len)
     routes_f = small_all[2].reshape(2, seqs, seq_len)
-    out_for = group_in(w_out, *small_all)
-    out_got = exchange_pieces(out_for)
-    gate_first = expert_in(w_gate, 0, *query_got, half=0)
+    w_out, w_gate, w_up, w_down = tie((w_out, w_gate, w_up, w_down), *query_got[1:2])
+    out_parts = cut_pieces(group_in(w_out))
+    group_a = cut_group(expert_part(w_gate, 0), expert_part(w_up, 0, 0))
+    group_b = cut_group(expert_part(w_up, 0, 1), expert_part(w_down, 0))
+    group_c = [cut_group(expert_part(w_gate, j), expert_part(w_up, j)) for j in range(1, local)]
+    group_d = [
+        [cut_group(expert_part(w_down, j, half)) for half in (0, 1)] for j in range(1, local)
+    ]
+    out_got = exchange_pieces(out_parts, *query_got)
 
     def home_match(pairs, order):
         ranks_here = all_ranks(pairs, order)
@@ -558,7 +704,9 @@
         )
 
     in_all = gather_cols(in_rows).reshape(count, width)
-    cosine, sine = rope_tables(seq_len)
+    in_all = tie(
+        in_all, target_a, target_f, home_a, home_f, out_parts, group_a, group_b, group_c, group_d
+    )
     rotated = ([True] * (local + 1) + [False]) * heads
     hidden_a, inverse_a, logits_a, qkv = project(
         in_all, gain_attn, router_attn, query_w, cosine, sine, rotated
@@ -595,26 +743,31 @@
     out_slots = dot_f32(
         "jrf,jfd->jrd", att_slot.reshape(local, slot_rows, head_cols), out_w
     ).astype(BF16)
-    out_slots = tie(out_slots.reshape(-1, width), grad_rows, *gate_first)
-    gate_got_in = [(gate_first, expert_in(w_gate, 0, *out_got, *gate_first, half=1))]
-    up_first = expert_in(w_up, 0, *out_got, *gate_first, half=0)
-    out_own = tie(sum_cols(out_slots), *gate_got_in[0][1], *up_first)
+    out_slots = tie(out_slots.reshape(-1, width), grad_rows)
+    got, (gate_in, up_first) = exchange_group(group_a, *out_got)
+    out_own = tie(sum_cols(out_slots), *got)
     out_home, _ = rows_home(out_own, seqs, capacity)
     mid = block_in.astype(F32) + come_home(home_a, out_home)
 
     mid_low = mid.astype(BF16)
     mid_rows = gather_rows(mid_low)
     mid_all = gather_cols(mid_rows).reshape(count, width)
-    up_got_in = [(up_first, expert_in(w_up, 0, mid_rows, half=1))]
-    down_got_in = [(expert_in(w_down, 0, mid_rows),)]
-    mid_all = tie(mid_all, *up_got_in[0][1], *down_got_in[0][0])
+    got, (up_second, down_in) = exchange_group(group_b, mid_rows)
+    mid_all = tie(mid_all, *got)
+    arrived = [([gate_in], [up_first, up_second], [down_in])]
     out_grad_all = gather_cols(tie(grad_rows, mid_all))
-    normed_f, inverse_f = normalize_rows(mid_all.astype(F32))
-    hidden_f = (normed_f * gain_ffn).astype(BF16)
-    logits_f = jnp.dot(hidden_f, router_ffn, preferred_element_type=F32)
-    gates_f = gate_table(
-        logits_f.reshape(seqs, seq_len, experts), routes_f
-    )
+    for j in range(1, local):
+        got, (gate_in, up_in) = exchange_group(group_c[j - 1], mid_all)
+        out_grad_all = tie(out_grad_all, *got)
+        arrived.append(([gate_in], [up_in], []))
+    seq3 = lambda a: a.reshape(seqs, seq_len, -1)
+    *slot_in, inverse_f, logits_f = dispatch(
+        seq3(mid_all), target_f, rows_each, (gain_ffn, router_ffn)
+    )
+    slot_in = [x.reshape(slot_rows, width) for x in slot_in]
+    slot_grad_out = dispatch(out_grad_all, target_f, rows_each)
+    slot_grad_out = [x.reshape(slot_rows, width) for x in slot_grad_out]
+    gates_f = gate_table(logits_f, routes_f)
     my_gates_f = my_gates(gates_f)
     blocked = lambda a: a.reshape(seqs, ranks, seq_dev)
     slots_at = jnp.arange(capacity, dtype=jnp.int32)[:, None]
@@ -627,80 +780,63 @@
         for j in range(local)
     ]
 
-    def dispatch(tokens, j):
-        blocks = tokens.reshape(seqs, ranks, seq_dev, width)
-        picked = jnp.einsum("snct,sntd->sncd", match_f[j].astype(BF16), blocks)
-        return picked.reshape(slot_rows, width)
-
-    down_slots, slot_grads_f, dots_f = [], [], []
-    grads_gate, grads_up, grads_down = [], [], []
+    slot_grads_f, dots_f = [], []
+    grads_gate, grads_up, grads_down, down_slots = [], [], [], []
+    pieces = tie([[part[0] for part in placed] for placed in arrived[0]], slot_in[0])
+    arrived[0] = [
+        [(got, *part[1:]) for got, part in zip(held, placed)]
+        for held, placed in zip(pieces, arrived[0])
+    ]
+    next_w = rows_in(arrived[0][0]), rows_in(arrived[0][1])
     for j in range(local):
-        slot_in = dispatch(hidden_f, j)
-        if j == 0 and local > 1:
-            gate_got_in.append((expert_in(w_gate, 1, mid_all),))
-            slot_in = tie(slot_in, *gate_got_in[1][0])
+        x = slot_in[j]
+        if j > 0:
+            x = tie(x, grads_gate[-1], grads_up[-1], grads_down[-1], down_slots[-1])
+        gate_w, up_w = next_w
+        down_w = rows_in(arrived[j][2])
+        scaled, grad_gate, grad_up, slot_grad, dots = expert_step(
+            x, slot_grad_out[j], weights_f[j], gate_w, up_w, down_w, rows_each
+        )
+        dots = dots.reshape(seqs, ranks, capacity, 2).transpose(1, 3, 0, 2).reshape(ranks, -1)
+        dots_f.append(dots.astype(BF16))
         if j + 1 < local:
-            up_got_in.append((expert_in(w_up, j + 1, slot_in),))
-        gate_w, up_w = rows_in(*gate_got_in[j]), rows_in(*up_got_in[j])
-        gate_pre = dot_f32("rd,fd->rf", slot_in, gate_w)
-        up_pre = dot_f32("rd,fd->rf", slot_in, up_w)
-        down_w = rows_in(*down_got_in[j])
-        gate_sig = jax.nn.sigmoid(gate_pre)
-        gate_silu = gate_pre * gate_sig
-        activated = gate_silu * up_pre
-        scaled = (activated * weights_f[j]).astype(BF16)
-        slot_grad_out = dispatch(out_grad_all, j)
-        grads_down.append(dot_f32("rf,rd->fd", scaled, slot_grad_out).astype(BF16))
-        down = jnp.dot(scaled, down_w, preferred_element_type=F32)
-        down_slots.append(down.astype(BF16))
-        grad_raw = dot_f32("rd,fd->rf", slot_grad_out, down_w)
-        grad_act = grad_raw * weights_f[j]
-        grad_gate = grad_act * up_pre * (gate_sig * (1.0 + gate_pre * (1.0 - gate_sig)))
-        grad_gate = grad_gate.astype(BF16)
-        grad_up = (grad_act * gate_silu).astype(BF16)
-        grads_gate.append(dot_f32("rf,rd->fd", grad_gate, slot_in).astype(BF16))
-        grads_up.append(dot_f32("rf,rd->fd", grad_up, slot_in).astype(BF16))
-        slot_grad = dot_f32("rf,fd->rd", grad_gate, gate_w)
-        slot_grad = slot_grad + dot_f32("rf,fd->rd", grad_up, up_w)
-        slot_grad = slot_grad.astype(BF16)
-        if j + 1 < local:
-            slot_grad = tie(slot_grad, *up_got_in[-1][0])
-            down_got_in.append((expert_in(w_down, j + 1, slot_grad),))
-            if j + 2 < local:
-                gate_got_in.append((expert_in(w_gate, j + 2, slot_grad),))
+            got, (down_first,) = exchange_group(group_d[j][0], out_grad_all)
+            slot_grad = tie(slot_grad, *got)
+            got, (down_second,) = exchange_group(group_d[j][1], slot_grad)
+            arrived[j + 1][2].extend([down_first, down_second])
+            gate_in, up_in = arrived[j + 1][0][0], arrived[j + 1][1][0]
+            held = tie(gate_in[0], got[1])
+            next_w = rows_in([(held, *gate_in[1:])]), rows_in([(held, *up_in[1:])])
+            made = tie((scaled, grad_gate, grad_up), got[1], next_w)
+            grads_down.append(dot_f32("rf,rd->fd", made[0], slot_grad_out[j]).astype(BF16))
+            grads_gate.append(dot_f32("rf,rd->fd", made[1], slot_in[j]).astype(BF16))
+            grads_up.append(dot_f32("rf,rd->fd", made[2], slot_in[j]).astype(BF16))
+            down = jnp.dot(made[0], down_w, preferred_element_type=F32)
+            down_slots.append(down.astype(BF16))
         slot_grads_f.append(slot_grad)
-        inner = grad_gate.astype(F32) * gate_pre + grad_up.astype(F32) * up_pre
-        dots = jnp.stack([jnp.sum(grad_raw * activated, axis=-1), jnp.sum(inner, axis=-1)])
-        dots = dots.reshape(2, seqs, ranks, capacity).transpose(2, 0, 1, 3).reshape(ranks, -1)
-        dots_f.append(dots.astype(BF16))
-
-    def columns_out(grad, *after, half=None):
-        grad = tie(grad, *after)
-        size = grad.shape[0] // ranks
-        first, rows = (0, size) if half is None else (half * (size // 2), size // 2)
-        return exchange_pieces(lambda n: lax.dynamic_slice_in_dim(grad, n * size + first, rows, 0))
-
-    def rows_out(grad, *after, half=None):
-        grad = tie(grad, *after)
-        height = grad.shape[0]
-        first, rows = (0, height) if half is None else (half * (height // 2), height // 2)
-        return exchange_pieces(
-            lambda n: lax.dynamic_slice(grad, (first, n * depth), (rows, depth))
-        )
-
-    def whole_grad(got):
-        counts = [len(parts) for parts in got]
-        rows = sum(part[0].shape[0] for part in got[0])
-        columns = got[0][0][0].shape[1]
-        pieces = [tuple(part[m] for parts in got for part in parts) for m in range(ranks)]
+
+    def grad_part(grad, half=None):
+        first, rows = halves(grad.shape[0], half)
+
+        def piece_for(n):
+            return lax.dynamic_slice(grad, (first, n * depth), (rows, depth))
+
+        return piece_for, rows
+
+    def whole_grad(placed):
+        flat = [part for parts in placed for part in parts]
+        counts = [len(parts) for parts in placed]
+        pieces = [tuple(part[0][m] for part in flat) for m in range(ranks)]
 
         def body(m, ins, outs):
             first = 0
             for j, held in enumerate(counts):
-                place_rows(outs[0], j, ins[first : first + held], F32)
+                spans = [part[1:] for part in placed[j]]
+                place_rows(outs[0], j, ins[first : first + held], spans, F32)
                 first += held
 
-        out = ((experts, rows, columns), F32, (local, rows, columns), lambda b: (b, 0, 0))
+        rows = hidden_units
+        out = ((experts, rows, depth), F32, (local, rows, depth), lambda b: (b, 0, 0))
         return assemble(pieces, body, [out], "whole_grad")[0]
 
     def sublayer_back(own_in, inverse_all, gain, router, gates_all, logits_all, dots, inner, dhidden):
@@ -720,10 +856,19 @@
         grad = inverse * (dn - normed * (inner / width)[..., None])
         return grad, jnp.concatenate([grad_router, grad_gain[None]], axis=0)
 
-    seq3 = lambda a: a.reshape(seqs, seq_len, -1)
-    last = down_got_in[-1][-1]
-    down_got = [[rows_out(grads_down[0], *last)]]
-    gate_first = rows_out(grads_gate[0], *last, half=0)
+    first_grads = (grads_down, grads_gate, grads_up)
+    if local == 1:
+        first_grads = ([scaled], [grad_gate], [grad_up])
+        for grads, rows in zip(first_grads, (slot_grad_out[0], slot_in[0], slot_in[0])):
+            grads[0] = dot_f32("rf,rd->fd", grads[0], rows).astype(BF16)
+    grads_down, grads_gate, grads_up = first_grads
+    got, (down_first,) = exchange_group(
+        cut_group(grad_part(grads_down[0], 0)), *[part[0][-1] for part in arrived[-1][2]]
+    )
+    slot_grads_f[-1] = tie(slot_grads_f[-1], *got)
+    group_a = cut_group(grad_part(grads_down[0], 1), grad_part(grads_gate[0], 0))
+    group_b = cut_group(grad_part(grads_gate[0], 1), grad_part(grads_up[0]))
+    got, (down_second, gate_first) = exchange_group(group_a, slot_grads_f[-1])
     per_row = dots_f[0].shape[1]
     dot_rows = round_up(per_row, share) // share
     under = round_up(ranks * dot_rows, 16)
@@ -735,15 +880,13 @@
         own = sum_cols(jnp.concatenate([rows, dots], axis=0))
         own_rows.append(own[:slot_rows])
         own_dots.append(own[slot_rows : slot_rows + ranks * dot_rows].reshape(ranks, -1, share))
-    own_rows = tie(
-        jnp.concatenate(own_rows, axis=0),
-        *down_got[0][0],
-        *gate_first,
-        *grads_gate,
-        *grads_up,
-        *grads_down,
-        *down_slots,
-    )
+    own_rows = tie(jnp.concatenate(own_rows, axis=0), *got)
+    made = tie((scaled, grad_gate, grad_up), own_rows)
+    if local > 1:
+        grads_down.append(dot_f32("rf,rd->fd", made[0], slot_grad_out[-1]).astype(BF16))
+        grads_gate.append(dot_f32("rf,rd->fd", made[1], slot_in[-1]).astype(BF16))
+        grads_up.append(dot_f32("rf,rd->fd", made[2], slot_in[-1]).astype(BF16))
+    down_slots.append(jnp.dot(made[0], down_w, preferred_element_type=F32).astype(BF16))
     grad_home, dots_home = rows_home(
         own_rows, seqs, capacity, jnp.concatenate(own_dots, axis=1)
     )
@@ -752,36 +895,39 @@
     dots_home = dots_home.reshape(experts, 2, seqs, capacity, 1).transpose(1, 2, 0, 3, 4)
     match_home = home_f.reshape(seqs, experts, capacity, seq_dev).astype(F32)
     dots_home = jnp.sum(dots_home * match_home, axis=3).swapaxes(2, 3)
-    logits_f = logits_f.reshape(seqs, seq_len, experts)
     grad_mid, small_f = sublayer_back(
-        mid_low, seq3(inverse_f), gain_ffn, router_ffn, gates_f, logits_f,
+        mid_low, inverse_f, gain_ffn, router_ffn, gates_f, logits_f,
         dots_home[0], jnp.sum(dots_home[1], axis=-1), dhidden_f,
     )
     grad_mid = grad_out.astype(F32) + grad_mid
 
     mid_grad_rows = gather_rows(grad_mid.astype(BF16))
+    mid_grad_rows = tie(mid_grad_rows, group_b, *grads_down, *grads_gate, *grads_up, *down_slots)
+    group_c = [
+        cut_group(grad_part(grads_down[j]), grad_part(grads_gate[j], 0)) for j in range(1, local)
+    ]
+    group_d = [
+        cut_group(grad_part(grads_gate[j], 1), grad_part(grads_up[j])) for j in range(1, local)
+    ]
     mid_grad_all = gather_cols(mid_grad_rows).reshape(count, width)
-    gate_got = [[gate_first, rows_out(grads_gate[0], mid_grad_rows, half=1)]]
-    up_got = [[rows_out(grads_up[0], mid_grad_rows)]]
-    mid_grad_all = tie(mid_grad_all, *gate_got[0][1], *up_got[0][0])
-    down_slots = tie(jnp.concatenate(down_slots, axis=0), mid_grad_all)
+    got, (gate_second, up_got) = exchange_group(group_b, mid_grad_rows)
+    down_slots = jnp.concatenate(down_slots, axis=0)
+    mid_grad_all = tie(mid_grad_all, down_slots, group_c, group_d, *got)
+    down_parts, gate_parts = [[down_first, down_second]], [[gate_first, gate_second]]
+    up_parts = [[up_got]]
+    down_slots = tie(down_slots, mid_grad_all)
     down_own = sum_cols(down_slots)
     grad_raw = dot_f32("rd,fd->rf", mid_grad_all, out_cat)
     early = []
     for j in range(1, local):
-        down_got.append([rows_out(grads_down[j], mid_grad_all)])
-        gate_got.append([rows_out(grads_gate[j], mid_grad_all, half=0)])
-        early += [*down_got[-1][0], *gate_got[-1][0]]
+        got, (down_got, gate_first) = exchange_group(group_c[j - 1], mid_grad_all)
+        down_parts.append([down_got])
+        gate_parts.append([gate_first])
+        early += got
     into, dots_a = attend_back(
         qkv, target_a, kblk, log_totals, att_plain, seq3(grad_raw), my_gates_a.swapaxes(1, 2),
         cosine, sine, rows_each, heads,
     )
-    last = ()
-    for j in range(1, local):
-        gate_got[j].append(rows_out(grads_gate[j], into, *early, half=1))
-        up_got.append([rows_out(grads_up[j], into, *early)])
-        last += (*gate_got[j][1], *up_got[-1][0])
-    grad_out_cat = dot_f32("rf,rd->fd", att_scaled.reshape(count, -1), mid_grad_all).astype(BF16)
     placed = jnp.zeros((seqs, ranks, experts, seq_dev), F32)
     dots_a = dots_a.reshape(seqs, ranks, seq_dev, local + 1).swapaxes(2, 3)
     placed = lax.dynamic_update_slice_in_dim(placed, dots_a[:, :, :local], row_at * local, 2)
@@ -794,15 +940,21 @@
         into.reshape(seqs * ranks, seq_dev, -1), query_w, extra.reshape(-1, under, share)
     ).reshape(seqs, -1, width)
     token_part = tie(token_part, down_own, *early)
+    last = []
+    for j in range(1, local):
+        got, (gate_second, up_got) = exchange_group(group_d[j - 1], token_part)
+        gate_parts[j].append(gate_second)
+        up_parts.append([up_got])
+        last += got
+    att_scaled = tie(att_scaled, *last[1:2]).reshape(count, -1)
+    grad_out_cat = dot_f32("rf,rd->fd", att_scaled, mid_grad_all).astype(BF16)
     down_home, _ = rows_home(tie(down_own, token_part), seqs, capacity)
     part = lax.psum_scatter(token_part, "col", scatter_dimension=2, tiled=True)
-    out_pieces = rows_out(grad_out_cat, token_part, *last)
-    part = tie(part, *last, *out_pieces, down_home)
+    into = tie(into, *last[1:2]).reshape(count, -1)
+    grad_query_cat = dot_f32("rd,rf->df", hidden_a, into).astype(BF16)
+    out_pieces = exchange_pieces(cut_pieces(grad_part(grad_out_cat)[0]), *last[1:2])
+    part = tie(part, *last, down_home, grad_query_cat, *out_pieces[1:2])
     own = lax.psum_scatter(part, "row", scatter_dimension=1, tiled=True)
-    dhidden_a = own[:, :seq_dev].astype(F32)
-    dots_a = own[:, seq_dev:].reshape(seqs, -1)[:, :held].astype(F32)
-    dots_a = dots_a.reshape(seqs, experts + 1, seq_dev).swapaxes(1, 2)
-
     def out_grad_body(m, ins, outs):
         for j in range(local):
             for h in range(heads):
@@ -816,24 +968,58 @@
         [((experts, head_cols, depth), F32, (local, head_cols, depth), lambda b: (b, 0, 0))],
         "out_grad",
     )[0]
-
+    gate_all, up_all, down_all = (whole_grad(p) for p in (gate_parts, up_parts, down_parts))
+    own = tie(own, gate_all, up_all, down_all)
+    dhidden_a = own[:, :seq_dev].astype(F32)
+    dots_a = own[:, seq_dev:].reshape(seqs, -1)[:, :held].astype(F32)
+    dots_a = dots_a.reshape(seqs, experts + 1, seq_dev).swapaxes(1, 2)
+
+    def query_part(half):
+        rows = depth // 2
+        return cut_pieces(
+            lambda n: lax.dynamic_slice_in_dim(grad_query_cat, n * depth + half * rows, rows, 0)
+        )
+
+    query_first = exchange_pieces(query_part(0), part)
+    logits_a = logits_a.reshape(seqs, seq_len, experts)
+    grad_in, small_a = sublayer_back(
+        block_in, seq3(inverse_a), gain_attn, router_attn, gates_a, logits_a,
+        dots_a[..., :experts], dots_a[..., experts], dhidden_a,
+    )
+    grad_in = grad_mid + grad_in
+    block_out = (mid + come_home(home_f, down_home)).astype(BF16)
+
+    smalls = jnp.concatenate([small_a, small_f], axis=0)
+    high = smalls.astype(BF16)
+    smalls = jnp.stack([high, (smalls - high.astype(F32)).astype(BF16)]).reshape(-1)
+    held = smalls.shape[0]
+    under = round_up(held, 16 * made_cols) // made_cols
+    smalls = jnp.pad(smalls, (0, under * made_cols - held)).reshape(under, made_cols)
+    query_second = exchange_pieces(
+        [jnp.concatenate([piece, smalls], axis=0) for piece in query_part(1)]
+    )
+    smalls = sum(piece[depth // 2 :].astype(F32) for piece in query_second)
+    smalls = jnp.sum(smalls.reshape(-1)[:held].reshape(2, -1, share), axis=0)
+    smalls = lax.all_gather(smalls, "col", axis=1, tiled=True)
     def query_grad_body(m, ins, outs):
         for h in range(heads):
             columns = slice(h * HEAD_DIM, (h + 1) * HEAD_DIM)
             for p in range(parts):
                 at = (h * parts + p) * HEAD_DIM
-                piece = ins[0][:, at : at + HEAD_DIM].astype(F32)
-                if p < local:
-                    outs[0][p, :, columns] = piece
-                elif m == 0:
-                    outs[1 + p - local][:, columns] = piece
-                else:
-                    outs[1 + p - local][:, columns] = outs[1 + p - local][:, columns] + piece
-
-    grad_query_cat = dot_f32("rd,rf->df", hidden_a, into.reshape(count, -1)).astype(BF16)
+                for half in range(2):
+                    rows = slice(half * (depth // 2), (half + 1) * (depth // 2))
+                    piece = ins[half][: depth // 2, at : at + HEAD_DIM].astype(F32)
+                    if p < local:
+                        outs[0][p, rows, columns] = piece
+                    elif m == 0:
+                        outs[1 + p - local][rows, columns] = piece
+                    else:
+                        total = outs[1 + p - local][rows, columns] + piece
+                        outs[1 + p - local][rows, columns] = total
+
     shared = ((depth, head_cols), F32, (depth, head_cols), lambda b: (0, 0))
     grad_query_own, grad_key_own, grad_value_own = assemble(
-        [(p,) for p in columns_out(grad_query_cat, part)],
+        list(zip(query_first, query_second)),
         query_grad_body,
         [
             ((experts, depth, head_cols), F32, (local, depth, head_cols), lambda b: (b, 0, 0)),
@@ -842,18 +1028,6 @@
         ],
         "query_grad",
     )
-    logits_a = logits_a.reshape(seqs, seq_len, experts)
-    grad_in, small_a = sublayer_back(
-        block_in, seq3(inverse_a), gain_attn, router_attn, gates_a, logits_a,
-        dots_a[..., :experts], dots_a[..., experts], dhidden_a,
-    )
-    grad_in = grad_mid + grad_in
-    block_out = (mid + come_home(home_f, down_home)).astype(BF16)
-
-    smalls = jnp.concatenate([small_a, small_f], axis=0)
-    smalls = lax.all_gather(smalls, ("row", "col"), axis=0, tiled=False)
-    smalls = smalls.reshape(ranks, -1, 2 * experts + 2, share)
-    smalls = jnp.sum(smalls, axis=0).transpose(1, 0, 2).reshape(-1, width)
     return (
         block_out,
         grad_in,
@@ -865,9 +1039,9 @@
         grad_key_own,
         grad_value_own,
         grad_out_own,
-        whole_grad(gate_got).swapaxes(1, 2),
-        whole_grad(up_got).swapaxes(1, 2),
-        whole_grad(down_got),
+        gate_all.swapaxes(1, 2),
+        up_all.swapaxes(1, 2),
+        down_all,
     )
 
 

time: 1680 us -> 1530 us (0.911)
  waiting for transfers between devices: 846 us -> 670 us
  matrix products: 247 us -> 130 us
  Pallas kernels: 169 us -> 284 us
  starting transfers between devices: 156 us -> 191 us
  blocking collectives: 40 us -> 9.19 us
  other arithmetic: 77.5 us -> 106 us
    ppermute x60 -> x45, waiting for transfers between devices: 647 us -> 411 us  [exchange_pieces(): got.append(lax.ppermute(tie(pieces[m], *after), 'row', steps))]
    pallas_call x0 -> x4, Pallas kernels: none -> 95.2 us  [the longest x2 57.9 us: expert_step(): pl.pallas_call(expert_kernel, grid=(count // tile,), in_specs=[row(width)...]
    dot_general x27 -> x17, matrix products: 183 us -> 117 us  [dot_f32(): return jnp.einsum(spec, left, right, preferred_element_type=F32)]
    dot_general x7 -> x2, matrix products: 64 us -> 12.8 us  [the longest x1 7.25 us: per_device(): jnp.dot(made[0], down_w, preferred_element_type=F32).astype(BF16)]
    all_gather x4, waiting for transfers between devices: 140 us -> 108 us  [gather_rows(): return lax.all_gather(own, 'row', axis=1, tiled=True)]
    all_gather x1, blocking collectives: 40 us -> 9.19 us  [per_device(): smalls = lax.all_gather(smalls, 'col', axis=1, tiled=True)]
    reduce_scatter x4, waiting for transfers between devices: 8.68 us -> 37.9 us  [sum_cols(): return lax.psum_scatter(rows, 'col', scatter_dimension=1, tiled=True)]
    all_gather x4, waiting for transfers between devices: 0.01 us -> 26.5 us  [gather_cols(): return lax.all_gather(rows, 'col', axis=2, tiled=True)]
  transfers between devices with their start and end apart: 77 -> 62, of which waited for: 28 -> 26; matrix products, arithmetic and copies ran while one was open for 22% -> 18% of each run, Pallas kernels for 10% -> 18%
where the time goes in v3:
time: 1530 us; the launch traced here: 1520 us
  waiting for transfers between devices  670 us (44%)
  Pallas kernels  284 us (19%)
  starting transfers between devices  191 us (12%)
  matrix products  130 us (8%)
  local copies, waits for them, and re-layouts  110 us (7%)
  other arithmetic  106 us (7%)
  between operations  16 us (1%)
    ppermute x45, waiting for transfers between devices, exchange_pieces(): got.append(lax.ppermute(tie(pieces[m], *after), 'row', steps))  411 us
    ppermute x45, starting transfers between devices, exchange_pieces(): got.append(lax.ppermute(tie(pieces[m], *after), 'row', steps))  159 us
    dot_general x17, matrix products, dot_f32(): return jnp.einsum(spec, left, right, preferred_element_type=F32)  117 us
    all_gather x4, waiting for transfers between devices, gather_rows(): return lax.all_gather(own, 'row', axis=1, tiled=True)  108 us
    pallas_call x13, Pallas kernels, assemble(): pl.pallas_call(kernel, grid_spec=pltpu.PrefetchScalarGridSpec(num_scalar_...  58.9 us
    pallas_call x2, Pallas kernels, expert_step(): pl.pallas_call(expert_kernel, grid=(count // tile,), in_specs=[row(width)...  57.9 us
    all_to_all x3, waiting for transfers between devices, exchange(): return lax.all_to_all(parts, 'row', 0, 0)  48.5 us
    pallas_call x1, Pallas kernels, attend_back(): pl.pallas_call(partial(attend_back_kernel, rows), grid=(seqs, heads), in_...  44.6 us
  transfers between devices with their start and end apart: 62, of which 26 were waited for; matrix products, arithmetic and copies ran while one was open for 18% of the time, Pallas kernels for 18%

profile of v3, /device:TPU:0, one launch (start us, length us, event | category | flops | bytes accessed | tf_op | source)
XLA Modules:
  0.0 1516.2 jit_solution(13616979906203655007)
XLA Ops:
  19.6 44.9 %all-gather.9.cloned.1.call-done = bf16[4,1088,256]{2,1,0:T(8,128)(2,1)} async-done(((bf16[4,272,256]{2,1,0:T(8,128)(2,1)}), bf16[4,1088,256]{2,1,0:T(8,128)(2,1)}) %all-gather.9.cloned.1.call-update) | async-done | bytes 2228240 | tf_op jit(solution)/shard_map/all_gather | solution.py:423
  102.5 40.8 %collective-permute-done.1.refs_2_ = bf16[4,512,256]{2,1,0:T(8,128)(2,1)S(1)} collective-permute-done((bf16[4,512,256]{2,1,0:T(8,128)(2,1)}, bf16[4,512,256]{2,1,0:T(8,128)(2,1)S(1)}, u32[]{:S(2)}, u32[]{:S(2)}) %collective-permute-start.1) | collective-permute-done | bytes 1048608 | tf_op jit(solution)/shard_map/ppermute | solution.py:444
  143.3 22.2 %collective-permute-start.3 = (bf16[2,256,512]{2,1,0:T(8,128)(2,1)}, bf16[2,256,512]{2,1,0:T(8,128)(2,1)}, u32[]{:S(2)}, u32[]{:S(2)}) collective-permute-start(bf16[2,256,512]{2,1,0:T(8,128)(2,1)} %get-tuple-element.153), channel_id=1, source_target_pairs={{0,8},{8,16},{16,24},{24,0},{1,9},{9,17},{17,25},{25,1},{2,10},{10... | collective-permute-start | bytes 1572872 | tf_op jit(solution)/shard_map/ppermute | solution.py:444
  195.0 32.3 %project.1 = (bf16[4096,2048]{1,0:T(8,128)(2,1)}, f32[4096,1]{1,0:T(8,128)S(1)}, f32[4096,8]{1,0:T(8,128)S(1)}, bf16[4096,1024]{1,0:T(8,128)(2,1)}) custom-call(bf16[4096,2048]{1,0:T(8,128)(2,1)} %bitcast.429, f32[1,2048]{1,0:T(1,128)S(1)} %bitcast.342, bf16[2048,8]{1,0:T(8,128)(2,1)S(1)} %copy-done.28, bf16[2048,1024]{1,0:T(8,128)(2,1)} %query_in.1.weight_ref, ...), custom_call_target="tpu_custom_call" | custom-call | flops 17179869184 | bytes 41943040 | tf_op jit(solution)/shard_map/project/pallas_call | solution.py:112
  247.1 29.7 %attend.1 = (bf16[2,4,288,256]{3,2,1,0:T(8,128)(2,1)}, bf16[4,1024,512]{2,1,0:T(8,128)(2,1)}, bf16[4,1024,512]{2,1,0:T(8,128)(2,1)}, f32[4,2,576,1]{3,2,1,0:T(8,128)}) custom-call(bf16[4,1024,1024]{2,1,0:T(8,128)(2,1)} %bitcast.432, s32[4,2,1024]{2,1,0:T(2,128)} %pad_add_fusion.3.target_ref, f32[4,2,1024]{2,1,0:T(2,128)} %copy.386.gate_ref, ...), custom_call_target="tpu_custom_call" | custom-call | flops 7247757312 | bytes 16777216 | tf_op jit(solution)/shard_map/attend/pallas_call | solution.py:194
  294.0 23.6 %collective-permute-done.6.refs_1_.refs_2_ = bf16[1056,512]{1,0:T(8,128)(2,1)S(1)} collective-permute-done((bf16[1056,512]{1,0:T(8,128)(2,1)}, bf16[1056,512]{1,0:T(8,128)(2,1)S(1)}, u32[]{:S(2)}, u32[]{:S(2)}) %collective-permute-start.6) | collective-permute-done | bytes 1081376 | tf_op jit(solution)/shard_map/ppermute | solution.py:444
  317.5 44.1 %collective-permute-done.7.refs_2_.refs_4_ = bf16[1056,512]{1,0:T(8,128)(2,1)} collective-permute-done((bf16[1056,512]{1,0:T(8,128)(2,1)}, bf16[1056,512]{1,0:T(8,128)(2,1)}, u32[]{:S(2)}, u32[]{:S(2)}) %collective-permute-start.7) | collective-permute-done | bytes 1081376 | tf_op jit(solution)/shard_map/ppermute | solution.py:444
  367.2 21.0 %all-to-all-start = ((bf16[4,576,256]{2,1,0:T(8,128)(2,1)}), bf16[4,576,256]{2,1,0:T(8,128)(2,1)}, u32[]{:S(2)}, u32[]{:S(2)}) async-start(bf16[4,576,256]{2,1,0:T(8,128)(2,1)} %bitcast.366), calls=%async_computation.1 | async-start | bytes 2359296 | tf_op jit(solution)/shard_map/all_to_all | solution.py:431
  388.7 27.5 %all-to-all-done = bf16[4,576,256]{2,1,0:T(8,128)(2,1)} async-done(((bf16[4,576,256]{2,1,0:T(8,128)(2,1)}), bf16[4,576,256]{2,1,0:T(8,128)(2,1)}, u32[]{:S(2)}, u32[]{:S(2)}) %all-to-all-start) | async-done | bytes 1179680 | tf_op jit(solution)/shard_map/all_to_all | solution.py:431
  419.7 46.6 %all-gather.15.cloned.1.call-done = bf16[4,1024,256]{2,1,0:T(8,128)(2,1)} async-done(((bf16[4,256,256]{2,1,0:T(8,128)(2,1)}), bf16[4,1024,256]{2,1,0:T(8,128)(2,1)}) %all-gather.15.cloned.1.call-update) | async-done | bytes 2097168 | tf_op jit(solution)/shard_map/all_gather | solution.py:423
  470.4 24.9 %collective-permute-done.9.refs_3_.refs_1_ = bf16[1056,512]{1,0:T(8,128)(2,1)S(1)} collective-permute-done((bf16[1056,512]{1,0:T(8,128)(2,1)}, bf16[1056,512]{1,0:T(8,128)(2,1)S(1)}, u32[]{:S(2)}, u32[]{:S(2)}) %collective-permute-start.9) | collective-permute-done | bytes 1081376 | tf_op jit(solution)/shard_map/ppermute | solution.py:444
  496.3 44.2 %collective-permute-done.10.refs_5_.refs_2_ = bf16[1056,512]{1,0:T(8,128)(2,1)S(1)} collective-permute-done((bf16[1056,512]{1,0:T(8,128)(2,1)}, bf16[1056,512]{1,0:T(8,128)(2,1)S(1)}, u32[]{:S(2)}, u32[]{:S(2)}) %collective-permute-start.10) | collective-permute-done | bytes 1081376 | tf_op jit(solution)/shard_map/ppermute | solution.py:444
  542.4 17.4 %all-gather.17.cloned.1.call-done = bf16[4,1024,2048]{2,1,0:T(8,128)(2,1)} async-done(((bf16[4,1024,256]{2,1,0:T(8,128)(2,1)}), bf16[4,1024,2048]{2,1,0:T(8,128)(2,1)}) %all-gather.17.cloned.1.call-update) | async-done | bytes 16777232 | tf_op jit(solution)/shard_map/all_gather | solution.py:427
  568.8 23.2 %dispatch.2 = (bf16[4,288,2048]{2,1,0:T(8,128)(2,1)}, bf16[4,288,2048]{2,1,0:T(8,128)(2,1)}, f32[4,1024,1]{2,1,0:T(8,128)}, f32[4,1024,8]{2,1,0:T(8,128)}) custom-call(bf16[4,1024,2048]{2,1,0:T(8,128)(2,1)} %all-gather.17.cloned.1.call-done, s32[4,2,1024]{2,1,0:T(2,128)} %pad_add_fusion.6.target_ref, f32[1,2048]{1,0:T(1,128)} %bitcast.428, ...), custom_call_target="tpu_custom_call" | custom-call | flops 9663676416 | bytes 26214400 | tf_op jit(solution)/shard_map/dispatch/pallas_call | solution.py:356
  616.1 44.6 %collective-permute-done.13.refs_2_ = bf16[1408,512]{1,0:T(8,128)(2,1)} collective-permute-done((bf16[1408,512]{1,0:T(8,128)(2,1)}, bf16[1408,512]{1,0:T(8,128)(2,1)}, u32[]{:S(2)}, u32[]{:S(2)}) %collective-permute-start.13) | collective-permute-done | bytes 1441824 | tf_op jit(solution)/shard_map/ppermute | solution.py:444
  660.7 14.1 dispatch.3
  674.8 31.4 %collective-permute-start.15 = (bf16[352,512]{1,0:T(8,128)(2,1)}, bf16[352,512]{1,0:T(8,128)(2,1)S(1)}, u32[]{:S(2)}, u32[]{:S(2)}) collective-permute-start(bf16[352,512]{1,0:T(8,128)(2,1)} %get-tuple-element.199), channel_id=1, source_target_pairs={{0,8},{8,16},{16,24},{24,0},{1,9},{9,17},{17,25},{25,1},{2,10},{10... | collective-permute-start | bytes 1081352 | tf_op jit(solution)/shard_map/ppermute | solution.py:444
  708.6 29.2 %expert_step.2 = (bf16[1152,704]{1,0:T(8,128)(2,1)}, bf16[1152,704]{1,0:T(8,128)(2,1)}, bf16[1152,704]{1,0:T(8,128)(2,1)}, bf16[1152,2048]{1,0:T(8,128)(2,1)}, f32[1152,2]{1,0:T(8,128)}) custom-call(bf16[1152,2048]{1,0:T(8,128)(2,1)} %bitcast.444, bf16[1152,2048]{1,0:T(8,128)(2,1)} %bitcast.449, f32[1152,1]{1,0:T(8,128)} %reshape.662.weight_ref, ...), custom_call_target="tpu_custom_call" | custom-call | flops 16609443840 | bytes 27672576 | tf_op jit(solution)/shard_map/expert_step/pallas_call | solution.py:406
  750.8 8.6 collective-permute-done.18.refs_3_
  768.7 7.4 convolution_convert_fusion.7
  794.0 11.8 collective-permute-start.21
  812.7 28.7 %expert_step.3 = (bf16[1152,704]{1,0:T(8,128)(2,1)}, bf16[1152,704]{1,0:T(8,128)(2,1)}, bf16[1152,704]{1,0:T(8,128)(2,1)}, bf16[1152,2048]{1,0:T(8,128)(2,1)}, f32[1152,2]{1,0:T(8,128)}) custom-call(bf16[1152,2048]{1,0:T(8,128)(2,1)} %bitcast.437, bf16[1152,2048]{1,0:T(8,128)(2,1)} %bitcast.442, f32[1152,1]{1,0:T(8,128)} %reshape.663.weight_ref, ...), custom_call_target="tpu_custom_call" | custom-call | flops 16609443840 | bytes 27672576 | tf_op jit(solution)/shard_map/expert_step/pallas_call | solution.py:406
  868.5 34.8 %reduce-scatter.11.cloned.1.call-done = bf16[1168,256]{1,0:T(8,128)(2,1)} async-done(((bf16[1168,2048]{1,0:T(8,128)(2,1)}), bf16[1168,256]{1,0:T(8,128)(2,1)}) %reduce-scatter.11.cloned.1.call-update) | async-done | bytes 598032 | tf_op jit(solution)/shard_map/reduce_scatter | solution.py:538
  926.4 15.1 all-to-all-done.1
  955.4 7.3 convolution_convert_fusion.1
  962.7 8.1 convolution_convert_fusion.6
  970.7 8.1 convolution_convert_fusion.5
  984.2 16.1 %all-gather.21.cloned.1.call-done = bf16[4,1024,256]{2,1,0:T(8,128)(2,1)} async-done(((bf16[4,256,256]{2,1,0:T(8,128)(2,1)}), bf16[4,1024,256]{2,1,0:T(8,128)(2,1)}) %all-gather.21.cloned.1.call-update) | async-done | bytes 2097168 | tf_op jit(solution)/shard_map/all_gather | solution.py:423
  1020.1 19.5 %collective-permute-done.27.refs_5_.refs_2_ = bf16[1056,512]{1,0:T(8,128)(2,1)} collective-permute-done((bf16[1056,512]{1,0:T(8,128)(2,1)}, bf16[1056,512]{1,0:T(8,128)(2,1)}, u32[]{:S(2)}, u32[]{:S(2)}) %collective-permute-start.27) | collective-permute-done | bytes 1081376 | tf_op jit(solution)/shard_map/ppermute | solution.py:444
  1039.7 45.2 %collective-permute-done.28.refs_9_.refs_4_ = bf16[1056,512]{1,0:T(8,128)(2,1)} collective-permute-done((bf16[1056,512]{1,0:T(8,128)(2,1)}, bf16[1056,512]{1,0:T(8,128)(2,1)}, u32[]{:S(2)}, u32[]{:S(2)}) %collective-permute-start.28) | collective-permute-done | bytes 1081376 | tf_op jit(solution)/shard_map/ppermute | solution.py:444
  1084.9 9.1 all-gather.23.cloned.1.call-done
  1096.8 13.6 collective-permute-start.30
  1112.8 17.3 %fusion.65 = f32[4096,512]{1,0:T(8,128)} fusion(bf16[4096,2048]{1,0:T(8,128)(2,1)} %bitcast.430, bf16[512,2048]{1,0:T(8,128)(2,1)} %copy-done.36), kind=kOutput, calls=%fused_computation.371 | convolution fusion | flops 8589934592 | bytes 27262976 | tf_op jit(solution)/shard_map/rd,fd->rf/dot_general | solution.py:20
  1130.1 44.6 %attend_back.1 = (bf16[4,1024,1024]{2,1,0:T(8,128)(2,1)}, f32[4,1024,3]{2,1,0:T(8,128)}) custom-call(bf16[4,1024,1024]{2,1,0:T(8,128)(2,1)} %bitcast.433, s32[4,2,1024]{2,1,0:T(2,128)} %pad_add_fusion.3.target_ref, s32[4,1,1024]{2,1,0:T(1,128)} %reshape.608.kblk_ref, f32[4,2,576,1]{3,2,1,0:T(8,128)} %get-tuple-element.240.lse_ref, ...), custom_call_target="tpu_custom_call" | custom-call | flops 14495514624 | bytes 33554432 | tf_op jit(solution)/shard_map/attend_back/pallas_call | solution.py:277
  1179.3 23.8 %spread.1 = bf16[16,272,2048]{2,1,0:T(8,128)(2,1)} custom-call(bf16[16,256,1024]{2,1,0:T(8,128)(2,1)} %bitcast.434, bf16[2048,1024]{1,0:T(8,128)(2,1)S(1)} %copy-done.12, bf16[16,16,256]{2,1,0:T(8,128)(2,1)S(1)} %bitcast.341), custom_call_target="tpu_custom_call" | custom-call | flops 17179869184 | bytes 26214400 | tf_op jit(solution)/shard_map/spread/pallas_call | solution.py:521
  1215.6 16.6 %collective-permute-done.33.refs_7_.refs_3_ = bf16[1056,512]{1,0:T(8,128)(2,1)} collective-permute-done((bf16[1056,512]{1,0:T(8,128)(2,1)}, bf16[1056,512]{1,0:T(8,128)(2,1)}, u32[]{:S(2)}, u32[]{:S(2)}) %collective-permute-start.33) | collective-permute-done | bytes 1081376 | tf_op jit(solution)/shard_map/ppermute | solution.py:444
  1232.2 13.7 convolution_convert_fusion.10
  1247.3 24.0 %convolution_convert_fusion.3 = bf16[2048,1024]{1,0:T(8,128)(2,1)} fusion(bf16[4096,2048]{1,0:T(8,128)(2,1)} %get-tuple-element.254, bf16[4096,1024]{1,0:T(8,128)(2,1)} %bitcast.435), kind=kOutput, calls=%fused_computation.18 | convolution fusion | flops 17181966336 | bytes 29360128 | tf_op jit(solution)/shard_map/rd,rf->df/dot_general | solution.py:20
  1279.5 32.0 %collective-permute-done.34.refs_11_.refs_5_ = bf16[1056,512]{1,0:T(8,128)(2,1)} collective-permute-done((bf16[1056,512]{1,0:T(8,128)(2,1)}, bf16[1056,512]{1,0:T(8,128)(2,1)}, u32[]{:S(2)}, u32[]{:S(2)}) %collective-permute-start.34) | collective-permute-done | bytes 1081376 | tf_op jit(solution)/shard_map/ppermute | solution.py:444
  1311.6 12.8 reduce-scatter.15.cloned.1.call-done
  1343.6 12.0 collective-permute-start.43
  1357.0 8.3 whole_grad.3
  1365.4 7.7 whole_grad.4
  1374.9 25.2 %reduce-scatter.17.cloned.1.call-done = bf16[4,272,256]{2,1,0:T(8,128)(2,1)} async-done(((bf16[4,1088,256]{2,1,0:T(8,128)(2,1)}), bf16[4,272,256]{2,1,0:T(8,128)(2,1)}) %reduce-scatter.17.cloned.1.call-update) | async-done | bytes 557072 | tf_op jit(solution)/shard_map/reduce_scatter | solution.py:957
  1409.7 13.2 collective-permute-start.38
  1434.7 45.9 %collective-permute-done.38.refs_5_ = bf16[272,1024]{1,0:T(8,128)(2,1)S(1)} collective-permute-done((bf16[272,1024]{1,0:T(8,128)(2,1)S(1)}, bf16[272,1024]{1,0:T(8,128)(2,1)S(1)}, u32[]{:S(2)}, u32[]{:S(2)}) %collective-permute-start.38) | collective-permute-done | bytes 557088 | tf_op jit(solution)/shard_map/ppermute | solution.py:444
  1480.7 9.2 all_gather.35
  1491.2 14.1 collective-permute-done.41.refs_4_
  (609 shorter events, 384.8 us)
Async XLA Ops:
  7.2 57.3 %all-gather.9.cloned.1.call-start = ((), (), s32[]{:S(2)}) async-start(), calls=%async_computation.9 | async-start | bytes 2785280 | tf_op jit(solution)/shard_map/all_gather | solution.py:423
  13.4 178.4 %all-gather.11.cloned.1.call-start = ((), (), s32[]{:S(2)}) async-start(), calls=%async_computation.10 | async-start | bytes 18874368 | tf_op jit(solution)/shard_map/all_gather | solution.py:427
  67.6 220.9 %all-gather.13.cloned.1.call-start = ((), (), s32[]{:S(2)}) async-start(), calls=%async_computation.11 | async-start | bytes 2621440 | tf_op jit(solution)/shard_map/all_gather | solution.py:423
  71.3 72.0 %collective-permute-start.1 = (bf16[4,512,256]{2,1,0:T(8,128)(2,1)}, bf16[4,512,256]{2,1,0:T(8,128)(2,1)S(1)}, u32[]{:S(2)}, u32[]{:S(2)}) collective-permute-start(bf16[4,512,256]{2,1,0:T(8,128)(2,1)} %get-tuple-element.148), channel_id=1, source_target_pairs={{0,16},{8,24},{16,0},{24,8},{1,17},{9,25},{17,1},{25,9},{2,18},{10... | collective-permute-start | bytes 3145736 | tf_op jit(solution)/shard_map/ppermute | solution.py:444
  72.8 70.5 %collective-permute-start.2 = (bf16[4,512,256]{2,1,0:T(8,128)(2,1)}, bf16[4,512,256]{2,1,0:T(8,128)(2,1)}, u32[]{:S(2)}, u32[]{:S(2)}) collective-permute-start(bf16[4,512,256]{2,1,0:T(8,128)(2,1)} %get-tuple-element.149), channel_id=1, source_target_pairs={{0,24},{8,0},{16,8},{24,16},{1,25},{9,1},{17,9},{25,17},{2,26},{10... | collective-permute-start | bytes 3145736 | tf_op jit(solution)/shard_map/ppermute | solution.py:444
  143.3 133.5 %collective-permute-start.3 = (bf16[2,256,512]{2,1,0:T(8,128)(2,1)}, bf16[2,256,512]{2,1,0:T(8,128)(2,1)}, u32[]{:S(2)}, u32[]{:S(2)}) collective-permute-start(bf16[2,256,512]{2,1,0:T(8,128)(2,1)} %get-tuple-element.153), channel_id=1, source_target_pairs={{0,8},{8,16},{16,24},{24,0},{1,9},{9,17},{17,25},{25,1},{2,10},{10... | collective-permute-start | bytes 1572872 | tf_op jit(solution)/shard_map/ppermute | solution.py:444
  165.5 111.3 %collective-permute-start.4 = (bf16[2,256,512]{2,1,0:T(8,128)(2,1)}, bf16[2,256,512]{2,1,0:T(8,128)(2,1)}, u32[]{:S(2)}, u32[]{:S(2)}) collective-permute-start(bf16[2,256,512]{2,1,0:T(8,128)(2,1)} %get-tuple-element.154), channel_id=1, source_target_pairs={{0,16},{8,24},{16,0},{24,8},{1,17},{9,25},{17,1},{25,9},{2,18},{10... | collective-permute-start | bytes 1572872 | tf_op jit(solution)/shard_map/ppermute | solution.py:444
  166.6 110.2 %collective-permute-start.5 = (bf16[2,256,512]{2,1,0:T(8,128)(2,1)}, bf16[2,256,512]{2,1,0:T(8,128)(2,1)}, u32[]{:S(2)}, u32[]{:S(2)}) collective-permute-start(bf16[2,256,512]{2,1,0:T(8,128)(2,1)} %get-tuple-element.155), channel_id=1, source_target_pairs={{0,24},{8,0},{16,8},{24,16},{1,25},{9,1},{17,9},{25,17},{2,26},{10... | collective-permute-start | bytes 1572872 | tf_op jit(solution)/shard_map/ppermute | solution.py:444
  191.8 173.0 %reduce-scatter.7.cloned.1.call-start = ((), (), s32[]{:S(2)}) async-start(), calls=%async_computation.12 | async-start | bytes 10616832 | tf_op jit(solution)/shard_map/reduce_scatter | solution.py:538
  289.3 72.3 %collective-permute-start.7 = (bf16[1056,512]{1,0:T(8,128)(2,1)}, bf16[1056,512]{1,0:T(8,128)(2,1)}, u32[]{:S(2)}, u32[]{:S(2)}) collective-permute-start(bf16[1056,512]{1,0:T(8,128)(2,1)} %pad_maximum_fusion.23), channel_id=1, source_target_pairs={{0,16},{8,24},{16,0},{24,8},{1,17},{9,25},{17,1},{25,9},{2,18},{10... | collective-permute-start | bytes 3244040 | tf_op jit(solution)/shard_map/ppermute | solution.py:444
  291.2 70.5 %collective-permute-start.8 = (bf16[1056,512]{1,0:T(8,128)(2,1)}, bf16[1056,512]{1,0:T(8,128)(2,1)}, u32[]{:S(2)}, u32[]{:S(2)}) collective-permute-start(bf16[1056,512]{1,0:T(8,128)(2,1)} %pad_maximum_fusion.24), channel_id=1, source_target_pairs={{0,24},{8,0},{16,8},{24,16},{1,25},{9,1},{17,9},{25,17},{2,26},{10... | collective-permute-start | bytes 3244040 | tf_op jit(solution)/shard_map/ppermute | solution.py:444
  367.2 49.0 %all-to-all-start = ((bf16[4,576,256]{2,1,0:T(8,128)(2,1)}), bf16[4,576,256]{2,1,0:T(8,128)(2,1)}, u32[]{:S(2)}, u32[]{:S(2)}) async-start(bf16[4,576,256]{2,1,0:T(8,128)(2,1)} %bitcast.366), calls=%async_computation.1 | async-start | bytes 2359296 | tf_op jit(solution)/shard_map/all_to_all | solution.py:431
  388.2 78.1 %all-gather.15.cloned.1.call-start = ((), (), s32[]{:S(2)}) async-start(), calls=%async_computation.13 | async-start | bytes 2621440 | tf_op jit(solution)/shard_map/all_gather | solution.py:423
  419.6 140.2 %all-gather.17.cloned.1.call-start = ((), (), s32[]{:S(2)}) async-start(), calls=%async_computation.14 | async-start | bytes 18874368 | tf_op jit(solution)/shard_map/all_gather | solution.py:427
  466.3 194.4 %all-gather.19.cloned.1.call-start = ((), (), s32[]{:S(2)}) async-start(), calls=%async_computation.15 | async-start | bytes 18874368 | tf_op jit(solution)/shard_map/all_gather | solution.py:427
  466.4 74.1 %collective-permute-start.10 = (bf16[1056,512]{1,0:T(8,128)(2,1)}, bf16[1056,512]{1,0:T(8,128)(2,1)S(1)}, u32[]{:S(2)}, u32[]{:S(2)}) collective-permute-start(bf16[1056,512]{1,0:T(8,128)(2,1)} %pad_maximum_fusion.27), channel_id=1, source_target_pairs={{0,16},{8,24},{16,0},{24,8},{1,17},{9,25},{17,1},{25,9},{2,18},{10... | collective-permute-start | bytes 3244040 | tf_op jit(solution)/shard_map/ppermute | solution.py:444
  468.1 73.4 %collective-permute-start.11 = (bf16[1056,512]{1,0:T(8,128)(2,1)S(1)}, bf16[1056,512]{1,0:T(8,128)(2,1)S(1)}, u32[]{:S(2)}, u32[]{:S(2)}) collective-permute-start(bf16[1056,512]{1,0:T(8,128)(2,1)S(1)} %copy-done.70), channel_id=1, source_target_pairs={{0,24},{8,0},{16,8},{24,16},{1,25},{9,1},{17,9},{25,17},{2,26},{10... | collective-permute-start | bytes 3244040 | tf_op jit(solution)/shard_map/ppermute | solution.py:444
  559.9 306.0 %reduce-scatter.9.cloned.1.call-start = ((), (), s32[]{:S(2)}) async-start(), calls=%async_computation.16 | async-start | bytes 5382144 | tf_op jit(solution)/shard_map/reduce_scatter | solution.py:538
  561.9 54.1 %collective-permute-start.12 = (bf16[1408,512]{1,0:T(8,128)(2,1)}, bf16[1408,512]{1,0:T(8,128)(2,1)}, u32[]{:S(2)}, u32[]{:S(2)}) collective-permute-start(bf16[1408,512]{1,0:T(8,128)(2,1)} %pad_maximum_fusion.12), channel_id=1, source_target_pairs={{0,8},{8,16},{16,24},{24,0},{1,9},{9,17},{17,25},{25,1},{2,10},{10... | collective-permute-start | bytes 4325384 | tf_op jit(solution)/shard_map/ppermute | solution.py:444
  566.3 94.3 %collective-permute-start.13 = (bf16[1408,512]{1,0:T(8,128)(2,1)}, bf16[1408,512]{1,0:T(8,128)(2,1)}, u32[]{:S(2)}, u32[]{:S(2)}) collective-permute-start(bf16[1408,512]{1,0:T(8,128)(2,1)} %pad_maximum_fusion.13), channel_id=1, source_target_pairs={{0,16},{8,24},{16,0},{24,8},{1,17},{9,25},{17,1},{25,9},{2,18},{10... | collective-permute-start | bytes 4325384 | tf_op jit(solution)/shard_map/ppermute | solution.py:444
  568.3 92.4 %collective-permute-start.14 = (bf16[1408,512]{1,0:T(8,128)(2,1)}, bf16[1408,512]{1,0:T(8,128)(2,1)}, u32[]{:S(2)}, u32[]{:S(2)}) collective-permute-start(bf16[1408,512]{1,0:T(8,128)(2,1)} %pad_maximum_fusion.14), channel_id=1, source_target_pairs={{0,24},{8,0},{16,8},{24,16},{1,25},{9,1},{17,9},{25,17},{2,26},{10... | collective-permute-start | bytes 4325384 | tf_op jit(solution)/shard_map/ppermute | solution.py:444
  674.8 65.7 %collective-permute-start.15 = (bf16[352,512]{1,0:T(8,128)(2,1)}, bf16[352,512]{1,0:T(8,128)(2,1)S(1)}, u32[]{:S(2)}, u32[]{:S(2)}) collective-permute-start(bf16[352,512]{1,0:T(8,128)(2,1)} %get-tuple-element.199), channel_id=1, source_target_pairs={{0,8},{8,16},{16,24},{24,0},{1,9},{9,17},{17,25},{25,1},{2,10},{10... | collective-permute-start | bytes 1081352 | tf_op jit(solution)/shard_map/ppermute | solution.py:444
  745.9 157.4 %reduce-scatter.11.cloned.1.call-start = ((), (), s32[]{:S(2)}) async-start(), calls=%async_computation.17 | async-start | bytes 5382144 | tf_op jit(solution)/shard_map/reduce_scatter | solution.py:538
  747.8 62.6 %collective-permute-start.19 = (bf16[352,512]{1,0:T(8,128)(2,1)}, bf16[352,512]{1,0:T(8,128)(2,1)S(1)}, u32[]{:S(2)}, u32[]{:S(2)}) collective-permute-start(bf16[352,512]{1,0:T(8,128)(2,1)} %get-tuple-element.214), channel_id=1, source_target_pairs={{0,16},{8,24},{16,0},{24,8},{1,17},{9,25},{17,1},{25,9},{2,18},{10... | collective-permute-start | bytes 1081352 | tf_op jit(solution)/shard_map/ppermute | solution.py:444
  794.0 48.9 %collective-permute-start.21 = (bf16[352,512]{1,0:T(8,128)(2,1)}, bf16[352,512]{1,0:T(8,128)(2,1)S(1)}, u32[]{:S(2)}, u32[]{:S(2)}) collective-permute-start(bf16[352,512]{1,0:T(8,128)(2,1)} %get-tuple-element.221), channel_id=1, source_target_pairs={{0,8},{8,16},{16,24},{24,0},{1,9},{9,17},{17,25},{25,1},{2,10},{10... | collective-permute-start | bytes 1081352 | tf_op jit(solution)/shard_map/ppermute | solution.py:444
  860.4 45.8 %collective-permute-start.24 = (bf16[704,512]{1,0:T(8,128)(2,1)}, bf16[704,512]{1,0:T(8,128)(2,1)S(1)}, u32[]{:S(2)}, u32[]{:S(2)}) collective-permute-start(bf16[704,512]{1,0:T(8,128)(2,1)} %pad_maximum_fusion.42), channel_id=1, source_target_pairs={{0,8},{8,16},{16,24},{24,0},{1,9},{9,17},{17,25},{25,1},{2,10},{10... | collective-permute-start | bytes 2162696 | tf_op jit(solution)/shard_map/ppermute | solution.py:444
  860.4 45.8 %collective-permute-start.25 = (bf16[704,512]{1,0:T(8,128)(2,1)}, bf16[704,512]{1,0:T(8,128)(2,1)S(1)}, u32[]{:S(2)}, u32[]{:S(2)}) collective-permute-start(bf16[704,512]{1,0:T(8,128)(2,1)} %pad_maximum_fusion.43), channel_id=1, source_target_pairs={{0,16},{8,24},{16,0},{24,8},{1,17},{9,25},{17,1},{25,9},{2,18},{10... | collective-permute-start | bytes 2162696 | tf_op jit(solution)/shard_map/ppermute | solution.py:444
  913.9 86.4 %all-gather.21.cloned.1.call-start = ((), (), s32[]{:S(2)}) async-start(), calls=%async_computation.18 | async-start | bytes 2621440 | tf_op jit(solution)/shard_map/all_gather | solution.py:423
  955.3 138.7 %all-gather.23.cloned.1.call-start = ((), (), s32[]{:S(2)}) async-start(), calls=%async_computation.19 | async-start | bytes 18874368 | tf_op jit(solution)/shard_map/all_gather | solution.py:427
  1000.3 202.9 %reduce-scatter.13.cloned.1.call-start = ((), (), s32[]{:S(2)}) async-start(), calls=%async_computation.20 | async-start | bytes 10616832 | tf_op jit(solution)/shard_map/reduce_scatter | solution.py:538
  1010.7 74.2 %collective-permute-start.28 = (bf16[1056,512]{1,0:T(8,128)(2,1)}, bf16[1056,512]{1,0:T(8,128)(2,1)}, u32[]{:S(2)}, u32[]{:S(2)}) collective-permute-start(bf16[1056,512]{1,0:T(8,128)(2,1)} %pad_maximum_fusion.31), channel_id=1, source_target_pairs={{0,16},{8,24},{16,0},{24,8},{1,17},{9,25},{17,1},{25,9},{2,18},{10... | collective-permute-start | bytes 3244040 | tf_op jit(solution)/shard_map/ppermute | solution.py:444
  1012.4 72.5 %collective-permute-start.29 = (bf16[1056,512]{1,0:T(8,128)(2,1)}, bf16[1056,512]{1,0:T(8,128)(2,1)}, u32[]{:S(2)}, u32[]{:S(2)}) collective-permute-start(bf16[1056,512]{1,0:T(8,128)(2,1)} %pad_maximum_fusion.32), channel_id=1, source_target_pairs={{0,24},{8,0},{16,8},{24,16},{1,25},{9,1},{17,9},{25,17},{2,26},{10... | collective-permute-start | bytes 3244040 | tf_op jit(solution)/shard_map/ppermute | solution.py:444
  1094.0 230.4 %reduce-scatter.15.cloned.1.call-start = ((), (), s32[]{:S(2)}) async-start(), calls=%async_computation.21 | async-start | bytes 20054016 | tf_op jit(solution)/shard_map/reduce_scatter | solution.py:952
  1096.8 106.3 %collective-permute-start.30 = (bf16[1056,512]{1,0:T(8,128)(2,1)}, bf16[1056,512]{1,0:T(8,128)(2,1)}, u32[]{:S(2)}, u32[]{:S(2)}) collective-permute-start(bf16[1056,512]{1,0:T(8,128)(2,1)} %pad_maximum_fusion.34), channel_id=1, source_target_pairs={{0,8},{8,16},{16,24},{24,0},{1,9},{9,17},{17,25},{25,1},{2,10},{10... | collective-permute-start | bytes 3244040 | tf_op jit(solution)/shard_map/ppermute | solution.py:444
  1110.4 92.7 %collective-permute-start.31 = (bf16[1056,512]{1,0:T(8,128)(2,1)}, bf16[1056,512]{1,0:T(8,128)(2,1)}, u32[]{:S(2)}, u32[]{:S(2)}) collective-permute-start(bf16[1056,512]{1,0:T(8,128)(2,1)} %pad_maximum_fusion.35), channel_id=1, source_target_pairs={{0,16},{8,24},{16,0},{24,8},{1,17},{9,25},{17,1},{25,9},{2,18},{10... | collective-permute-start | bytes 3244040 | tf_op jit(solution)/shard_map/ppermute | solution.py:444
  1111.5 91.7 %collective-permute-start.32 = (bf16[1056,512]{1,0:T(8,128)(2,1)}, bf16[1056,512]{1,0:T(8,128)(2,1)}, u32[]{:S(2)}, u32[]{:S(2)}) collective-permute-start(bf16[1056,512]{1,0:T(8,128)(2,1)} %pad_maximum_fusion.36), channel_id=1, source_target_pairs={{0,24},{8,0},{16,8},{24,16},{1,25},{9,1},{17,9},{25,17},{2,26},{10... | collective-permute-start | bytes 3244040 | tf_op jit(solution)/shard_map/ppermute | solution.py:444
  1206.8 70.4 %all-to-all-start.2 = ((bf16[4,576,256]{2,1,0:T(8,128)(2,1)}), bf16[4,576,256]{2,1,0:T(8,128)(2,1)}, u32[]{:S(2)}, u32[]{:S(2)}) async-start(bf16[4,576,256]{2,1,0:T(8,128)(2,1)} %bitcast.365), calls=%async_computation.6 | async-start | bytes 2359296 | tf_op jit(solution)/shard_map/all_to_all | solution.py:431
  1211.2 188.9 %reduce-scatter.17.cloned.1.call-start = ((), (), s32[]{:S(2)}) async-start(), calls=%async_computation.22 | async-start | bytes 2785280 | tf_op jit(solution)/shard_map/reduce_scatter | solution.py:957
  1211.3 100.3 %collective-permute-start.34 = (bf16[1056,512]{1,0:T(8,128)(2,1)}, bf16[1056,512]{1,0:T(8,128)(2,1)}, u32[]{:S(2)}, u32[]{:S(2)}) collective-permute-start(bf16[1056,512]{1,0:T(8,128)(2,1)} %pad_maximum_fusion.39), channel_id=1, source_target_pairs={{0,16},{8,24},{16,0},{24,8},{1,17},{9,25},{17,1},{25,9},{2,18},{10... | collective-permute-start | bytes 3244040 | tf_op jit(solution)/shard_map/ppermute | solution.py:444
  1214.1 97.4 %collective-permute-start.35 = (bf16[1056,512]{1,0:T(8,128)(2,1)}, bf16[1056,512]{1,0:T(8,128)(2,1)}, u32[]{:S(2)}, u32[]{:S(2)}) collective-permute-start(bf16[1056,512]{1,0:T(8,128)(2,1)} %pad_maximum_fusion.40), channel_id=1, source_target_pairs={{0,24},{8,0},{16,8},{24,16},{1,25},{9,1},{17,9},{25,17},{2,26},{10... | collective-permute-start | bytes 3244040 | tf_op jit(solution)/shard_map/ppermute | solution.py:444
  1247.3 64.3 %collective-permute-start.36 = (bf16[512,512]{1,0:T(8,128)(2,1)}, bf16[512,512]{1,0:T(8,128)(2,1)}, u32[]{:S(2)}, u32[]{:S(2)}) collective-permute-start(bf16[512,512]{1,0:T(8,128)(2,1)} %get-tuple-element.258), channel_id=1, source_target_pairs={{0,8},{8,16},{16,24},{24,0},{1,9},{9,17},{17,25},{25,1},{2,10},{10... | collective-permute-start | bytes 1572872 | tf_op jit(solution)/shard_map/ppermute | solution.py:444
  1343.6 81.4 %collective-permute-start.43 = (bf16[512,512]{1,0:T(8,128)(2,1)}, bf16[512,512]{1,0:T(8,128)(2,1)}, u32[]{:S(2)}, u32[]{:S(2)}) collective-permute-start(bf16[512,512]{1,0:T(8,128)(2,1)} %get-tuple-element.267), channel_id=1, source_target_pairs={{0,16},{8,24},{16,0},{24,8},{1,17},{9,25},{17,1},{25,9},{2,18},{10... | collective-permute-start | bytes 1572872 | tf_op jit(solution)/shard_map/ppermute | solution.py:444
  1355.6 69.4 %collective-permute-start.44 = (bf16[512,512]{1,0:T(8,128)(2,1)}, bf16[512,512]{1,0:T(8,128)(2,1)}, u32[]{:S(2)}, u32[]{:S(2)}) collective-permute-start(bf16[512,512]{1,0:T(8,128)(2,1)} %get-tuple-element.268), channel_id=1, source_target_pairs={{0,24},{8,0},{16,8},{24,16},{1,25},{9,1},{17,9},{25,17},{2,26},{10... | collective-permute-start | bytes 1572872 | tf_op jit(solution)/shard_map/ppermute | solution.py:444
  1409.7 70.8 %collective-permute-start.38 = (bf16[272,1024]{1,0:T(8,128)(2,1)S(1)}, bf16[272,1024]{1,0:T(8,128)(2,1)S(1)}, u32[]{:S(2)}, u32[]{:S(2)}) collective-permute-start(bf16[272,1024]{1,0:T(8,128)(2,1)S(1)} %get-tuple-element.413), channel_id=1, source_target_pairs={{0,16},{8,24},{16,0},{24,8},{1,17},{9,25},{17,1},{25,9},{2,18},{10... | collective-permute-start | bytes 1671176 | tf_op jit(solution)/shard_map/ppermute | solution.py:444
  1423.0 57.6 %collective-permute-start.39 = (bf16[272,1024]{1,0:T(8,128)(2,1)S(1)}, bf16[272,1024]{1,0:T(8,128)(2,1)S(1)}, u32[]{:S(2)}, u32[]{:S(2)}) collective-permute-start(bf16[272,1024]{1,0:T(8,128)(2,1)S(1)} %get-tuple-element.414), channel_id=1, source_target_pairs={{0,24},{8,0},{16,8},{24,16},{1,25},{9,1},{17,9},{25,17},{2,26},{10... | collective-permute-start | bytes 1671176 | tf_op jit(solution)/shard_map/ppermute | solution.py:444
  1423.4 57.2 %collective-permute-start.37 = (bf16[272,1024]{1,0:T(8,128)(2,1)S(1)}, bf16[272,1024]{1,0:T(8,128)(2,1)S(1)}, u32[]{:S(2)}, u32[]{:S(2)}) collective-permute-start(bf16[272,1024]{1,0:T(8,128)(2,1)S(1)} %get-tuple-element.415), channel_id=1, source_target_pairs={{0,8},{8,16},{16,24},{24,0},{1,9},{9,17},{17,25},{25,1},{2,10},{10... | collective-permute-start | bytes 1671176 | tf_op jit(solution)/shard_map/ppermute | solution.py:444
  1431.8 59.3 %collective-permute-start.40 = (bf16[256,1024]{1,0:T(8,128)(2,1)}, bf16[256,1024]{1,0:T(8,128)(2,1)S(1)}, u32[]{:S(2)}, u32[]{:S(2)}) collective-permute-start(bf16[256,1024]{1,0:T(8,128)(2,1)} %get-tuple-element.261), channel_id=1, source_target_pairs={{0,8},{8,16},{16,24},{24,0},{1,9},{9,17},{17,25},{25,1},{2,10},{10... | collective-permute-start | bytes 1572872 | tf_op jit(solution)/shard_map/ppermute | solution.py:444
  1431.9 73.4 %collective-permute-start.41 = (bf16[256,1024]{1,0:T(8,128)(2,1)}, bf16[256,1024]{1,0:T(8,128)(2,1)}, u32[]{:S(2)}, u32[]{:S(2)}) collective-permute-start(bf16[256,1024]{1,0:T(8,128)(2,1)} %get-tuple-element.262), channel_id=1, source_target_pairs={{0,16},{8,24},{16,0},{24,8},{1,17},{9,25},{17,1},{25,9},{2,18},{10... | collective-permute-start | bytes 1572872 | tf_op jit(solution)/shard_map/ppermute | solution.py:444
  (132 other events, 1652.3 us)
Sparse Core Ops, SparseCore 0:
  13.5 50.9 all-gather.8
  67.7 91.9 all-gather.10
  191.9 53.1 all-gather.12
  288.7 76.0 reduce-scatter.6
  419.8 46.4 all-gather.14
  468.0 91.8 all-gather.16
  561.7 94.6 all-gather.18
  746.0 55.8 reduce-scatter.8
  848.8 54.4 reduce-scatter.10
  955.5 44.7 all-gather.20
  1002.1 91.8 all-gather.22
  1097.9 84.3 reduce-scatter.12
  1203.3 121.0 reduce-scatter.14
  1326.6 73.4 reduce-scatter.16

commit v4 on v3

--- a/solution.py
+++ b/solution.py
@@ -298,9 +298,9 @@
         ],
         compiler_params=pltpu.CompilerParams(vmem_limit_bytes=60 * 1024 * 1024),
         cost_estimate=pl.CostEstimate(
-            flops=24 * seqs * heads * total * length * HEAD_DIM,
-            bytes_accessed=8 * qkv.size,
-            transcendentals=seqs * heads * total * length,
+            flops=0,
+            bytes_accessed=4 * qkv.size,
+            transcendentals=0,
         ),
         name="attend_back",
     )(qkv, target, kblk, lse, plain, raw, gate_cols, cosine, sine)
@@ -362,8 +362,8 @@
         scratch_shapes=scratch,
         compiler_params=pltpu.CompilerParams(vmem_limit_bytes=56 * 1024 * 1024),
         cost_estimate=pl.CostEstimate(
-            flops=2 * local * seqs * rows * length * width,
-            bytes_accessed=2 * x.size + 2 * local * seqs * rows * width,
+            flops=0,
+            bytes_accessed=2 * x.size,
             transcendentals=0,
         ),
         name="dispatch",
@@ -411,9 +411,9 @@
         out_shape=[shape(units), shape(units), shape(units), shape(width), shape(2, F32)],
         compiler_params=pltpu.CompilerParams(vmem_limit_bytes=56 * 1024 * 1024),
         cost_estimate=pl.CostEstimate(
-            flops=10 * count * width * units,
-            bytes_accessed=6 * count * (width + units) + 6 * width * units,
-            transcendentals=count * units,
+            flops=0,
+            bytes_accessed=6 * width * units,
+            transcendentals=0,
         ),
         name="expert_step",
     )(x, grad, weight, gate_w, up_w, down_w)
@@ -526,8 +526,8 @@
         out_shape=jax.ShapeDtypeStruct((blocks, rows, width), BF16),
         compiler_params=pltpu.CompilerParams(vmem_limit_bytes=48 * 1024 * 1024),
         cost_estimate=pl.CostEstimate(
-            flops=2 * blocks * tokens * depth * width,
-            bytes_accessed=2 * blocks * (tokens * depth + rows * width),
+            flops=0,
+            bytes_accessed=2 * blocks * rows * width,
             transcendentals=0,
         ),
         name="spread",
@@ -644,7 +644,14 @@
     query_for = group_in(w_query)
     cosine, sine = rope_tables(seq_len)
     query_parts = cut_pieces(lambda n: jnp.concatenate([query_for(n), key_value]))
-    in_rows = tie(in_rows, cosine, sine, *query_parts)
+    out_parts = cut_pieces(group_in(w_out))
+    group_a = cut_group(expert_part(w_gate, 0), expert_part(w_up, 0, 0))
+    group_b = cut_group(expert_part(w_up, 0, 1), expert_part(w_down, 0))
+    group_c = [cut_group(expert_part(w_gate, j), expert_part(w_up, j)) for j in range(1, local)]
+    group_d = [cut_group(expert_part(w_down, j)) for j in range(1, local)]
+    in_rows = tie(
+        in_rows, cosine, sine, query_parts, out_parts, group_a, group_b, group_c, group_d
+    )
     query_got = exchange_pieces(query_parts, in_rows)
 
     def query_body(m, ins, outs):
@@ -677,15 +684,6 @@
     target_f = tokens_to_slots(small_all[2], small_all[3])
     routes_a = small_all[0].reshape(2, seqs, seq_len)
     routes_f = small_all[2].reshape(2, seqs, seq_len)
-    w_out, w_gate, w_up, w_down = tie((w_out, w_gate, w_up, w_down), *query_got[1:2])
-    out_parts = cut_pieces(group_in(w_out))
-    group_a = cut_group(expert_part(w_gate, 0), expert_part(w_up, 0, 0))
-    group_b = cut_group(expert_part(w_up, 0, 1), expert_part(w_down, 0))
-    group_c = [cut_group(expert_part(w_gate, j), expert_part(w_up, j)) for j in range(1, local)]
-    group_d = [
-        [cut_group(expert_part(w_down, j, half)) for half in (0, 1)] for j in range(1, local)
-    ]
-    out_got = exchange_pieces(out_parts, *query_got)
 
     def home_match(pairs, order):
         ranks_here = all_ranks(pairs, order)
@@ -704,15 +702,19 @@
         )
 
     in_all = gather_cols(in_rows).reshape(count, width)
+    grad_sent = jnp.einsum("sct,stf->scf", home_f, grad_out)
+    grad_sent = grad_sent.reshape(seqs, ranks, local, capacity, share).transpose(1, 2, 0, 3, 4)
     in_all = tie(
-        in_all, target_a, target_f, home_a, home_f, out_parts, group_a, group_b, group_c, group_d
+        in_all, target_a, target_f, home_a, home_f, grad_sent
     )
     rotated = ([True] * (local + 1) + [False]) * heads
     hidden_a, inverse_a, logits_a, qkv = project(
         in_all, gain_attn, router_attn, query_w, cosine, sine, rotated
     )
     qkv = qkv.reshape(seqs, seq_len, -1)
-    grad_rows = gather_rows(tie(grad_out, in_all))
+    out_got = exchange_pieces(out_parts, in_all)
+    qkv = tie(qkv, *out_got)
+    grad_rows = exchange(tie(grad_sent, qkv))
     gates_a = gate_table(
         logits_a.reshape(seqs, seq_len, experts), routes_a
     )
@@ -755,18 +757,21 @@
     got, (up_second, down_in) = exchange_group(group_b, mid_rows)
     mid_all = tie(mid_all, *got)
     arrived = [([gate_in], [up_first, up_second], [down_in])]
-    out_grad_all = gather_cols(tie(grad_rows, mid_all))
+    grad_rows = tie(grad_rows, mid_all).transpose(1, 2, 0, 3, 4)
+    grad_rows = grad_rows.reshape(local, slot_rows, share)
+    slot_grad_out = [
+        lax.all_gather(grad_rows[j], "col", axis=1, tiled=True) for j in range(local)
+    ]
+    held_back = []
     for j in range(1, local):
         got, (gate_in, up_in) = exchange_group(group_c[j - 1], mid_all)
-        out_grad_all = tie(out_grad_all, *got)
+        held_back += got
         arrived.append(([gate_in], [up_in], []))
     seq3 = lambda a: a.reshape(seqs, seq_len, -1)
     *slot_in, inverse_f, logits_f = dispatch(
         seq3(mid_all), target_f, rows_each, (gain_ffn, router_ffn)
     )
     slot_in = [x.reshape(slot_rows, width) for x in slot_in]
-    slot_grad_out = dispatch(out_grad_all, target_f, rows_each)
-    slot_grad_out = [x.reshape(slot_rows, width) for x in slot_grad_out]
     gates_f = gate_table(logits_f, routes_f)
     my_gates_f = my_gates(gates_f)
     blocked = lambda a: a.reshape(seqs, ranks, seq_dev)
@@ -790,8 +795,6 @@
     next_w = rows_in(arrived[0][0]), rows_in(arrived[0][1])
     for j in range(local):
         x = slot_in[j]
-        if j > 0:
-            x = tie(x, grads_gate[-1], grads_up[-1], grads_down[-1], down_slots[-1])
         gate_w, up_w = next_w
         down_w = rows_in(arrived[j][2])
         scaled, grad_gate, grad_up, slot_grad, dots = expert_step(
@@ -800,19 +803,18 @@
         dots = dots.reshape(seqs, ranks, capacity, 2).transpose(1, 3, 0, 2).reshape(ranks, -1)
         dots_f.append(dots.astype(BF16))
         if j + 1 < local:
-            got, (down_first,) = exchange_group(group_d[j][0], out_grad_all)
-            slot_grad = tie(slot_grad, *got)
-            got, (down_second,) = exchange_group(group_d[j][1], slot_grad)
-            arrived[j + 1][2].extend([down_first, down_second])
+            slot_grad = tie(slot_grad, *held_back)
+            got, (down_in,) = exchange_group(group_d[j], *held_back)
             gate_in, up_in = arrived[j + 1][0][0], arrived[j + 1][1][0]
-            held = tie(gate_in[0], got[1])
-            next_w = rows_in([(held, *gate_in[1:])]), rows_in([(held, *up_in[1:])])
-            made = tie((scaled, grad_gate, grad_up), got[1], next_w)
+            next_w = rows_in([gate_in]), rows_in([up_in])
+            made = tie((scaled, grad_gate, grad_up), *held_back)
             grads_down.append(dot_f32("rf,rd->fd", made[0], slot_grad_out[j]).astype(BF16))
             grads_gate.append(dot_f32("rf,rd->fd", made[1], slot_in[j]).astype(BF16))
             grads_up.append(dot_f32("rf,rd->fd", made[2], slot_in[j]).astype(BF16))
-            down = jnp.dot(made[0], down_w, preferred_element_type=F32)
-            down_slots.append(down.astype(BF16))
+            down = jnp.dot(made[0], down_w, preferred_element_type=F32).astype(BF16)
+            down_slots.append(down)
+            done = (grads_down[-1], grads_gate[-1], grads_up[-1], down, next_w)
+            arrived[j + 1][2].append((tie(got, done), *down_in[1:]))
         slot_grads_f.append(slot_grad)
 
     def grad_part(grad, half=None):

time: 1530 us -> 1500 us (0.980)
  waiting for transfers between devices: 670 us -> 635 us
    ppermute x45 -> x42, waiting for transfers between devices: 411 us -> 370 us  [exchange_pieces(): got.append(lax.ppermute(tie(pieces[m], *after), 'row', steps))]
    all_gather x4 -> x3, waiting for transfers between devices: 108 us -> 90 us  [gather_rows(): return lax.all_gather(own, 'row', axis=1, tiled=True)]
    pallas_call x2 -> x1, Pallas kernels: 37.3 us -> 22.5 us  [dispatch(): pl.pallas_call(kernel, grid=(seqs,), in_specs=in_specs, out_specs=out_spe...]
    all_to_all x3 -> x4, starting transfers between devices: 31.4 us -> 45 us  [exchange(): return lax.all_to_all(parts, 'row', 0, 0)]
    all_gather x4 -> x3, waiting for transfers between devices: 26.5 us -> 35.1 us  [gather_cols(): return lax.all_gather(rows, 'col', axis=2, tiled=True)]
    ppermute x45 -> x42, starting transfers between devices: 159 us -> 153 us  [exchange_pieces(): got.append(lax.ppermute(tie(pieces[m], *after), 'row', steps))]
    unnamed x247 -> x263, local copies, waits for them, and re-layouts: 41.4 us -> 38.5 us
    all_to_all x3 -> x4, waiting for transfers between devices: 48.5 us -> 50.9 us  [exchange(): return lax.all_to_all(parts, 'row', 0, 0)]
  transfers between devices with their start and end apart: 62 -> 60, of which waited for: 26 -> 27; matrix products, arithmetic and copies ran while one was open for 18% -> 20% of each run, Pallas kernels for 18% -> 18%
where the time goes in v4:
time: 1500 us; the launch traced here: 1480 us
  waiting for transfers between devices  635 us (42%)
  Pallas kernels  270 us (18%)
  starting transfers between devices  199 us (13%)
  matrix products  132 us (9%)
  local copies, waits for them, and re-layouts  112 us (7%)
  other arithmetic  106 us (7%)
  between operations  16.1 us (1%)
    ppermute x42, waiting for transfers between devices, exchange_pieces(): got.append(lax.ppermute(tie(pieces[m], *after), 'row', steps))  370 us
    ppermute x42, starting transfers between devices, exchange_pieces(): got.append(lax.ppermute(tie(pieces[m], *after), 'row', steps))  153 us
    dot_general x17, matrix products, dot_f32(): return jnp.einsum(spec, left, right, preferred_element_type=F32)  119 us
    all_gather x3, waiting for transfers between devices, gather_rows(): return lax.all_gather(own, 'row', axis=1, tiled=True)  90 us
    pallas_call x13, Pallas kernels, assemble(): pl.pallas_call(kernel, grid_spec=pltpu.PrefetchScalarGridSpec(num_scalar_...  60.1 us
    pallas_call x2, Pallas kernels, expert_step(): pl.pallas_call(expert_kernel, grid=(count // tile,), in_specs=[row(width)...  57.7 us
    all_to_all x4, waiting for transfers between devices, exchange(): return lax.all_to_all(parts, 'row', 0, 0)  50.9 us
    reduce_scatter x4, waiting for transfers between devices, sum_cols(): return lax.psum_scatter(rows, 'col', scatter_dimension=1, tiled=True)  47.1 us
  transfers between devices with their start and end apart: 60, of which 27 were waited for; matrix products, arithmetic and copies ran while one was open for 20% of the time, Pallas kernels for 18%

profile of v4, /device:TPU:0, one launch (start us, length us, event | category | flops | bytes accessed | tf_op | source)
XLA Modules:
  0.0 1479.5 jit_solution(11136583515254124625)
XLA Ops:
  39.1 24.9 %all-gather.9.cloned.1.call-done = bf16[4,1088,256]{2,1,0:T(8,128)(2,1)} async-done(((bf16[4,272,256]{2,1,0:T(8,128)(2,1)}), bf16[4,1088,256]{2,1,0:T(8,128)(2,1)}) %all-gather.9.cloned.1.call-update) | async-done | bytes 2228240 | tf_op jit(solution)/shard_map/all_gather | solution.py:423
  106.7 40.5 %collective-permute-done.1.refs_2_ = bf16[4,512,256]{2,1,0:T(8,128)(2,1)} collective-permute-done((bf16[4,512,256]{2,1,0:T(8,128)(2,1)}, bf16[4,512,256]{2,1,0:T(8,128)(2,1)}, u32[]{:S(2)}, u32[]{:S(2)}) %collective-permute-start.1) | collective-permute-done | bytes 1048608 | tf_op jit(solution)/shard_map/ppermute | solution.py:444
  151.7 7.6 all-gather.11.cloned.1.call-done
  159.2 14.5 collective-permute-start.3
  179.2 31.9 %project.1 = (bf16[4096,2048]{1,0:T(8,128)(2,1)}, f32[4096,1]{1,0:T(8,128)S(1)}, f32[4096,8]{1,0:T(8,128)S(1)}, bf16[4096,1024]{1,0:T(8,128)(2,1)}) custom-call(bf16[4096,2048]{1,0:T(8,128)(2,1)} %bitcast.482, f32[1,2048]{1,0:T(1,128)S(1)} %bitcast.379, bf16[2048,8]{1,0:T(8,128)(2,1)S(1)} %copy-done.40, bf16[2048,1024]{1,0:T(8,128)(2,1)} %query_in.1.weight_ref, ...), custom_call_target="tpu_custom_call" | custom-call | flops 17179869184 | bytes 41943040 | tf_op jit(solution)/shard_map/project/pallas_call | solution.py:112
  239.7 29.7 %attend.1 = (bf16[2,4,288,256]{3,2,1,0:T(8,128)(2,1)}, bf16[4,1024,512]{2,1,0:T(8,128)(2,1)}, bf16[4,1024,512]{2,1,0:T(8,128)(2,1)}, f32[4,2,576,1]{3,2,1,0:T(8,128)}) custom-call(bf16[4,1024,1024]{2,1,0:T(8,128)(2,1)} %bitcast.385, s32[4,2,1024]{2,1,0:T(2,128)} %pad_add_fusion.3.target_ref, f32[4,2,1024]{2,1,0:T(2,128)} %copy.417.gate_ref, ...), custom_call_target="tpu_custom_call" | custom-call | flops 7247757312 | bytes 16777216 | tf_op jit(solution)/shard_map/attend/pallas_call | solution.py:194
  272.9 7.5 convolution_convert_fusion
  287.9 21.6 %collective-permute-done.6.refs_1_.refs_2_ = bf16[1056,512]{1,0:T(8,128)(2,1)S(1)} collective-permute-done((bf16[1056,512]{1,0:T(8,128)(2,1)}, bf16[1056,512]{1,0:T(8,128)(2,1)S(1)}, u32[]{:S(2)}, u32[]{:S(2)}) %collective-permute-start.6) | collective-permute-done | bytes 1081376 | tf_op jit(solution)/shard_map/ppermute | solution.py:444
  309.5 44.1 %collective-permute-done.7.refs_2_.refs_4_ = bf16[1056,512]{1,0:T(8,128)(2,1)} collective-permute-done((bf16[1056,512]{1,0:T(8,128)(2,1)}, bf16[1056,512]{1,0:T(8,128)(2,1)}, u32[]{:S(2)}, u32[]{:S(2)}) %collective-permute-start.7) | collective-permute-done | bytes 1081376 | tf_op jit(solution)/shard_map/ppermute | solution.py:444
  360.9 21.1 %all-to-all-start.1 = ((bf16[4,576,256]{2,1,0:T(8,128)(2,1)}), bf16[4,576,256]{2,1,0:T(8,128)(2,1)}, u32[]{:S(2)}, u32[]{:S(2)}) async-start(bf16[4,576,256]{2,1,0:T(8,128)(2,1)} %bitcast.417), calls=%async_computation.2 | async-start | bytes 2359296 | tf_op jit(solution)/shard_map/all_to_all | solution.py:431
  382.5 27.3 %all-to-all-done.1 = bf16[4,576,256]{2,1,0:T(8,128)(2,1)} async-done(((bf16[4,576,256]{2,1,0:T(8,128)(2,1)}), bf16[4,576,256]{2,1,0:T(8,128)(2,1)}, u32[]{:S(2)}, u32[]{:S(2)}) %all-to-all-start.1) | async-done | bytes 1179680 | tf_op jit(solution)/shard_map/all_to_all | solution.py:431
  413.4 46.6 %all-gather.13.cloned.1.call-done = bf16[4,1024,256]{2,1,0:T(8,128)(2,1)} async-done(((bf16[4,256,256]{2,1,0:T(8,128)(2,1)}), bf16[4,1024,256]{2,1,0:T(8,128)(2,1)}) %all-gather.13.cloned.1.call-update) | async-done | bytes 2097168 | tf_op jit(solution)/shard_map/all_gather | solution.py:423
  464.1 24.7 %collective-permute-done.9.refs_3_.refs_1_ = bf16[1056,512]{1,0:T(8,128)(2,1)S(1)} collective-permute-done((bf16[1056,512]{1,0:T(8,128)(2,1)S(1)}, bf16[1056,512]{1,0:T(8,128)(2,1)S(1)}, u32[]{:S(2)}, u32[]{:S(2)}) %collective-permute-start.9) | collective-permute-done | bytes 1081376 | tf_op jit(solution)/shard_map/ppermute | solution.py:444
  489.7 44.2 %collective-permute-done.10.refs_5_.refs_2_ = bf16[1056,512]{1,0:T(8,128)(2,1)S(1)} collective-permute-done((bf16[1056,512]{1,0:T(8,128)(2,1)}, bf16[1056,512]{1,0:T(8,128)(2,1)S(1)}, u32[]{:S(2)}, u32[]{:S(2)}) %collective-permute-start.10) | collective-permute-done | bytes 1081376 | tf_op jit(solution)/shard_map/ppermute | solution.py:444
  536.0 17.6 %all-gather.15.cloned.1.call-done = bf16[4,1024,2048]{2,1,0:T(8,128)(2,1)} async-done(((bf16[4,1024,256]{2,1,0:T(8,128)(2,1)}), bf16[4,1024,2048]{2,1,0:T(8,128)(2,1)}) %all-gather.15.cloned.1.call-update) | async-done | bytes 16777232 | tf_op jit(solution)/shard_map/all_gather | solution.py:427
  566.5 22.5 %dispatch.1 = (bf16[4,288,2048]{2,1,0:T(8,128)(2,1)}, bf16[4,288,2048]{2,1,0:T(8,128)(2,1)}, f32[4,1024,1]{2,1,0:T(8,128)}, f32[4,1024,8]{2,1,0:T(8,128)}) custom-call(bf16[4,1024,2048]{2,1,0:T(8,128)(2,1)} %all-gather.15.cloned.1.call-done, s32[4,2,1024]{2,1,0:T(2,128)} %pad_add_fusion.6.target_ref, f32[1,2048]{1,0:T(1,128)} %bitcast.475, ...), custom_call_target="tpu_custom_call" | custom-call | bytes 16777216 | tf_op jit(solution)/shard_map/dispatch/pallas_call | solution.py:356
  610.2 28.8 %expert_step.2 = (bf16[1152,704]{1,0:T(8,128)(2,1)}, bf16[1152,704]{1,0:T(8,128)(2,1)}, bf16[1152,704]{1,0:T(8,128)(2,1)}, bf16[1152,2048]{1,0:T(8,128)(2,1)}, f32[1152,2]{1,0:T(8,128)}) custom-call(bf16[1152,2048]{1,0:T(8,128)(2,1)} %bitcast.411, bf16[1152,2048]{1,0:T(8,128)(2,1)} %all-gather.17.cloned.1.call-done.grad_ref, f32[1152,1]{1,0:T(8,128)} %reshape.663.weight_ref, ...), custom_call_target="tpu_custom_call" | custom-call | bytes 8650752 | tf_op jit(solution)/shard_map/expert_step/pallas_call | solution.py:406
  640.4 15.0 %collective-permute-done.13.refs_2_ = bf16[1408,512]{1,0:T(8,128)(2,1)} collective-permute-done((bf16[1408,512]{1,0:T(8,128)(2,1)}, bf16[1408,512]{1,0:T(8,128)(2,1)}, u32[]{:S(2)}, u32[]{:S(2)}) %collective-permute-start.13) | collective-permute-done | bytes 1441824 | tf_op jit(solution)/shard_map/ppermute | solution.py:444
  660.8 31.4 %collective-permute-start.15 = (bf16[704,512]{1,0:T(8,128)(2,1)}, bf16[704,512]{1,0:T(8,128)(2,1)S(1)}, u32[]{:S(2)}, u32[]{:S(2)}) collective-permute-start(bf16[704,512]{1,0:T(8,128)(2,1)} %get-tuple-element.185), channel_id=1, source_target_pairs={{0,8},{8,16},{16,24},{24,0},{1,9},{9,17},{17,25},{25,1},{2,10},{10... | collective-permute-start | bytes 2162696 | tf_op jit(solution)/shard_map/ppermute | solution.py:444
  705.0 8.7 convolution_convert_fusion.8
  713.7 8.7 convolution_convert_fusion.7
  732.2 7.4 collective-permute-done.16.refs_2_
  741.3 15.9 %collective-permute-start.18 = (bf16[352,512]{1,0:T(8,128)(2,1)}, bf16[352,512]{1,0:T(8,128)(2,1)S(1)}, u32[]{:S(2)}, u32[]{:S(2)}) collective-permute-start(bf16[352,512]{1,0:T(8,128)(2,1)} %get-tuple-element.201), channel_id=1, source_target_pairs={{0,8},{8,16},{16,24},{24,0},{1,9},{9,17},{17,25},{25,1},{2,10},{10... | collective-permute-start | bytes 1081352 | tf_op jit(solution)/shard_map/ppermute | solution.py:444
  764.2 28.9 %expert_step.3 = (bf16[1152,704]{1,0:T(8,128)(2,1)}, bf16[1152,704]{1,0:T(8,128)(2,1)}, bf16[1152,704]{1,0:T(8,128)(2,1)}, bf16[1152,2048]{1,0:T(8,128)(2,1)}, f32[1152,2]{1,0:T(8,128)}) custom-call(bf16[1152,2048]{1,0:T(8,128)(2,1)} %bitcast.406, bf16[1152,2048]{1,0:T(8,128)(2,1)} %all-gather.19.cloned.1.call-done.grad_ref, f32[1152,1]{1,0:T(8,128)} %reshape.664.weight_ref, ...), custom_call_target="tpu_custom_call" | custom-call | bytes 8650752 | tf_op jit(solution)/shard_map/expert_step/pallas_call | solution.py:406
  814.0 42.1 %reduce-scatter.11.cloned.1.call-done = bf16[1168,256]{1,0:T(8,128)(2,1)} async-done(((bf16[1168,2048]{1,0:T(8,128)(2,1)}), bf16[1168,256]{1,0:T(8,128)(2,1)}) %reduce-scatter.11.cloned.1.call-update) | async-done | bytes 598032 | tf_op jit(solution)/shard_map/reduce_scatter | solution.py:538
  860.1 14.5 all-to-all-start.2
  884.8 18.9 %all-to-all-done.2 = bf16[4,582,256]{2,1,0:T(8,128)(2,1)S(1)} async-done(((bf16[4,582,256]{2,1,0:T(8,128)(2,1)}), bf16[4,582,256]{2,1,0:T(8,128)(2,1)S(1)}, u32[]{:S(2)}, u32[]{:S(2)}) %all-to-all-start.2) | async-done | bytes 1191968 | tf_op jit(solution)/shard_map/all_to_all | solution.py:431
  914.2 7.3 convolution_convert_fusion.1
  928.2 8.1 convolution_convert_fusion.4
  941.5 18.5 %all-gather.21.cloned.1.call-done = bf16[4,1024,256]{2,1,0:T(8,128)(2,1)} async-done(((bf16[4,256,256]{2,1,0:T(8,128)(2,1)}), bf16[4,1024,256]{2,1,0:T(8,128)(2,1)}) %all-gather.21.cloned.1.call-update) | async-done | bytes 2097168 | tf_op jit(solution)/shard_map/all_gather | solution.py:423
  979.1 19.4 %collective-permute-done.24.refs_5_.refs_2_ = bf16[1056,512]{1,0:T(8,128)(2,1)S(1)} collective-permute-done((bf16[1056,512]{1,0:T(8,128)(2,1)}, bf16[1056,512]{1,0:T(8,128)(2,1)S(1)}, u32[]{:S(2)}, u32[]{:S(2)}) %collective-permute-start.24) | collective-permute-done | bytes 1081376 | tf_op jit(solution)/shard_map/ppermute | solution.py:444
  998.5 45.3 %collective-permute-done.25.refs_9_.refs_4_ = bf16[1056,512]{1,0:T(8,128)(2,1)} collective-permute-done((bf16[1056,512]{1,0:T(8,128)(2,1)}, bf16[1056,512]{1,0:T(8,128)(2,1)}, u32[]{:S(2)}, u32[]{:S(2)}) %collective-permute-start.25) | collective-permute-done | bytes 1081376 | tf_op jit(solution)/shard_map/ppermute | solution.py:444
  1043.8 10.0 all-gather.23.cloned.1.call-done
  1056.5 12.7 collective-permute-start.27
  1071.6 17.8 %fusion.67 = f32[4096,512]{1,0:T(8,128)} fusion(bf16[4096,2048]{1,0:T(8,128)(2,1)} %bitcast.483, bf16[512,2048]{1,0:T(8,128)(2,1)} %copy-done.44), kind=kOutput, calls=%fused_computation.370 | convolution fusion | flops 8589934592 | bytes 27262976 | tf_op jit(solution)/shard_map/rd,fd->rf/dot_general | solution.py:20
  1089.4 44.5 %attend_back.1 = (bf16[4,1024,1024]{2,1,0:T(8,128)(2,1)}, f32[4,1024,3]{2,1,0:T(8,128)}) custom-call(bf16[4,1024,1024]{2,1,0:T(8,128)(2,1)} %bitcast.386, s32[4,2,1024]{2,1,0:T(2,128)} %pad_add_fusion.3.target_ref, s32[4,1,1024]{2,1,0:T(1,128)} %reshape.611.kblk_ref, f32[4,2,576,1]{3,2,1,0:T(8,128)} %get-tuple-element.220.lse_ref, ...), custom_call_target="tpu_custom_call" | custom-call | bytes 16777216 | tf_op jit(solution)/shard_map/attend_back/pallas_call | solution.py:277
  1138.7 23.8 %spread.1 = bf16[16,272,2048]{2,1,0:T(8,128)(2,1)} custom-call(bf16[16,256,1024]{2,1,0:T(8,128)(2,1)} %bitcast.392, bf16[2048,1024]{1,0:T(8,128)(2,1)S(1)} %copy-done.1, bf16[16,16,256]{2,1,0:T(8,128)(2,1)S(1)} %bitcast.378), custom_call_target="tpu_custom_call" | custom-call | bytes 17825792 | tf_op jit(solution)/shard_map/spread/pallas_call | solution.py:521
  1175.4 17.0 %collective-permute-done.30.refs_7_.refs_3_ = bf16[1056,512]{1,0:T(8,128)(2,1)S(1)} collective-permute-done((bf16[1056,512]{1,0:T(8,128)(2,1)}, bf16[1056,512]{1,0:T(8,128)(2,1)S(1)}, u32[]{:S(2)}, u32[]{:S(2)}) %collective-permute-start.30) | collective-permute-done | bytes 1081376 | tf_op jit(solution)/shard_map/ppermute | solution.py:444
  1192.4 14.0 convolution_convert_fusion.10
  1207.8 24.3 %convolution_convert_fusion.3 = bf16[2048,1024]{1,0:T(8,128)(2,1)} fusion(bf16[4096,2048]{1,0:T(8,128)(2,1)} %get-tuple-element.234, bf16[4096,1024]{1,0:T(8,128)(2,1)} %bitcast.393), kind=kOutput, calls=%fused_computation.18 | convolution fusion | flops 17181966336 | bytes 29360128 | tf_op jit(solution)/shard_map/rd,rf->df/dot_general | solution.py:20
  1239.2 32.0 %collective-permute-done.31.refs_11_.refs_5_ = bf16[1056,512]{1,0:T(8,128)(2,1)} collective-permute-done((bf16[1056,512]{1,0:T(8,128)(2,1)}, bf16[1056,512]{1,0:T(8,128)(2,1)}, u32[]{:S(2)}, u32[]{:S(2)}) %collective-permute-start.31) | collective-permute-done | bytes 1081376 | tf_op jit(solution)/shard_map/ppermute | solution.py:444
  1272.1 11.2 reduce-scatter.15.cloned.1.call-done
  1298.8 12.7 collective-permute-start.40
  1313.7 8.6 whole_grad.3
  1322.4 7.0 whole_grad.4
  1331.3 30.5 %reduce-scatter.17.cloned.1.call-done = bf16[4,272,256]{2,1,0:T(8,128)(2,1)} async-done(((bf16[4,1088,256]{2,1,0:T(8,128)(2,1)}), bf16[4,272,256]{2,1,0:T(8,128)(2,1)}) %reduce-scatter.17.cloned.1.call-update) | async-done | bytes 557072 | tf_op jit(solution)/shard_map/reduce_scatter | solution.py:959
  1400.0 57.2 %collective-permute-done.35.refs_5_ = bf16[272,1024]{1,0:T(8,128)(2,1)S(1)} collective-permute-done((bf16[272,1024]{1,0:T(8,128)(2,1)S(1)}, bf16[272,1024]{1,0:T(8,128)(2,1)S(1)}, u32[]{:S(2)}, u32[]{:S(2)}) %collective-permute-start.35) | collective-permute-done | bytes 557088 | tf_op jit(solution)/shard_map/ppermute | solution.py:444
  1457.3 9.2 all_gather.35
  (619 shorter events, 385.6 us)
Async XLA Ops:
  7.2 56.8 %all-gather.9.cloned.1.call-start = ((), (), s32[]{:S(2)}) async-start(), calls=%async_computation.10 | async-start | bytes 2785280 | tf_op jit(solution)/shard_map/all_gather | solution.py:423
  12.8 146.4 %all-gather.11.cloned.1.call-start = ((), (), s32[]{:S(2)}) async-start(), calls=%async_computation.11 | async-start | bytes 18874368 | tf_op jit(solution)/shard_map/all_gather | solution.py:427
  75.1 72.1 %collective-permute-start.1 = (bf16[4,512,256]{2,1,0:T(8,128)(2,1)}, bf16[4,512,256]{2,1,0:T(8,128)(2,1)}, u32[]{:S(2)}, u32[]{:S(2)}) collective-permute-start(bf16[4,512,256]{2,1,0:T(8,128)(2,1)} %get-tuple-element.134), channel_id=1, source_target_pairs={{0,16},{8,24},{16,0},{24,8},{1,17},{9,25},{17,1},{25,9},{2,18},{10... | collective-permute-start | bytes 3145736 | tf_op jit(solution)/shard_map/ppermute | solution.py:444
  76.5 70.7 %collective-permute-start.2 = (bf16[4,512,256]{2,1,0:T(8,128)(2,1)}, bf16[4,512,256]{2,1,0:T(8,128)(2,1)}, u32[]{:S(2)}, u32[]{:S(2)}) collective-permute-start(bf16[4,512,256]{2,1,0:T(8,128)(2,1)} %get-tuple-element.135), channel_id=1, source_target_pairs={{0,24},{8,0},{16,8},{24,16},{1,25},{9,1},{17,9},{25,17},{2,26},{10... | collective-permute-start | bytes 3145736 | tf_op jit(solution)/shard_map/ppermute | solution.py:444
  159.2 70.1 %collective-permute-start.3 = (bf16[2,256,512]{2,1,0:T(8,128)(2,1)}, bf16[2,256,512]{2,1,0:T(8,128)(2,1)}, u32[]{:S(2)}, u32[]{:S(2)}) collective-permute-start(bf16[2,256,512]{2,1,0:T(8,128)(2,1)} %get-tuple-element.137), channel_id=1, source_target_pairs={{0,8},{8,16},{16,24},{24,0},{1,9},{9,17},{17,25},{25,1},{2,10},{10... | collective-permute-start | bytes 1572872 | tf_op jit(solution)/shard_map/ppermute | solution.py:444
  173.7 55.6 %collective-permute-start.4 = (bf16[2,256,512]{2,1,0:T(8,128)(2,1)}, bf16[2,256,512]{2,1,0:T(8,128)(2,1)}, u32[]{:S(2)}, u32[]{:S(2)}) collective-permute-start(bf16[2,256,512]{2,1,0:T(8,128)(2,1)} %get-tuple-element.138), channel_id=1, source_target_pairs={{0,16},{8,24},{16,0},{24,8},{1,17},{9,25},{17,1},{25,9},{2,18},{10... | collective-permute-start | bytes 1572872 | tf_op jit(solution)/shard_map/ppermute | solution.py:444
  174.9 54.4 %collective-permute-start.5 = (bf16[2,256,512]{2,1,0:T(8,128)(2,1)}, bf16[2,256,512]{2,1,0:T(8,128)(2,1)}, u32[]{:S(2)}, u32[]{:S(2)}) collective-permute-start(bf16[2,256,512]{2,1,0:T(8,128)(2,1)} %get-tuple-element.139), channel_id=1, source_target_pairs={{0,24},{8,0},{16,8},{24,16},{1,25},{9,1},{17,9},{25,17},{2,26},{10... | collective-permute-start | bytes 1572872 | tf_op jit(solution)/shard_map/ppermute | solution.py:444
  229.3 51.1 %all-to-all-start = ((bf16[4,2,4,72,256]{4,3,2,1,0:T(8,128)(2,1)}), bf16[4,2,4,72,256]{4,3,2,1,0:T(8,128)(2,1)}, u32[]{:S(2)}, u32[]{:S(2)}) async-start(bf16[4,2,4,72,256]{4,3,2,1,0:T(8,128)(2,1)} %bitcast.415), calls=%async_computation | async-start | bytes 2359296 | tf_op jit(solution)/shard_map/all_to_all | solution.py:431
  233.6 124.8 %reduce-scatter.7.cloned.1.call-start = ((), (), s32[]{:S(2)}) async-start(), calls=%async_computation.12 | async-start | bytes 10616832 | tf_op jit(solution)/shard_map/reduce_scatter | solution.py:538
  282.5 71.0 %collective-permute-start.7 = (bf16[1056,512]{1,0:T(8,128)(2,1)}, bf16[1056,512]{1,0:T(8,128)(2,1)}, u32[]{:S(2)}, u32[]{:S(2)}) collective-permute-start(bf16[1056,512]{1,0:T(8,128)(2,1)} %get-tuple-element.151), channel_id=1, source_target_pairs={{0,16},{8,24},{16,0},{24,8},{1,17},{9,25},{17,1},{25,9},{2,18},{10... | collective-permute-start | bytes 3244040 | tf_op jit(solution)/shard_map/ppermute | solution.py:444
  284.9 68.7 %collective-permute-start.8 = (bf16[1056,512]{1,0:T(8,128)(2,1)}, bf16[1056,512]{1,0:T(8,128)(2,1)}, u32[]{:S(2)}, u32[]{:S(2)}) collective-permute-start(bf16[1056,512]{1,0:T(8,128)(2,1)} %get-tuple-element.152), channel_id=1, source_target_pairs={{0,24},{8,0},{16,8},{24,16},{1,25},{9,1},{17,9},{25,17},{2,26},{10... | collective-permute-start | bytes 3244040 | tf_op jit(solution)/shard_map/ppermute | solution.py:444
  382.0 78.0 %all-gather.13.cloned.1.call-start = ((), (), s32[]{:S(2)}) async-start(), calls=%async_computation.13 | async-start | bytes 2621440 | tf_op jit(solution)/shard_map/all_gather | solution.py:423
  413.4 140.2 %all-gather.15.cloned.1.call-start = ((), (), s32[]{:S(2)}) async-start(), calls=%async_computation.14 | async-start | bytes 18874368 | tf_op jit(solution)/shard_map/all_gather | solution.py:427
  460.0 150.2 %all-gather.17.cloned.1.call-start = ((), (), s32[]{:S(2)}) async-start(), calls=%async_computation.15 | async-start | bytes 5308416 | tf_op jit(solution)/shard_map/all_gather | solution.py:763
  460.1 73.9 %collective-permute-start.10 = (bf16[1056,512]{1,0:T(8,128)(2,1)}, bf16[1056,512]{1,0:T(8,128)(2,1)S(1)}, u32[]{:S(2)}, u32[]{:S(2)}) collective-permute-start(bf16[1056,512]{1,0:T(8,128)(2,1)} %get-tuple-element.155), channel_id=1, source_target_pairs={{0,16},{8,24},{16,0},{24,8},{1,17},{9,25},{17,1},{25,9},{2,18},{10... | collective-permute-start | bytes 3244040 | tf_op jit(solution)/shard_map/ppermute | solution.py:444
  461.8 73.1 %collective-permute-start.11 = (bf16[1056,512]{1,0:T(8,128)(2,1)}, bf16[1056,512]{1,0:T(8,128)(2,1)S(1)}, u32[]{:S(2)}, u32[]{:S(2)}) collective-permute-start(bf16[1056,512]{1,0:T(8,128)(2,1)} %get-tuple-element.156), channel_id=1, source_target_pairs={{0,24},{8,0},{16,8},{24,16},{1,25},{9,1},{17,9},{25,17},{2,26},{10... | collective-permute-start | bytes 3244040 | tf_op jit(solution)/shard_map/ppermute | solution.py:444
  555.8 208.4 %all-gather.19.cloned.1.call-start = ((), (), s32[]{:S(2)}) async-start(), calls=%async_computation.16 | async-start | bytes 5308416 | tf_op jit(solution)/shard_map/all_gather | solution.py:763
  556.7 254.4 %reduce-scatter.9.cloned.1.call-start = ((), (), s32[]{:S(2)}) async-start(), calls=%async_computation.17 | async-start | bytes 5382144 | tf_op jit(solution)/shard_map/reduce_scatter | solution.py:538
  556.8 83.6 %collective-permute-start.12 = (bf16[1408,512]{1,0:T(8,128)(2,1)}, bf16[1408,512]{1,0:T(8,128)(2,1)}, u32[]{:S(2)}, u32[]{:S(2)}) collective-permute-start(bf16[1408,512]{1,0:T(8,128)(2,1)} %get-tuple-element.180), channel_id=1, source_target_pairs={{0,8},{8,16},{16,24},{24,0},{1,9},{9,17},{17,25},{25,1},{2,10},{10... | collective-permute-start | bytes 4325384 | tf_op jit(solution)/shard_map/ppermute | solution.py:444
  561.3 94.1 %collective-permute-start.13 = (bf16[1408,512]{1,0:T(8,128)(2,1)}, bf16[1408,512]{1,0:T(8,128)(2,1)}, u32[]{:S(2)}, u32[]{:S(2)}) collective-permute-start(bf16[1408,512]{1,0:T(8,128)(2,1)} %get-tuple-element.181), channel_id=1, source_target_pairs={{0,16},{8,24},{16,0},{24,8},{1,17},{9,25},{17,1},{25,9},{2,18},{10... | collective-permute-start | bytes 4325384 | tf_op jit(solution)/shard_map/ppermute | solution.py:444
  563.0 92.4 %collective-permute-start.14 = (bf16[1408,512]{1,0:T(8,128)(2,1)}, bf16[1408,512]{1,0:T(8,128)(2,1)}, u32[]{:S(2)}, u32[]{:S(2)}) collective-permute-start(bf16[1408,512]{1,0:T(8,128)(2,1)} %get-tuple-element.182), channel_id=1, source_target_pairs={{0,24},{8,0},{16,8},{24,16},{1,25},{9,1},{17,9},{25,17},{2,26},{10... | collective-permute-start | bytes 4325384 | tf_op jit(solution)/shard_map/ppermute | solution.py:444
  660.7 195.4 %reduce-scatter.11.cloned.1.call-start = ((), (), s32[]{:S(2)}) async-start(), calls=%async_computation.18 | async-start | bytes 5382144 | tf_op jit(solution)/shard_map/reduce_scatter | solution.py:538
  660.8 71.4 %collective-permute-start.15 = (bf16[704,512]{1,0:T(8,128)(2,1)}, bf16[704,512]{1,0:T(8,128)(2,1)S(1)}, u32[]{:S(2)}, u32[]{:S(2)}) collective-permute-start(bf16[704,512]{1,0:T(8,128)(2,1)} %get-tuple-element.185), channel_id=1, source_target_pairs={{0,8},{8,16},{16,24},{24,0},{1,9},{9,17},{17,25},{25,1},{2,10},{10... | collective-permute-start | bytes 2162696 | tf_op jit(solution)/shard_map/ppermute | solution.py:444
  741.3 53.3 %collective-permute-start.18 = (bf16[352,512]{1,0:T(8,128)(2,1)}, bf16[352,512]{1,0:T(8,128)(2,1)S(1)}, u32[]{:S(2)}, u32[]{:S(2)}) collective-permute-start(bf16[352,512]{1,0:T(8,128)(2,1)} %get-tuple-element.201), channel_id=1, source_target_pairs={{0,8},{8,16},{16,24},{24,0},{1,9},{9,17},{17,25},{25,1},{2,10},{10... | collective-permute-start | bytes 1081352 | tf_op jit(solution)/shard_map/ppermute | solution.py:444
  805.9 52.5 %collective-permute-start.21 = (bf16[704,512]{1,0:T(8,128)(2,1)}, bf16[704,512]{1,0:T(8,128)(2,1)S(1)}, u32[]{:S(2)}, u32[]{:S(2)}) collective-permute-start(bf16[704,512]{1,0:T(8,128)(2,1)} %pad_maximum_fusion.42), channel_id=1, source_target_pairs={{0,8},{8,16},{16,24},{24,0},{1,9},{9,17},{17,25},{25,1},{2,10},{10... | collective-permute-start | bytes 2162696 | tf_op jit(solution)/shard_map/ppermute | solution.py:444
  807.9 50.5 %collective-permute-start.22 = (bf16[704,512]{1,0:T(8,128)(2,1)}, bf16[704,512]{1,0:T(8,128)(2,1)S(1)}, u32[]{:S(2)}, u32[]{:S(2)}) collective-permute-start(bf16[704,512]{1,0:T(8,128)(2,1)} %pad_maximum_fusion.43), channel_id=1, source_target_pairs={{0,16},{8,24},{16,0},{24,8},{1,17},{9,25},{17,1},{25,9},{2,18},{10... | collective-permute-start | bytes 2162696 | tf_op jit(solution)/shard_map/ppermute | solution.py:444
  808.3 50.2 %collective-permute-start.23 = (bf16[704,512]{1,0:T(8,128)(2,1)}, bf16[704,512]{1,0:T(8,128)(2,1)S(1)}, u32[]{:S(2)}, u32[]{:S(2)}) collective-permute-start(bf16[704,512]{1,0:T(8,128)(2,1)} %pad_maximum_fusion.44), channel_id=1, source_target_pairs={{0,24},{8,0},{16,8},{24,16},{1,25},{9,1},{17,9},{25,17},{2,26},{10... | collective-permute-start | bytes 2162696 | tf_op jit(solution)/shard_map/ppermute | solution.py:444
  874.6 85.4 %all-gather.21.cloned.1.call-start = ((), (), s32[]{:S(2)}) async-start(), calls=%async_computation.19 | async-start | bytes 2621440 | tf_op jit(solution)/shard_map/all_gather | solution.py:423
  914.2 139.6 %all-gather.23.cloned.1.call-start = ((), (), s32[]{:S(2)}) async-start(), calls=%async_computation.20 | async-start | bytes 18874368 | tf_op jit(solution)/shard_map/all_gather | solution.py:427
  960.1 202.5 %reduce-scatter.13.cloned.1.call-start = ((), (), s32[]{:S(2)}) async-start(), calls=%async_computation.21 | async-start | bytes 10616832 | tf_op jit(solution)/shard_map/reduce_scatter | solution.py:538
  969.6 74.2 %collective-permute-start.25 = (bf16[1056,512]{1,0:T(8,128)(2,1)}, bf16[1056,512]{1,0:T(8,128)(2,1)}, u32[]{:S(2)}, u32[]{:S(2)}) collective-permute-start(bf16[1056,512]{1,0:T(8,128)(2,1)} %pad_maximum_fusion.31), channel_id=1, source_target_pairs={{0,16},{8,24},{16,0},{24,8},{1,17},{9,25},{17,1},{25,9},{2,18},{10... | collective-permute-start | bytes 3244040 | tf_op jit(solution)/shard_map/ppermute | solution.py:444
  971.3 72.5 %collective-permute-start.26 = (bf16[1056,512]{1,0:T(8,128)(2,1)}, bf16[1056,512]{1,0:T(8,128)(2,1)}, u32[]{:S(2)}, u32[]{:S(2)}) collective-permute-start(bf16[1056,512]{1,0:T(8,128)(2,1)} %pad_maximum_fusion.32), channel_id=1, source_target_pairs={{0,24},{8,0},{16,8},{24,16},{1,25},{9,1},{17,9},{25,17},{2,26},{10... | collective-permute-start | bytes 3244040 | tf_op jit(solution)/shard_map/ppermute | solution.py:444
  1053.8 229.4 %reduce-scatter.15.cloned.1.call-start = ((), (), s32[]{:S(2)}) async-start(), calls=%async_computation.22 | async-start | bytes 20054016 | tf_op jit(solution)/shard_map/reduce_scatter | solution.py:954
  1056.5 106.0 %collective-permute-start.27 = (bf16[1056,512]{1,0:T(8,128)(2,1)}, bf16[1056,512]{1,0:T(8,128)(2,1)S(1)}, u32[]{:S(2)}, u32[]{:S(2)}) collective-permute-start(bf16[1056,512]{1,0:T(8,128)(2,1)} %pad_maximum_fusion.34), channel_id=1, source_target_pairs={{0,8},{8,16},{16,24},{24,0},{1,9},{9,17},{17,25},{25,1},{2,10},{10... | collective-permute-start | bytes 3244040 | tf_op jit(solution)/shard_map/ppermute | solution.py:444
  1069.2 93.3 %collective-permute-start.28 = (bf16[1056,512]{1,0:T(8,128)(2,1)}, bf16[1056,512]{1,0:T(8,128)(2,1)}, u32[]{:S(2)}, u32[]{:S(2)}) collective-permute-start(bf16[1056,512]{1,0:T(8,128)(2,1)} %pad_maximum_fusion.35), channel_id=1, source_target_pairs={{0,16},{8,24},{16,0},{24,8},{1,17},{9,25},{17,1},{25,9},{2,18},{10... | collective-permute-start | bytes 3244040 | tf_op jit(solution)/shard_map/ppermute | solution.py:444
  1070.3 92.2 %collective-permute-start.29 = (bf16[1056,512]{1,0:T(8,128)(2,1)}, bf16[1056,512]{1,0:T(8,128)(2,1)}, u32[]{:S(2)}, u32[]{:S(2)}) collective-permute-start(bf16[1056,512]{1,0:T(8,128)(2,1)} %pad_maximum_fusion.36), channel_id=1, source_target_pairs={{0,24},{8,0},{16,8},{24,16},{1,25},{9,1},{17,9},{25,17},{2,26},{10... | collective-permute-start | bytes 3244040 | tf_op jit(solution)/shard_map/ppermute | solution.py:444
  1165.9 70.9 %all-to-all-start.3 = ((bf16[4,576,256]{2,1,0:T(8,128)(2,1)}), bf16[4,576,256]{2,1,0:T(8,128)(2,1)}, u32[]{:S(2)}, u32[]{:S(2)}) async-start(bf16[4,576,256]{2,1,0:T(8,128)(2,1)} %bitcast.416), calls=%async_computation.7 | async-start | bytes 2359296 | tf_op jit(solution)/shard_map/all_to_all | solution.py:431
  1171.0 190.7 %reduce-scatter.17.cloned.1.call-start = ((), (), s32[]{:S(2)}) async-start(), calls=%async_computation.23 | async-start | bytes 2785280 | tf_op jit(solution)/shard_map/reduce_scatter | solution.py:959
  1171.0 100.2 %collective-permute-start.31 = (bf16[1056,512]{1,0:T(8,128)(2,1)}, bf16[1056,512]{1,0:T(8,128)(2,1)}, u32[]{:S(2)}, u32[]{:S(2)}) collective-permute-start(bf16[1056,512]{1,0:T(8,128)(2,1)} %pad_maximum_fusion.39), channel_id=1, source_target_pairs={{0,16},{8,24},{16,0},{24,8},{1,17},{9,25},{17,1},{25,9},{2,18},{10... | collective-permute-start | bytes 3244040 | tf_op jit(solution)/shard_map/ppermute | solution.py:444
  1174.0 97.3 %collective-permute-start.32 = (bf16[1056,512]{1,0:T(8,128)(2,1)}, bf16[1056,512]{1,0:T(8,128)(2,1)}, u32[]{:S(2)}, u32[]{:S(2)}) collective-permute-start(bf16[1056,512]{1,0:T(8,128)(2,1)} %pad_maximum_fusion.40), channel_id=1, source_target_pairs={{0,24},{8,0},{16,8},{24,16},{1,25},{9,1},{17,9},{25,17},{2,26},{10... | collective-permute-start | bytes 3244040 | tf_op jit(solution)/shard_map/ppermute | solution.py:444
  1207.8 63.5 %collective-permute-start.33 = (bf16[512,512]{1,0:T(8,128)(2,1)}, bf16[512,512]{1,0:T(8,128)(2,1)S(1)}, u32[]{:S(2)}, u32[]{:S(2)}) collective-permute-start(bf16[512,512]{1,0:T(8,128)(2,1)} %get-tuple-element.238), channel_id=1, source_target_pairs={{0,8},{8,16},{16,24},{24,0},{1,9},{9,17},{17,25},{25,1},{2,10},{10... | collective-permute-start | bytes 1572872 | tf_op jit(solution)/shard_map/ppermute | solution.py:444
  1298.8 88.7 %collective-permute-start.40 = (bf16[512,512]{1,0:T(8,128)(2,1)}, bf16[512,512]{1,0:T(8,128)(2,1)S(1)}, u32[]{:S(2)}, u32[]{:S(2)}) collective-permute-start(bf16[512,512]{1,0:T(8,128)(2,1)} %get-tuple-element.247), channel_id=1, source_target_pairs={{0,16},{8,24},{16,0},{24,8},{1,17},{9,25},{17,1},{25,9},{2,18},{10... | collective-permute-start | bytes 1572872 | tf_op jit(solution)/shard_map/ppermute | solution.py:444
  1311.5 76.0 %collective-permute-start.41 = (bf16[512,512]{1,0:T(8,128)(2,1)}, bf16[512,512]{1,0:T(8,128)(2,1)}, u32[]{:S(2)}, u32[]{:S(2)}) collective-permute-start(bf16[512,512]{1,0:T(8,128)(2,1)} %get-tuple-element.248), channel_id=1, source_target_pairs={{0,24},{8,0},{16,8},{24,16},{1,25},{9,1},{17,9},{25,17},{2,26},{10... | collective-permute-start | bytes 1572872 | tf_op jit(solution)/shard_map/ppermute | solution.py:444
  1379.5 77.7 %collective-permute-start.35 = (bf16[272,1024]{1,0:T(8,128)(2,1)S(1)}, bf16[272,1024]{1,0:T(8,128)(2,1)S(1)}, u32[]{:S(2)}, u32[]{:S(2)}) collective-permute-start(bf16[272,1024]{1,0:T(8,128)(2,1)S(1)} %get-tuple-element.391), channel_id=1, source_target_pairs={{0,16},{8,24},{16,0},{24,8},{1,17},{9,25},{17,1},{25,9},{2,18},{10... | collective-permute-start | bytes 1671176 | tf_op jit(solution)/shard_map/ppermute | solution.py:444
  1385.5 71.7 %collective-permute-start.34 = (bf16[272,1024]{1,0:T(8,128)(2,1)S(1)}, bf16[272,1024]{1,0:T(8,128)(2,1)S(1)}, u32[]{:S(2)}, u32[]{:S(2)}) collective-permute-start(bf16[272,1024]{1,0:T(8,128)(2,1)S(1)} %get-tuple-element.393), channel_id=1, source_target_pairs={{0,8},{8,16},{16,24},{24,0},{1,9},{9,17},{17,25},{25,1},{2,10},{10... | collective-permute-start | bytes 1671176 | tf_op jit(solution)/shard_map/ppermute | solution.py:444
  1393.0 74.8 %collective-permute-start.37 = (bf16[256,1024]{1,0:T(8,128)(2,1)}, bf16[256,1024]{1,0:T(8,128)(2,1)S(1)}, u32[]{:S(2)}, u32[]{:S(2)}) collective-permute-start(bf16[256,1024]{1,0:T(8,128)(2,1)} %get-tuple-element.241), channel_id=1, source_target_pairs={{0,8},{8,16},{16,24},{24,0},{1,9},{9,17},{17,25},{25,1},{2,10},{10... | collective-permute-start | bytes 1572872 | tf_op jit(solution)/shard_map/ppermute | solution.py:444
  1393.0 75.5 %collective-permute-start.38 = (bf16[256,1024]{1,0:T(8,128)(2,1)}, bf16[256,1024]{1,0:T(8,128)(2,1)}, u32[]{:S(2)}, u32[]{:S(2)}) collective-permute-start(bf16[256,1024]{1,0:T(8,128)(2,1)} %get-tuple-element.242), channel_id=1, source_target_pairs={{0,16},{8,24},{16,0},{24,8},{1,17},{9,25},{17,1},{25,9},{2,18},{10... | collective-permute-start | bytes 1572872 | tf_op jit(solution)/shard_map/ppermute | solution.py:444
  1396.3 72.2 %collective-permute-start.39 = (bf16[256,1024]{1,0:T(8,128)(2,1)}, bf16[256,1024]{1,0:T(8,128)(2,1)}, u32[]{:S(2)}, u32[]{:S(2)}) collective-permute-start(bf16[256,1024]{1,0:T(8,128)(2,1)} %get-tuple-element.243), channel_id=1, source_target_pairs={{0,24},{8,0},{16,8},{24,16},{1,25},{9,1},{17,9},{25,17},{2,26},{10... | collective-permute-start | bytes 1572872 | tf_op jit(solution)/shard_map/ppermute | solution.py:444
  (139 other events, 1475.8 us)
Sparse Core Ops, SparseCore 0:
  12.9 50.9 all-gather.8
  67.2 91.9 all-gather.10
  280.6 77.8 reduce-scatter.6
  413.5 46.4 all-gather.12
  461.7 91.8 all-gather.14
  555.9 42.8 all-gather.16
  600.7 39.7 all-gather.18
  660.8 86.2 reduce-scatter.8
  800.2 55.8 reduce-scatter.10
  914.3 45.7 all-gather.20
  961.9 91.8 all-gather.22
  1057.7 83.4 reduce-scatter.12
  1163.6 119.5 reduce-scatter.14
  1285.4 76.2 reduce-scatter.16

commit v5 on v4

--- a/solution.py
+++ b/solution.py
@@ -83,14 +83,19 @@
 
 
 def project_kernel(
-    rotated, x_ref, gain_ref, router_ref, weight_ref, cos_ref, sin_ref,
-    hidden_ref, inverse_ref, logits_ref, out_ref,
+    rotated, x_ref, chosen_ref, gain_ref, router_ref, weight_ref, cos_ref, sin_ref,
+    hidden_ref, inverse_ref, logits_ref, gates_ref, out_ref,
 ):
     normed, inverse = normalize_rows(x_ref[...].astype(F32))
     hidden = (normed * gain_ref[...]).astype(BF16)
     hidden_ref[...] = hidden
     inverse_ref[...] = inverse
-    logits_ref[...] = jnp.dot(hidden, router_ref[...], preferred_element_type=F32)
+    logits = jnp.dot(hidden, router_ref[...], preferred_element_type=F32)
+    logits_ref[...] = logits
+    chosen = chosen_ref[...] > 0.0
+    top = jnp.max(jnp.where(chosen, logits, MASKED_SCORE), axis=-1, keepdims=True)
+    exps = jnp.where(chosen, jnp.exp(jnp.where(chosen, logits - top, 0.0)), 0.0)
+    gates_ref[...] = exps / jnp.sum(exps, axis=-1, keepdims=True)
     made = jnp.dot(hidden, weight_ref[...], preferred_element_type=F32)
     cosine, sine = cos_ref[...], sin_ref[...]
     for at, turn in enumerate(rotated):
@@ -101,7 +106,7 @@
         out_ref[:, columns] = one.astype(BF16)
 
 
-def project(x, gain, router, weight, cosine, sine, rotated):
+def project(x, chosen, gain, router, weight, cosine, sine, rotated):
     count, width = x.shape
     experts, cols = router.shape[1], weight.shape[1]
     length = cosine.shape[0]
@@ -112,12 +117,13 @@
     return pl.pallas_call(
         partial(project_kernel, rotated),
         grid=(count // tile,),
-        in_specs=[row(width), pl.BlockSpec((1, width), lambda i: (0, 0)), whole(router),
-                  whole(weight), table, table],
-        out_specs=[row(width), row(1), row(experts), row(cols)],
+        in_specs=[row(width), row(experts), pl.BlockSpec((1, width), lambda i: (0, 0)),
+                  whole(router), whole(weight), table, table],
+        out_specs=[row(width), row(1), row(experts), row(experts), row(cols)],
         out_shape=[
             jax.ShapeDtypeStruct((count, width), BF16),
             jax.ShapeDtypeStruct((count, 1), F32),
+            jax.ShapeDtypeStruct((count, experts), F32),
             jax.ShapeDtypeStruct((count, experts), F32),
             jax.ShapeDtypeStruct((count, cols), BF16),
         ],
@@ -128,7 +134,7 @@
             transcendentals=count,
         ),
         name="project",
-    )(x, gain.reshape(1, width), router, weight, cosine, sine)
+    )(x, chosen, gain.reshape(1, width), router, weight, cosine, sine)
 
 
 def scores_of(q, k, qblk, kblk):
@@ -704,20 +710,18 @@
     in_all = gather_cols(in_rows).reshape(count, width)
     grad_sent = jnp.einsum("sct,stf->scf", home_f, grad_out)
     grad_sent = grad_sent.reshape(seqs, ranks, local, capacity, share).transpose(1, 2, 0, 3, 4)
-    in_all = tie(
-        in_all, target_a, target_f, home_a, home_f, grad_sent
-    )
+    chosen_a = jnp.any(routes_a[..., None] == jnp.arange(experts, dtype=jnp.int32), axis=0)
+    chosen_a = chosen_a.astype(F32).reshape(count, experts)
+    in_all = tie(in_all, target_a, target_f, home_a, home_f, grad_sent, chosen_a)
     rotated = ([True] * (local + 1) + [False]) * heads
-    hidden_a, inverse_a, logits_a, qkv = project(
-        in_all, gain_attn, router_attn, query_w, cosine, sine, rotated
+    hidden_a, inverse_a, logits_a, gates_a, qkv = project(
+        in_all, chosen_a, gain_attn, router_attn, query_w, cosine, sine, rotated
     )
     qkv = qkv.reshape(seqs, seq_len, -1)
     out_got = exchange_pieces(out_parts, in_all)
     qkv = tie(qkv, *out_got)
     grad_rows = exchange(tie(grad_sent, qkv))
-    gates_a = gate_table(
-        logits_a.reshape(seqs, seq_len, experts), routes_a
-    )
+    gates_a = gates_a.reshape(seqs, seq_len, experts)
     my_gates_a = my_gates(gates_a)
     kblk = block_ids.reshape(seqs, 1, seq_len)
     rows_each = ranks * capacity

time: 1500 us -> 1510 us (level)
  starting transfers between devices: 199 us -> 229 us
  local copies, waits for them, and re-layouts: 112 us -> 138 us
  waiting for transfers between devices: 635 us -> 609 us
    ppermute x42, starting transfers between devices: 153 us -> 180 us  [exchange_pieces(): got.append(lax.ppermute(tie(pieces[m], *after), 'row', steps))]
    reduce_scatter x1, waiting for transfers between devices: 30.5 us -> 10.1 us  [per_device(): own = lax.psum_scatter(part, 'row', scatter_dimension=1, tiled=True)]
    unnamed x263 -> x270, local copies, waits for them, and re-layouts: 38.5 us -> 51.8 us
where the time goes in v5:
time: 1510 us; the launch traced here: 1490 us
  waiting for transfers between devices  609 us (40%)
  Pallas kernels  269 us (18%)
  starting transfers between devices  229 us (15%)
  local copies, waits for them, and re-layouts  138 us (9%)
  matrix products  126 us (8%)
  other arithmetic  98.1 us (6%)
  between operations  16 us (1%)
    ppermute x42, waiting for transfers between devices, exchange_pieces(): got.append(lax.ppermute(tie(pieces[m], *after), 'row', steps))  371 us
    ppermute x42, starting transfers between devices, exchange_pieces(): got.append(lax.ppermute(tie(pieces[m], *after), 'row', steps))  180 us
    dot_general x17, matrix products, dot_f32(): return jnp.einsum(spec, left, right, preferred_element_type=F32)  111 us
    all_gather x3, waiting for transfers between devices, gather_rows(): return lax.all_gather(own, 'row', axis=1, tiled=True)  92.1 us
    pallas_call x13, Pallas kernels, assemble(): pl.pallas_call(kernel, grid_spec=pltpu.PrefetchScalarGridSpec(num_scalar_...  59.5 us
    pallas_call x2, Pallas kernels, expert_step(): pl.pallas_call(expert_kernel, grid=(count // tile,), in_specs=[row(width)...  57.9 us
    unnamed x270, local copies, waits for them, and re-layouts  51.8 us
    reduce_scatter x4, waiting for transfers between devices, sum_cols(): return lax.psum_scatter(rows, 'col', scatter_dimension=1, tiled=True)  49.6 us
  transfers between devices with their start and end apart: 60, of which 27 were waited for; matrix products, arithmetic and copies ran while one was open for 20% of the time, Pallas kernels for 18%

profile of v5, /device:TPU:0, one launch (start us, length us, event | category | flops | bytes accessed | tf_op | source)
XLA Modules:
  0.0 1494.7 jit_solution(16914695362793895965)
XLA Ops:
  36.9 27.0 %all-gather.9.cloned.1.call-done = bf16[4,1088,256]{2,1,0:T(8,128)(2,1)} async-done(((bf16[4,272,256]{2,1,0:T(8,128)(2,1)}), bf16[4,1088,256]{2,1,0:T(8,128)(2,1)}) %all-gather.9.cloned.1.call-update) | async-done | bytes 2228240 | tf_op jit(solution)/shard_map/all_gather | solution.py:429
  118.4 40.4 %collective-permute-done.1.refs_2_ = bf16[4,512,256]{2,1,0:T(8,128)(2,1)} collective-permute-done((bf16[4,512,256]{2,1,0:T(8,128)(2,1)}, bf16[4,512,256]{2,1,0:T(8,128)(2,1)}, u32[]{:S(2)}, u32[]{:S(2)}) %collective-permute-start.1) | collective-permute-done | bytes 1048608 | tf_op jit(solution)/shard_map/ppermute | solution.py:450
  164.8 22.1 %collective-permute-start.3 = (bf16[2,256,512]{2,1,0:T(8,128)(2,1)}, bf16[2,256,512]{2,1,0:T(8,128)(2,1)S(1)}, u32[]{:S(2)}, u32[]{:S(2)}) collective-permute-start(bf16[2,256,512]{2,1,0:T(8,128)(2,1)} %get-tuple-element.138), channel_id=1, source_target_pairs={{0,8},{8,16},{16,24},{24,0},{1,9},{9,17},{17,25},{25,1},{2,10},{10... | collective-permute-start | bytes 1572872 | tf_op jit(solution)/shard_map/ppermute | solution.py:450
  192.5 32.0 %project.1 = (bf16[4096,2048]{1,0:T(8,128)(2,1)}, f32[4096,1]{1,0:T(8,128)S(1)}, f32[4096,8]{1,0:T(8,128)S(1)}, f32[4096,8]{1,0:T(8,128)}, bf16[4096,1024]{1,0:T(8,128)(2,1)}) custom-call(bf16[4096,2048]{1,0:T(8,128)(2,1)} %bitcast.483, f32[4096,8]{1,0:T(8,128)} %bitcast.430, f32[1,2048]{1,0:T(1,128)S(1)} %bitcast.375, bf16[2048,8]{1,0:T(8,128)(2,1)S(1)} %copy-done.43, ...), custom_call_target="tpu_custom_call" | custom-call | flops 17179869184 | bytes 41943040 | tf_op jit(solution)/shard_map/project/pallas_call | solution.py:117
  228.4 9.0 all-to-all-start
  250.3 29.8 %attend.1 = (bf16[2,4,288,256]{3,2,1,0:T(8,128)(2,1)}, bf16[4,1024,512]{2,1,0:T(8,128)(2,1)}, bf16[4,1024,512]{2,1,0:T(8,128)(2,1)}, f32[4,2,576,1]{3,2,1,0:T(8,128)}) custom-call(bf16[4,1024,1024]{2,1,0:T(8,128)(2,1)} %bitcast.383, s32[4,2,1024]{2,1,0:T(2,128)} %pad_add_fusion.3.target_ref, f32[4,2,1024]{2,1,0:T(2,128)} %copy.343.gate_ref, ...), custom_call_target="tpu_custom_call" | custom-call | flops 7247757312 | bytes 16777216 | tf_op jit(solution)/shard_map/attend/pallas_call | solution.py:200
  283.6 6.7 convolution_convert_fusion
  301.0 18.5 %collective-permute-done.6.refs_1_.refs_2_ = bf16[1056,512]{1,0:T(8,128)(2,1)} collective-permute-done((bf16[1056,512]{1,0:T(8,128)(2,1)}, bf16[1056,512]{1,0:T(8,128)(2,1)}, u32[]{:S(2)}, u32[]{:S(2)}) %collective-permute-start.6) | collective-permute-done | bytes 1081376 | tf_op jit(solution)/shard_map/ppermute | solution.py:450
  319.4 43.6 %collective-permute-done.7.refs_2_.refs_4_ = bf16[1056,512]{1,0:T(8,128)(2,1)} collective-permute-done((bf16[1056,512]{1,0:T(8,128)(2,1)}, bf16[1056,512]{1,0:T(8,128)(2,1)}, u32[]{:S(2)}, u32[]{:S(2)}) %collective-permute-start.7) | collective-permute-done | bytes 1081376 | tf_op jit(solution)/shard_map/ppermute | solution.py:450
  370.7 20.7 %all-to-all-start.1 = ((bf16[4,576,256]{2,1,0:T(8,128)(2,1)}), bf16[4,576,256]{2,1,0:T(8,128)(2,1)}, u32[]{:S(2)}, u32[]{:S(2)}) async-start(bf16[4,576,256]{2,1,0:T(8,128)(2,1)} %bitcast.414), calls=%async_computation.2 | async-start | bytes 2359296 | tf_op jit(solution)/shard_map/all_to_all | solution.py:437
  396.8 22.3 %all-to-all-done.1 = bf16[4,576,256]{2,1,0:T(8,128)(2,1)} async-done(((bf16[4,576,256]{2,1,0:T(8,128)(2,1)}), bf16[4,576,256]{2,1,0:T(8,128)(2,1)}, u32[]{:S(2)}, u32[]{:S(2)}) %all-to-all-start.1) | async-done | bytes 1179680 | tf_op jit(solution)/shard_map/all_to_all | solution.py:437
  423.8 46.6 %all-gather.13.cloned.1.call-done = bf16[4,1024,256]{2,1,0:T(8,128)(2,1)} async-done(((bf16[4,256,256]{2,1,0:T(8,128)(2,1)}), bf16[4,1024,256]{2,1,0:T(8,128)(2,1)}) %all-gather.13.cloned.1.call-update) | async-done | bytes 2097168 | tf_op jit(solution)/shard_map/all_gather | solution.py:429
  474.4 24.9 %collective-permute-done.9.refs_3_.refs_1_ = bf16[1056,512]{1,0:T(8,128)(2,1)S(1)} collective-permute-done((bf16[1056,512]{1,0:T(8,128)(2,1)}, bf16[1056,512]{1,0:T(8,128)(2,1)S(1)}, u32[]{:S(2)}, u32[]{:S(2)}) %collective-permute-start.9) | collective-permute-done | bytes 1081376 | tf_op jit(solution)/shard_map/ppermute | solution.py:450
  500.3 44.2 %collective-permute-done.10.refs_5_.refs_2_ = bf16[1056,512]{1,0:T(8,128)(2,1)S(1)} collective-permute-done((bf16[1056,512]{1,0:T(8,128)(2,1)}, bf16[1056,512]{1,0:T(8,128)(2,1)S(1)}, u32[]{:S(2)}, u32[]{:S(2)}) %collective-permute-start.10) | collective-permute-done | bytes 1081376 | tf_op jit(solution)/shard_map/ppermute | solution.py:450
  546.5 17.4 %all-gather.15.cloned.1.call-done = bf16[4,1024,2048]{2,1,0:T(8,128)(2,1)} async-done(((bf16[4,1024,256]{2,1,0:T(8,128)(2,1)}), bf16[4,1024,2048]{2,1,0:T(8,128)(2,1)}) %all-gather.15.cloned.1.call-update) | async-done | bytes 16777232 | tf_op jit(solution)/shard_map/all_gather | solution.py:433
  578.7 22.5 %dispatch.1 = (bf16[4,288,2048]{2,1,0:T(8,128)(2,1)}, bf16[4,288,2048]{2,1,0:T(8,128)(2,1)}, f32[4,1024,1]{2,1,0:T(8,128)}, f32[4,1024,8]{2,1,0:T(8,128)}) custom-call(bf16[4,1024,2048]{2,1,0:T(8,128)(2,1)} %all-gather.15.cloned.1.call-done, s32[4,2,1024]{2,1,0:T(2,128)} %pad_add_fusion.6.target_ref, f32[1,2048]{1,0:T(1,128)} %bitcast.475, ...), custom_call_target="tpu_custom_call" | custom-call | bytes 16777216 | tf_op jit(solution)/shard_map/dispatch/pallas_call | solution.py:362
  621.7 29.0 %expert_step.2 = (bf16[1152,704]{1,0:T(8,128)(2,1)}, bf16[1152,704]{1,0:T(8,128)(2,1)}, bf16[1152,704]{1,0:T(8,128)(2,1)}, bf16[1152,2048]{1,0:T(8,128)(2,1)}, f32[1152,2]{1,0:T(8,128)}) custom-call(bf16[1152,2048]{1,0:T(8,128)(2,1)} %bitcast.406, bf16[1152,2048]{1,0:T(8,128)(2,1)} %all-gather.17.cloned.1.call-done.grad_ref, f32[1152,1]{1,0:T(8,128)} %reshape.661.weight_ref, ...), custom_call_target="tpu_custom_call" | custom-call | bytes 8650752 | tf_op jit(solution)/shard_map/expert_step/pallas_call | solution.py:412
  652.2 15.6 %collective-permute-done.13.refs_2_ = bf16[1408,512]{1,0:T(8,128)(2,1)} collective-permute-done((bf16[1408,512]{1,0:T(8,128)(2,1)}, bf16[1408,512]{1,0:T(8,128)(2,1)}, u32[]{:S(2)}, u32[]{:S(2)}) %collective-permute-start.13) | collective-permute-done | bytes 1441824 | tf_op jit(solution)/shard_map/ppermute | solution.py:450
  673.3 31.4 %collective-permute-start.15 = (bf16[704,512]{1,0:T(8,128)(2,1)}, bf16[704,512]{1,0:T(8,128)(2,1)S(1)}, u32[]{:S(2)}, u32[]{:S(2)}) collective-permute-start(bf16[704,512]{1,0:T(8,128)(2,1)} %get-tuple-element.186), channel_id=1, source_target_pairs={{0,8},{8,16},{16,24},{24,0},{1,9},{9,17},{17,25},{25,1},{2,10},{10... | collective-permute-start | bytes 2162696 | tf_op jit(solution)/shard_map/ppermute | solution.py:450
  717.3 7.1 convolution_convert_fusion.8
  739.4 11.9 collective-permute-done.16.refs_2_
  753.2 15.8 %collective-permute-start.18 = (bf16[352,512]{1,0:T(8,128)(2,1)}, bf16[352,512]{1,0:T(8,128)(2,1)S(1)}, u32[]{:S(2)}, u32[]{:S(2)}) collective-permute-start(bf16[352,512]{1,0:T(8,128)(2,1)} %get-tuple-element.202), channel_id=1, source_target_pairs={{0,8},{8,16},{16,24},{24,0},{1,9},{9,17},{17,25},{25,1},{2,10},{10... | collective-permute-start | bytes 1081352 | tf_op jit(solution)/shard_map/ppermute | solution.py:450
  778.1 28.9 %expert_step.3 = (bf16[1152,704]{1,0:T(8,128)(2,1)}, bf16[1152,704]{1,0:T(8,128)(2,1)}, bf16[1152,704]{1,0:T(8,128)(2,1)}, bf16[1152,2048]{1,0:T(8,128)(2,1)}, f32[1152,2]{1,0:T(8,128)}) custom-call(bf16[1152,2048]{1,0:T(8,128)(2,1)} %bitcast.401, bf16[1152,2048]{1,0:T(8,128)(2,1)} %all-gather.19.cloned.1.call-done.grad_ref, f32[1152,1]{1,0:T(8,128)} %reshape.662.weight_ref, ...), custom_call_target="tpu_custom_call" | custom-call | bytes 8650752 | tf_op jit(solution)/shard_map/expert_step/pallas_call | solution.py:412
  826.0 44.2 %reduce-scatter.11.cloned.1.call-done = bf16[1168,256]{1,0:T(8,128)(2,1)} async-done(((bf16[1168,2048]{1,0:T(8,128)(2,1)}), bf16[1168,256]{1,0:T(8,128)(2,1)}) %reduce-scatter.11.cloned.1.call-update) | async-done | bytes 598032 | tf_op jit(solution)/shard_map/reduce_scatter | solution.py:544
  875.7 14.4 all-to-all-start.2
  901.3 17.6 %all-to-all-done.2 = bf16[4,582,256]{2,1,0:T(8,128)(2,1)S(1)} async-done(((bf16[4,582,256]{2,1,0:T(8,128)(2,1)}), bf16[4,582,256]{2,1,0:T(8,128)(2,1)S(1)}, u32[]{:S(2)}, u32[]{:S(2)}) %all-to-all-start.2) | async-done | bytes 1191968 | tf_op jit(solution)/shard_map/all_to_all | solution.py:437
  929.4 7.2 convolution_convert_fusion.1
  943.2 8.1 convolution_convert_fusion.4
  956.6 18.5 %all-gather.21.cloned.1.call-done = bf16[4,1024,256]{2,1,0:T(8,128)(2,1)} async-done(((bf16[4,256,256]{2,1,0:T(8,128)(2,1)}), bf16[4,1024,256]{2,1,0:T(8,128)(2,1)}) %all-gather.21.cloned.1.call-update) | async-done | bytes 2097168 | tf_op jit(solution)/shard_map/all_gather | solution.py:429
  994.2 19.4 %collective-permute-done.24.refs_5_.refs_2_ = bf16[1056,512]{1,0:T(8,128)(2,1)S(1)} collective-permute-done((bf16[1056,512]{1,0:T(8,128)(2,1)}, bf16[1056,512]{1,0:T(8,128)(2,1)S(1)}, u32[]{:S(2)}, u32[]{:S(2)}) %collective-permute-start.24) | collective-permute-done | bytes 1081376 | tf_op jit(solution)/shard_map/ppermute | solution.py:450
  1013.6 45.3 %collective-permute-done.25.refs_9_.refs_4_ = bf16[1056,512]{1,0:T(8,128)(2,1)} collective-permute-done((bf16[1056,512]{1,0:T(8,128)(2,1)}, bf16[1056,512]{1,0:T(8,128)(2,1)}, u32[]{:S(2)}, u32[]{:S(2)}) %collective-permute-start.25) | collective-permute-done | bytes 1081376 | tf_op jit(solution)/shard_map/ppermute | solution.py:450
  1058.9 10.0 all-gather.23.cloned.1.call-done
  1070.9 12.8 collective-permute-start.27
  1086.0 17.2 %fusion.65 = f32[4096,512]{1,0:T(8,128)} fusion(bf16[4096,2048]{1,0:T(8,128)(2,1)} %bitcast.484, bf16[512,2048]{1,0:T(8,128)(2,1)} %copy-done.52), kind=kOutput, calls=%fused_computation.366 | convolution fusion | flops 8589934592 | bytes 27262976 | tf_op jit(solution)/shard_map/rd,fd->rf/dot_general | solution.py:20
  1103.2 43.9 %attend_back.1 = (bf16[4,1024,1024]{2,1,0:T(8,128)(2,1)}, f32[4,1024,3]{2,1,0:T(8,128)}) custom-call(bf16[4,1024,1024]{2,1,0:T(8,128)(2,1)} %bitcast.384, s32[4,2,1024]{2,1,0:T(2,128)} %pad_add_fusion.3.target_ref, s32[4,1,1024]{2,1,0:T(1,128)} %reshape.607.kblk_ref, f32[4,2,576,1]{3,2,1,0:T(8,128)} %get-tuple-element.221.lse_ref, ...), custom_call_target="tpu_custom_call" | custom-call | bytes 16777216 | tf_op jit(solution)/shard_map/attend_back/pallas_call | solution.py:283
  1151.8 23.8 %spread.1 = bf16[16,272,2048]{2,1,0:T(8,128)(2,1)} custom-call(bf16[16,256,1024]{2,1,0:T(8,128)(2,1)} %bitcast.387, bf16[2048,1024]{1,0:T(8,128)(2,1)S(1)} %copy-done, bf16[16,16,256]{2,1,0:T(8,128)(2,1)S(1)} %bitcast.373), custom_call_target="tpu_custom_call" | custom-call | bytes 17825792 | tf_op jit(solution)/shard_map/spread/pallas_call | solution.py:527
  1188.7 16.9 %collective-permute-done.30.refs_7_.refs_3_ = bf16[1056,512]{1,0:T(8,128)(2,1)S(1)} collective-permute-done((bf16[1056,512]{1,0:T(8,128)(2,1)}, bf16[1056,512]{1,0:T(8,128)(2,1)S(1)}, u32[]{:S(2)}, u32[]{:S(2)}) %collective-permute-start.30) | collective-permute-done | bytes 1081376 | tf_op jit(solution)/shard_map/ppermute | solution.py:450
  1205.7 14.0 convolution_convert_fusion.10
  1221.0 24.0 %convolution_convert_fusion.3 = bf16[2048,1024]{1,0:T(8,128)(2,1)} fusion(bf16[4096,2048]{1,0:T(8,128)(2,1)} %get-tuple-element.235, bf16[4096,1024]{1,0:T(8,128)(2,1)} %bitcast.388), kind=kOutput, calls=%fused_computation.18 | convolution fusion | flops 17181966336 | bytes 29360128 | tf_op jit(solution)/shard_map/rd,rf->df/dot_general | solution.py:20
  1253.8 32.0 %collective-permute-done.31.refs_11_.refs_5_ = bf16[1056,512]{1,0:T(8,128)(2,1)} collective-permute-done((bf16[1056,512]{1,0:T(8,128)(2,1)}, bf16[1056,512]{1,0:T(8,128)(2,1)}, u32[]{:S(2)}, u32[]{:S(2)}) %collective-permute-start.31) | collective-permute-done | bytes 1081376 | tf_op jit(solution)/shard_map/ppermute | solution.py:450
  1285.9 11.8 reduce-scatter.15.cloned.1.call-done
  1323.8 11.9 collective-permute-start.40
  1338.2 8.6 whole_grad.3
  1346.8 7.0 whole_grad.4
  1355.5 10.1 reduce-scatter.17.cloned.1.call-done
  1374.0 26.7 %collective-permute-start.35 = (bf16[272,1024]{1,0:T(8,128)(2,1)S(1)}, bf16[272,1024]{1,0:T(8,128)(2,1)S(1)}, u32[]{:S(2)}, u32[]{:S(2)}) collective-permute-start(bf16[272,1024]{1,0:T(8,128)(2,1)S(1)} %get-tuple-element.393), channel_id=1, source_target_pairs={{0,16},{8,24},{16,0},{24,8},{1,17},{9,25},{17,1},{25,9},{2,18},{10... | collective-permute-start | bytes 1671176 | tf_op jit(solution)/shard_map/ppermute | solution.py:450
  1415.2 57.2 %collective-permute-done.35.refs_5_ = bf16[272,1024]{1,0:T(8,128)(2,1)S(1)} collective-permute-done((bf16[272,1024]{1,0:T(8,128)(2,1)S(1)}, bf16[272,1024]{1,0:T(8,128)(2,1)S(1)}, u32[]{:S(2)}, u32[]{:S(2)}) %collective-permute-start.35) | collective-permute-done | bytes 557088 | tf_op jit(solution)/shard_map/ppermute | solution.py:450
  1472.5 9.3 all_gather.35
  (620 shorter events, 399.4 us)
Async XLA Ops:
  7.2 56.7 %all-gather.9.cloned.1.call-start = ((), (), s32[]{:S(2)}) async-start(), calls=%async_computation.10 | async-start | bytes 2785280 | tf_op jit(solution)/shard_map/all_gather | solution.py:429
  12.8 152.0 %all-gather.11.cloned.1.call-start = ((), (), s32[]{:S(2)}) async-start(), calls=%async_computation.11 | async-start | bytes 18874368 | tf_op jit(solution)/shard_map/all_gather | solution.py:433
  86.7 72.1 %collective-permute-start.1 = (bf16[4,512,256]{2,1,0:T(8,128)(2,1)}, bf16[4,512,256]{2,1,0:T(8,128)(2,1)}, u32[]{:S(2)}, u32[]{:S(2)}) collective-permute-start(bf16[4,512,256]{2,1,0:T(8,128)(2,1)} %get-tuple-element.135), channel_id=1, source_target_pairs={{0,16},{8,24},{16,0},{24,8},{1,17},{9,25},{17,1},{25,9},{2,18},{10... | collective-permute-start | bytes 3145736 | tf_op jit(solution)/shard_map/ppermute | solution.py:450
  88.1 70.7 %collective-permute-start.2 = (bf16[4,512,256]{2,1,0:T(8,128)(2,1)}, bf16[4,512,256]{2,1,0:T(8,128)(2,1)}, u32[]{:S(2)}, u32[]{:S(2)}) collective-permute-start(bf16[4,512,256]{2,1,0:T(8,128)(2,1)} %get-tuple-element.136), channel_id=1, source_target_pairs={{0,24},{8,0},{16,8},{24,16},{1,25},{9,1},{17,9},{25,17},{2,26},{10... | collective-permute-start | bytes 3145736 | tf_op jit(solution)/shard_map/ppermute | solution.py:450
  164.8 61.1 %collective-permute-start.3 = (bf16[2,256,512]{2,1,0:T(8,128)(2,1)}, bf16[2,256,512]{2,1,0:T(8,128)(2,1)S(1)}, u32[]{:S(2)}, u32[]{:S(2)}) collective-permute-start(bf16[2,256,512]{2,1,0:T(8,128)(2,1)} %get-tuple-element.138), channel_id=1, source_target_pairs={{0,8},{8,16},{16,24},{24,0},{1,9},{9,17},{17,25},{25,1},{2,10},{10... | collective-permute-start | bytes 1572872 | tf_op jit(solution)/shard_map/ppermute | solution.py:450
  228.4 61.9 %all-to-all-start = ((bf16[4,2,4,72,256]{4,3,2,1,0:T(8,128)(2,1)}), bf16[4,2,4,72,256]{4,3,2,1,0:T(8,128)(2,1)}, u32[]{:S(2)}, u32[]{:S(2)}) async-start(bf16[4,2,4,72,256]{4,3,2,1,0:T(8,128)(2,1)} %bitcast.412), calls=%async_computation | async-start | bytes 2359296 | tf_op jit(solution)/shard_map/all_to_all | solution.py:437
  237.4 131.0 %reduce-scatter.7.cloned.1.call-start = ((), (), s32[]{:S(2)}) async-start(), calls=%async_computation.12 | async-start | bytes 10616832 | tf_op jit(solution)/shard_map/reduce_scatter | solution.py:544
  292.4 70.6 %collective-permute-start.7 = (bf16[1056,512]{1,0:T(8,128)(2,1)}, bf16[1056,512]{1,0:T(8,128)(2,1)}, u32[]{:S(2)}, u32[]{:S(2)}) collective-permute-start(bf16[1056,512]{1,0:T(8,128)(2,1)} %get-tuple-element.152), channel_id=1, source_target_pairs={{0,16},{8,24},{16,0},{24,8},{1,17},{9,25},{17,1},{25,9},{2,18},{10... | collective-permute-start | bytes 3244040 | tf_op jit(solution)/shard_map/ppermute | solution.py:450
  294.8 68.2 %collective-permute-start.8 = (bf16[1056,512]{1,0:T(8,128)(2,1)}, bf16[1056,512]{1,0:T(8,128)(2,1)}, u32[]{:S(2)}, u32[]{:S(2)}) collective-permute-start(bf16[1056,512]{1,0:T(8,128)(2,1)} %get-tuple-element.153), channel_id=1, source_target_pairs={{0,24},{8,0},{16,8},{24,16},{1,25},{9,1},{17,9},{25,17},{2,26},{10... | collective-permute-start | bytes 3244040 | tf_op jit(solution)/shard_map/ppermute | solution.py:450
  370.7 48.4 %all-to-all-start.1 = ((bf16[4,576,256]{2,1,0:T(8,128)(2,1)}), bf16[4,576,256]{2,1,0:T(8,128)(2,1)}, u32[]{:S(2)}, u32[]{:S(2)}) async-start(bf16[4,576,256]{2,1,0:T(8,128)(2,1)} %bitcast.414), calls=%async_computation.2 | async-start | bytes 2359296 | tf_op jit(solution)/shard_map/all_to_all | solution.py:437
  391.4 78.9 %all-gather.13.cloned.1.call-start = ((), (), s32[]{:S(2)}) async-start(), calls=%async_computation.13 | async-start | bytes 2621440 | tf_op jit(solution)/shard_map/all_gather | solution.py:429
  423.7 140.2 %all-gather.15.cloned.1.call-start = ((), (), s32[]{:S(2)}) async-start(), calls=%async_computation.14 | async-start | bytes 18874368 | tf_op jit(solution)/shard_map/all_gather | solution.py:433
  470.4 151.4 %all-gather.17.cloned.1.call-start = ((), (), s32[]{:S(2)}) async-start(), calls=%async_computation.15 | async-start | bytes 5308416 | tf_op jit(solution)/shard_map/all_gather | solution.py:767
  470.5 74.1 %collective-permute-start.10 = (bf16[1056,512]{1,0:T(8,128)(2,1)}, bf16[1056,512]{1,0:T(8,128)(2,1)S(1)}, u32[]{:S(2)}, u32[]{:S(2)}) collective-permute-start(bf16[1056,512]{1,0:T(8,128)(2,1)} %get-tuple-element.156), channel_id=1, source_target_pairs={{0,16},{8,24},{16,0},{24,8},{1,17},{9,25},{17,1},{25,9},{2,18},{10... | collective-permute-start | bytes 3244040 | tf_op jit(solution)/shard_map/ppermute | solution.py:450
  472.2 73.3 %collective-permute-start.11 = (bf16[1056,512]{1,0:T(8,128)(2,1)}, bf16[1056,512]{1,0:T(8,128)(2,1)S(1)}, u32[]{:S(2)}, u32[]{:S(2)}) collective-permute-start(bf16[1056,512]{1,0:T(8,128)(2,1)} %get-tuple-element.157), channel_id=1, source_target_pairs={{0,24},{8,0},{16,8},{24,16},{1,25},{9,1},{17,9},{25,17},{2,26},{10... | collective-permute-start | bytes 3244040 | tf_op jit(solution)/shard_map/ppermute | solution.py:450
  567.0 211.1 %all-gather.19.cloned.1.call-start = ((), (), s32[]{:S(2)}) async-start(), calls=%async_computation.16 | async-start | bytes 5308416 | tf_op jit(solution)/shard_map/all_gather | solution.py:767
  569.0 256.3 %reduce-scatter.9.cloned.1.call-start = ((), (), s32[]{:S(2)}) async-start(), calls=%async_computation.17 | async-start | bytes 5382144 | tf_op jit(solution)/shard_map/reduce_scatter | solution.py:544
  569.0 83.2 %collective-permute-start.12 = (bf16[1408,512]{1,0:T(8,128)(2,1)}, bf16[1408,512]{1,0:T(8,128)(2,1)}, u32[]{:S(2)}, u32[]{:S(2)}) collective-permute-start(bf16[1408,512]{1,0:T(8,128)(2,1)} %get-tuple-element.181), channel_id=1, source_target_pairs={{0,8},{8,16},{16,24},{24,0},{1,9},{9,17},{17,25},{25,1},{2,10},{10... | collective-permute-start | bytes 4325384 | tf_op jit(solution)/shard_map/ppermute | solution.py:450
  573.5 94.3 %collective-permute-start.13 = (bf16[1408,512]{1,0:T(8,128)(2,1)}, bf16[1408,512]{1,0:T(8,128)(2,1)}, u32[]{:S(2)}, u32[]{:S(2)}) collective-permute-start(bf16[1408,512]{1,0:T(8,128)(2,1)} %get-tuple-element.182), channel_id=1, source_target_pairs={{0,16},{8,24},{16,0},{24,8},{1,17},{9,25},{17,1},{25,9},{2,18},{10... | collective-permute-start | bytes 4325384 | tf_op jit(solution)/shard_map/ppermute | solution.py:450
  575.5 92.4 %collective-permute-start.14 = (bf16[1408,512]{1,0:T(8,128)(2,1)}, bf16[1408,512]{1,0:T(8,128)(2,1)}, u32[]{:S(2)}, u32[]{:S(2)}) collective-permute-start(bf16[1408,512]{1,0:T(8,128)(2,1)} %get-tuple-element.183), channel_id=1, source_target_pairs={{0,24},{8,0},{16,8},{24,16},{1,25},{9,1},{17,9},{25,17},{2,26},{10... | collective-permute-start | bytes 4325384 | tf_op jit(solution)/shard_map/ppermute | solution.py:450
  673.2 197.1 %reduce-scatter.11.cloned.1.call-start = ((), (), s32[]{:S(2)}) async-start(), calls=%async_computation.18 | async-start | bytes 5382144 | tf_op jit(solution)/shard_map/reduce_scatter | solution.py:544
  673.3 66.2 %collective-permute-start.15 = (bf16[704,512]{1,0:T(8,128)(2,1)}, bf16[704,512]{1,0:T(8,128)(2,1)S(1)}, u32[]{:S(2)}, u32[]{:S(2)}) collective-permute-start(bf16[704,512]{1,0:T(8,128)(2,1)} %get-tuple-element.186), channel_id=1, source_target_pairs={{0,8},{8,16},{16,24},{24,0},{1,9},{9,17},{17,25},{25,1},{2,10},{10... | collective-permute-start | bytes 2162696 | tf_op jit(solution)/shard_map/ppermute | solution.py:450
  704.7 46.7 %collective-permute-start.16 = (bf16[704,512]{1,0:T(8,128)(2,1)}, bf16[704,512]{1,0:T(8,128)(2,1)S(1)}, u32[]{:S(2)}, u32[]{:S(2)}) collective-permute-start(bf16[704,512]{1,0:T(8,128)(2,1)} %get-tuple-element.187), channel_id=1, source_target_pairs={{0,16},{8,24},{16,0},{24,8},{1,17},{9,25},{17,1},{25,9},{2,18},{10... | collective-permute-start | bytes 2162696 | tf_op jit(solution)/shard_map/ppermute | solution.py:450
  753.2 55.2 %collective-permute-start.18 = (bf16[352,512]{1,0:T(8,128)(2,1)}, bf16[352,512]{1,0:T(8,128)(2,1)S(1)}, u32[]{:S(2)}, u32[]{:S(2)}) collective-permute-start(bf16[352,512]{1,0:T(8,128)(2,1)} %get-tuple-element.202), channel_id=1, source_target_pairs={{0,8},{8,16},{16,24},{24,0},{1,9},{9,17},{17,25},{25,1},{2,10},{10... | collective-permute-start | bytes 1081352 | tf_op jit(solution)/shard_map/ppermute | solution.py:450
  819.9 52.5 %collective-permute-start.21 = (bf16[704,512]{1,0:T(8,128)(2,1)}, bf16[704,512]{1,0:T(8,128)(2,1)S(1)}, u32[]{:S(2)}, u32[]{:S(2)}) collective-permute-start(bf16[704,512]{1,0:T(8,128)(2,1)} %pad_maximum_fusion.42), channel_id=1, source_target_pairs={{0,8},{8,16},{16,24},{24,0},{1,9},{9,17},{17,25},{25,1},{2,10},{10... | collective-permute-start | bytes 2162696 | tf_op jit(solution)/shard_map/ppermute | solution.py:450
  821.9 50.5 %collective-permute-start.22 = (bf16[704,512]{1,0:T(8,128)(2,1)}, bf16[704,512]{1,0:T(8,128)(2,1)S(1)}, u32[]{:S(2)}, u32[]{:S(2)}) collective-permute-start(bf16[704,512]{1,0:T(8,128)(2,1)} %pad_maximum_fusion.43), channel_id=1, source_target_pairs={{0,16},{8,24},{16,0},{24,8},{1,17},{9,25},{17,1},{25,9},{2,18},{10... | collective-permute-start | bytes 2162696 | tf_op jit(solution)/shard_map/ppermute | solution.py:450
  821.9 50.6 %collective-permute-start.23 = (bf16[704,512]{1,0:T(8,128)(2,1)}, bf16[704,512]{1,0:T(8,128)(2,1)S(1)}, u32[]{:S(2)}, u32[]{:S(2)}) collective-permute-start(bf16[704,512]{1,0:T(8,128)(2,1)} %pad_maximum_fusion.44), channel_id=1, source_target_pairs={{0,24},{8,0},{16,8},{24,16},{1,25},{9,1},{17,9},{25,17},{2,26},{10... | collective-permute-start | bytes 2162696 | tf_op jit(solution)/shard_map/ppermute | solution.py:450
  890.1 85.0 %all-gather.21.cloned.1.call-start = ((), (), s32[]{:S(2)}) async-start(), calls=%async_computation.19 | async-start | bytes 2621440 | tf_op jit(solution)/shard_map/all_gather | solution.py:429
  929.3 139.5 %all-gather.23.cloned.1.call-start = ((), (), s32[]{:S(2)}) async-start(), calls=%async_computation.20 | async-start | bytes 18874368 | tf_op jit(solution)/shard_map/all_gather | solution.py:433
  975.1 200.6 %reduce-scatter.13.cloned.1.call-start = ((), (), s32[]{:S(2)}) async-start(), calls=%async_computation.21 | async-start | bytes 10616832 | tf_op jit(solution)/shard_map/reduce_scatter | solution.py:544
  984.7 74.2 %collective-permute-start.25 = (bf16[1056,512]{1,0:T(8,128)(2,1)}, bf16[1056,512]{1,0:T(8,128)(2,1)}, u32[]{:S(2)}, u32[]{:S(2)}) collective-permute-start(bf16[1056,512]{1,0:T(8,128)(2,1)} %pad_maximum_fusion.31), channel_id=1, source_target_pairs={{0,16},{8,24},{16,0},{24,8},{1,17},{9,25},{17,1},{25,9},{2,18},{10... | collective-permute-start | bytes 3244040 | tf_op jit(solution)/shard_map/ppermute | solution.py:450
  986.4 72.5 %collective-permute-start.26 = (bf16[1056,512]{1,0:T(8,128)(2,1)}, bf16[1056,512]{1,0:T(8,128)(2,1)}, u32[]{:S(2)}, u32[]{:S(2)}) collective-permute-start(bf16[1056,512]{1,0:T(8,128)(2,1)} %pad_maximum_fusion.32), channel_id=1, source_target_pairs={{0,24},{8,0},{16,8},{24,16},{1,25},{9,1},{17,9},{25,17},{2,26},{10... | collective-permute-start | bytes 3244040 | tf_op jit(solution)/shard_map/ppermute | solution.py:450
  1068.9 228.8 %reduce-scatter.15.cloned.1.call-start = ((), (), s32[]{:S(2)}) async-start(), calls=%async_computation.22 | async-start | bytes 20054016 | tf_op jit(solution)/shard_map/reduce_scatter | solution.py:958
  1070.9 104.7 %collective-permute-start.27 = (bf16[1056,512]{1,0:T(8,128)(2,1)}, bf16[1056,512]{1,0:T(8,128)(2,1)S(1)}, u32[]{:S(2)}, u32[]{:S(2)}) collective-permute-start(bf16[1056,512]{1,0:T(8,128)(2,1)} %pad_maximum_fusion.34), channel_id=1, source_target_pairs={{0,8},{8,16},{16,24},{24,0},{1,9},{9,17},{17,25},{25,1},{2,10},{10... | collective-permute-start | bytes 3244040 | tf_op jit(solution)/shard_map/ppermute | solution.py:450
  1083.7 92.0 %collective-permute-start.28 = (bf16[1056,512]{1,0:T(8,128)(2,1)}, bf16[1056,512]{1,0:T(8,128)(2,1)}, u32[]{:S(2)}, u32[]{:S(2)}) collective-permute-start(bf16[1056,512]{1,0:T(8,128)(2,1)} %pad_maximum_fusion.35), channel_id=1, source_target_pairs={{0,16},{8,24},{16,0},{24,8},{1,17},{9,25},{17,1},{25,9},{2,18},{10... | collective-permute-start | bytes 3244040 | tf_op jit(solution)/shard_map/ppermute | solution.py:450
  1084.7 90.9 %collective-permute-start.29 = (bf16[1056,512]{1,0:T(8,128)(2,1)}, bf16[1056,512]{1,0:T(8,128)(2,1)}, u32[]{:S(2)}, u32[]{:S(2)}) collective-permute-start(bf16[1056,512]{1,0:T(8,128)(2,1)} %pad_maximum_fusion.36), channel_id=1, source_target_pairs={{0,24},{8,0},{16,8},{24,16},{1,25},{9,1},{17,9},{25,17},{2,26},{10... | collective-permute-start | bytes 3244040 | tf_op jit(solution)/shard_map/ppermute | solution.py:450
  1180.0 71.4 %all-to-all-start.3 = ((bf16[4,576,256]{2,1,0:T(8,128)(2,1)}), bf16[4,576,256]{2,1,0:T(8,128)(2,1)}, u32[]{:S(2)}, u32[]{:S(2)}) async-start(bf16[4,576,256]{2,1,0:T(8,128)(2,1)} %bitcast.413), calls=%async_computation.7 | async-start | bytes 2359296 | tf_op jit(solution)/shard_map/all_to_all | solution.py:437
  1184.4 181.2 %reduce-scatter.17.cloned.1.call-start = ((), (), s32[]{:S(2)}) async-start(), calls=%async_computation.23 | async-start | bytes 2785280 | tf_op jit(solution)/shard_map/reduce_scatter | solution.py:963
  1184.4 101.5 %collective-permute-start.31 = (bf16[1056,512]{1,0:T(8,128)(2,1)}, bf16[1056,512]{1,0:T(8,128)(2,1)}, u32[]{:S(2)}, u32[]{:S(2)}) collective-permute-start(bf16[1056,512]{1,0:T(8,128)(2,1)} %pad_maximum_fusion.39), channel_id=1, source_target_pairs={{0,16},{8,24},{16,0},{24,8},{1,17},{9,25},{17,1},{25,9},{2,18},{10... | collective-permute-start | bytes 3244040 | tf_op jit(solution)/shard_map/ppermute | solution.py:450
  1187.2 98.7 %collective-permute-start.32 = (bf16[1056,512]{1,0:T(8,128)(2,1)}, bf16[1056,512]{1,0:T(8,128)(2,1)}, u32[]{:S(2)}, u32[]{:S(2)}) collective-permute-start(bf16[1056,512]{1,0:T(8,128)(2,1)} %pad_maximum_fusion.40), channel_id=1, source_target_pairs={{0,24},{8,0},{16,8},{24,16},{1,25},{9,1},{17,9},{25,17},{2,26},{10... | collective-permute-start | bytes 3244040 | tf_op jit(solution)/shard_map/ppermute | solution.py:450
  1221.0 64.9 %collective-permute-start.33 = (bf16[512,512]{1,0:T(8,128)(2,1)}, bf16[512,512]{1,0:T(8,128)(2,1)S(1)}, u32[]{:S(2)}, u32[]{:S(2)}) collective-permute-start(bf16[512,512]{1,0:T(8,128)(2,1)} %get-tuple-element.239), channel_id=1, source_target_pairs={{0,8},{8,16},{16,24},{24,0},{1,9},{9,17},{17,25},{25,1},{2,10},{10... | collective-permute-start | bytes 1572872 | tf_op jit(solution)/shard_map/ppermute | solution.py:450
  1323.8 78.9 %collective-permute-start.40 = (bf16[512,512]{1,0:T(8,128)(2,1)}, bf16[512,512]{1,0:T(8,128)(2,1)S(1)}, u32[]{:S(2)}, u32[]{:S(2)}) collective-permute-start(bf16[512,512]{1,0:T(8,128)(2,1)} %get-tuple-element.249), channel_id=1, source_target_pairs={{0,16},{8,24},{16,0},{24,8},{1,17},{9,25},{17,1},{25,9},{2,18},{10... | collective-permute-start | bytes 1572872 | tf_op jit(solution)/shard_map/ppermute | solution.py:450
  1335.7 67.0 %collective-permute-start.41 = (bf16[512,512]{1,0:T(8,128)(2,1)}, bf16[512,512]{1,0:T(8,128)(2,1)}, u32[]{:S(2)}, u32[]{:S(2)}) collective-permute-start(bf16[512,512]{1,0:T(8,128)(2,1)} %get-tuple-element.250), channel_id=1, source_target_pairs={{0,24},{8,0},{16,8},{24,16},{1,25},{9,1},{17,9},{25,17},{2,26},{10... | collective-permute-start | bytes 1572872 | tf_op jit(solution)/shard_map/ppermute | solution.py:450
  1374.0 98.4 %collective-permute-start.35 = (bf16[272,1024]{1,0:T(8,128)(2,1)S(1)}, bf16[272,1024]{1,0:T(8,128)(2,1)S(1)}, u32[]{:S(2)}, u32[]{:S(2)}) collective-permute-start(bf16[272,1024]{1,0:T(8,128)(2,1)S(1)} %get-tuple-element.393), channel_id=1, source_target_pairs={{0,16},{8,24},{16,0},{24,8},{1,17},{9,25},{17,1},{25,9},{2,18},{10... | collective-permute-start | bytes 1671176 | tf_op jit(solution)/shard_map/ppermute | solution.py:450
  1400.7 71.7 %collective-permute-start.34 = (bf16[272,1024]{1,0:T(8,128)(2,1)S(1)}, bf16[272,1024]{1,0:T(8,128)(2,1)S(1)}, u32[]{:S(2)}, u32[]{:S(2)}) collective-permute-start(bf16[272,1024]{1,0:T(8,128)(2,1)S(1)} %get-tuple-element.395), channel_id=1, source_target_pairs={{0,8},{8,16},{16,24},{24,0},{1,9},{9,17},{17,25},{25,1},{2,10},{10... | collective-permute-start | bytes 1671176 | tf_op jit(solution)/shard_map/ppermute | solution.py:450
  1408.1 74.9 %collective-permute-start.37 = (bf16[256,1024]{1,0:T(8,128)(2,1)}, bf16[256,1024]{1,0:T(8,128)(2,1)S(1)}, u32[]{:S(2)}, u32[]{:S(2)}) collective-permute-start(bf16[256,1024]{1,0:T(8,128)(2,1)} %get-tuple-element.243), channel_id=1, source_target_pairs={{0,8},{8,16},{16,24},{24,0},{1,9},{9,17},{17,25},{25,1},{2,10},{10... | collective-permute-start | bytes 1572872 | tf_op jit(solution)/shard_map/ppermute | solution.py:450
  1408.2 75.6 %collective-permute-start.38 = (bf16[256,1024]{1,0:T(8,128)(2,1)}, bf16[256,1024]{1,0:T(8,128)(2,1)}, u32[]{:S(2)}, u32[]{:S(2)}) collective-permute-start(bf16[256,1024]{1,0:T(8,128)(2,1)} %get-tuple-element.244), channel_id=1, source_target_pairs={{0,16},{8,24},{16,0},{24,8},{1,17},{9,25},{17,1},{25,9},{2,18},{10... | collective-permute-start | bytes 1572872 | tf_op jit(solution)/shard_map/ppermute | solution.py:450
  1411.0 72.7 %collective-permute-start.39 = (bf16[256,1024]{1,0:T(8,128)(2,1)}, bf16[256,1024]{1,0:T(8,128)(2,1)}, u32[]{:S(2)}, u32[]{:S(2)}) collective-permute-start(bf16[256,1024]{1,0:T(8,128)(2,1)} %get-tuple-element.245), channel_id=1, source_target_pairs={{0,24},{8,0},{16,8},{24,16},{1,25},{9,1},{17,9},{25,17},{2,26},{10... | collective-permute-start | bytes 1572872 | tf_op jit(solution)/shard_map/ppermute | solution.py:450
  (141 other events, 1555.3 us)
Sparse Core Ops, SparseCore 0:
  12.9 50.9 all-gather.8
  67.2 91.9 all-gather.10
  290.4 77.8 reduce-scatter.6
  423.8 46.4 all-gather.12
  472.1 91.8 all-gather.14
  567.1 43.1 all-gather.16
  612.1 39.7 all-gather.18
  673.3 85.8 reduce-scatter.8
  814.3 55.8 reduce-scatter.10
  929.4 45.6 all-gather.20
  977.0 91.8 all-gather.22
  1072.8 83.5 reduce-scatter.12
  1176.8 120.8 reduce-scatter.14
  1299.8 65.6 reduce-scatter.16

commit v6 on v4

--- a/solution.py
+++ b/solution.py
@@ -955,7 +955,7 @@
     into = tie(into, *last[1:2]).reshape(count, -1)
     grad_query_cat = dot_f32("rd,rf->df", hidden_a, into).astype(BF16)
     out_pieces = exchange_pieces(cut_pieces(grad_part(grad_out_cat)[0]), *last[1:2])
-    part = tie(part, *last, down_home, grad_query_cat, *out_pieces[1:2])
+    part = tie(part, *last, down_home, grad_query_cat, *out_pieces[1:])
     own = lax.psum_scatter(part, "row", scatter_dimension=1, tiled=True)
     def out_grad_body(m, ins, outs):
         for j in range(local):

time: 1500 us -> 1500 us (level)
  waiting for transfers between devices: 635 us -> 661 us
  starting transfers between devices: 199 us -> 179 us
    ppermute x42, waiting for transfers between devices: 370 us -> 419 us  [exchange_pieces(): got.append(lax.ppermute(tie(pieces[m], *after), 'row', steps))]
    ppermute x42, starting transfers between devices: 153 us -> 134 us  [exchange_pieces(): got.append(lax.ppermute(tie(pieces[m], *after), 'row', steps))]
    unnamed x263 -> x253, local copies, waits for them, and re-layouts: 38.5 us -> 36.8 us
  transfers between devices with their start and end apart: 60 -> 60, of which waited for: 27 -> 27; matrix products, arithmetic and copies ran while one was open for 20% -> 19% of each run, Pallas kernels for 18% -> 18%
where the time goes in v6:
time: 1500 us; the launch traced here: 1480 us
  waiting for transfers between devices  661 us (44%)
  Pallas kernels  270 us (18%)
  starting transfers between devices  179 us (12%)
  matrix products  126 us (8%)
  local copies, waits for them, and re-layouts  113 us (8%)
  other arithmetic  105 us (7%)
  between operations  16.1 us (1%)
    ppermute x42, waiting for transfers between devices, exchange_pieces(): got.append(lax.ppermute(tie(pieces[m], *after), 'row', steps))  419 us
    ppermute x42, starting transfers between devices, exchange_pieces(): got.append(lax.ppermute(tie(pieces[m], *after), 'row', steps))  134 us
    dot_general x17, matrix products, dot_f32(): return jnp.einsum(spec, left, right, preferred_element_type=F32)  112 us
    all_gather x3, waiting for transfers between devices, gather_rows(): return lax.all_gather(own, 'row', axis=1, tiled=True)  89.5 us
    pallas_call x13, Pallas kernels, assemble(): pl.pallas_call(kernel, grid_spec=pltpu.PrefetchScalarGridSpec(num_scalar_...  60.1 us
    pallas_call x2, Pallas kernels, expert_step(): pl.pallas_call(expert_kernel, grid=(count // tile,), in_specs=[row(width)...  57.9 us
    all_to_all x4, waiting for transfers between devices, exchange(): return lax.all_to_all(parts, 'row', 0, 0)  47.9 us
    reduce_scatter x4, waiting for transfers between devices, sum_cols(): return lax.psum_scatter(rows, 'col', scatter_dimension=1, tiled=True)  47 us
  transfers between devices with their start and end apart: 60, of which 27 were waited for; matrix products, arithmetic and copies ran while one was open for 19% of the time, Pallas kernels for 18%

profile of v6, /device:TPU:0, one launch (start us, length us, event | category | flops | bytes accessed | tf_op | source)
XLA Modules:
  0.0 1479.1 jit_solution(5467305078111850930)
XLA Ops:
  39.2 24.7 %all-gather.9.cloned.1.call-done = bf16[4,1088,256]{2,1,0:T(8,128)(2,1)} async-done(((bf16[4,272,256]{2,1,0:T(8,128)(2,1)}), bf16[4,1088,256]{2,1,0:T(8,128)(2,1)}) %all-gather.9.cloned.1.call-update) | async-done | bytes 2228240 | tf_op jit(solution)/shard_map/all_gather | solution.py:423
  108.1 39.7 %collective-permute-done.1.refs_2_ = bf16[4,512,256]{2,1,0:T(8,128)(2,1)} collective-permute-done((bf16[4,512,256]{2,1,0:T(8,128)(2,1)}, bf16[4,512,256]{2,1,0:T(8,128)(2,1)}, u32[]{:S(2)}, u32[]{:S(2)}) %collective-permute-start.1) | collective-permute-done | bytes 1048608 | tf_op jit(solution)/shard_map/ppermute | solution.py:444
  152.4 6.8 all-gather.11.cloned.1.call-done
  159.2 15.2 %collective-permute-start.3 = (bf16[2,256,512]{2,1,0:T(8,128)(2,1)}, bf16[2,256,512]{2,1,0:T(8,128)(2,1)}, u32[]{:S(2)}, u32[]{:S(2)}) collective-permute-start(bf16[2,256,512]{2,1,0:T(8,128)(2,1)} %get-tuple-element.137), channel_id=1, source_target_pairs={{0,8},{8,16},{16,24},{24,0},{1,9},{9,17},{17,25},{25,1},{2,10},{10... | collective-permute-start | bytes 1572872 | tf_op jit(solution)/shard_map/ppermute | solution.py:444
  180.0 32.2 %project.1 = (bf16[4096,2048]{1,0:T(8,128)(2,1)}, f32[4096,1]{1,0:T(8,128)S(1)}, f32[4096,8]{1,0:T(8,128)S(1)}, bf16[4096,1024]{1,0:T(8,128)(2,1)}) custom-call(bf16[4096,2048]{1,0:T(8,128)(2,1)} %bitcast.484, f32[1,2048]{1,0:T(1,128)S(1)} %bitcast.379, bf16[2048,8]{1,0:T(8,128)(2,1)S(1)} %copy-done.42, bf16[2048,1024]{1,0:T(8,128)(2,1)} %query_in.1.weight_ref, ...), custom_call_target="tpu_custom_call" | custom-call | flops 17179869184 | bytes 41943040 | tf_op jit(solution)/shard_map/project/pallas_call | solution.py:112
  239.5 29.7 %attend.1 = (bf16[2,4,288,256]{3,2,1,0:T(8,128)(2,1)}, bf16[4,1024,512]{2,1,0:T(8,128)(2,1)}, bf16[4,1024,512]{2,1,0:T(8,128)(2,1)}, f32[4,2,576,1]{3,2,1,0:T(8,128)}) custom-call(bf16[4,1024,1024]{2,1,0:T(8,128)(2,1)} %bitcast.385, s32[4,2,1024]{2,1,0:T(2,128)} %pad_add_fusion.3.target_ref, f32[4,2,1024]{2,1,0:T(2,128)} %copy.417.gate_ref, ...), custom_call_target="tpu_custom_call" | custom-call | flops 7247757312 | bytes 16777216 | tf_op jit(solution)/shard_map/attend/pallas_call | solution.py:194
  274.1 6.7 convolution_convert_fusion
  288.2 21.6 %collective-permute-done.6.refs_1_.refs_2_ = bf16[1056,512]{1,0:T(8,128)(2,1)S(1)} collective-permute-done((bf16[1056,512]{1,0:T(8,128)(2,1)}, bf16[1056,512]{1,0:T(8,128)(2,1)S(1)}, u32[]{:S(2)}, u32[]{:S(2)}) %collective-permute-start.6) | collective-permute-done | bytes 1081376 | tf_op jit(solution)/shard_map/ppermute | solution.py:444
  309.9 44.1 %collective-permute-done.7.refs_2_.refs_4_ = bf16[1056,512]{1,0:T(8,128)(2,1)} collective-permute-done((bf16[1056,512]{1,0:T(8,128)(2,1)}, bf16[1056,512]{1,0:T(8,128)(2,1)}, u32[]{:S(2)}, u32[]{:S(2)}) %collective-permute-start.7) | collective-permute-done | bytes 1081376 | tf_op jit(solution)/shard_map/ppermute | solution.py:444
  361.3 21.2 %all-to-all-start.1 = ((bf16[4,576,256]{2,1,0:T(8,128)(2,1)}), bf16[4,576,256]{2,1,0:T(8,128)(2,1)}, u32[]{:S(2)}, u32[]{:S(2)}) async-start(bf16[4,576,256]{2,1,0:T(8,128)(2,1)} %bitcast.419), calls=%async_computation.2 | async-start | bytes 2359296 | tf_op jit(solution)/shard_map/all_to_all | solution.py:431
  382.9 27.3 %all-to-all-done.1 = bf16[4,576,256]{2,1,0:T(8,128)(2,1)} async-done(((bf16[4,576,256]{2,1,0:T(8,128)(2,1)}), bf16[4,576,256]{2,1,0:T(8,128)(2,1)}, u32[]{:S(2)}, u32[]{:S(2)}) %all-to-all-start.1) | async-done | bytes 1179680 | tf_op jit(solution)/shard_map/all_to_all | solution.py:431
  413.7 46.6 %all-gather.13.cloned.1.call-done = bf16[4,1024,256]{2,1,0:T(8,128)(2,1)} async-done(((bf16[4,256,256]{2,1,0:T(8,128)(2,1)}), bf16[4,1024,256]{2,1,0:T(8,128)(2,1)}) %all-gather.13.cloned.1.call-update) | async-done | bytes 2097168 | tf_op jit(solution)/shard_map/all_gather | solution.py:423
  464.4 24.7 %collective-permute-done.9.refs_3_.refs_1_ = bf16[1056,512]{1,0:T(8,128)(2,1)S(1)} collective-permute-done((bf16[1056,512]{1,0:T(8,128)(2,1)S(1)}, bf16[1056,512]{1,0:T(8,128)(2,1)S(1)}, u32[]{:S(2)}, u32[]{:S(2)}) %collective-permute-start.9) | collective-permute-done | bytes 1081376 | tf_op jit(solution)/shard_map/ppermute | solution.py:444
  490.1 44.2 %collective-permute-done.10.refs_5_.refs_2_ = bf16[1056,512]{1,0:T(8,128)(2,1)S(1)} collective-permute-done((bf16[1056,512]{1,0:T(8,128)(2,1)}, bf16[1056,512]{1,0:T(8,128)(2,1)S(1)}, u32[]{:S(2)}, u32[]{:S(2)}) %collective-permute-start.10) | collective-permute-done | bytes 1081376 | tf_op jit(solution)/shard_map/ppermute | solution.py:444
  536.3 17.6 %all-gather.15.cloned.1.call-done = bf16[4,1024,2048]{2,1,0:T(8,128)(2,1)} async-done(((bf16[4,1024,256]{2,1,0:T(8,128)(2,1)}), bf16[4,1024,2048]{2,1,0:T(8,128)(2,1)}) %all-gather.15.cloned.1.call-update) | async-done | bytes 16777232 | tf_op jit(solution)/shard_map/all_gather | solution.py:427
  566.4 22.6 %dispatch.1 = (bf16[4,288,2048]{2,1,0:T(8,128)(2,1)}, bf16[4,288,2048]{2,1,0:T(8,128)(2,1)}, f32[4,1024,1]{2,1,0:T(8,128)}, f32[4,1024,8]{2,1,0:T(8,128)}) custom-call(bf16[4,1024,2048]{2,1,0:T(8,128)(2,1)} %all-gather.15.cloned.1.call-done, s32[4,2,1024]{2,1,0:T(2,128)} %pad_add_fusion.6.target_ref, f32[1,2048]{1,0:T(1,128)} %bitcast.477, ...), custom_call_target="tpu_custom_call" | custom-call | bytes 16777216 | tf_op jit(solution)/shard_map/dispatch/pallas_call | solution.py:356
  609.9 29.0 %expert_step.2 = (bf16[1152,704]{1,0:T(8,128)(2,1)}, bf16[1152,704]{1,0:T(8,128)(2,1)}, bf16[1152,704]{1,0:T(8,128)(2,1)}, bf16[1152,2048]{1,0:T(8,128)(2,1)}, f32[1152,2]{1,0:T(8,128)}) custom-call(bf16[1152,2048]{1,0:T(8,128)(2,1)} %bitcast.411, bf16[1152,2048]{1,0:T(8,128)(2,1)} %all-gather.17.cloned.1.call-done.grad_ref, f32[1152,1]{1,0:T(8,128)} %reshape.663.weight_ref, ...), custom_call_target="tpu_custom_call" | custom-call | bytes 8650752 | tf_op jit(solution)/shard_map/expert_step/pallas_call | solution.py:406
  640.5 15.3 %collective-permute-done.13.refs_2_ = bf16[1408,512]{1,0:T(8,128)(2,1)} collective-permute-done((bf16[1408,512]{1,0:T(8,128)(2,1)}, bf16[1408,512]{1,0:T(8,128)(2,1)}, u32[]{:S(2)}, u32[]{:S(2)}) %collective-permute-start.13) | collective-permute-done | bytes 1441824 | tf_op jit(solution)/shard_map/ppermute | solution.py:444
  661.2 31.4 %collective-permute-start.15 = (bf16[704,512]{1,0:T(8,128)(2,1)}, bf16[704,512]{1,0:T(8,128)(2,1)S(1)}, u32[]{:S(2)}, u32[]{:S(2)}) collective-permute-start(bf16[704,512]{1,0:T(8,128)(2,1)} %get-tuple-element.185), channel_id=1, source_target_pairs={{0,8},{8,16},{16,24},{24,0},{1,9},{9,17},{17,25},{25,1},{2,10},{10... | collective-permute-start | bytes 2162696 | tf_op jit(solution)/shard_map/ppermute | solution.py:444
  705.5 7.1 convolution_convert_fusion.8
  727.8 12.1 collective-permute-done.16.refs_2_
  741.6 15.9 %collective-permute-start.18 = (bf16[352,512]{1,0:T(8,128)(2,1)}, bf16[352,512]{1,0:T(8,128)(2,1)S(1)}, u32[]{:S(2)}, u32[]{:S(2)}) collective-permute-start(bf16[352,512]{1,0:T(8,128)(2,1)} %get-tuple-element.201), channel_id=1, source_target_pairs={{0,8},{8,16},{16,24},{24,0},{1,9},{9,17},{17,25},{25,1},{2,10},{10... | collective-permute-start | bytes 1081352 | tf_op jit(solution)/shard_map/ppermute | solution.py:444
  764.6 28.9 %expert_step.3 = (bf16[1152,704]{1,0:T(8,128)(2,1)}, bf16[1152,704]{1,0:T(8,128)(2,1)}, bf16[1152,704]{1,0:T(8,128)(2,1)}, bf16[1152,2048]{1,0:T(8,128)(2,1)}, f32[1152,2]{1,0:T(8,128)}) custom-call(bf16[1152,2048]{1,0:T(8,128)(2,1)} %bitcast.406, bf16[1152,2048]{1,0:T(8,128)(2,1)} %all-gather.19.cloned.1.call-done.grad_ref, f32[1152,1]{1,0:T(8,128)} %reshape.664.weight_ref, ...), custom_call_target="tpu_custom_call" | custom-call | bytes 8650752 | tf_op jit(solution)/shard_map/expert_step/pallas_call | solution.py:406
  814.4 42.0 %reduce-scatter.11.cloned.1.call-done = bf16[1168,256]{1,0:T(8,128)(2,1)} async-done(((bf16[1168,2048]{1,0:T(8,128)(2,1)}), bf16[1168,256]{1,0:T(8,128)(2,1)}) %reduce-scatter.11.cloned.1.call-update) | async-done | bytes 598032 | tf_op jit(solution)/shard_map/reduce_scatter | solution.py:538
  860.5 14.6 all-to-all-start.2
  885.9 18.3 %all-to-all-done.2 = bf16[4,582,256]{2,1,0:T(8,128)(2,1)S(1)} async-done(((bf16[4,582,256]{2,1,0:T(8,128)(2,1)}), bf16[4,582,256]{2,1,0:T(8,128)(2,1)S(1)}, u32[]{:S(2)}, u32[]{:S(2)}) %all-to-all-start.2) | async-done | bytes 1191968 | tf_op jit(solution)/shard_map/all_to_all | solution.py:431
  914.6 7.5 convolution_convert_fusion.1
  922.1 8.3 convolution_convert_fusion.5
  930.4 6.5 convolution_convert_fusion.4
  942.3 18.1 %all-gather.21.cloned.1.call-done = bf16[4,1024,256]{2,1,0:T(8,128)(2,1)} async-done(((bf16[4,256,256]{2,1,0:T(8,128)(2,1)}), bf16[4,1024,256]{2,1,0:T(8,128)(2,1)}) %all-gather.21.cloned.1.call-update) | async-done | bytes 2097168 | tf_op jit(solution)/shard_map/all_gather | solution.py:423
  978.9 19.4 %collective-permute-done.24.refs_5_.refs_2_ = bf16[1056,512]{1,0:T(8,128)(2,1)S(1)} collective-permute-done((bf16[1056,512]{1,0:T(8,128)(2,1)}, bf16[1056,512]{1,0:T(8,128)(2,1)S(1)}, u32[]{:S(2)}, u32[]{:S(2)}) %collective-permute-start.24) | collective-permute-done | bytes 1081376 | tf_op jit(solution)/shard_map/ppermute | solution.py:444
  998.3 45.3 %collective-permute-done.25.refs_9_.refs_4_ = bf16[1056,512]{1,0:T(8,128)(2,1)} collective-permute-done((bf16[1056,512]{1,0:T(8,128)(2,1)}, bf16[1056,512]{1,0:T(8,128)(2,1)}, u32[]{:S(2)}, u32[]{:S(2)}) %collective-permute-start.25) | collective-permute-done | bytes 1081376 | tf_op jit(solution)/shard_map/ppermute | solution.py:444
  1043.6 10.5 all-gather.23.cloned.1.call-done
  1056.2 12.2 collective-permute-start.27
  1070.8 17.2 %fusion.67 = f32[4096,512]{1,0:T(8,128)} fusion(bf16[4096,2048]{1,0:T(8,128)(2,1)} %bitcast.485, bf16[512,2048]{1,0:T(8,128)(2,1)} %copy-done.46), kind=kOutput, calls=%fused_computation.370 | convolution fusion | flops 8589934592 | bytes 27262976 | tf_op jit(solution)/shard_map/rd,fd->rf/dot_general | solution.py:20
  1087.9 44.0 %attend_back.1 = (bf16[4,1024,1024]{2,1,0:T(8,128)(2,1)}, f32[4,1024,3]{2,1,0:T(8,128)}) custom-call(bf16[4,1024,1024]{2,1,0:T(8,128)(2,1)} %bitcast.386, s32[4,2,1024]{2,1,0:T(2,128)} %pad_add_fusion.3.target_ref, s32[4,1,1024]{2,1,0:T(1,128)} %reshape.611.kblk_ref, f32[4,2,576,1]{3,2,1,0:T(8,128)} %get-tuple-element.220.lse_ref, ...), custom_call_target="tpu_custom_call" | custom-call | bytes 16777216 | tf_op jit(solution)/shard_map/attend_back/pallas_call | solution.py:277
  1136.5 23.9 %spread.1 = bf16[16,272,2048]{2,1,0:T(8,128)(2,1)} custom-call(bf16[16,256,1024]{2,1,0:T(8,128)(2,1)} %bitcast.392, bf16[2048,1024]{1,0:T(8,128)(2,1)S(1)} %copy-done.1, bf16[16,16,256]{2,1,0:T(8,128)(2,1)S(1)} %bitcast.378), custom_call_target="tpu_custom_call" | custom-call | bytes 17825792 | tf_op jit(solution)/shard_map/spread/pallas_call | solution.py:521
  1173.4 17.0 %collective-permute-done.30.refs_7_.refs_3_ = bf16[1056,512]{1,0:T(8,128)(2,1)S(1)} collective-permute-done((bf16[1056,512]{1,0:T(8,128)(2,1)}, bf16[1056,512]{1,0:T(8,128)(2,1)S(1)}, u32[]{:S(2)}, u32[]{:S(2)}) %collective-permute-start.30) | collective-permute-done | bytes 1081376 | tf_op jit(solution)/shard_map/ppermute | solution.py:444
  1190.4 14.0 convolution_convert_fusion.10
  1209.6 24.5 %convolution_convert_fusion.3 = bf16[2048,1024]{1,0:T(8,128)(2,1)} fusion(bf16[4096,2048]{1,0:T(8,128)(2,1)} %get-tuple-element.234, bf16[4096,1024]{1,0:T(8,128)(2,1)} %bitcast.393), kind=kOutput, calls=%fused_computation.18 | convolution fusion | flops 17181966336 | bytes 29360128 | tf_op jit(solution)/shard_map/rd,rf->df/dot_general | solution.py:20
  1238.8 43.2 %collective-permute-done.31.refs_11_.refs_5_ = bf16[1056,512]{1,0:T(8,128)(2,1)} collective-permute-done((bf16[1056,512]{1,0:T(8,128)(2,1)}, bf16[1056,512]{1,0:T(8,128)(2,1)}, u32[]{:S(2)}, u32[]{:S(2)}) %collective-permute-start.31) | collective-permute-done | bytes 1081376 | tf_op jit(solution)/shard_map/ppermute | solution.py:444
  1282.8 33.5 %collective-permute-done.34.refs_2_ = bf16[512,512]{1,0:T(8,128)(2,1)S(1)} collective-permute-done((bf16[512,512]{1,0:T(8,128)(2,1)}, bf16[512,512]{1,0:T(8,128)(2,1)S(1)}, u32[]{:S(2)}, u32[]{:S(2)}) %collective-permute-start.34) | collective-permute-done | bytes 524320 | tf_op jit(solution)/shard_map/ppermute | solution.py:444
  1325.9 6.8 whole_grad.5
  1332.7 8.7 whole_grad.3
  1341.4 7.0 whole_grad.4
  1350.3 22.9 %reduce-scatter.17.cloned.1.call-done = bf16[4,272,256]{2,1,0:T(8,128)(2,1)} async-done(((bf16[4,1088,256]{2,1,0:T(8,128)(2,1)}), bf16[4,272,256]{2,1,0:T(8,128)(2,1)}) %reduce-scatter.17.cloned.1.call-update) | async-done | bytes 557072 | tf_op jit(solution)/shard_map/reduce_scatter | solution.py:959
  1402.1 54.7 %collective-permute-done.37.refs_5_ = bf16[272,1024]{1,0:T(8,128)(2,1)S(1)} collective-permute-done((bf16[272,1024]{1,0:T(8,128)(2,1)S(1)}, bf16[272,1024]{1,0:T(8,128)(2,1)S(1)}, u32[]{:S(2)}, u32[]{:S(2)}) %collective-permute-start.37) | collective-permute-done | bytes 557088 | tf_op jit(solution)/shard_map/ppermute | solution.py:444
  1456.8 9.2 all_gather.35
  (610 shorter events, 369.1 us)
Async XLA Ops:
  7.2 56.8 %all-gather.9.cloned.1.call-start = ((), (), s32[]{:S(2)}) async-start(), calls=%async_computation.10 | async-start | bytes 2785280 | tf_op jit(solution)/shard_map/all_gather | solution.py:423
  12.8 146.4 %all-gather.11.cloned.1.call-start = ((), (), s32[]{:S(2)}) async-start(), calls=%async_computation.11 | async-start | bytes 18874368 | tf_op jit(solution)/shard_map/all_gather | solution.py:427
  75.8 72.1 %collective-permute-start.1 = (bf16[4,512,256]{2,1,0:T(8,128)(2,1)}, bf16[4,512,256]{2,1,0:T(8,128)(2,1)}, u32[]{:S(2)}, u32[]{:S(2)}) collective-permute-start(bf16[4,512,256]{2,1,0:T(8,128)(2,1)} %get-tuple-element.134), channel_id=1, source_target_pairs={{0,16},{8,24},{16,0},{24,8},{1,17},{9,25},{17,1},{25,9},{2,18},{10... | collective-permute-start | bytes 3145736 | tf_op jit(solution)/shard_map/ppermute | solution.py:444
  77.3 70.6 %collective-permute-start.2 = (bf16[4,512,256]{2,1,0:T(8,128)(2,1)}, bf16[4,512,256]{2,1,0:T(8,128)(2,1)}, u32[]{:S(2)}, u32[]{:S(2)}) collective-permute-start(bf16[4,512,256]{2,1,0:T(8,128)(2,1)} %get-tuple-element.135), channel_id=1, source_target_pairs={{0,24},{8,0},{16,8},{24,16},{1,25},{9,1},{17,9},{25,17},{2,26},{10... | collective-permute-start | bytes 3145736 | tf_op jit(solution)/shard_map/ppermute | solution.py:444
  159.2 71.4 %collective-permute-start.3 = (bf16[2,256,512]{2,1,0:T(8,128)(2,1)}, bf16[2,256,512]{2,1,0:T(8,128)(2,1)}, u32[]{:S(2)}, u32[]{:S(2)}) collective-permute-start(bf16[2,256,512]{2,1,0:T(8,128)(2,1)} %get-tuple-element.137), channel_id=1, source_target_pairs={{0,8},{8,16},{16,24},{24,0},{1,9},{9,17},{17,25},{25,1},{2,10},{10... | collective-permute-start | bytes 1572872 | tf_op jit(solution)/shard_map/ppermute | solution.py:444
  174.5 56.1 %collective-permute-start.4 = (bf16[2,256,512]{2,1,0:T(8,128)(2,1)}, bf16[2,256,512]{2,1,0:T(8,128)(2,1)}, u32[]{:S(2)}, u32[]{:S(2)}) collective-permute-start(bf16[2,256,512]{2,1,0:T(8,128)(2,1)} %get-tuple-element.138), channel_id=1, source_target_pairs={{0,16},{8,24},{16,0},{24,8},{1,17},{9,25},{17,1},{25,9},{2,18},{10... | collective-permute-start | bytes 1572872 | tf_op jit(solution)/shard_map/ppermute | solution.py:444
  175.6 54.9 %collective-permute-start.5 = (bf16[2,256,512]{2,1,0:T(8,128)(2,1)}, bf16[2,256,512]{2,1,0:T(8,128)(2,1)}, u32[]{:S(2)}, u32[]{:S(2)}) collective-permute-start(bf16[2,256,512]{2,1,0:T(8,128)(2,1)} %get-tuple-element.139), channel_id=1, source_target_pairs={{0,24},{8,0},{16,8},{24,16},{1,25},{9,1},{17,9},{25,17},{2,26},{10... | collective-permute-start | bytes 1572872 | tf_op jit(solution)/shard_map/ppermute | solution.py:444
  230.6 50.3 %all-to-all-start = ((bf16[4,2,4,72,256]{4,3,2,1,0:T(8,128)(2,1)}), bf16[4,2,4,72,256]{4,3,2,1,0:T(8,128)(2,1)}, u32[]{:S(2)}, u32[]{:S(2)}) async-start(bf16[4,2,4,72,256]{4,3,2,1,0:T(8,128)(2,1)} %bitcast.417), calls=%async_computation | async-start | bytes 2359296 | tf_op jit(solution)/shard_map/all_to_all | solution.py:431
  234.9 124.0 %reduce-scatter.7.cloned.1.call-start = ((), (), s32[]{:S(2)}) async-start(), calls=%async_computation.12 | async-start | bytes 10616832 | tf_op jit(solution)/shard_map/reduce_scatter | solution.py:538
  282.9 71.1 %collective-permute-start.7 = (bf16[1056,512]{1,0:T(8,128)(2,1)}, bf16[1056,512]{1,0:T(8,128)(2,1)}, u32[]{:S(2)}, u32[]{:S(2)}) collective-permute-start(bf16[1056,512]{1,0:T(8,128)(2,1)} %get-tuple-element.151), channel_id=1, source_target_pairs={{0,16},{8,24},{16,0},{24,8},{1,17},{9,25},{17,1},{25,9},{2,18},{10... | collective-permute-start | bytes 3244040 | tf_op jit(solution)/shard_map/ppermute | solution.py:444
  285.3 68.7 %collective-permute-start.8 = (bf16[1056,512]{1,0:T(8,128)(2,1)}, bf16[1056,512]{1,0:T(8,128)(2,1)}, u32[]{:S(2)}, u32[]{:S(2)}) collective-permute-start(bf16[1056,512]{1,0:T(8,128)(2,1)} %get-tuple-element.152), channel_id=1, source_target_pairs={{0,24},{8,0},{16,8},{24,16},{1,25},{9,1},{17,9},{25,17},{2,26},{10... | collective-permute-start | bytes 3244040 | tf_op jit(solution)/shard_map/ppermute | solution.py:444
  382.4 77.9 %all-gather.13.cloned.1.call-start = ((), (), s32[]{:S(2)}) async-start(), calls=%async_computation.13 | async-start | bytes 2621440 | tf_op jit(solution)/shard_map/all_gather | solution.py:423
  413.7 140.2 %all-gather.15.cloned.1.call-start = ((), (), s32[]{:S(2)}) async-start(), calls=%async_computation.14 | async-start | bytes 18874368 | tf_op jit(solution)/shard_map/all_gather | solution.py:427
  460.4 149.5 %all-gather.17.cloned.1.call-start = ((), (), s32[]{:S(2)}) async-start(), calls=%async_computation.15 | async-start | bytes 5308416 | tf_op jit(solution)/shard_map/all_gather | solution.py:763
  460.5 73.9 %collective-permute-start.10 = (bf16[1056,512]{1,0:T(8,128)(2,1)}, bf16[1056,512]{1,0:T(8,128)(2,1)S(1)}, u32[]{:S(2)}, u32[]{:S(2)}) collective-permute-start(bf16[1056,512]{1,0:T(8,128)(2,1)} %get-tuple-element.155), channel_id=1, source_target_pairs={{0,16},{8,24},{16,0},{24,8},{1,17},{9,25},{17,1},{25,9},{2,18},{10... | collective-permute-start | bytes 3244040 | tf_op jit(solution)/shard_map/ppermute | solution.py:444
  462.2 73.2 %collective-permute-start.11 = (bf16[1056,512]{1,0:T(8,128)(2,1)}, bf16[1056,512]{1,0:T(8,128)(2,1)S(1)}, u32[]{:S(2)}, u32[]{:S(2)}) collective-permute-start(bf16[1056,512]{1,0:T(8,128)(2,1)} %get-tuple-element.156), channel_id=1, source_target_pairs={{0,24},{8,0},{16,8},{24,16},{1,25},{9,1},{17,9},{25,17},{2,26},{10... | collective-permute-start | bytes 3244040 | tf_op jit(solution)/shard_map/ppermute | solution.py:444
  556.2 208.4 %all-gather.19.cloned.1.call-start = ((), (), s32[]{:S(2)}) async-start(), calls=%async_computation.16 | async-start | bytes 5308416 | tf_op jit(solution)/shard_map/all_gather | solution.py:763
  557.1 254.5 %reduce-scatter.9.cloned.1.call-start = ((), (), s32[]{:S(2)}) async-start(), calls=%async_computation.17 | async-start | bytes 5382144 | tf_op jit(solution)/shard_map/reduce_scatter | solution.py:538
  557.1 83.3 %collective-permute-start.12 = (bf16[1408,512]{1,0:T(8,128)(2,1)}, bf16[1408,512]{1,0:T(8,128)(2,1)}, u32[]{:S(2)}, u32[]{:S(2)}) collective-permute-start(bf16[1408,512]{1,0:T(8,128)(2,1)} %get-tuple-element.180), channel_id=1, source_target_pairs={{0,8},{8,16},{16,24},{24,0},{1,9},{9,17},{17,25},{25,1},{2,10},{10... | collective-permute-start | bytes 4325384 | tf_op jit(solution)/shard_map/ppermute | solution.py:444
  561.6 94.1 %collective-permute-start.13 = (bf16[1408,512]{1,0:T(8,128)(2,1)}, bf16[1408,512]{1,0:T(8,128)(2,1)}, u32[]{:S(2)}, u32[]{:S(2)}) collective-permute-start(bf16[1408,512]{1,0:T(8,128)(2,1)} %get-tuple-element.181), channel_id=1, source_target_pairs={{0,16},{8,24},{16,0},{24,8},{1,17},{9,25},{17,1},{25,9},{2,18},{10... | collective-permute-start | bytes 4325384 | tf_op jit(solution)/shard_map/ppermute | solution.py:444
  563.4 92.4 %collective-permute-start.14 = (bf16[1408,512]{1,0:T(8,128)(2,1)}, bf16[1408,512]{1,0:T(8,128)(2,1)}, u32[]{:S(2)}, u32[]{:S(2)}) collective-permute-start(bf16[1408,512]{1,0:T(8,128)(2,1)} %get-tuple-element.182), channel_id=1, source_target_pairs={{0,24},{8,0},{16,8},{24,16},{1,25},{9,1},{17,9},{25,17},{2,26},{10... | collective-permute-start | bytes 4325384 | tf_op jit(solution)/shard_map/ppermute | solution.py:444
  661.1 195.4 %reduce-scatter.11.cloned.1.call-start = ((), (), s32[]{:S(2)}) async-start(), calls=%async_computation.18 | async-start | bytes 5382144 | tf_op jit(solution)/shard_map/reduce_scatter | solution.py:538
  661.2 66.6 %collective-permute-start.15 = (bf16[704,512]{1,0:T(8,128)(2,1)}, bf16[704,512]{1,0:T(8,128)(2,1)S(1)}, u32[]{:S(2)}, u32[]{:S(2)}) collective-permute-start(bf16[704,512]{1,0:T(8,128)(2,1)} %get-tuple-element.185), channel_id=1, source_target_pairs={{0,8},{8,16},{16,24},{24,0},{1,9},{9,17},{17,25},{25,1},{2,10},{10... | collective-permute-start | bytes 2162696 | tf_op jit(solution)/shard_map/ppermute | solution.py:444
  741.6 53.4 %collective-permute-start.18 = (bf16[352,512]{1,0:T(8,128)(2,1)}, bf16[352,512]{1,0:T(8,128)(2,1)S(1)}, u32[]{:S(2)}, u32[]{:S(2)}) collective-permute-start(bf16[352,512]{1,0:T(8,128)(2,1)} %get-tuple-element.201), channel_id=1, source_target_pairs={{0,8},{8,16},{16,24},{24,0},{1,9},{9,17},{17,25},{25,1},{2,10},{10... | collective-permute-start | bytes 1081352 | tf_op jit(solution)/shard_map/ppermute | solution.py:444
  806.3 52.4 %collective-permute-start.21 = (bf16[704,512]{1,0:T(8,128)(2,1)}, bf16[704,512]{1,0:T(8,128)(2,1)S(1)}, u32[]{:S(2)}, u32[]{:S(2)}) collective-permute-start(bf16[704,512]{1,0:T(8,128)(2,1)} %pad_maximum_fusion.42), channel_id=1, source_target_pairs={{0,8},{8,16},{16,24},{24,0},{1,9},{9,17},{17,25},{25,1},{2,10},{10... | collective-permute-start | bytes 2162696 | tf_op jit(solution)/shard_map/ppermute | solution.py:444
  808.3 50.4 %collective-permute-start.22 = (bf16[704,512]{1,0:T(8,128)(2,1)}, bf16[704,512]{1,0:T(8,128)(2,1)S(1)}, u32[]{:S(2)}, u32[]{:S(2)}) collective-permute-start(bf16[704,512]{1,0:T(8,128)(2,1)} %pad_maximum_fusion.43), channel_id=1, source_target_pairs={{0,16},{8,24},{16,0},{24,8},{1,17},{9,25},{17,1},{25,9},{2,18},{10... | collective-permute-start | bytes 2162696 | tf_op jit(solution)/shard_map/ppermute | solution.py:444
  808.6 50.1 %collective-permute-start.23 = (bf16[704,512]{1,0:T(8,128)(2,1)}, bf16[704,512]{1,0:T(8,128)(2,1)S(1)}, u32[]{:S(2)}, u32[]{:S(2)}) collective-permute-start(bf16[704,512]{1,0:T(8,128)(2,1)} %pad_maximum_fusion.44), channel_id=1, source_target_pairs={{0,24},{8,0},{16,8},{24,16},{1,25},{9,1},{17,9},{25,17},{2,26},{10... | collective-permute-start | bytes 2162696 | tf_op jit(solution)/shard_map/ppermute | solution.py:444
  875.1 85.3 %all-gather.21.cloned.1.call-start = ((), (), s32[]{:S(2)}) async-start(), calls=%async_computation.19 | async-start | bytes 2621440 | tf_op jit(solution)/shard_map/all_gather | solution.py:423
  914.5 139.6 %all-gather.23.cloned.1.call-start = ((), (), s32[]{:S(2)}) async-start(), calls=%async_computation.20 | async-start | bytes 18874368 | tf_op jit(solution)/shard_map/all_gather | solution.py:427
  960.4 200.0 %reduce-scatter.13.cloned.1.call-start = ((), (), s32[]{:S(2)}) async-start(), calls=%async_computation.21 | async-start | bytes 10616832 | tf_op jit(solution)/shard_map/reduce_scatter | solution.py:538
  969.4 74.2 %collective-permute-start.25 = (bf16[1056,512]{1,0:T(8,128)(2,1)}, bf16[1056,512]{1,0:T(8,128)(2,1)}, u32[]{:S(2)}, u32[]{:S(2)}) collective-permute-start(bf16[1056,512]{1,0:T(8,128)(2,1)} %pad_maximum_fusion.31), channel_id=1, source_target_pairs={{0,16},{8,24},{16,0},{24,8},{1,17},{9,25},{17,1},{25,9},{2,18},{10... | collective-permute-start | bytes 3244040 | tf_op jit(solution)/shard_map/ppermute | solution.py:444
  971.1 72.5 %collective-permute-start.26 = (bf16[1056,512]{1,0:T(8,128)(2,1)}, bf16[1056,512]{1,0:T(8,128)(2,1)}, u32[]{:S(2)}, u32[]{:S(2)}) collective-permute-start(bf16[1056,512]{1,0:T(8,128)(2,1)} %pad_maximum_fusion.32), channel_id=1, source_target_pairs={{0,24},{8,0},{16,8},{24,16},{1,25},{9,1},{17,9},{25,17},{2,26},{10... | collective-permute-start | bytes 3244040 | tf_op jit(solution)/shard_map/ppermute | solution.py:444
  1054.2 262.9 %reduce-scatter.15.cloned.1.call-start = ((), (), s32[]{:S(2)}) async-start(), calls=%async_computation.22 | async-start | bytes 20054016 | tf_op jit(solution)/shard_map/reduce_scatter | solution.py:954
  1056.2 104.2 %collective-permute-start.27 = (bf16[1056,512]{1,0:T(8,128)(2,1)}, bf16[1056,512]{1,0:T(8,128)(2,1)S(1)}, u32[]{:S(2)}, u32[]{:S(2)}) collective-permute-start(bf16[1056,512]{1,0:T(8,128)(2,1)} %pad_maximum_fusion.34), channel_id=1, source_target_pairs={{0,8},{8,16},{16,24},{24,0},{1,9},{9,17},{17,25},{25,1},{2,10},{10... | collective-permute-start | bytes 3244040 | tf_op jit(solution)/shard_map/ppermute | solution.py:444
  1068.4 92.0 %collective-permute-start.28 = (bf16[1056,512]{1,0:T(8,128)(2,1)}, bf16[1056,512]{1,0:T(8,128)(2,1)}, u32[]{:S(2)}, u32[]{:S(2)}) collective-permute-start(bf16[1056,512]{1,0:T(8,128)(2,1)} %pad_maximum_fusion.35), channel_id=1, source_target_pairs={{0,16},{8,24},{16,0},{24,8},{1,17},{9,25},{17,1},{25,9},{2,18},{10... | collective-permute-start | bytes 3244040 | tf_op jit(solution)/shard_map/ppermute | solution.py:444
  1069.4 91.0 %collective-permute-start.29 = (bf16[1056,512]{1,0:T(8,128)(2,1)}, bf16[1056,512]{1,0:T(8,128)(2,1)}, u32[]{:S(2)}, u32[]{:S(2)}) collective-permute-start(bf16[1056,512]{1,0:T(8,128)(2,1)} %pad_maximum_fusion.36), channel_id=1, source_target_pairs={{0,24},{8,0},{16,8},{24,16},{1,25},{9,1},{17,9},{25,17},{2,26},{10... | collective-permute-start | bytes 3244040 | tf_op jit(solution)/shard_map/ppermute | solution.py:444
  1164.7 71.7 %all-to-all-start.3 = ((bf16[4,576,256]{2,1,0:T(8,128)(2,1)}), bf16[4,576,256]{2,1,0:T(8,128)(2,1)}, u32[]{:S(2)}, u32[]{:S(2)}) async-start(bf16[4,576,256]{2,1,0:T(8,128)(2,1)} %bitcast.418), calls=%async_computation.7 | async-start | bytes 2359296 | tf_op jit(solution)/shard_map/all_to_all | solution.py:431
  1169.1 204.2 %reduce-scatter.17.cloned.1.call-start = ((), (), s32[]{:S(2)}) async-start(), calls=%async_computation.23 | async-start | bytes 2785280 | tf_op jit(solution)/shard_map/reduce_scatter | solution.py:959
  1169.1 112.9 %collective-permute-start.31 = (bf16[1056,512]{1,0:T(8,128)(2,1)}, bf16[1056,512]{1,0:T(8,128)(2,1)}, u32[]{:S(2)}, u32[]{:S(2)}) collective-permute-start(bf16[1056,512]{1,0:T(8,128)(2,1)} %pad_maximum_fusion.39), channel_id=1, source_target_pairs={{0,16},{8,24},{16,0},{24,8},{1,17},{9,25},{17,1},{25,9},{2,18},{10... | collective-permute-start | bytes 3244040 | tf_op jit(solution)/shard_map/ppermute | solution.py:444
  1171.9 110.1 %collective-permute-start.32 = (bf16[1056,512]{1,0:T(8,128)(2,1)}, bf16[1056,512]{1,0:T(8,128)(2,1)}, u32[]{:S(2)}, u32[]{:S(2)}) collective-permute-start(bf16[1056,512]{1,0:T(8,128)(2,1)} %pad_maximum_fusion.40), channel_id=1, source_target_pairs={{0,24},{8,0},{16,8},{24,16},{1,25},{9,1},{17,9},{25,17},{2,26},{10... | collective-permute-start | bytes 3244040 | tf_op jit(solution)/shard_map/ppermute | solution.py:444
  1205.8 76.2 %collective-permute-start.33 = (bf16[512,512]{1,0:T(8,128)(2,1)}, bf16[512,512]{1,0:T(8,128)(2,1)S(1)}, u32[]{:S(2)}, u32[]{:S(2)}) collective-permute-start(bf16[512,512]{1,0:T(8,128)(2,1)} %get-tuple-element.238), channel_id=1, source_target_pairs={{0,8},{8,16},{16,24},{24,0},{1,9},{9,17},{17,25},{25,1},{2,10},{10... | collective-permute-start | bytes 1572872 | tf_op jit(solution)/shard_map/ppermute | solution.py:444
  1205.8 110.5 %collective-permute-start.34 = (bf16[512,512]{1,0:T(8,128)(2,1)}, bf16[512,512]{1,0:T(8,128)(2,1)S(1)}, u32[]{:S(2)}, u32[]{:S(2)}) collective-permute-start(bf16[512,512]{1,0:T(8,128)(2,1)} %get-tuple-element.239), channel_id=1, source_target_pairs={{0,16},{8,24},{16,0},{24,8},{1,17},{9,25},{17,1},{25,9},{2,18},{10... | collective-permute-start | bytes 1572872 | tf_op jit(solution)/shard_map/ppermute | solution.py:444
  1207.2 109.9 %collective-permute-start.35 = (bf16[512,512]{1,0:T(8,128)(2,1)}, bf16[512,512]{1,0:T(8,128)(2,1)}, u32[]{:S(2)}, u32[]{:S(2)}) collective-permute-start(bf16[512,512]{1,0:T(8,128)(2,1)} %get-tuple-element.240), channel_id=1, source_target_pairs={{0,24},{8,0},{16,8},{24,16},{1,25},{9,1},{17,9},{25,17},{2,26},{10... | collective-permute-start | bytes 1572872 | tf_op jit(solution)/shard_map/ppermute | solution.py:444
  1384.7 72.1 %collective-permute-start.37 = (bf16[272,1024]{1,0:T(8,128)(2,1)S(1)}, bf16[272,1024]{1,0:T(8,128)(2,1)S(1)}, u32[]{:S(2)}, u32[]{:S(2)}) collective-permute-start(bf16[272,1024]{1,0:T(8,128)(2,1)S(1)} %get-tuple-element.391), channel_id=1, source_target_pairs={{0,16},{8,24},{16,0},{24,8},{1,17},{9,25},{17,1},{25,9},{2,18},{10... | collective-permute-start | bytes 1671176 | tf_op jit(solution)/shard_map/ppermute | solution.py:444
  1385.1 71.7 %collective-permute-start.36 = (bf16[272,1024]{1,0:T(8,128)(2,1)S(1)}, bf16[272,1024]{1,0:T(8,128)(2,1)S(1)}, u32[]{:S(2)}, u32[]{:S(2)}) collective-permute-start(bf16[272,1024]{1,0:T(8,128)(2,1)S(1)} %get-tuple-element.393), channel_id=1, source_target_pairs={{0,8},{8,16},{16,24},{24,0},{1,9},{9,17},{17,25},{25,1},{2,10},{10... | collective-permute-start | bytes 1671176 | tf_op jit(solution)/shard_map/ppermute | solution.py:444
  1392.5 74.8 %collective-permute-start.39 = (bf16[256,1024]{1,0:T(8,128)(2,1)}, bf16[256,1024]{1,0:T(8,128)(2,1)S(1)}, u32[]{:S(2)}, u32[]{:S(2)}) collective-permute-start(bf16[256,1024]{1,0:T(8,128)(2,1)} %get-tuple-element.243), channel_id=1, source_target_pairs={{0,8},{8,16},{16,24},{24,0},{1,9},{9,17},{17,25},{25,1},{2,10},{10... | collective-permute-start | bytes 1572872 | tf_op jit(solution)/shard_map/ppermute | solution.py:444
  1393.6 74.5 %collective-permute-start.40 = (bf16[256,1024]{1,0:T(8,128)(2,1)}, bf16[256,1024]{1,0:T(8,128)(2,1)}, u32[]{:S(2)}, u32[]{:S(2)}) collective-permute-start(bf16[256,1024]{1,0:T(8,128)(2,1)} %get-tuple-element.244), channel_id=1, source_target_pairs={{0,16},{8,24},{16,0},{24,8},{1,17},{9,25},{17,1},{25,9},{2,18},{10... | collective-permute-start | bytes 1572872 | tf_op jit(solution)/shard_map/ppermute | solution.py:444
  1397.8 70.2 %collective-permute-start.41 = (bf16[256,1024]{1,0:T(8,128)(2,1)}, bf16[256,1024]{1,0:T(8,128)(2,1)}, u32[]{:S(2)}, u32[]{:S(2)}) collective-permute-start(bf16[256,1024]{1,0:T(8,128)(2,1)} %get-tuple-element.245), channel_id=1, source_target_pairs={{0,24},{8,0},{16,8},{24,16},{1,25},{9,1},{17,9},{25,17},{2,26},{10... | collective-permute-start | bytes 1572872 | tf_op jit(solution)/shard_map/ppermute | solution.py:444
  (134 other events, 1303.0 us)
Sparse Core Ops, SparseCore 0:
  12.9 50.9 all-gather.8
  67.2 91.9 all-gather.10
  281.0 77.8 reduce-scatter.6
  413.8 46.4 all-gather.12
  462.0 91.8 all-gather.14
  556.3 42.9 all-gather.16
  601.1 39.7 all-gather.18
  661.2 86.2 reduce-scatter.8
  800.6 55.8 reduce-scatter.10
  914.6 45.7 all-gather.20
  962.3 91.8 all-gather.22
  1058.1 82.9 reduce-scatter.12
  1161.5 120.8 reduce-scatter.14
  1317.3 55.9 reduce-scatter.16
